TPU v7x, 32 devices: a whole 2x2x4 slice. The times are simulated.
32 devices in a mesh: rows: 8 (over z, core), cols: 4 (over y, x).
Axes of the slice: x: 2, y: 2, z: 4, core: 2. Of those that a mesh axis runs over, the one named last changes fastest.
Arguments:
- matrix: float32 [32768, 4096], P('rows', 'cols'), may hold values from -80 to 80
- mixers: float32 [8, 128, 128], replicated, may hold values from -0.001953125 to 0.001953125
- bucket_pair: int32 [256, 2], P('rows'), may hold values from 0 to 63, all different within a row; in each aligned block of 32 rows (0 to 31, 32 to 63, ...) at most 2 rows name the same one
- mixer_index: int32 [256], P('rows'), may hold values from 0 to 7
- sign_seed: int32 [256], P('rows'), may hold values from 0 to 1073741823
Outputs:
- projected: float32 [256, 4096], P('rows', 'cols')
Inputs may be any that keep to these rules, and one draw needn't show every extreme that they name: `bucket_pair`: the two buckets of a tile differ; among the 32 tiles of one device no bucket is named more than 2 times, a bound that some block reaches.
All inputs are finite; a program needn't handle non-finite values.
Results may differ from a plain program's by a relative error of at most 0.0012.
Values may be sent and summed in bfloat16 or wider, within the bound.
No kernel may reach another device: no remote copies, remote signals or barrier semaphores. Data moves between devices by JAX's collectives and lax.ppermute only.
A program may use at most 128 MiB of HBM per device.

v0:
```python
import jax
import jax.numpy as jnp
from jax import lax
from jax.sharding import PartitionSpec as P

TILE = 128
P_SIZE = 256
MOST = 2
NB = 64


def spread(value, axis, root):
    mine = lax.axis_index(axis) == root
    return lax.psum(jnp.where(mine, value, jnp.zeros_like(value)), axis)


def row_signs(seed_vals):
    position = jnp.arange(TILE, dtype=jnp.int32)
    hashed = (seed_vals[:, None] ^ position[None, :] * 40503) * 69069
    hashed_bit = hashed >> 16 & 1
    return (1 - 2 * hashed_bit).astype(jnp.float32)


def tile_flips(seed_vals):
    return (1 - 2 * (seed_vals >> 29 & 1)).astype(jnp.float32)


def local(matrix, mixers, bucket_pair, mixer_index, sign_seed):
    col_width = matrix.shape[1]
    tile_count = bucket_pair.shape[0]
    blocks = matrix.reshape(tile_count, TILE, col_width)
    row_sign = row_signs(sign_seed)
    tile_flip = tile_flips(sign_seed).astype(jnp.bfloat16)
    chosen = mixers[mixer_index]
    mixed_tiles = jnp.einsum(
        "tij,tjc->tic",
        chosen,
        row_sign[:, :, None] * blocks,
        precision=lax.Precision.HIGHEST,
        preferred_element_type=jnp.float32,
    ).astype(jnp.bfloat16)
    contrib = jnp.concatenate(
        [mixed_tiles, mixed_tiles * tile_flip[:, None, None]], axis=0
    ).reshape(2 * tile_count, TILE * col_width)
    target = jnp.concatenate([bucket_pair[:, 0], bucket_pair[:, 1]])
    order_pos = jnp.arange(2 * tile_count, dtype=jnp.int32)
    earlier = (target[None, :] == target[:, None]) & (order_pos[None, :] < order_pos[:, None])
    slot_rank = jnp.sum(earlier.astype(jnp.int32), axis=1)
    placement = target * MOST + slot_rank
    select = (jnp.arange(NB * MOST, dtype=jnp.int32)[:, None] == placement[None, :]).astype(
        jnp.bfloat16
    )
    buffer = jnp.dot(select, contrib, preferred_element_type=jnp.float32).astype(jnp.bfloat16)
    buffer = buffer.reshape(1, NB, MOST, TILE, col_width)
    arrived = lax.all_to_all(buffer, "rows", split_axis=1, concat_axis=0, tiled=True)
    received = jnp.sum(arrived, axis=(0, 2), dtype=jnp.float32)
    sketch = received.reshape(-1, col_width)
    panel_cols = sketch[:, :P_SIZE]
    row_parts = lax.axis_size("rows")
    panel_owner = spread(panel_cols, "cols", 0)
    gram_part = jnp.dot(
        panel_owner.T,
        panel_owner,
        precision=lax.Precision.HIGHEST,
        preferred_element_type=jnp.float32,
    )
    cross_part = jnp.dot(
        panel_owner.T, sketch, precision=lax.Precision.HIGHEST, preferred_element_type=jnp.float32
    )
    gram_total, cross_total = lax.psum((gram_part, cross_part), "rows")
    factor = jnp.linalg.cholesky(gram_total)
    solved = lax.linalg.triangular_solve(factor, cross_total, left_side=True, lower=True)
    share = P_SIZE // row_parts
    return lax.dynamic_slice_in_dim(solved, lax.axis_index("rows") * share, share, 0)


def solution(mesh):
    in_specs = (P("rows", "cols"), P(), P("rows", None), P("rows"), P("rows"))
    out_specs = P("rows", "cols")
    return jax.shard_map(local, mesh=mesh, in_specs=in_specs, out_specs=out_specs, check_vma=False)
```

profile of v0, /device:TPU:0, one launch (start us, length us, event | category | flops | bytes accessed | tf_op | source)
XLA Modules:
  0.0 1083.2 jit_solution(4320895893330918784)
XLA Ops:
  6.5 0.0 copy-start
  6.5 0.8 slice_bitcast_fusion.5
  7.3 0.1 pad_add_fusion
  7.4 0.2 convert_reduce_fusion.1
  7.6 0.1 multiply_add_fusion
  7.6 0.7 compare_select_fusion
  8.3 0.7 convert_convert_fusion
  9.0 0.7 subtract_convert_fusion
  9.7 0.0 copy-done
  9.7 0.7 gather_fusion
  10.4 22.2 %broadcast_multiply_fusion = (bf16[32,128,1024]{2,1,0:T(8,128)(2,1)}, bf16[32,128,1024]{2,1,0:T(8,128)(2,1)}) fusion(bf16[32]{0:T(256)(128)(2,1)S(1)} %convert_convert_fusion, f32[32,128,128]{2,1,0:T(8,128)S(1)} %gather_fusion, f32[32,128,1024]{2,1,0:T(8,128)} %bitcast.58, f32[32,128]{1,0:T(8,128)S(1)} %subtract_convert_fusion), kind=kOutput, calls=%fused_computation.10 | convolution fusion | flops 6455033856 | bytes 35668032 | tf_op jit(solution)/shard_map/tij,tjc->tic/dot_general | solution.py:35
  32.6 8.0 pad_maximum_fusion
  40.6 11.1 %copy.15 = bf16[8,8,128,1024]{3,1,2,0:T(8,128)(2,1)} copy(bf16[8,8,128,1024]{3,2,1,0:T(8,128)(2,1)S(1)} %bitcast.55) | data formatting | bytes 33554432
  51.7 23.2 %convolution_convert_fusion = bf16[128,131072]{1,0:T(8,128)(2,1)} fusion(bf16[64,131072]{1,0:T(8,128)(2,1)} %bitcast.54, s32[64]{0:T(128)S(1)} %multiply_add_fusion), kind=kOutput, calls=%fused_computation.3 | convolution fusion | flops 2164269056 | bytes 50331904 | tf_op jit(solution)/shard_map/dot_general | solution.py:53
  74.9 30.7 %copy.16 = bf16[16,8,128,1024]{3,2,1,0:T(8,128)(2,1)} copy(bf16[16,8,128,1024]{3,1,2,0:T(8,128)(2,1)} %bitcast.51) | data formatting | bytes 67108864
  105.6 7.1 all-to-all-start
  112.6 0.0 all-reduce.5.cloned.1.call-start
  112.7 724.0 %all-to-all-done = bf16[1,64,2,128,1024]{4,3,2,0,1:T(8,128)(2,1)} async-done(((bf16[1,64,2,128,1024]{4,3,2,0,1:T(8,128)(2,1)}), bf16[1,64,2,128,1024]{4,3,2,0,1:T(8,128)(2,1)}, u32[]{:S(2)}, u32[]{:S(2)}) %all-to-all-start) | async-done | bytes 33554464 | tf_op jit(solution)/shard_map/all_to_all | solution.py:55
  836.7 32.3 %convert_reduce_fusion = f32[64,128,1024]{2,1,0:T(8,128)} fusion(bf16[1,64,2,128,1024]{4,3,2,0,1:T(8,128)(2,1)} %all-to-all-done), kind=kLoop, calls=%fused_computation.4 | loop fusion | flops 25165824 | bytes 67108864 | tf_op jit(solution)/shard_map/reduce_sum | solution.py:56
  869.0 14.6 %reduce_sum.28 = f32[8,128,1024]{2,1,0:T(8,128)} reduce(f32[8,8,128,1024]{3,2,1,0:T(8,128)} %bitcast.53, f32[]{:T(128)} %constant.102.clone.1), dimensions={0}, to_apply=%region_2.3 | reduce | flops 7340032 | bytes 37748740 | tf_op jit(solution)/shard_map/reduce_sum | solution.py:56
  883.6 2.3 slice_select_fusion
  885.8 0.0 all-reduce.5.cloned.1.call-update
  885.9 0.0 all-reduce.7.cloned.1.call-start
  885.9 52.2 %all-reduce.5.cloned.1.call-done = f32[1024,256]{1,0:T(8,128)} async-done(((f32[1024,256]{1,0:T(8,128)}), f32[1024,256]{1,0:T(8,128)}) %all-reduce.5.cloned.1.call-update) | async-done | bytes 1048592 | tf_op jit(solution)/shard_map/psum | solution.py:14
  938.1 7.1 fusion.19
  945.1 4.1 fusion.18
  949.2 0.0 all-reduce.7.cloned.1.call-update
  949.3 60.3 %all-reduce.7.cloned.1.call-done = (f32[256,1024]{1,0:T(8,128)}, f32[256,256]{0,1:T(8,128)}) async-done(((f32[256,1024]{1,0:T(8,128)}, f32[256,256]{0,1:T(8,128)}), (f32[256,1024]{1,0:T(8,128)}, f32[256,256]{0,1:T(8,128)})) %all-reduce.7.cloned.1.call-update) | async-done | bytes 1310736 | tf_op jit(solution)/shard_map/psum | solution.py:70
  1009.6 1.1 copy.13
  1010.7 1.0 fusion.8
  1011.7 11.7 %cholesky.50 = f32[128,128]{1,0:T(8,128)S(1)} custom-call(f32[128,128]{1,0:T(8,128)S(1)} %cholesky.118), custom_call_target="Cholesky" | custom-call | tf_op jit(solution)/shard_map/jit(cholesky)/cholesky | solution.py:71
  1023.5 9.8 custom-call.14
  1033.3 0.2 constant_dynamic-update-slice_fusion
  1033.5 0.3 convolution_subtract_fusion.1
  1033.8 11.9 %cholesky.105 = f32[128,128]{1,0:T(8,128)S(1)} custom-call(f32[128,128]{1,0:T(8,128)S(1)} %convolution_subtract_fusion.1), custom_call_target="Cholesky" | custom-call | tf_op jit(solution)/shard_map/jit(cholesky)/cholesky | solution.py:71
  1045.7 0.7 compare_reduce_fusion
  1047.7 0.1 triangular_solve.57
  1047.8 4.1 while.1
  1047.8 0.7 fusion.31
  1048.4 1.3 bitcast_dynamic-update-slice_fusion.2
  1049.8 0.7 fusion.31
  1050.5 1.3 bitcast_dynamic-update-slice_fusion.2
  1051.8 19.7 %custom-call.15 = f32[2,128,128]{1,2,0:T(8,128)S(1)} custom-call(f32[2,128,128]{2,1,0:T(8,128)S(1)} %get-tuple-element.12), custom_call_target="InvertDiagBlocksLowerTriangular" | custom-call | tf_op jit(solution)/shard_map/triangular_solve | solution.py:72
  1071.5 1.7 fusion.6
  1073.2 1.6 convolution_subtract_fusion
  1074.8 0.6 fusion.11
  1075.5 0.7 fusion.9
  1076.1 0.0 copy-done.1
  (12 shorter events, 0.2 us)
Async XLA Ops:
  6.5 3.2 copy-start
  105.6 731.1 %all-to-all-start = ((bf16[1,64,2,128,1024]{4,3,2,0,1:T(8,128)(2,1)}), bf16[1,64,2,128,1024]{4,3,2,0,1:T(8,128)(2,1)}, u32[]{:S(2)}, u32[]{:S(2)}) async-start(bf16[1,64,2,128,1024]{4,3,2,0,1:T(8,128)(2,1)} %bitcast.52), calls=%async_computation | async-start | bytes 67108864 | tf_op jit(solution)/shard_map/all_to_all | solution.py:55
  112.6 825.4 %all-reduce.5.cloned.1.call-start = ((), (), s32[]{:S(2)}) async-start(), calls=%async_computation.1 | async-start | bytes 2097152 | tf_op jit(solution)/shard_map/psum | solution.py:14
  869.0 207.2 %copy-start.1 = (f32[8,128,128]{2,1,0:T(8,128)S(1)}, f32[8,128,128]{2,1,0:T(8,128)}, u32[]{:S(2)}) copy-start(f32[8,128,128]{2,1,0:T(8,128)} %param.6) | copy-start | bytes 1572868
  885.9 123.8 %all-reduce.7.cloned.1.call-start = ((), (), s32[]{:S(2)}) async-start(), calls=%async_computation.2 | async-start | bytes 2621440 | tf_op jit(solution)/shard_map/psum | solution.py:70
Sparse Core Ops, SparseCore 0:
  886.0 52.0 all-reduce.4
  949.4 60.1 all-reduce.6
where the time goes:
time: 1100 us; the launch traced here: 1080 us
  waiting for transfers between devices  836 us (76%)
  other arithmetic  115 us (10%)
  matrix products  61 us (6%)
  local copies, waits for them, and re-layouts  48.4 us (4%)
  between operations  15 us (1%)
    all_to_all x1, waiting for transfers between devices, local(): lax.all_to_all(buffer, 'rows', split_axis=1, concat_axis=0, tiled=True)  724 us
    psum x1, waiting for transfers between devices, local(): gram_total, cross_total = lax.psum((gram_part, cross_part), 'rows')  60.3 us
    psum x1, waiting for transfers between devices, spread(): return lax.psum(jnp.where(mine, value, jnp.zeros_like(value)), axis)  52.2 us
    reduce_sum x2, other arithmetic, local(): received = jnp.sum(arrived, axis=(0, 2), dtype=jnp.float32)  46.9 us
    unnamed x6, local copies, waits for them, and re-layouts  41.7 us
    another operation x6, other arithmetic, local(): factor = jnp.linalg.cholesky(gram_total)  34.2 us
    dot_general x1, matrix products, local(): jnp.dot(select, contrib, preferred_element_type=jnp.float32)  23.2 us
    dot_general x1, matrix products, local(): jnp.einsum('tij,tjc->tic', chosen, row_sign[:, :, None] * blocks, precisi...  22.2 us
  transfers between devices with their start and end apart: 3, of which 3 were waited for; matrix products, arithmetic and copies ran while one was open for 0% of the time, Pallas kernels for 0%

commit v1 on v0

v1 whole, which is shorter than its diff:
```python
import functools
import jax
import jax.numpy as jnp
from jax import lax
from jax.experimental import pallas as pl
from jax.experimental.pallas import tpu as pltpu
from jax.sharding import PartitionSpec as P

TILE = 128
P_SIZE = 256
NB = 64
CHUNKS = 1
F32, BF16, F16 = jnp.float32, jnp.bfloat16, jnp.float16
HI = lax.Precision.HIGHEST
MIB = 1 << 20


def vmem():
    return pl.BlockSpec(memory_space=pltpu.VMEM)


def smem():
    return pl.BlockSpec(memory_space=pltpu.SMEM)


def params(mib):
    return pltpu.CompilerParams(vmem_limit_bytes=mib * MIB)


def cost(flops, bytes_accessed):
    return pl.CostEstimate(flops=flops, bytes_accessed=bytes_accessed, transcendentals=0)


def signed_mixer(mixers_ref, index_ref, seed_ref, tile):
    position = lax.broadcasted_iota(jnp.int32, (1, TILE), 1)
    hashed = (seed_ref[tile] ^ position * 40503) * 69069
    sign = (1 - 2 * (hashed >> 16 & 1)).astype(F32)
    return mixers_ref[index_ref[tile]] * sign


def panel_kernel(per_step, parts, width, index_ref, seed_ref, core_ref, matrix_ref, mixers_ref, *refs):
    outs, turned = refs[:-1], refs[-1]
    core = core_ref[0]
    chunk_cols = P_SIZE // CHUNKS
    for u in range(per_step):
        mixer = signed_mixer(mixers_ref, index_ref, seed_ref, pl.program_id(0) * per_step + u)
        block = matrix_ref[u * TILE : (u + 1) * TILE, :]
        turned[...] = jnp.dot(mixer, block, precision=HI, preferred_element_type=F32).T
        for h in range(CHUNKS):
            for c in range(parts):
                for s in range(2):
                    who = core if s == 0 else 1 - core
                    start = pl.multiple_of(h * chunk_cols + c * width + who * (chunk_cols // 2), width)
                    outs[h * parts + c][s, u] = turned[pl.ds(start, width), :].astype(BF16)


def mix_panel(matrix, mixers, mixer_index, sign_seed, core, parts, width):
    tiles = mixer_index.shape[0]
    per_step = 4
    spec = pl.BlockSpec((2, per_step, width, TILE), lambda i, *_: (0, i, 0, 0))
    return pl.pallas_call(
        functools.partial(panel_kernel, per_step, parts, width),
        grid_spec=pltpu.PrefetchScalarGridSpec(
            num_scalar_prefetch=3,
            grid=(tiles // per_step,),
            in_specs=[
                pl.BlockSpec((per_step * TILE, P_SIZE), lambda i, *_: (i, 0)),
                pl.BlockSpec(mixers.shape, lambda i, *_: (0, 0, 0)),
            ],
            out_specs=[spec] * (CHUNKS * parts),
            scratch_shapes=[pltpu.VMEM((P_SIZE, TILE), F32)],
        ),
        out_shape=[jax.ShapeDtypeStruct((2, tiles, width, TILE), BF16)] * (CHUNKS * parts),
        compiler_params=params(24),
        cost_estimate=cost(12 * tiles * TILE * TILE * P_SIZE, 6 * tiles * TILE * P_SIZE),
        name="mix_panel",
    )(mixer_index, sign_seed, core, matrix, mixers)


def mix_kernel(per_step, index_ref, seed_ref, matrix_ref, mixers_ref, out_ref):
    for u in range(per_step):
        mixer = signed_mixer(mixers_ref, index_ref, seed_ref, pl.program_id(0) * per_step + u)
        block = matrix_ref[u * TILE : (u + 1) * TILE, :]
        mixed = jnp.dot(mixer, block, precision=HI, preferred_element_type=F32)
        out_ref[u * TILE : (u + 1) * TILE, :] = mixed.astype(BF16)


def mix_all(matrix, mixers, mixer_index, sign_seed):
    tiles = mixer_index.shape[0]
    rows, cols = matrix.shape
    per_step = 2
    return pl.pallas_call(
        functools.partial(mix_kernel, per_step),
        grid_spec=pltpu.PrefetchScalarGridSpec(
            num_scalar_prefetch=2,
            grid=(tiles // per_step,),
            in_specs=[
                pl.BlockSpec((per_step * TILE, cols), lambda i, *_: (i, 0)),
                pl.BlockSpec(mixers.shape, lambda i, *_: (0, 0, 0)),
            ],
            out_specs=pl.BlockSpec((per_step * TILE, cols), lambda i, *_: (i, 0)),
        ),
        out_shape=jax.ShapeDtypeStruct((rows, cols), BF16),
        compiler_params=params(24),
        cost_estimate=cost(12 * rows * TILE * cols, 6 * rows * cols),
        name="mix_all",
    )(mixer_index, sign_seed, matrix, mixers)


def bucket_kernel(first_ref, second_ref, flip_ref, *refs):
    pieces, out_ref, total = refs[:-2], refs[-2], refs[-1]
    total[...] = jnp.zeros_like(total)
    for j, piece in enumerate(pieces):
        count = piece.shape[0]

        def add(i, carry):
            at = j * count + i
            value = piece[i].astype(F32)
            one, two = first_ref[at], second_ref[at]
            total[one] = total[one] + value
            total[two] = total[two] + flip_ref[at] * value
            return carry

        lax.fori_loop(0, count, add, 0, unroll=8)
    summed = total[...]
    largest = jnp.max(jnp.max(jnp.abs(summed), axis=0), axis=1, keepdims=True)
    scale = jnp.where(largest > 1e-37, 1.0 / largest, 1.0)
    out_ref[...] = summed * scale


def sum_buckets(first, second, flip, pieces):
    width = pieces[0].shape[1]
    return pl.pallas_call(
        bucket_kernel,
        in_specs=[smem()] * 3 + [vmem()] * len(pieces),
        out_specs=vmem(),
        out_shape=jax.ShapeDtypeStruct((NB, width, TILE), F32),
        scratch_shapes=[pltpu.VMEM((NB, width, TILE), F32)],
        compiler_params=params(24),
        cost_estimate=cost(10**6, 4 * 10**6),
        name="sum_buckets",
    )(first, second, flip, *pieces)


def split(value):
    high = value.astype(BF16)
    return high, (value - high.astype(F32)).astype(BF16)


def cross_kernel(parts, groups, first_ref, second_ref, flip_ref, where_ref, mine_ref, other_ref, *refs):
    pieces = refs[: CHUNKS * parts]
    outs = refs[CHUNKS * parts : CHUNKS * parts + groups]
    panel, total = refs[-2:]
    width = pieces[0].shape[1]
    half = P_SIZE // 2
    step, tiles = pl.program_id(0), 2 * pl.num_programs(0)

    @pl.when(step == 0)
    def start():
        total[...] = jnp.zeros_like(total)
        for h in range(CHUNKS):
            for j in range(parts):
                at = h * (half // CHUNKS) + (where_ref[0] ^ j) * width
                panel[:, pl.ds(pl.multiple_of(at, width), width), :] = pieces[h * parts + j][...]

    for side, mixed_ref in enumerate((mine_ref, other_ref)):
        halves = []
        for u in range(2):
            t = side * tiles + 2 * step + u
            weights = panel[first_ref[t]] + flip_ref[t] * panel[second_ref[t]]
            halves.append(split(weights))
        high = jnp.concatenate([halves[0][0], halves[1][0]], axis=1)
        low = jnp.concatenate([halves[0][1], halves[1][1]], axis=1)
        both = jnp.concatenate([high, low], axis=0)
        total[...] += jnp.dot(both, mixed_ref[...], preferred_element_type=F32)

    @pl.when(step == pl.num_programs(0) - 1)
    def finish():
        total[:half, :] = total[:half, :] + total[half:, :]
        size = total.shape[1] // groups
        for j in range(groups):
            if groups == 1:
                outs[j][...] = total[:half, :]
            else:
                group = lax.rem(where_ref[1] + j, groups)
                outs[j][...] = total[:half, pl.ds(pl.multiple_of(group * size, size), size)]


def cross_parts(first, second, flip, where, mine, other, pieces, parts, groups):
    rows, cols = mine.shape
    half = P_SIZE // 2
    block = pl.BlockSpec((2 * TILE, cols), lambda i: (i, 0))
    return pl.pallas_call(
        functools.partial(cross_kernel, parts, groups),
        grid=(rows // (2 * TILE),),
        in_specs=[smem()] * 4 + [block] * 2 + [vmem()] * len(pieces),
        out_specs=[pl.BlockSpec((half, cols // groups), lambda i: (0, 0))] * groups,
        out_shape=[jax.ShapeDtypeStruct((half, cols // groups), F32)] * groups,
        scratch_shapes=[pltpu.VMEM((NB, half, TILE), F32), pltpu.VMEM((2 * half, cols), F32)],
        compiler_params=params(32),
        cost_estimate=cost(8 * rows * half * cols, 4 * rows * cols),
        name="cross_parts",
    )(first, second, flip, where, mine, other, *pieces)


def gram_kernel(parts, where_ref, *refs):
    pieces = refs[: 2 * CHUNKS * parts]
    out_ref, panel = refs[2 * CHUNKS * parts :]
    width = pieces[0].shape[1]
    half = P_SIZE // 2
    for s in range(2):
        core = where_ref[2] if s == 0 else 1 - where_ref[2]
        for h in range(CHUNKS):
            for j in range(parts):
                at = (2 * h + core) * (half // CHUNKS) + (where_ref[0] ^ j) * width
                at = pl.ds(pl.multiple_of(at, width), width)
                panel[:, at, :] = pieces[(s * CHUNKS + h) * parts + j][...]

    def nt(a, b):
        return lax.dot_general(a, b, (((1,), (1,)), ((), ())), preferred_element_type=F32)

    def pair(i, carry):
        square, mixed = carry
        one, two = split(jnp.concatenate([panel[2 * i], panel[2 * i + 1]], axis=1))
        return square + (nt(one, one) + nt(two, two)), mixed + nt(one, two)

    zero = jnp.zeros((P_SIZE, P_SIZE), F32)
    square, mixed = lax.fori_loop(0, NB // 2, pair, (zero, zero), unroll=2)
    out_ref[...] = square + (mixed + mixed.T)


def gram_of(where, pieces, parts):
    return pl.pallas_call(
        functools.partial(gram_kernel, parts),
        in_specs=[smem()] + [vmem()] * len(pieces),
        out_specs=vmem(),
        out_shape=jax.ShapeDtypeStruct((P_SIZE, P_SIZE), F32),
        scratch_shapes=[pltpu.VMEM((NB, P_SIZE, TILE), F32)],
        compiler_params=params(32),
        cost_estimate=cost(6 * NB * TILE * P_SIZE * P_SIZE, 2 * NB * TILE * P_SIZE),
        name="gram_of",
    )(where, *pieces)


def local(matrix, mixers, bucket_pair, mixer_index, sign_seed):
    cols = matrix.shape[1]
    tiles = bucket_pair.shape[0]
    rows_n, parts = lax.axis_size("rows"), lax.axis_size("cols")
    chips = rows_n // 2
    row, part = lax.axis_index("rows"), lax.axis_index("cols")
    core, chip = row % 2, row // 2
    width = P_SIZE // (2 * CHUNKS * parts)
    swap = [(i, i ^ 1) for i in range(rows_n)]

    def shift(value, j):
        return lax.ppermute(value, "rows", [(i, (i + 2 * j) % rows_n) for i in range(rows_n)])

    def across(value, j):
        return lax.ppermute(value, "cols", [(i, i ^ j) for i in range(parts)])

    with jax.named_scope("names"):
        flips = 1 - 2 * (sign_seed >> 29 & 1)
        names = jnp.concatenate([bucket_pair, flips[:, None]], axis=1).T
        names = lax.all_gather(names, "rows")
        order = [(row - 2 * j) % rows_n ^ s for j in range(chips) for s in range(2)]
        named = names[jnp.stack(order)]
        first, second, flip = (named[:, i].reshape(-1) for i in range(3))
        flip = flip.astype(F32)
        where = jnp.stack([part, chip, core]).astype(jnp.int32)

    with jax.named_scope("panel_mix"):
        pieces = mix_panel(matrix, mixers, mixer_index, sign_seed, core[None].astype(jnp.int32), parts, width)
    mine, others = [], []
    for h in range(CHUNKS):
        with jax.named_scope("panel_spread"):
            held = pieces[h * parts]
            for j in range(1, parts):
                got = lax.ppermute(pieces[h * parts + j], "cols", [(0, j)])
                held = jnp.where(part == j, got, held)
            held = jnp.concatenate([held[0], lax.ppermute(held[1], "rows", swap)])
        with jax.named_scope("panel_rows"):
            arrived = [held] + [shift(held, j) for j in range(1, chips)]
        with jax.named_scope("panel_sum"):
            summed = sum_buckets(first, second, flip, arrived).astype(F16)
        with jax.named_scope("panel_cols"):
            all_parts = [summed] + [across(summed, j) for j in range(1, parts)]
            mine += [v.astype(F32) for v in all_parts]
            others += [lax.ppermute(v, "rows", swap).astype(F32) for v in all_parts]

    with jax.named_scope("mix"):
        mixed = mix_all(matrix, mixers, mixer_index, sign_seed)
        mixed_other = lax.ppermute(mixed, "rows", swap)

    fast = cols % (TILE * rows_n) == 0
    with jax.named_scope("cross"):
        crossed = cross_parts(
            first[: 2 * tiles], second[: 2 * tiles], flip[: 2 * tiles], where, mixed, mixed_other, mine, parts, chips if fast else 1
        )
    with jax.named_scope("gram"):
        gram = gram_of(where, mine + others, parts)
    with jax.named_scope("factor"):
        lower = jnp.linalg.cholesky(gram)
        inverse = lax.linalg.triangular_solve(lower, jnp.eye(P_SIZE, dtype=F32), left_side=True, lower=True)

    def both_cores(own, other):
        low, high = jnp.where(core == 0, own, other), jnp.where(core == 0, other, own)
        shape = (CHUNKS, -1, own.shape[1])
        return jnp.concatenate([low.reshape(shape), high.reshape(shape)], axis=1).reshape(P_SIZE, -1)

    share = P_SIZE // rows_n
    if fast:
        with jax.named_scope("cross_sum"):
            total = crossed[0]
            for j in range(1, chips):
                total = total + shift(crossed[j], j)
            size = total.shape[1] // 2
            left, right = total[:, :size], total[:, size:]
            keep = jnp.where(core == 0, left, right)
            give = jnp.where(core == 0, right, left)
            total = both_cores(keep, lax.ppermute(give, "rows", swap))
        with jax.named_scope("solve"):
            solved = jnp.dot(inverse, total, precision=HI, preferred_element_type=F32)
            return lax.all_to_all(solved, "rows", split_axis=0, concat_axis=1, tiled=True)
    zero = jnp.zeros_like(crossed[0])
    total = lax.psum(both_cores(crossed[0], zero), "rows")
    solved = jnp.dot(inverse, total, precision=HI, preferred_element_type=F32)
    return lax.dynamic_slice_in_dim(solved, row * share, share, 0)


def solution(mesh):
    in_specs = (P("rows", "cols"), P(), P("rows", None), P("rows"), P("rows"))
    out_specs = P("rows", "cols")
    return jax.shard_map(local, mesh=mesh, in_specs=in_specs, out_specs=out_specs, check_vma=False)
```

time: 1100 us -> 293 us (0.27); the launches traced: 1080 us -> 291 us
  waiting for transfers between devices: 836 us -> 53.4 us
  blocking collectives: 0 us -> 63.4 us
  matrix products: 61 us -> 4.86 us
  Pallas kernels: 0 us -> 50.4 us
  other arithmetic: 115 us -> 70.2 us
  local copies, waits for them, and re-layouts: 48.4 us -> 24.4 us
  starting transfers between devices: 7.15 us -> 23.1 us
  between operations: 15 us -> 1.68 us
    all_to_all x1 -> x0, waiting for transfers between devices: 724 us -> none  [local(): lax.all_to_all(buffer, 'rows', split_axis=1, concat_axis=0, tiled=True)]
    psum x2 -> x0, waiting for transfers between devices: 112 us -> none  [the longest x1 60.3 us: local(): gram_total, cross_total = lax.psum((gram_part, cross_part), 'rows')]
    dot_general x4 -> x1, matrix products: 56.6 us -> 0.38 us  [local(): solved = jnp.dot(inverse, total, precision=HI, preferred_element_type=F32)]
    ppermute x0 -> x19, waiting for transfers between devices: none -> 53.4 us  [the longest x3 22.5 us: across(): return lax.ppermute(value, 'cols', [(i, i ^ j) for i in range(parts)])]
    all_gather x0 -> x1, blocking collectives: none -> 52.5 us  [local(): names = lax.all_gather(names, 'rows')]
    pallas_call x0 -> x5, Pallas kernels: none -> 50.4 us  [the longest x1 17.3 us: mix_all(): pl.pallas_call(functools.partial(mix_kernel, per_step), grid_spec=pltpu.P...]
    reduce_sum x3 -> x0, other arithmetic: 47.1 us -> none  [the longest x2 46.9 us: local(): received = jnp.sum(arrived, axis=(0, 2), dtype=jnp.float32)]
    unnamed x6 -> x28, local copies, waits for them, and re-layouts: 41.7 us -> 15.9 us
  transfers between devices with their start and end apart: 3 -> 19, of which waited for: 3 -> 10; matrix products, arithmetic and copies ran while one was open for 0% -> 28% of each run, Pallas kernels for 0% -> 6%
where the time goes in v1:
time: 293 us; the launch traced here: 291 us
  other arithmetic  70.2 us (24%)
  blocking collectives  63.4 us (22%)
  waiting for transfers between devices  53.4 us (18%)
  Pallas kernels  50.4 us (17%)
  local copies, waits for them, and re-layouts  24.4 us (8%)
  starting transfers between devices  23.1 us (8%)
  matrix products  4.86 us (2%)
    all_gather x1, blocking collectives, local(): names = lax.all_gather(names, 'rows')  52.5 us
    another operation x6, other arithmetic, local(): lower = jnp.linalg.cholesky(gram)  36.5 us
    another operation x4, other arithmetic, local(): lax.linalg.triangular_solve(lower, jnp.eye(P_SIZE, dtype=F32), left_side=...  22.7 us
    ppermute x3, waiting for transfers between devices, across(): return lax.ppermute(value, 'cols', [(i, i ^ j) for i in range(parts)])  22.5 us
    ppermute x3, waiting for transfers between devices, local(): got = lax.ppermute(pieces[h * parts + j], 'cols', [(0, j)])  19.6 us
    pallas_call x1, Pallas kernels, mix_all(): pl.pallas_call(functools.partial(mix_kernel, per_step), grid_spec=pltpu.P...  17.3 us
    unnamed x28, local copies, waits for them, and re-layouts  15.9 us
    pallas_call x1, Pallas kernels, cross_parts(): pl.pallas_call(functools.partial(cross_kernel, parts, groups), grid=(rows...  14.8 us
  transfers between devices with their start and end apart: 19, of which 10 were waited for; matrix products, arithmetic and copies ran while one was open for 28% of the time, Pallas kernels for 6%

profile of v1, /device:TPU:0, one launch (start us, length us, event | category | flops | bytes accessed | tf_op | source)
XLA Modules:
  0.0 291.4 jit_solution(9085308432437276483)
XLA Ops:
  0.0 5.8 %copy-done = f32[4096,1024]{1,0:T(8,128)S(1)} copy-done((f32[4096,1024]{1,0:T(8,128)S(1)}, f32[4096,1024]{1,0:T(8,128)}, u32[]{:S(2)}) %copy-start) | copy-done | bytes 16777240
  5.8 1.0 copy-done.4
  8.1 17.3 %mix_all.1.mine_ref = bf16[4096,1024]{1,0:T(8,128)(2,1)} custom-call(s32[32]{0:T(128)S(1)} %copy-done.6, s32[32]{0:T(128)S(1)} %copy-done.8, f32[4096,1024]{1,0:T(8,128)S(1)} %copy-done, f32[8,128,128]{2,1,0:T(8,128)S(1)} %copy-done.4), custom_call_target="tpu_custom_call" | custom-call | flops 6442450944 | bytes 25165824 | tf_op jit(solution)/shard_map/mix/mix_all/pallas_call | solution.py:92
  25.9 5.8 %copy-done.1 = f32[4096,1024]{1,0:T(8,128)S(1)} copy-done((f32[4096,1024]{1,0:T(8,128)S(1)}, f32[4096,1024]{1,0:T(8,128)}, u32[]{:S(2)}) %copy-start.1) | copy-done | bytes 16777240
  31.7 6.7 %mix_panel.1 = (bf16[2,32,32,128]{3,2,1,0:T(8,128)(2,1)S(1)}, bf16[2,32,32,128]{3,2,1,0:T(8,128)(2,1)S(1)}, bf16[2,32,32,128]{3,2,1,0:T(8,128)(2,1)S(1)}, bf16[2,32,32,128]{3,2,1,0:T(8,128)(2,1)S(1)}) custom-call(s32[32]{0:T(128)S(1)} %copy-done.7, s32[32]{0:T(128)S(1)} %copy-done.9, s32[1]{0:T(128)} %bitcast.2.core_ref, f32[4096,1024]{1,0:T(8,128)S(1)} %copy-done.1, ...), custom_call_target="tpu_custom_call" | custom-call | flops 1610612736 | bytes 6291456 | tf_op jit(solution)/shard_map/panel_mix/mix_panel/pallas_call | solution.py:61
  38.4 5.4 %collective-permute-start = (bf16[2,32,32,128]{3,2,1,0:T(8,128)(2,1)S(1)}, bf16[2,32,32,128]{3,2,1,0:T(8,128)(2,1)S(1)}, u32[]{:S(2)}, u32[]{:S(2)}) collective-permute-start(bf16[2,32,32,128]{3,2,1,0:T(8,128)(2,1)S(1)} %get-tuple-element.13), channel_id=1, source_target_pairs={{0,3},{4,7},{8,11},{12,15},{16,19},{20,23},{24,27},{28,31}} | collective-permute-start | bytes 1572872 | tf_op jit(solution)/shard_map/panel_spread/ppermute | solution.py:278
  43.8 1.3 collective-permute-start.1
  45.1 2.1 collective-permute-start.2
  47.2 8.8 %collective-permute-done = bf16[2,32,32,128]{3,2,1,0:T(8,128)(2,1)S(1)} collective-permute-done((bf16[2,32,32,128]{3,2,1,0:T(8,128)(2,1)S(1)}, bf16[2,32,32,128]{3,2,1,0:T(8,128)(2,1)S(1)}, u32[]{:S(2)}, u32[]{:S(2)}) %collective-permute-start) | collective-permute-done | bytes 524320 | tf_op jit(solution)/shard_map/panel_spread/ppermute | solution.py:278
  56.9 9.9 %collective-permute-done.2 = bf16[2,32,32,128]{3,2,1,0:T(8,128)(2,1)} collective-permute-done((bf16[2,32,32,128]{3,2,1,0:T(8,128)(2,1)S(1)}, bf16[2,32,32,128]{3,2,1,0:T(8,128)(2,1)}, u32[]{:S(2)}, u32[]{:S(2)}) %collective-permute-start.2) | collective-permute-done | bytes 524320 | tf_op jit(solution)/shard_map/panel_spread/ppermute | solution.py:278
  67.3 1.3 collective-permute-done.3
  68.6 3.7 %collective-permute-start.6 = (bf16[64,32,128]{2,1,0:T(8,128)(2,1)S(1)}, bf16[64,32,128]{2,1,0:T(8,128)(2,1)S(1)}, u32[]{:S(2)}, u32[]{:S(2)}) collective-permute-start(bf16[64,32,128]{2,1,0:T(8,128)(2,1)S(1)} %pad_maximum_fusion.refs_0_), channel_id=1, source_target_pairs={{0,24},{4,28},{8,0},{12,4},{16,8},{20,12},{24,16},{28,20},{1,25},{... | collective-permute-start | bytes 1572872 | tf_op jit(solution)/shard_map/panel_rows/ppermute | solution.py:256
  72.3 1.0 collective-permute-start.4
  73.3 52.5 %all-gather.1 = s32[8,3,32]{2,1,0:T(4,128)S(1)} all-gather(s32[1,3,32]{2,1,0:T(4,128)S(1)} %add_bitcast_fusion), channel_id=2, replica_groups=mesh['rows'=8,'cols'=4] {'rows'}, dimensions={0}, use_global_device_ids=true | all-gather | bytes 3456 | tf_op jit(solution)/shard_map/names/all_gather | solution.py:264
  126.7 2.9 sum_buckets.1
  129.6 1.0 fusion.14
  130.6 5.1 %collective-permute-start.8 = (f16[64,32,128]{2,1,0:T(8,128)(2,1)}, f16[64,32,128]{2,1,0:T(8,128)(2,1)}, u32[]{:S(2)}, u32[]{:S(2)}) collective-permute-start(f16[64,32,128]{2,1,0:T(8,128)(2,1)} %get-tuple-element.42), channel_id=1, source_target_pairs={{0,2},{1,3},{2,0},{3,1},{4,6},{5,7},{6,4},{7,5},{8,10},{9,11},{10,... | collective-permute-start | bytes 1572872 | tf_op jit(solution)/shard_map/panel_cols/ppermute | solution.py:259
  135.7 10.9 %collective-permute-done.9 = f16[64,32,128]{2,1,0:T(8,128)(2,1)} collective-permute-done((f16[64,32,128]{2,1,0:T(8,128)(2,1)}, f16[64,32,128]{2,1,0:T(8,128)(2,1)}, u32[]{:S(2)}, u32[]{:S(2)}) %collective-permute-start.9) | collective-permute-done | bytes 524320 | tf_op jit(solution)/shard_map/panel_cols/ppermute | solution.py:259
  146.7 10.6 %collective-permute-done.8 = f16[64,32,128]{2,1,0:T(8,128)(2,1)} collective-permute-done((f16[64,32,128]{2,1,0:T(8,128)(2,1)}, f16[64,32,128]{2,1,0:T(8,128)(2,1)}, u32[]{:S(2)}, u32[]{:S(2)}) %collective-permute-start.8) | collective-permute-done | bytes 524320 | tf_op jit(solution)/shard_map/panel_cols/ppermute | solution.py:259
  157.3 1.0 collective-permute-done.7
  159.2 1.2 convert_element_type.37.refs_1_
  160.4 1.2 convert_element_type.38.refs_2_
  161.6 1.2 convert_element_type.39.refs_3_
  162.8 1.5 convert_element_type.40.refs_4_
  164.3 1.2 convert_element_type.43.refs_7_
  165.5 1.2 convert_element_type.42.refs_6_
  166.7 1.2 convert_element_type.41.refs_5_
  167.9 8.7 %gram_of.1 = f32[256,256]{1,0:T(8,128)S(1)} custom-call(s32[3]{0:T(128)S(1)} %pad_add_fusion.where_ref, f32[64,32,128]{2,1,0:T(8,128)S(1)} %get-tuple-element.41.refs_0_, f32[64,32,128]{2,1,0:T(8,128)S(1)} %convert_element_type.37.refs_1_, f32[64,32,128]{2,1,0:T(8,128)S(1)} %convert_element_type.38.refs_2_, f32[64,32,128]{2,1,0:T(8,128)S(1)} %convert_element_type.39.refs_3_, ...), custom_call_target="tpu_custom_call" | custom-call | flops 3221225472 | bytes 4194304 | tf_op jit(solution)/shard_map/gram/gram_of/pallas_call | solution.py:233
  177.4 1.0 fusion
  179.2 11.7 %cholesky.50 = f32[128,128]{1,0:T(8,128)S(1)} custom-call(f32[128,128]{1,0:T(8,128)S(1)} %cholesky.118), custom_call_target="Cholesky" | custom-call | tf_op jit(solution)/shard_map/factor/jit(cholesky)/cholesky | solution.py:302
  191.4 10.4 %custom-call.14 = f32[1,128,128]{1,2,0:T(8,128)} custom-call(f32[1,128,128]{2,1,0:T(8,128)S(1)} %get-tuple-element.52), custom_call_target="InvertDiagBlocksLowerTriangular" | custom-call | tf_op jit(solution)/shard_map/factor/jit(cholesky)/cholesky | solution.py:302
  201.9 1.1 constant_dynamic-update-slice_fusion.1
  202.9 1.7 slice_subtract_fusion
  204.7 12.5 %cholesky.105 = f32[128,128]{1,0:T(8,128)S(1)} custom-call(f32[128,128]{1,0:T(8,128)} %slice_subtract_fusion), custom_call_target="Cholesky" | custom-call | tf_op jit(solution)/shard_map/factor/jit(cholesky)/cholesky | solution.py:302
  217.3 1.3 compare_reduce_fusion
  219.8 1.0 select_select_fusion.1
  221.5 5.1 %while.1 = (s32[]{:T(128)}, f32[256,256]{1,0:T(8,128)S(1)}, s32[2,2]{1,0:T(2,128)S(1)}, f32[2,128,128]{2,1,0:T(8,128)}, s32[]{:T(128)}) while((s32[]{:T(128)}, f32[256,256]{1,0:T(8,128)S(1)}, s32[2,2]{1,0:T(2,128)S(1)}, f32[2,128,128]{2,1,0:T(8,128)}, s32[]{:T(128)}) %tuple.29), condition=%wide.while_cond, body=%wide.while_body.sunk | while | flops 2 | bytes 132205 | solution.py:303
  222.1 1.9 bitcast_dynamic-update-slice_fusion.2
  224.7 1.9 bitcast_dynamic-update-slice_fusion.2
  226.6 21.1 %custom-call.15 = f32[2,128,128]{1,2,0:T(8,128)} custom-call(f32[2,128,128]{2,1,0:T(8,128)} %get-tuple-element.28), custom_call_target="InvertDiagBlocksLowerTriangular" | custom-call | tf_op jit(solution)/shard_map/factor/triangular_solve | solution.py:303
  247.7 1.1 fusion.4
  249.1 1.2 copy-done.3
  250.3 14.8 %cross_parts.1 = (f32[128,256]{1,0:T(8,128)S(1)}, f32[128,256]{1,0:T(8,128)S(1)}, f32[128,256]{1,0:T(8,128)S(1)}, f32[128,256]{1,0:T(8,128)S(1)}) custom-call(s32[64]{0:T(128)S(1)} %slice.90.first_ref, s32[64]{0:T(128)S(1)} %slice.92.second_ref, f32[64]{0:T(128)S(1)} %slice.94.flip_ref, s32[3]{0:T(128)S(1)} %pad_add_fusion.where_ref, ...), custom_call_target="tpu_custom_call" | custom-call | flops 4294967296 | bytes 16777216 | tf_op jit(solution)/shard_map/cross/cross_parts/pallas_call | solution.py:193
  265.3 3.7 %collective-permute-start.17 = (f32[128,256]{1,0:T(8,128)S(1)}, f32[128,256]{1,0:T(8,128)S(1)}, u32[]{:S(2)}, u32[]{:S(2)}) collective-permute-start(f32[128,256]{1,0:T(8,128)S(1)} %get-tuple-element.20), channel_id=1, source_target_pairs={{0,24},{4,28},{8,0},{12,4},{16,8},{20,12},{24,16},{28,20},{1,25},{... | collective-permute-start | bytes 393224 | tf_op jit(solution)/shard_map/cross_sum/ppermute | solution.py:256
  269.3 4.1 %collective-permute-done.15 = f32[128,256]{1,0:T(8,128)S(1)} collective-permute-done((f32[128,256]{1,0:T(8,128)S(1)}, f32[128,256]{1,0:T(8,128)S(1)}, u32[]{:S(2)}, u32[]{:S(2)}) %collective-permute-start.15) | collective-permute-done | bytes 131104 | tf_op jit(solution)/shard_map/cross_sum/ppermute | solution.py:256
  273.4 4.7 %collective-permute-done.16 = f32[128,256]{1,0:T(8,128)S(1)} collective-permute-done((f32[128,256]{1,0:T(8,128)S(1)}, f32[128,256]{1,0:T(8,128)S(1)}, u32[]{:S(2)}, u32[]{:S(2)}) %collective-permute-start.16) | collective-permute-done | bytes 131104 | tf_op jit(solution)/shard_map/cross_sum/ppermute | solution.py:256
  278.3 1.2 collective-permute-done.18
  279.9 10.9 %all_to_all.16 = f32[8,32,128]{2,1,0:T(8,128)S(1)} all-to-all(f32[8,32,128]{2,1,0:T(8,128)S(1)} %fusion.1), channel_id=1, replica_groups=mesh['rows'=8,'cols'=4] {'rows'}, dimensions={0} | all-to-all | bytes 262144 | tf_op jit(solution)/shard_map/solve/all_to_all | solution.py:323
  (87 shorter events, 11.1 us)
Async XLA Ops:
  0.0 5.8 %copy-start = (f32[4096,1024]{1,0:T(8,128)S(1)}, f32[4096,1024]{1,0:T(8,128)}, u32[]{:S(2)}) copy-start(f32[4096,1024]{1,0:T(8,128)} %matrix_ref.3) | copy-start | bytes 50331652
  5.8 1.0 copy-start.4
  6.8 0.7 copy-start.6
  7.5 0.7 copy-start.8
  8.1 17.8 %copy-start.5 = (f32[8,128,128]{2,1,0:T(8,128)S(1)}, f32[8,128,128]{2,1,0:T(8,128)}, u32[]{:S(2)}) copy-start(f32[8,128,128]{2,1,0:T(8,128)} %mixers_ref.3) | copy-start | bytes 1572868
  8.1 17.8 %copy-start.7 = (s32[32]{0:T(128)S(1)}, s32[32]{0:T(128)}, u32[]{:S(2)}) copy-start(s32[32]{0:T(128)} %index_ref.3) | copy-start | bytes 388
  8.1 17.8 %copy-start.9 = (s32[32]{0:T(128)S(1)}, s32[32]{0:T(128)}, u32[]{:S(2)}) copy-start(s32[32]{0:T(128)} %seed_ref.3) | copy-start | bytes 388
  25.4 223.6 %collective-permute-start.14 = (bf16[4096,1024]{1,0:T(8,128)(2,1)}, bf16[4096,1024]{1,0:T(8,128)(2,1)}, u32[]{:S(2)}, u32[]{:S(2)}) collective-permute-start(bf16[4096,1024]{1,0:T(8,128)(2,1)} %mix_all.1.mine_ref), channel_id=1, source_target_pairs={{0,4},{4,0},{8,12},{12,8},{16,20},{20,16},{24,28},{28,24},{1,5},{5... | collective-permute-start | bytes 25165832 | tf_op jit(solution)/shard_map/mix/ppermute | solution.py:292
  25.9 5.8 %copy-start.1 = (f32[4096,1024]{1,0:T(8,128)S(1)}, f32[4096,1024]{1,0:T(8,128)}, u32[]{:S(2)}) copy-start(f32[4096,1024]{1,0:T(8,128)} %matrix_ref.3) | copy-start | bytes 50331652
  31.7 41.7 %copy-start.13 = (s32[32,2]{0,1:T(2,128)S(1)}, s32[32,2]{0,1:T(2,128)}, u32[]{:S(2)}) copy-start(s32[32,2]{0,1:T(2,128)} %param.7) | copy-start | bytes 772
  38.4 17.6 %collective-permute-start = (bf16[2,32,32,128]{3,2,1,0:T(8,128)(2,1)S(1)}, bf16[2,32,32,128]{3,2,1,0:T(8,128)(2,1)S(1)}, u32[]{:S(2)}, u32[]{:S(2)}) collective-permute-start(bf16[2,32,32,128]{3,2,1,0:T(8,128)(2,1)S(1)} %get-tuple-element.13), channel_id=1, source_target_pairs={{0,3},{4,7},{8,11},{12,15},{16,19},{20,23},{24,27},{28,31}} | collective-permute-start | bytes 1572872 | tf_op jit(solution)/shard_map/panel_spread/ppermute | solution.py:278
  43.8 13.1 %collective-permute-start.1 = (bf16[2,32,32,128]{3,2,1,0:T(8,128)(2,1)S(1)}, bf16[2,32,32,128]{3,2,1,0:T(8,128)(2,1)S(1)}, u32[]{:S(2)}, u32[]{:S(2)}) collective-permute-start(bf16[2,32,32,128]{3,2,1,0:T(8,128)(2,1)S(1)} %get-tuple-element.14), channel_id=1, source_target_pairs={{0,2},{4,6},{8,10},{12,14},{16,18},{20,22},{24,26},{28,30}} | collective-permute-start | bytes 1572872 | tf_op jit(solution)/shard_map/panel_spread/ppermute | solution.py:278
  45.1 21.7 %collective-permute-start.2 = (bf16[2,32,32,128]{3,2,1,0:T(8,128)(2,1)S(1)}, bf16[2,32,32,128]{3,2,1,0:T(8,128)(2,1)}, u32[]{:S(2)}, u32[]{:S(2)}) collective-permute-start(bf16[2,32,32,128]{3,2,1,0:T(8,128)(2,1)S(1)} %get-tuple-element.15), channel_id=1, source_target_pairs={{0,1},{4,5},{8,9},{12,13},{16,17},{20,21},{24,25},{28,29}} | collective-permute-start | bytes 1572872 | tf_op jit(solution)/shard_map/panel_spread/ppermute | solution.py:278
  67.0 1.6 collective-permute-start.3
  68.6 58.1 %collective-permute-start.6 = (bf16[64,32,128]{2,1,0:T(8,128)(2,1)S(1)}, bf16[64,32,128]{2,1,0:T(8,128)(2,1)S(1)}, u32[]{:S(2)}, u32[]{:S(2)}) collective-permute-start(bf16[64,32,128]{2,1,0:T(8,128)(2,1)S(1)} %pad_maximum_fusion.refs_0_), channel_id=1, source_target_pairs={{0,24},{4,28},{8,0},{12,4},{16,8},{20,12},{24,16},{28,20},{1,25},{... | collective-permute-start | bytes 1572872 | tf_op jit(solution)/shard_map/panel_rows/ppermute | solution.py:256
  72.3 54.4 %collective-permute-start.5 = (bf16[64,32,128]{2,1,0:T(8,128)(2,1)S(1)}, bf16[64,32,128]{2,1,0:T(8,128)(2,1)S(1)}, u32[]{:S(2)}, u32[]{:S(2)}) collective-permute-start(bf16[64,32,128]{2,1,0:T(8,128)(2,1)S(1)} %pad_maximum_fusion.refs_0_), channel_id=1, source_target_pairs={{0,16},{4,20},{8,24},{12,28},{16,0},{20,4},{24,8},{28,12},{1,17},{... | collective-permute-start | bytes 1572872 | tf_op jit(solution)/shard_map/panel_rows/ppermute | solution.py:256
  72.3 54.4 %collective-permute-start.4 = (bf16[64,32,128]{2,1,0:T(8,128)(2,1)S(1)}, bf16[64,32,128]{2,1,0:T(8,128)(2,1)S(1)}, u32[]{:S(2)}, u32[]{:S(2)}) collective-permute-start(bf16[64,32,128]{2,1,0:T(8,128)(2,1)S(1)} %pad_maximum_fusion.refs_0_), channel_id=1, source_target_pairs={{0,8},{4,12},{8,16},{12,20},{16,24},{20,28},{24,0},{28,4},{1,9},{5... | collective-permute-start | bytes 1572872 | tf_op jit(solution)/shard_map/panel_rows/ppermute | solution.py:256
  130.6 16.0 %collective-permute-start.9 = (f16[64,32,128]{2,1,0:T(8,128)(2,1)}, f16[64,32,128]{2,1,0:T(8,128)(2,1)}, u32[]{:S(2)}, u32[]{:S(2)}) collective-permute-start(f16[64,32,128]{2,1,0:T(8,128)(2,1)} %get-tuple-element.42), channel_id=1, source_target_pairs={{0,3},{1,2},{2,1},{3,0},{4,7},{5,6},{6,5},{7,4},{8,11},{9,10},{10,... | collective-permute-start | bytes 1572872 | tf_op jit(solution)/shard_map/panel_cols/ppermute | solution.py:259
  130.6 26.6 %collective-permute-start.8 = (f16[64,32,128]{2,1,0:T(8,128)(2,1)}, f16[64,32,128]{2,1,0:T(8,128)(2,1)}, u32[]{:S(2)}, u32[]{:S(2)}) collective-permute-start(f16[64,32,128]{2,1,0:T(8,128)(2,1)} %get-tuple-element.42), channel_id=1, source_target_pairs={{0,2},{1,3},{2,0},{3,1},{4,6},{5,7},{6,4},{7,5},{8,10},{9,11},{10,... | collective-permute-start | bytes 1572872 | tf_op jit(solution)/shard_map/panel_cols/ppermute | solution.py:259
  135.7 22.5 %collective-permute-start.7 = (f16[64,32,128]{2,1,0:T(8,128)(2,1)}, f16[64,32,128]{2,1,0:T(8,128)(2,1)}, u32[]{:S(2)}, u32[]{:S(2)}) collective-permute-start(f16[64,32,128]{2,1,0:T(8,128)(2,1)} %get-tuple-element.42), channel_id=1, source_target_pairs={{0,1},{1,0},{2,3},{3,2},{4,5},{5,4},{6,7},{7,6},{8,9},{9,8},{10,11... | collective-permute-start | bytes 1572872 | tf_op jit(solution)/shard_map/panel_cols/ppermute | solution.py:259
  135.7 27.0 %collective-permute-start.10 = (f16[64,32,128]{2,1,0:T(8,128)(2,1)}, f16[64,32,128]{2,1,0:T(8,128)(2,1)}, u32[]{:S(2)}, u32[]{:S(2)}) collective-permute-start(f16[64,32,128]{2,1,0:T(8,128)(2,1)} %get-tuple-element.42), channel_id=1, source_target_pairs={{0,4},{4,0},{8,12},{12,8},{16,20},{20,16},{24,28},{28,24},{1,5},{5... | collective-permute-start | bytes 1572872 | tf_op jit(solution)/shard_map/panel_cols/ppermute | solution.py:288
  146.6 17.7 %collective-permute-start.13 = (f16[64,32,128]{2,1,0:T(8,128)(2,1)}, f16[64,32,128]{2,1,0:T(8,128)(2,1)}, u32[]{:S(2)}, u32[]{:S(2)}) collective-permute-start(f16[64,32,128]{2,1,0:T(8,128)(2,1)} %collective-permute-done.9), channel_id=1, source_target_pairs={{0,4},{4,0},{8,12},{12,8},{16,20},{20,16},{24,28},{28,24},{1,5},{5... | collective-permute-start | bytes 1572872 | tf_op jit(solution)/shard_map/panel_cols/ppermute | solution.py:288
  157.2 8.3 %collective-permute-start.12 = (f16[64,32,128]{2,1,0:T(8,128)(2,1)}, f16[64,32,128]{2,1,0:T(8,128)(2,1)}, u32[]{:S(2)}, u32[]{:S(2)}) collective-permute-start(f16[64,32,128]{2,1,0:T(8,128)(2,1)} %collective-permute-done.8), channel_id=1, source_target_pairs={{0,4},{4,0},{8,12},{12,8},{16,20},{20,16},{24,28},{28,24},{1,5},{5... | collective-permute-start | bytes 1572872 | tf_op jit(solution)/shard_map/panel_cols/ppermute | solution.py:288
  158.3 8.4 %collective-permute-start.11 = (f16[64,32,128]{2,1,0:T(8,128)(2,1)}, f16[64,32,128]{2,1,0:T(8,128)(2,1)}, u32[]{:S(2)}, u32[]{:S(2)}) collective-permute-start(f16[64,32,128]{2,1,0:T(8,128)(2,1)} %collective-permute-done.7), channel_id=1, source_target_pairs={{0,4},{4,0},{8,12},{12,8},{16,20},{20,16},{24,28},{28,24},{1,5},{5... | collective-permute-start | bytes 1572872 | tf_op jit(solution)/shard_map/panel_cols/ppermute | solution.py:288
  162.7 5.1 %copy-start.2 = (f32[64,32,128]{2,1,0:T(8,128)}, f32[64,32,128]{2,1,0:T(8,128)S(1)}, u32[]{:S(2)}) copy-start(f32[64,32,128]{2,1,0:T(8,128)S(1)} %convert_element_type.39.refs_3_) | copy-start | bytes 3145732
  178.4 0.7 copy-start.11
  217.3 2.5 copy-start.10
  249.0 1.2 copy-start.3
  250.3 18.7 %copy-start.12 = (f32[2,128,128]{1,2,0:T(8,128)S(1)}, f32[2,128,128]{1,2,0:T(8,128)}, u32[]{:S(2)}) copy-start(f32[2,128,128]{1,2,0:T(8,128)} %custom-call.15) | copy-start | bytes 393220
  265.1 8.3 %collective-permute-start.15 = (f32[128,256]{1,0:T(8,128)S(1)}, f32[128,256]{1,0:T(8,128)S(1)}, u32[]{:S(2)}, u32[]{:S(2)}) collective-permute-start(f32[128,256]{1,0:T(8,128)S(1)} %get-tuple-element.18), channel_id=1, source_target_pairs={{0,8},{4,12},{8,16},{12,20},{16,24},{20,28},{24,0},{28,4},{1,9},{5... | collective-permute-start | bytes 393224 | tf_op jit(solution)/shard_map/cross_sum/ppermute | solution.py:256
  265.2 12.9 %collective-permute-start.16 = (f32[128,256]{1,0:T(8,128)S(1)}, f32[128,256]{1,0:T(8,128)S(1)}, u32[]{:S(2)}, u32[]{:S(2)}) collective-permute-start(f32[128,256]{1,0:T(8,128)S(1)} %get-tuple-element.19), channel_id=1, source_target_pairs={{0,16},{4,20},{8,24},{12,28},{16,0},{20,4},{24,8},{28,12},{1,17},{... | collective-permute-start | bytes 393224 | tf_op jit(solution)/shard_map/cross_sum/ppermute | solution.py:256
  265.3 12.8 %collective-permute-start.17 = (f32[128,256]{1,0:T(8,128)S(1)}, f32[128,256]{1,0:T(8,128)S(1)}, u32[]{:S(2)}, u32[]{:S(2)}) collective-permute-start(f32[128,256]{1,0:T(8,128)S(1)} %get-tuple-element.20), channel_id=1, source_target_pairs={{0,24},{4,28},{8,0},{12,4},{16,8},{20,12},{24,16},{28,20},{1,25},{... | collective-permute-start | bytes 393224 | tf_op jit(solution)/shard_map/cross_sum/ppermute | solution.py:256
  278.2 1.3 collective-permute-start.18

commit v2 on v0

v2 whole, which is shorter than its diff:
```python
import functools
import jax
import jax.numpy as jnp
from jax import lax
from jax.experimental import pallas as pl
from jax.experimental.pallas import tpu as pltpu
from jax.sharding import PartitionSpec as P

TILE = 128
P_SIZE = 256
NB = 64
CHUNKS = 2
WIDTH = 16
HALF = P_SIZE // CHUNKS
SLICES = HALF // (2 * WIDTH)
BASE = 64
F32, BF16, F16 = jnp.float32, jnp.bfloat16, jnp.float16
HI = lax.Precision.HIGHEST
MIB = 1 << 20


def vmem():
    return pl.BlockSpec(memory_space=pltpu.VMEM)


def smem():
    return pl.BlockSpec(memory_space=pltpu.SMEM)


def anywhere():
    return pl.BlockSpec(memory_space=pl.ANY)


def params(mib):
    return pltpu.CompilerParams(vmem_limit_bytes=mib * MIB)


def cost(flops, bytes_accessed):
    return pl.CostEstimate(flops=flops, bytes_accessed=bytes_accessed, transcendentals=0)


def signed_mixer(mixers_ref, names_ref, tile):
    position = lax.broadcasted_iota(jnp.int32, (1, TILE), 1)
    hashed = (names_ref[4, tile] ^ position * 40503) * 69069
    sign = (1 - 2 * (hashed >> 16 & 1)).astype(F32)
    return mixers_ref[names_ref[3, tile]] * sign


def split(value):
    high = value.astype(BF16)
    return high, (value - high.astype(F32)).astype(BF16)


def product(mixer, block):
    mixer_high, mixer_low = split(mixer)
    block_high, block_low = split(block)
    wide = jnp.dot(jnp.concatenate([mixer_high, mixer_low], axis=0), block_high, preferred_element_type=F32)
    low = jnp.dot(mixer_high, block_low, preferred_element_type=F32)
    return wide[:TILE] + (wide[TILE:] + low)


def panel_kernel(per_step, names_ref, order_ref, matrix_ref, mixers_ref, *refs):
    outs, turned = refs[:-1], refs[-1]
    first = pl.program_id(0) * per_step
    core = order_ref[2 * SLICES + 1]
    for u in range(per_step):
        mixer = signed_mixer(mixers_ref, names_ref, first + u)
        block = matrix_ref[u * TILE : (u + 1) * TILE, :]
        turned[u] = product(mixer, block).T
        for h in range(CHUNKS):
            for c in range(SLICES):
                for s in range(2):
                    who = core if s == 0 else 1 - core
                    start = pl.multiple_of(h * HALF + who * (HALF // 2) + c * WIDTH, WIDTH)
                    outs[h * SLICES + c][s, u] = turned[u, pl.ds(start, WIDTH), :].astype(BF16)


def mix_panel(matrix, mixers, names, order):
    tiles = names.shape[1]
    per_step = 4
    spec = pl.BlockSpec((2, per_step, WIDTH, TILE), lambda i, *_: (0, i, 0, 0))
    return pl.pallas_call(
        functools.partial(panel_kernel, per_step),
        grid_spec=pltpu.PrefetchScalarGridSpec(
            num_scalar_prefetch=2,
            grid=(tiles // per_step,),
            in_specs=[
                pl.BlockSpec((per_step * TILE, P_SIZE), lambda i, *_: (i, 0)),
                pl.BlockSpec(mixers.shape, lambda i, *_: (0, 0, 0)),
            ],
            out_specs=[spec] * (CHUNKS * SLICES),
            scratch_shapes=[pltpu.VMEM((per_step, P_SIZE, TILE), F32)],
        ),
        out_shape=[jax.ShapeDtypeStruct((2, tiles, WIDTH, TILE), BF16)] * (CHUNKS * SLICES),
        compiler_params=params(52),
        cost_estimate=cost(6 * tiles * TILE * TILE * P_SIZE, 6 * tiles * TILE * P_SIZE),
        name="mix_panel",
    )(names, order, matrix, mixers)


def mix_kernel(per_step, start, names_ref, matrix_ref, mixers_ref, after_ref, out_ref):
    first = start + pl.program_id(0) * per_step
    for u in range(per_step):
        mixer = signed_mixer(mixers_ref, names_ref, first + u)
        block = matrix_ref[u * TILE : (u + 1) * TILE, :]
        out_ref[u * TILE : (u + 1) * TILE, :] = product(mixer, block).astype(BF16)


def mix_tiles(matrix, mixers, names, after, start, count):
    cols = matrix.shape[1]
    per_step = 2
    return pl.pallas_call(
        functools.partial(mix_kernel, per_step, start),
        grid_spec=pltpu.PrefetchScalarGridSpec(
            num_scalar_prefetch=1,
            grid=(count // per_step,),
            in_specs=[
                pl.BlockSpec((per_step * TILE, cols), lambda i, *_: (i + start // per_step, 0)),
                pl.BlockSpec(mixers.shape, lambda i, *_: (0, 0, 0)),
                anywhere(),
            ],
            out_specs=pl.BlockSpec((per_step * TILE, cols), lambda i, *_: (i, 0)),
        ),
        out_shape=jax.ShapeDtypeStruct((count * TILE, cols), BF16),
        compiler_params=params(52),
        cost_estimate=cost(12 * count * TILE * TILE * cols, 6 * count * TILE * cols),
        name="mix_tiles",
    )(names, matrix, mixers, after)


def pick_kernel(order_ref, after_ref, *refs):
    sources, (keep_ref, give_ref) = refs[:-2], refs[-2:]
    part = order_ref[2 * SLICES + 2]
    for j, source in enumerate(sources):
        taken = part == j if j else (part == 0) | (part >= len(sources))

        @pl.when(taken)
        def copy():
            keep_ref[...] = source[0]
            give_ref[...] = source[1]


def pick(order, after, sources):
    return pl.pallas_call(
        pick_kernel,
        in_specs=[smem(), anywhere()] + [vmem()] * len(sources),
        out_specs=[vmem()] * 2,
        out_shape=[jax.ShapeDtypeStruct(sources[0].shape[1:], BF16)] * 2,
        compiler_params=params(16),
        cost_estimate=cost(0, 4 * 10**5),
        name="pick",
    )(order, after, *sources)


def tie_kernel(count, *refs):
    del count, refs


def tie(values, after):
    return pl.pallas_call(
        functools.partial(tie_kernel, len(values)),
        in_specs=[anywhere()] * (len(values) + 1),
        out_specs=[anywhere()] * len(values),
        out_shape=[jax.ShapeDtypeStruct(v.shape, v.dtype) for v in values],
        input_output_aliases={i: i for i in range(len(values))},
        cost_estimate=cost(0, 10**4),
        name="tie",
    )(*values, after)


def bucket_kernel(names_ref, after_ref, *refs):
    pieces, out_ref, total = refs[:-2], refs[-2], refs[-1]
    total[...] = jnp.zeros_like(total)
    for j, piece in enumerate(pieces):
        count = piece.shape[0]

        def add(i, carry):
            at = j * count + i
            value = piece[i].astype(F32)
            one, two = names_ref[0, at], names_ref[1, at]
            total[one] = total[one] + value
            total[two] = total[two] + names_ref[2, at].astype(F32) * value
            return carry

        lax.fori_loop(0, count, add, 0, unroll=8)
    summed = total[...]
    largest = jnp.max(jnp.max(jnp.abs(summed), axis=0), axis=1, keepdims=True)
    scale = jnp.where(largest > 1e-37, 1.0 / largest, 1.0)
    out_ref[...] = summed * scale


def sum_buckets(names, after, pieces):
    return pl.pallas_call(
        bucket_kernel,
        in_specs=[smem(), anywhere()] + [vmem()] * len(pieces),
        out_specs=vmem(),
        out_shape=jax.ShapeDtypeStruct((NB, WIDTH, TILE), F32),
        scratch_shapes=[pltpu.VMEM((NB, WIDTH, TILE), F32)],
        compiler_params=params(24),
        cost_estimate=cost(10**6, 4 * 10**6),
        name="sum_buckets",
    )(names, after, *pieces)


def nt(a, b, precision=None):
    return lax.dot_general(a, b, (((1,), (1,)), ((), ())), precision=precision, preferred_element_type=F32)


def nn(a, b):
    return jnp.dot(a, b, precision=HI, preferred_element_type=F32)


def join(order_ref, pieces, panel):
    for q, piece in enumerate(pieces):
        panel[:, pl.ds(pl.multiple_of(order_ref[q] * WIDTH, WIDTH), WIDTH), :] = piece[...]


def cross_kernel(per_step, groups, names_ref, order_ref, after_ref, early_ref, late_ref, *refs):
    pieces, panel, refs = refs[: 2 * SLICES], refs[2 * SLICES], refs[2 * SLICES + 1 :]
    outs, total = refs[:-1], refs[-1]
    step = pl.program_id(0)

    @pl.when(step == 0)
    def start():
        total[...] = jnp.zeros_like(total)
        join(order_ref, pieces, panel)

    for side, mixed_ref in enumerate((early_ref, late_ref)):
        high, low = [], []
        for u in range(per_step):
            t = per_step * (side * pl.num_programs(0) + step) + u
            one, two = split(panel[names_ref[0, t]] + names_ref[2, t].astype(F32) * panel[names_ref[1, t]])
            high.append(one)
            low.append(two)
        weights = jnp.concatenate([jnp.concatenate(high, axis=1), jnp.concatenate(low, axis=1)], axis=0)
        total[...] += jnp.dot(weights, mixed_ref[...], preferred_element_type=F32)

    @pl.when(step == pl.num_programs(0) - 1)
    def finish():
        total[:HALF, :] = total[:HALF, :] + total[HALF:, :]
        if groups == 1:
            outs[0][...] = total[:HALF, :]
        else:
            chip, core = order_ref[2 * SLICES], order_ref[2 * SLICES + 1]
            for s in range(2):
                who = core if s == 0 else 1 - core
                for j in range(groups):
                    at = (2 * lax.rem(chip + j, groups) + who) * TILE
                    outs[s][j] = total[:HALF, pl.ds(pl.multiple_of(at, TILE), TILE)]


def cross_parts(names, order, after, mixed, pieces, groups):
    rows, cols = mixed[0].shape
    per_step = 4
    if groups == 1:
        outs = [jax.ShapeDtypeStruct((HALF, cols), F32)]
    else:
        outs = [jax.ShapeDtypeStruct((groups, HALF, TILE), F32)] * 2
    outs = [jax.ShapeDtypeStruct((NB, HALF, TILE), F32)] + outs
    return pl.pallas_call(
        functools.partial(cross_kernel, per_step, groups),
        grid=(rows // (per_step * TILE),),
        in_specs=[smem(), smem(), anywhere()] + [pl.BlockSpec((per_step * TILE, cols), lambda i: (i, 0))] * 2 + [vmem()] * len(pieces),
        out_specs=[vmem()] * len(outs),
        out_shape=outs,
        scratch_shapes=[pltpu.VMEM((2 * HALF, cols), F32)],
        compiler_params=params(32),
        cost_estimate=cost(8 * rows * HALF * cols, 4 * rows * cols),
        name="cross_parts",
    )(names, order, after, *mixed, *pieces)


def factor_inverse(block):
    row = lax.broadcasted_iota(jnp.int32, (BASE, BASE), 0)
    lane = lax.broadcasted_iota(jnp.int32, (BASE, BASE), 1)
    eye = (row == lane).astype(F32)
    wide = jnp.concatenate([block, eye], axis=1)
    slabs = [wide[8 * g : 8 * g + 8, :] for g in range(BASE // 8)]
    below = lax.broadcasted_iota(jnp.int32, (8, 1), 0)
    for j in range(BASE):
        own, at = j // 8, j % 8
        pivot_row = slabs[own][at : at + 1, :]
        scaled = pivot_row * (1.0 / pivot_row[:, j : j + 1])
        for g in range(own, BASE // 8):
            column = slabs[g][:, j : j + 1]
            if g == own:
                if at == 7:
                    continue
                column = jnp.where(below > at, column, 0.0)
            slabs[g] = slabs[g] - column * scaled
    wide = jnp.concatenate(slabs, axis=0)
    pivots = jnp.sum(wide[:, :BASE] * eye, axis=1, keepdims=True)
    return wide[:, BASE:] * lax.rsqrt(pivots)


def factor_inverse_pair(block):
    first = factor_inverse(block[:BASE, :BASE])
    side = nt(block[BASE:, :BASE], first, HI)
    second = factor_inverse(block[BASE:, BASE:] - nt(side, side, HI))
    corner = -nn(second, nn(side, first))
    top = jnp.concatenate([first, jnp.zeros_like(first)], axis=1)
    return jnp.concatenate([top, jnp.concatenate([corner, second], axis=1)], axis=0)


GROUP = 8


def wide_buckets(panel, i):
    return jnp.concatenate([panel[GROUP * i + u] for u in range(GROUP)], axis=1)


def first_kernel(after_ref, panel, out_ref, acc):
    acc[...] = jnp.zeros_like(acc)

    def step(i, carry):
        one, two = split(wide_buckets(panel, i))
        acc[...] += nt(jnp.concatenate([one, two], axis=0), one)
        return carry

    lax.fori_loop(0, NB // GROUP, step, 0)
    mixed = acc[HALF:, :]
    out_ref[...] = acc[:HALF, :] + (mixed + mixed.T)


def first_gram(after, panel):
    return pl.pallas_call(
        first_kernel,
        in_specs=[anywhere(), vmem()],
        out_specs=vmem(),
        out_shape=jax.ShapeDtypeStruct((HALF, HALF), F32),
        scratch_shapes=[pltpu.VMEM((2 * HALF, HALF), F32)],
        compiler_params=params(32),
        cost_estimate=cost(3 * 10**9, 4 * NB * TILE * HALF),
        name="first_gram",
    )(after, panel)


def factor_kernel(block_ref, out_ref):
    out_ref[...] = factor_inverse_pair(block_ref[...])


def first_factor(block):
    return pl.pallas_call(
        factor_kernel,
        in_specs=[vmem()],
        out_specs=vmem(),
        out_shape=jax.ShapeDtypeStruct((HALF, HALF), F32),
        compiler_params=params(16),
        cost_estimate=cost(10**10, 8 * HALF * HALF),
        name="first_factor",
    )(block)


def second_kernel(after_ref, panel0, panel1, side_ref, block_ref, acc, extra):
    acc[...] = jnp.zeros_like(acc)
    extra[...] = jnp.zeros_like(extra)

    def step(i, carry):
        one0, two0 = split(wide_buckets(panel0, i))
        one1, two1 = split(wide_buckets(panel1, i))
        acc[...] += nt(jnp.concatenate([one1, two1], axis=0), jnp.concatenate([one0, one1], axis=0))
        extra[...] += nt(one1, two0)
        return carry

    lax.fori_loop(0, NB // GROUP, step, 0)
    side_ref[...] = acc[:HALF, :HALF] + (acc[HALF:, :HALF] + extra[...])
    mixed = acc[HALF:, HALF:]
    block_ref[...] = acc[:HALF, HALF:] + (mixed + mixed.T)


def second_gram(after, panel0, panel1):
    return pl.pallas_call(
        second_kernel,
        in_specs=[anywhere()] + [vmem()] * 2,
        out_specs=[vmem()] * 2,
        out_shape=[jax.ShapeDtypeStruct((HALF, HALF), F32)] * 2,
        scratch_shapes=[pltpu.VMEM((2 * HALF, 2 * HALF), F32), pltpu.VMEM((HALF, HALF), F32)],
        compiler_params=params(32),
        cost_estimate=cost(4 * 10**9, 4 * NB * TILE * P_SIZE),
        name="second_gram",
    )(after, panel0, panel1)


def last_kernel(after_ref, side_ref, block_ref, inverse_ref, out_ref):
    first = inverse_ref[...]
    side = nt(side_ref[...], first, HI)
    second = factor_inverse_pair(block_ref[...] - nt(side, side, HI))
    out_ref[:HALF, :HALF] = first
    out_ref[:HALF, HALF:] = jnp.zeros_like(first)
    out_ref[HALF:, :HALF] = -nn(second, nn(side, first))
    out_ref[HALF:, HALF:] = second


def second_factor(after, side, block, inverse):
    return pl.pallas_call(
        last_kernel,
        in_specs=[anywhere()] + [vmem()] * 3,
        out_specs=vmem(),
        out_shape=jax.ShapeDtypeStruct((P_SIZE, P_SIZE), F32),
        compiler_params=params(32),
        cost_estimate=cost(10**10, 4 * P_SIZE * P_SIZE),
        name="second_factor",
    )(after, side, block, inverse)


def local(matrix, mixers, bucket_pair, mixer_index, sign_seed):
    cols = matrix.shape[1]
    rows_n, parts = lax.axis_size("rows"), lax.axis_size("cols")
    chips = rows_n // 2
    row, part = lax.axis_index("rows"), lax.axis_index("cols")
    core, chip = row % 2, row // 2

    def swap(value):
        return lax.ppermute(value, "rows", [(i, i ^ 1) for i in range(rows_n)])

    def shift(value, j):
        return lax.ppermute(value, "rows", [(i, (i + 2 * j) % rows_n) for i in range(rows_n)])

    def across(value, j):
        return lax.ppermute(value, "cols", [(i, i ^ j) for i in range(parts)])

    with jax.named_scope("names"):
        flips = 1 - 2 * (sign_seed >> 29 & 1)
        names = jnp.stack([bucket_pair[:, 0], bucket_pair[:, 1], flips, mixer_index, sign_seed])
        place = [part ^ j if parts == SLICES else j for j in range(SLICES)]
        order = [who * SLICES + c for who in (core, 1 - core) for c in place]
        order = jnp.stack([jnp.asarray(v, jnp.int32) for v in order + [chip, core, part]])
    with jax.named_scope("panel_mix"):
        tiles = mix_panel(matrix, mixers, names, order)
    with jax.named_scope("names"):
        (later,) = tie([names], tiles[0])
        pair = jnp.concatenate([later, swap(later)], axis=1)
        all_names = jnp.concatenate([pair] + [shift(pair, j) for j in range(1, chips)], axis=1)
    groups = chips if cols % (TILE * rows_n) == 0 else 1

    def spread(h, after):
        with jax.named_scope("panel_spread"):
            slices = tiles[h * SLICES : (h + 1) * SLICES]
            got = [slices[0]] + [lax.ppermute(slices[j], "cols", [(0, j)]) for j in range(1, SLICES)]
            keep, give = pick(order, after, got)
            return jnp.concatenate([keep, swap(give)])

    def gather_rows(held):
        with jax.named_scope("panel_rows"):
            return [held] + [shift(held, j) for j in range(1, chips)]

    def gather_cols(summed):
        with jax.named_scope("panel_cols"):
            sent = summed.astype(F16)
            if parts == SLICES:
                mine = [sent] + [across(sent, j) for j in range(1, parts)]
            else:
                mine = list(lax.all_gather(sent, "cols")[:SLICES])
            return [v.astype(F32) for v in mine + [swap(v) for v in mine]]

    half = names.shape[1] // 2
    with jax.named_scope("mix"):
        early = mix_tiles(matrix, mixers, names, tiles[0], 0, half)
    held0 = spread(0, early)
    arrived0 = gather_rows(held0)
    with jax.named_scope("mix"):
        late = mix_tiles(matrix, mixers, names, held0, half, half)
    held1 = spread(1, late)
    arrived1 = gather_rows(held1)
    mixed = (early, late)
    with jax.named_scope("panel_sum"):
        summed0 = sum_buckets(all_names, held1, arrived0)
    pieces0 = gather_cols(summed0)
    with jax.named_scope("panel_sum"):
        summed1 = sum_buckets(all_names, summed0, arrived1)
    pieces1 = gather_cols(summed1)
    with jax.named_scope("cross0"):
        panel0, *crossed0 = cross_parts(names, order, summed1, mixed, pieces0, groups)
    with jax.named_scope("factor0"):
        inverse0 = first_factor(first_gram(summed1, panel0))
    with jax.named_scope("cross1"):
        panel1, *crossed1 = cross_parts(names, order, inverse0, mixed, pieces1, groups)
    with jax.named_scope("gram1"):
        side, block = second_gram(crossed1[0], panel0, panel1)

    if groups == 1:
        inverse = second_factor(side, side, block, inverse0)
        total = lax.psum(jnp.concatenate([crossed0[0], crossed1[0]], axis=0), "rows")
        share = P_SIZE // rows_n
        return lax.dynamic_slice_in_dim(nn(inverse, total), row * share, share, 0)
    with jax.named_scope("cross_sum"):
        on_chip = [keep + swap(give) for keep, give in (crossed0, crossed1)]
    with jax.named_scope("factor1"):
        inverse = second_factor(on_chip[1], side, block, inverse0)
    with jax.named_scope("cross_sum"):
        totals = []
        for v in on_chip:
            total = v[0]
            for j in range(1, chips):
                total = total + shift(v[j], j)
            totals.append(total)
    with jax.named_scope("solve"):
        solved = nn(inverse, jnp.concatenate(totals, axis=0))
        return lax.all_to_all(solved, "rows", split_axis=0, concat_axis=1, tiled=True)


def solution(mesh):
    in_specs = (P("rows", "cols"), P(), P("rows", None), P("rows"), P("rows"))
    out_specs = P("rows", "cols")
    return jax.shard_map(local, mesh=mesh, in_specs=in_specs, out_specs=out_specs, check_vma=False)
```

time: 1100 us -> 180 us (0.16); the launches traced: 1080 us -> 179 us
  waiting for transfers between devices: 836 us -> 35.9 us
  other arithmetic: 115 us -> 1.48 us
  Pallas kernels: 0 us -> 73.3 us
  matrix products: 61 us -> 0.38 us
  starting transfers between devices: 7.15 us -> 49.7 us
  local copies, waits for them, and re-layouts: 48.4 us -> 7.35 us
  between operations: 15 us -> 0.64 us
    all_to_all x1 -> x0, waiting for transfers between devices: 724 us -> none  [local(): lax.all_to_all(buffer, 'rows', split_axis=1, concat_axis=0, tiled=True)]
    psum x2 -> x0, waiting for transfers between devices: 112 us -> none  [the longest x1 60.3 us: local(): gram_total, cross_total = lax.psum((gram_part, cross_part), 'rows')]
    pallas_call x0 -> x14, Pallas kernels: none -> 73.3 us  [the longest x2 20.1 us: mix_tiles(): pl.pallas_call(functools.partial(mix_kernel, per_step, start), grid_spec=...]
    dot_general x4 -> x1, matrix products: 56.6 us -> 0.38 us  [nn(): return jnp.dot(a, b, precision=HI, preferred_element_type=F32)]
    another operation x10 -> x1, other arithmetic: 54.6 us -> 0.66 us  [local(): jnp.stack([bucket_pair[:, 0], bucket_pair[:, 1], flips, mixer_index, sign...]
    ppermute x0 -> x40, starting transfers between devices: none -> 49.7 us  [the longest x15 29 us: shift(): lax.ppermute(value, 'rows', [(i, (i + 2 * j) % rows_n) for i in range(row...]
    reduce_sum x3 -> x0, other arithmetic: 47.1 us -> none  [the longest x2 46.9 us: local(): received = jnp.sum(arrived, axis=(0, 2), dtype=jnp.float32)]
    unnamed x6 -> x19, local copies, waits for them, and re-layouts: 41.7 us -> 5.01 us
  transfers between devices with their start and end apart: 3 -> 40, of which waited for: 3 -> 8; matrix products, arithmetic and copies ran while one was open for 0% -> 1% of each run, Pallas kernels for 0% -> 36%
where the time goes in v2:
time: 180 us; the launch traced here: 179 us
  Pallas kernels  73.3 us (41%)
  starting transfers between devices  49.7 us (28%)
  waiting for transfers between devices  35.9 us (20%)
  blocking collectives  10.8 us (6%)
  local copies, waits for them, and re-layouts  7.35 us (4%)
    ppermute x15, starting transfers between devices, shift(): lax.ppermute(value, 'rows', [(i, (i + 2 * j) % rows_n) for i in range(row...  29 us
    ppermute x15, waiting for transfers between devices, shift(): lax.ppermute(value, 'rows', [(i, (i + 2 * j) % rows_n) for i in range(row...  25.8 us
    pallas_call x2, Pallas kernels, mix_tiles(): pl.pallas_call(functools.partial(mix_kernel, per_step, start), grid_spec=...  20.1 us
    ppermute x6, starting transfers between devices, spread(): lax.ppermute(slices[j], 'cols', [(0, j)])  12.6 us
    pallas_call x1, Pallas kernels, second_factor(): pl.pallas_call(last_kernel, in_specs=[anywhere()] + [vmem()] * 3, out_spe...  12.3 us
    pallas_call x1, Pallas kernels, first_factor(): pl.pallas_call(factor_kernel, in_specs=[vmem()], out_specs=vmem(), out_sh...  11.6 us
    all_to_all x1, blocking collectives, local(): lax.all_to_all(solved, 'rows', split_axis=0, concat_axis=1, tiled=True)  10.8 us
    ppermute x6, waiting for transfers between devices, across(): return lax.ppermute(value, 'cols', [(i, i ^ j) for i in range(parts)])  10 us
  transfers between devices with their start and end apart: 40, of which 8 were waited for; matrix products, arithmetic and copies ran while one was open for 1% of the time, Pallas kernels for 36%

profile of v2, /device:TPU:0, one launch (start us, length us, event | category | flops | bytes accessed | tf_op | source)
XLA Modules:
  0.0 179.5 jit_solution(2650817493858451633)
XLA Ops:
  0.0 0.7 subtract_bitcast_fusion
  0.7 0.8 slice_bitcast_fusion.8
  1.4 0.7 stack.51.names_ref
  2.2 8.4 %mix_panel.1 = (bf16[2,32,16,128]{3,2,1,0:T(8,128)(2,1)S(1)}, bf16[2,32,16,128]{3,2,1,0:T(8,128)(2,1)S(1)}, bf16[2,32,16,128]{3,2,1,0:T(8,128)(2,1)S(1)}, bf16[2...) custom-call(s32[5,32]{1,0:T(8,128)S(1)} %stack.51.names_ref, ...), custom_call_target="tpu_custom_call" | custom-call | flops 805306368 | bytes 6291456 | tf_op jit(solution)/shard_map/panel_mix/mix_panel/pallas_call | solution.py:82
  10.6 4.8 %collective-permute-start.4 = (bf16[2,32,16,128]{3,2,1,0:T(8,128)(2,1)S(1)}, bf16[2,32,16,128]{3,2,1,0:T(8,128)(2,1)S(1)}, u32[]{:S(2)}, u32[]{:S(2)}) collective-permute-start(bf16[2,32,16,128]{3,2,1,0:T(8,128)(2,1)S(1)} %get-tuple-element.26), channel_id=1, source_target_pairs={{0,1},{4,5},{8,9},{12,13},{16,17},{20,21},{24,25},{28,29}} | collective-permute-start | bytes 786440 | tf_op jit(solution)/shard_map/panel_spread/ppermute | solution.py:439
  15.4 1.3 collective-permute-start.5
  16.8 1.3 collective-permute-start.6
  18.1 10.0 %mix_tiles.2.after_ref.early_ref = bf16[2048,1024]{1,0:T(8,128)(2,1)} custom-call(s32[5,32]{1,0:T(8,128)S(1)} %stack.51.names_ref, f32[4096,1024]{1,0:T(8,128)} %matrix_ref.5, f32[8,128,128]{2,1,0:T(8,128)S(1)} %copy-done.4, bf16[2,32,16,128]{3,2,1,0:T(8,128)(2,1)S(1)} %get-tuple-element.25.refs_1_.after_ref.refs_0_), custom_call_target="tpu_custom_call" | custom-call | flops 3221225472 | bytes 12582912 | tf_op jit(solution)/shard_map/mix/mix_tiles/pallas_call | solution.py:112
  28.1 2.2 %copy-done = bf16[2048,1024]{1,0:T(8,128)(2,1)S(1)} copy-done((bf16[2048,1024]{1,0:T(8,128)(2,1)S(1)}, bf16[2048,1024]{1,0:T(8,128)(2,1)}, u32[]{:S(2)}) %copy-start) | copy-done | bytes 4194328
  30.3 0.6 pick.2
  31.0 0.6 copy.10.refs_0_
  32.1 1.3 collective-permute-start.8
  33.4 1.3 collective-permute-start.9
  34.7 2.5 %collective-permute-start.10 = (bf16[2,32,16,128]{3,2,1,0:T(8,128)(2,1)S(1)}, bf16[2,32,16,128]{3,2,1,0:T(8,128)(2,1)S(1)}, u32[]{:S(2)}, u32[]{:S(2)}) collective-permute-start(bf16[2,32,16,128]{3,2,1,0:T(8,128)(2,1)S(1)} %copy-done.7), channel_id=1, source_target_pairs={{0,3},{4,7},{8,11},{12,15},{16,19},{20,23},{24,27},{28,31}} | collective-permute-start | bytes 786440 | tf_op jit(solution)/shard_map/panel_spread/ppermute | solution.py:439
  37.3 3.7 %collective-permute-start.14 = (bf16[64,16,128]{2,1,0:T(8,128)(2,1)S(1)}, bf16[64,16,128]{2,1,0:T(8,128)(2,1)S(1)}, u32[]{:S(2)}, u32[]{:S(2)}) collective-permute-start(bf16[64,16,128]{2,1,0:T(8,128)(2,1)S(1)} %constant_dynamic-update-slice_fusion.after_ref.refs_0_), channel_id=1, source_target_pairs={{0,24},{4,28},{8,0},{12,4},{16,8},{20,12},{24,16},{28,20},{1,25},{... | collective-permute-start | bytes 786440 | tf_op jit(solution)/shard_map/panel_rows/ppermute | solution.py:417
  40.9 10.1 %mix_tiles.3.after_ref.late_ref = bf16[2048,1024]{1,0:T(8,128)(2,1)} custom-call(s32[5,32]{1,0:T(8,128)S(1)} %stack.51.names_ref, f32[4096,1024]{1,0:T(8,128)} %matrix_ref.5, f32[8,128,128]{2,1,0:T(8,128)S(1)} %copy-done.4, bf16[64,16,128]{2,1,0:T(8,128)(2,1)S(1)} %constant_dynamic-update-slice_fusion.after_ref.refs_0_), custom_call_target="tpu_custom_call" | custom-call | flops 3221225472 | bytes 12582912 | tf_op jit(solution)/shard_map/mix/mix_tiles/pallas_call | solution.py:112
  51.0 1.0 collective-permute-start.12
  52.0 2.2 %copy-done.2 = bf16[2048,1024]{1,0:T(8,128)(2,1)S(1)} copy-done((bf16[2048,1024]{1,0:T(8,128)(2,1)S(1)}, bf16[2048,1024]{1,0:T(8,128)(2,1)}, u32[]{:S(2)}) %copy-start.2) | copy-done | bytes 4194328
  54.2 0.6 pick.3
  55.0 2.9 %collective-permute-start.3 = (s32[5,64]{1,0:T(8,128)S(1)}, s32[5,64]{1,0:T(8,128)S(1)}, u32[]{:S(2)}, u32[]{:S(2)}) collective-permute-start(s32[5,64]{1,0:T(8,128)S(1)} %pad_add_fusion), channel_id=1, source_target_pairs={{0,24},{4,28},{8,0},{12,4},{16,8},{20,12},{24,16},{28,20},{1,25},{... | collective-permute-start | bytes 3848 | tf_op jit(solution)/shard_map/names/ppermute | solution.py:417
  57.8 4.4 %collective-permute-done.3 = s32[5,64]{1,0:T(8,128)S(1)} collective-permute-done((s32[5,64]{1,0:T(8,128)S(1)}, s32[5,64]{1,0:T(8,128)S(1)}, u32[]{:S(2)}, u32[]{:S(2)}) %collective-permute-start.3) | collective-permute-done | bytes 1312 | tf_op jit(solution)/shard_map/names/ppermute | solution.py:417
  62.2 6.1 %collective-permute-start.2 = (s32[5,64]{1,0:T(8,128)S(1)}, s32[5,64]{1,0:T(8,128)S(1)}, u32[]{:S(2)}, u32[]{:S(2)}) collective-permute-start(s32[5,64]{1,0:T(8,128)S(1)} %pad_add_fusion), channel_id=1, source_target_pairs={{0,16},{4,20},{8,24},{12,28},{16,0},{20,4},{24,8},{28,12},{1,17},{... | collective-permute-start | bytes 3848 | tf_op jit(solution)/shard_map/names/ppermute | solution.py:417
  68.3 1.6 collective-permute-done.2
  69.9 3.9 %collective-permute-start.1 = (s32[5,64]{1,0:T(8,128)S(1)}, s32[5,64]{1,0:T(8,128)S(1)}, u32[]{:S(2)}, u32[]{:S(2)}) collective-permute-start(s32[5,64]{1,0:T(8,128)S(1)} %pad_add_fusion), channel_id=1, source_target_pairs={{0,8},{4,12},{8,16},{12,20},{16,24},{20,28},{24,0},{28,4},{1,9},{5... | collective-permute-start | bytes 3848 | tf_op jit(solution)/shard_map/names/ppermute | solution.py:417
  73.8 1.5 collective-permute-done.1
  75.4 1.6 collective-permute-start.17
  77.0 2.1 %collective-permute-start.16 = (bf16[64,16,128]{2,1,0:T(8,128)(2,1)S(1)}, bf16[64,16,128]{2,1,0:T(8,128)(2,1)S(1)}, u32[]{:S(2)}, u32[]{:S(2)}) collective-permute-start(bf16[64,16,128]{2,1,0:T(8,128)(2,1)S(1)} %constant_dynamic-update-slice_fusion.2.after_ref.refs_0_), channel_id=1, source_target_pairs={{0,16},{4,20},{8,24},{12,28},{16,0},{20,4},{24,8},{28,12},{1,17},{... | collective-permute-start | bytes 786440 | tf_op jit(solution)/shard_map/panel_rows/ppermute | solution.py:417
  79.1 2.8 %sum_buckets.2.after_ref = f32[64,16,128]{2,1,0:T(8,128)S(1)} custom-call(s32[5,256]{1,0:T(8,128)S(1)} %concatenate.17.names_ref, bf16[64,16,128]{2,1,0:T(8,128)(2,1)S(1)} %constant_dynamic-update-slice_fusion.2.after_ref.refs_0_, bf16[64,16,128]{2,1,0:T(8,128)(2,1)S(1)} %constant_dynamic-update-slice_fusion.after_ref.refs_0_, ...), custom_call_target="tpu_custom_call" | custom-call | flops 1000000 | bytes 4000000 | tf_op jit(solution)/shard_map/panel_sum/sum_buckets/pallas_call | solution.py:193
  82.2 1.6 collective-permute-done.17.refs_3_
  83.8 1.8 collective-permute-start.18
  85.6 13.9 %collective-permute-done.16.refs_2_ = bf16[64,16,128]{2,1,0:T(8,128)(2,1)S(1)} collective-permute-done((bf16[64,16,128]{2,1,0:T(8,128)(2,1)S(1)}, bf16[64,16,128]{2,1,0:T(8,128)(2,1)S(1)}, u32[]{:S(2)}, u32[]{:S(2)}) %collective-permute-start.16) | collective-permute-done | bytes 262176 | tf_op jit(solution)/shard_map/panel_rows/ppermute | solution.py:417
  99.5 2.8 %sum_buckets.3.after_ref = f32[64,16,128]{2,1,0:T(8,128)S(1)} custom-call(s32[5,256]{1,0:T(8,128)S(1)} %concatenate.17.names_ref, f32[64,16,128]{2,1,0:T(8,128)S(1)} %sum_buckets.2.after_ref, bf16[64,16,128]{2,1,0:T(8,128)(2,1)S(1)} %constant_dynamic-update-slice_fusion.2.after_ref.refs_0_, bf16[64,16,128]{2,1,0:T(8,128)(2,1)S(1)} %collective-permute-done.15.refs_1_, ...), custom_call_target="tpu_custom_call" | custom-call | flops 1000000 | bytes 4000000 | tf_op jit(solution)/shard_map/panel_sum/sum_buckets/pallas_call | solution.py:193
  102.6 0.6 collective-permute-start.28
  103.1 3.1 %collective-permute-start.25 = (f16[64,16,128]{2,1,0:T(8,128)(2,1)S(1)}, f16[64,16,128]{2,1,0:T(8,128)(2,1)S(1)}, u32[]{:S(2)}, u32[]{:S(2)}) collective-permute-start(f16[64,16,128]{2,1,0:T(8,128)(2,1)S(1)} %get-tuple-element.46), channel_id=1, source_target_pairs={{0,1},{1,0},{2,3},{3,2},{4,5},{5,4},{6,7},{7,6},{8,9},{9,8},{10,11... | collective-permute-start | bytes 786440 | tf_op jit(solution)/shard_map/panel_cols/ppermute | solution.py:420
  106.3 6.3 %collective-permute-done.27 = f16[64,16,128]{2,1,0:T(8,128)(2,1)S(1)} collective-permute-done((f16[64,16,128]{2,1,0:T(8,128)(2,1)S(1)}, f16[64,16,128]{2,1,0:T(8,128)(2,1)S(1)}, u32[]{:S(2)}, u32[]{:S(2)}) %collective-permute-start.27) | collective-permute-done | bytes 262176 | tf_op jit(solution)/shard_map/panel_cols/ppermute | solution.py:420
  113.4 3.7 %collective-permute-done.26 = f16[64,16,128]{2,1,0:T(8,128)(2,1)S(1)} collective-permute-done((f16[64,16,128]{2,1,0:T(8,128)(2,1)S(1)}, f16[64,16,128]{2,1,0:T(8,128)(2,1)S(1)}, u32[]{:S(2)}, u32[]{:S(2)}) %collective-permute-start.26) | collective-permute-done | bytes 262176 | tf_op jit(solution)/shard_map/panel_cols/ppermute | solution.py:420
  118.0 4.1 %cross_parts.2 = (f32[64,128,128]{2,1,0:T(8,128)S(1)}, f32[4,128,128]{2,1,0:T(8,128)S(1)}, f32[4,128,128]{2,1,0:T(8,128)S(1)}) custom-call(s32[5,32]{1,0:T(8,128)S(1)} %stack.51.names_ref, s32[11]{0:T(128)S(1)} %stack.63.order_ref, f32[64,16,128]{2,1,0:T(8,128)S(1)} %sum_buckets.3.after_ref, bf16[2048,1024]{1,0:T(8,128)(2,1)S(1)} %copy-done.1, ...), custom_call_target="tpu_custom_call" | custom-call | flops 2147483648 | bytes 8388608 | tf_op jit(solution)/shard_map/cross0/cross_parts/pallas_call | solution.py:260
  122.1 2.5 %first_gram.1.block_ref = f32[128,128]{1,0:T(8,128)S(1)} custom-call(f32[64,16,128]{2,1,0:T(8,128)S(1)} %sum_buckets.3.after_ref, f32[64,128,128]{2,1,0:T(8,128)S(1)} %get-tuple-element.37.panel.panel0), custom_call_target="tpu_custom_call" | custom-call | flops 3000000000 | bytes 4194304 | tf_op jit(solution)/shard_map/factor0/first_gram/pallas_call | solution.py:326
  124.6 0.6 collective-permute-start.33
  125.2 11.6 %first_factor.1.after_ref.inverse_ref = f32[128,128]{1,0:T(8,128)S(1)} custom-call(f32[128,128]{1,0:T(8,128)S(1)} %first_gram.1.block_ref), custom_call_target="tpu_custom_call" | custom-call | flops 10000000000 | bytes 131072 | tf_op jit(solution)/shard_map/factor0/first_factor/pallas_call | solution.py:343
  136.9 4.1 %cross_parts.3 = (f32[64,128,128]{2,1,0:T(8,128)S(1)}, f32[4,128,128]{2,1,0:T(8,128)S(1)}, f32[4,128,128]{2,1,0:T(8,128)S(1)}) custom-call(s32[5,32]{1,0:T(8,128)S(1)} %stack.51.names_ref, s32[11]{0:T(128)S(1)} %stack.63.order_ref, f32[128,128]{1,0:T(8,128)S(1)} %first_factor.1.after_ref.inverse_ref, bf16[2048,1024]{1,0:T(8,128)(2,1)S(1)} %copy-done.1, ...), custom_call_target="tpu_custom_call" | custom-call | flops 2147483648 | bytes 8388608 | tf_op jit(solution)/shard_map/cross1/cross_parts/pallas_call | solution.py:260
  141.2 3.8 %collective-permute-start.36 = (f32[128,128]{1,0:T(8,128)S(1)}, f32[128,128]{1,0:T(8,128)S(1)}, u32[]{:S(2)}, u32[]{:S(2)}) collective-permute-start(f32[128,128]{1,0:T(8,128)S(1)} %get-tuple-element.50), channel_id=1, source_target_pairs={{0,24},{4,28},{8,0},{12,4},{16,8},{20,12},{24,16},{28,20},{1,25},{... | collective-permute-start | bytes 196616 | tf_op jit(solution)/shard_map/cross_sum/ppermute | solution.py:417
  145.0 3.4 %second_gram.1 = (f32[128,128]{1,0:T(8,128)S(1)}, f32[128,128]{1,0:T(8,128)S(1)}) custom-call(f32[4,128,128]{2,1,0:T(8,128)S(1)} %get-tuple-element.38.after_ref, f32[64,128,128]{2,1,0:T(8,128)S(1)} %get-tuple-element.37.panel.panel0, f32[64,128,128]{2,1,0:T(8,128)S(1)} %get-tuple-element.40.panel1), custom_call_target="tpu_custom_call" | custom-call | flops 4000000000 | bytes 8388608 | tf_op jit(solution)/shard_map/gram1/second_gram/pallas_call | solution.py:372
  148.5 2.7 %collective-permute-done.35 = f32[128,128]{1,0:T(8,128)S(1)} collective-permute-done((f32[128,128]{1,0:T(8,128)S(1)}, f32[128,128]{1,0:T(8,128)S(1)}, u32[]{:S(2)}, u32[]{:S(2)}) %collective-permute-start.35) | collective-permute-done | bytes 65568 | tf_op jit(solution)/shard_map/cross_sum/ppermute | solution.py:417
  151.4 3.8 %collective-permute-start.39 = (f32[128,128]{1,0:T(8,128)S(1)}, f32[128,128]{1,0:T(8,128)S(1)}, u32[]{:S(2)}, u32[]{:S(2)}) collective-permute-start(f32[128,128]{1,0:T(8,128)S(1)} %get-tuple-element.53), channel_id=1, source_target_pairs={{0,24},{4,28},{8,0},{12,4},{16,8},{20,12},{24,16},{28,20},{1,25},{... | collective-permute-start | bytes 196616 | tf_op jit(solution)/shard_map/cross_sum/ppermute | solution.py:417
  155.2 12.3 %second_factor.1 = f32[256,256]{1,0:T(8,128)S(1)} custom-call(f32[4,128,128]{2,1,0:T(8,128)S(1)} %add.62.after_ref, f32[128,128]{1,0:T(8,128)S(1)} %get-tuple-element.41.side_ref, f32[128,128]{1,0:T(8,128)S(1)} %get-tuple-element.42.block_ref, f32[128,128]{1,0:T(8,128)S(1)} %first_factor.1.after_ref.inverse_ref), custom_call_target="tpu_custom_call" | custom-call | flops 10000000000 | bytes 262144 | tf_op jit(solution)/shard_map/factor1/second_factor/pallas_call | solution.py:395
  168.0 10.8 %all_to_all.19 = f32[8,32,128]{2,1,0:T(8,128)S(1)} all-to-all(f32[8,32,128]{2,1,0:T(8,128)S(1)} %bitcast.55), channel_id=1, replica_groups=mesh['rows'=8,'cols'=4] {'rows'}, dimensions={0} | all-to-all | bytes 262144 | tf_op jit(solution)/shard_map/solve/all_to_all | solution.py:499
  178.8 0.7 copy_bitcast_fusion
  (98 shorter events, 3.8 us)
Async XLA Ops:
  2.2 15.9 %copy-start.4 = (f32[8,128,128]{2,1,0:T(8,128)S(1)}, f32[8,128,128]{2,1,0:T(8,128)}, u32[]{:S(2)}) copy-start(f32[8,128,128]{2,1,0:T(8,128)} %mixers_ref.5) | copy-start | bytes 1572868
  10.6 17.5 %copy-start.5 = (bf16[2,32,16,128]{3,2,1,0:T(8,128)(2,1)}, bf16[2,32,16,128]{3,2,1,0:T(8,128)(2,1)S(1)}, u32[]{:S(2)}) copy-start(bf16[2,32,16,128]{3,2,1,0:T(8,128)(2,1)S(1)} %get-tuple-element.25.refs_1_.after_ref.refs_0_) | copy-start | bytes 786436
  10.6 17.5 %collective-permute-start.4 = (bf16[2,32,16,128]{3,2,1,0:T(8,128)(2,1)S(1)}, bf16[2,32,16,128]{3,2,1,0:T(8,128)(2,1)S(1)}, u32[]{:S(2)}, u32[]{:S(2)}) collective-permute-start(bf16[2,32,16,128]{3,2,1,0:T(8,128)(2,1)S(1)} %get-tuple-element.26), channel_id=1, source_target_pairs={{0,1},{4,5},{8,9},{12,13},{16,17},{20,21},{24,25},{28,29}} | collective-permute-start | bytes 786440 | tf_op jit(solution)/shard_map/panel_spread/ppermute | solution.py:439
  15.4 12.7 %collective-permute-start.5 = (bf16[2,32,16,128]{3,2,1,0:T(8,128)(2,1)S(1)}, bf16[2,32,16,128]{3,2,1,0:T(8,128)(2,1)S(1)}, u32[]{:S(2)}, u32[]{:S(2)}) collective-permute-start(bf16[2,32,16,128]{3,2,1,0:T(8,128)(2,1)S(1)} %get-tuple-element.27), channel_id=1, source_target_pairs={{0,2},{4,6},{8,10},{12,14},{16,18},{20,22},{24,26},{28,30}} | collective-permute-start | bytes 786440 | tf_op jit(solution)/shard_map/panel_spread/ppermute | solution.py:439
  16.8 11.3 %collective-permute-start.6 = (bf16[2,32,16,128]{3,2,1,0:T(8,128)(2,1)S(1)}, bf16[2,32,16,128]{3,2,1,0:T(8,128)(2,1)S(1)}, u32[]{:S(2)}, u32[]{:S(2)}) collective-permute-start(bf16[2,32,16,128]{3,2,1,0:T(8,128)(2,1)S(1)} %get-tuple-element.28), channel_id=1, source_target_pairs={{0,3},{4,7},{8,11},{12,15},{16,19},{20,23},{24,27},{28,31}} | collective-permute-start | bytes 786440 | tf_op jit(solution)/shard_map/panel_spread/ppermute | solution.py:439
  18.1 16.6 %copy-start.7 = (bf16[2,32,16,128]{3,2,1,0:T(8,128)(2,1)S(1)}, bf16[2,32,16,128]{3,2,1,0:T(8,128)(2,1)}, u32[]{:S(2)}) copy-start(bf16[2,32,16,128]{3,2,1,0:T(8,128)(2,1)} %get-tuple-element.34) | copy-start | bytes 786436
  28.1 2.2 %copy-start = (bf16[2048,1024]{1,0:T(8,128)(2,1)S(1)}, bf16[2048,1024]{1,0:T(8,128)(2,1)}, u32[]{:S(2)}) copy-start(bf16[2048,1024]{1,0:T(8,128)(2,1)} %mix_tiles.2.after_ref.early_ref) | copy-start | bytes 12582916
  30.9 6.4 %collective-permute-start.7 = (bf16[32,16,128]{2,1,0:T(8,128)(2,1)S(1)}, bf16[32,16,128]{2,1,0:T(8,128)(2,1)S(1)}, u32[]{:S(2)}, u32[]{:S(2)}) collective-permute-start(bf16[32,16,128]{2,1,0:T(8,128)(2,1)S(1)} %get-tuple-element.30), channel_id=1, source_target_pairs={{0,4},{4,0},{8,12},{12,8},{16,20},{20,16},{24,28},{28,24},{1,5},{5... | collective-permute-start | bytes 393224 | tf_op jit(solution)/shard_map/panel_spread/ppermute | solution.py:414
  31.6 23.3 %collective-permute-start = (s32[5,32]{1,0:T(8,128)}, s32[5,32]{1,0:T(8,128)S(1)}, u32[]{:S(2)}, u32[]{:S(2)}) collective-permute-start(s32[5,32]{1,0:T(8,128)} %tie.1), channel_id=1, source_target_pairs={{0,4},{4,0},{8,12},{12,8},{16,20},{20,16},{24,28},{28,24},{1,5},{5... | collective-permute-start | bytes 1928 | tf_op jit(solution)/shard_map/names/ppermute | solution.py:414
  32.1 18.9 %collective-permute-start.8 = (bf16[2,32,16,128]{3,2,1,0:T(8,128)(2,1)S(1)}, bf16[2,32,16,128]{3,2,1,0:T(8,128)(2,1)S(1)}, u32[]{:S(2)}, u32[]{:S(2)}) collective-permute-start(bf16[2,32,16,128]{3,2,1,0:T(8,128)(2,1)S(1)} %get-tuple-element.32), channel_id=1, source_target_pairs={{0,1},{4,5},{8,9},{12,13},{16,17},{20,21},{24,25},{28,29}} | collective-permute-start | bytes 786440 | tf_op jit(solution)/shard_map/panel_spread/ppermute | solution.py:439
  33.4 17.6 %collective-permute-start.9 = (bf16[2,32,16,128]{3,2,1,0:T(8,128)(2,1)S(1)}, bf16[2,32,16,128]{3,2,1,0:T(8,128)(2,1)S(1)}, u32[]{:S(2)}, u32[]{:S(2)}) collective-permute-start(bf16[2,32,16,128]{3,2,1,0:T(8,128)(2,1)S(1)} %get-tuple-element.33), channel_id=1, source_target_pairs={{0,2},{4,6},{8,10},{12,14},{16,18},{20,22},{24,26},{28,30}} | collective-permute-start | bytes 786440 | tf_op jit(solution)/shard_map/panel_spread/ppermute | solution.py:439
  34.7 17.3 %collective-permute-start.10 = (bf16[2,32,16,128]{3,2,1,0:T(8,128)(2,1)S(1)}, bf16[2,32,16,128]{3,2,1,0:T(8,128)(2,1)S(1)}, u32[]{:S(2)}, u32[]{:S(2)}) collective-permute-start(bf16[2,32,16,128]{3,2,1,0:T(8,128)(2,1)S(1)} %copy-done.7), channel_id=1, source_target_pairs={{0,3},{4,7},{8,11},{12,15},{16,19},{20,23},{24,27},{28,31}} | collective-permute-start | bytes 786440 | tf_op jit(solution)/shard_map/panel_spread/ppermute | solution.py:439
  37.3 41.8 %collective-permute-start.14 = (bf16[64,16,128]{2,1,0:T(8,128)(2,1)S(1)}, bf16[64,16,128]{2,1,0:T(8,128)(2,1)S(1)}, u32[]{:S(2)}, u32[]{:S(2)}) collective-permute-start(bf16[64,16,128]{2,1,0:T(8,128)(2,1)S(1)} %constant_dynamic-update-slice_fusion.after_ref.refs_0_), channel_id=1, source_target_pairs={{0,24},{4,28},{8,0},{12,4},{16,8},{20,12},{24,16},{28,20},{1,25},{... | collective-permute-start | bytes 786440 | tf_op jit(solution)/shard_map/panel_rows/ppermute | solution.py:417
  40.9 13.9 %copy-start.6 = (s32[5,32]{1,0:T(8,128)S(1)}, s32[5,32]{1,0:T(8,128)}, u32[]{:S(2)}) copy-start(s32[5,32]{1,0:T(8,128)} %tie.1) | copy-start | bytes 1924
  51.0 28.1 %collective-permute-start.13 = (bf16[64,16,128]{2,1,0:T(8,128)(2,1)S(1)}, bf16[64,16,128]{2,1,0:T(8,128)(2,1)S(1)}, u32[]{:S(2)}, u32[]{:S(2)}) collective-permute-start(bf16[64,16,128]{2,1,0:T(8,128)(2,1)S(1)} %constant_dynamic-update-slice_fusion.after_ref.refs_0_), channel_id=1, source_target_pairs={{0,16},{4,20},{8,24},{12,28},{16,0},{20,4},{24,8},{28,12},{1,17},{... | collective-permute-start | bytes 786440 | tf_op jit(solution)/shard_map/panel_rows/ppermute | solution.py:417
  51.0 28.1 %collective-permute-start.12 = (bf16[64,16,128]{2,1,0:T(8,128)(2,1)S(1)}, bf16[64,16,128]{2,1,0:T(8,128)(2,1)S(1)}, u32[]{:S(2)}, u32[]{:S(2)}) collective-permute-start(bf16[64,16,128]{2,1,0:T(8,128)(2,1)S(1)} %constant_dynamic-update-slice_fusion.after_ref.refs_0_), channel_id=1, source_target_pairs={{0,8},{4,12},{8,16},{12,20},{16,24},{20,28},{24,0},{28,4},{1,9},{5... | collective-permute-start | bytes 786440 | tf_op jit(solution)/shard_map/panel_rows/ppermute | solution.py:417
  52.0 2.2 %copy-start.2 = (bf16[2048,1024]{1,0:T(8,128)(2,1)S(1)}, bf16[2048,1024]{1,0:T(8,128)(2,1)}, u32[]{:S(2)}) copy-start(bf16[2048,1024]{1,0:T(8,128)(2,1)} %mix_tiles.3.after_ref.late_ref) | copy-start | bytes 12582916
  54.8 20.6 %collective-permute-start.11 = (bf16[32,16,128]{2,1,0:T(8,128)(2,1)S(1)}, bf16[32,16,128]{2,1,0:T(8,128)(2,1)S(1)}, u32[]{:S(2)}, u32[]{:S(2)}) collective-permute-start(bf16[32,16,128]{2,1,0:T(8,128)(2,1)S(1)} %get-tuple-element.36), channel_id=1, source_target_pairs={{0,4},{4,0},{8,12},{12,8},{16,20},{20,16},{24,28},{28,24},{1,5},{5... | collective-permute-start | bytes 393224 | tf_op jit(solution)/shard_map/panel_spread/ppermute | solution.py:414
  55.0 7.3 %collective-permute-start.3 = (s32[5,64]{1,0:T(8,128)S(1)}, s32[5,64]{1,0:T(8,128)S(1)}, u32[]{:S(2)}, u32[]{:S(2)}) collective-permute-start(s32[5,64]{1,0:T(8,128)S(1)} %pad_add_fusion), channel_id=1, source_target_pairs={{0,24},{4,28},{8,0},{12,4},{16,8},{20,12},{24,16},{28,20},{1,25},{... | collective-permute-start | bytes 3848 | tf_op jit(solution)/shard_map/names/ppermute | solution.py:417
  62.2 7.7 %collective-permute-start.2 = (s32[5,64]{1,0:T(8,128)S(1)}, s32[5,64]{1,0:T(8,128)S(1)}, u32[]{:S(2)}, u32[]{:S(2)}) collective-permute-start(s32[5,64]{1,0:T(8,128)S(1)} %pad_add_fusion), channel_id=1, source_target_pairs={{0,16},{4,20},{8,24},{12,28},{16,0},{20,4},{24,8},{28,12},{1,17},{... | collective-permute-start | bytes 3848 | tf_op jit(solution)/shard_map/names/ppermute | solution.py:417
  69.9 5.4 %collective-permute-start.1 = (s32[5,64]{1,0:T(8,128)S(1)}, s32[5,64]{1,0:T(8,128)S(1)}, u32[]{:S(2)}, u32[]{:S(2)}) collective-permute-start(s32[5,64]{1,0:T(8,128)S(1)} %pad_add_fusion), channel_id=1, source_target_pairs={{0,8},{4,12},{8,16},{12,20},{16,24},{20,28},{24,0},{28,4},{1,9},{5... | collective-permute-start | bytes 3848 | tf_op jit(solution)/shard_map/names/ppermute | solution.py:417
  75.4 8.4 %collective-permute-start.17 = (bf16[64,16,128]{2,1,0:T(8,128)(2,1)S(1)}, bf16[64,16,128]{2,1,0:T(8,128)(2,1)S(1)}, u32[]{:S(2)}, u32[]{:S(2)}) collective-permute-start(bf16[64,16,128]{2,1,0:T(8,128)(2,1)S(1)} %constant_dynamic-update-slice_fusion.2.after_ref.refs_0_), channel_id=1, source_target_pairs={{0,24},{4,28},{8,0},{12,4},{16,8},{20,12},{24,16},{28,20},{1,25},{... | collective-permute-start | bytes 786440 | tf_op jit(solution)/shard_map/panel_rows/ppermute | solution.py:417
  77.0 22.5 %collective-permute-start.16 = (bf16[64,16,128]{2,1,0:T(8,128)(2,1)S(1)}, bf16[64,16,128]{2,1,0:T(8,128)(2,1)S(1)}, u32[]{:S(2)}, u32[]{:S(2)}) collective-permute-start(bf16[64,16,128]{2,1,0:T(8,128)(2,1)S(1)} %constant_dynamic-update-slice_fusion.2.after_ref.refs_0_), channel_id=1, source_target_pairs={{0,16},{4,20},{8,24},{12,28},{16,0},{20,4},{24,8},{28,12},{1,17},{... | collective-permute-start | bytes 786440 | tf_op jit(solution)/shard_map/panel_rows/ppermute | solution.py:417
  79.1 20.4 %collective-permute-start.15 = (bf16[64,16,128]{2,1,0:T(8,128)(2,1)S(1)}, bf16[64,16,128]{2,1,0:T(8,128)(2,1)S(1)}, u32[]{:S(2)}, u32[]{:S(2)}) collective-permute-start(bf16[64,16,128]{2,1,0:T(8,128)(2,1)S(1)} %constant_dynamic-update-slice_fusion.2.after_ref.refs_0_), channel_id=1, source_target_pairs={{0,8},{4,12},{8,16},{12,20},{16,24},{20,28},{24,0},{28,4},{1,9},{5... | collective-permute-start | bytes 786440 | tf_op jit(solution)/shard_map/panel_rows/ppermute | solution.py:417
  82.0 20.5 %collective-permute-start.20 = (f16[64,16,128]{2,1,0:T(8,128)(2,1)S(1)}, f16[64,16,128]{2,1,0:T(8,128)(2,1)S(1)}, u32[]{:S(2)}, u32[]{:S(2)}) collective-permute-start(f16[64,16,128]{2,1,0:T(8,128)(2,1)S(1)} %get-tuple-element.48), channel_id=1, source_target_pairs={{0,3},{1,2},{2,1},{3,0},{4,7},{5,6},{6,5},{7,4},{8,11},{9,10},{10,... | collective-permute-start | bytes 786440 | tf_op jit(solution)/shard_map/panel_cols/ppermute | solution.py:420
  82.1 21.0 %collective-permute-start.19 = (f16[64,16,128]{2,1,0:T(8,128)(2,1)S(1)}, f16[64,16,128]{2,1,0:T(8,128)(2,1)S(1)}, u32[]{:S(2)}, u32[]{:S(2)}) collective-permute-start(f16[64,16,128]{2,1,0:T(8,128)(2,1)S(1)} %get-tuple-element.48), channel_id=1, source_target_pairs={{0,2},{1,3},{2,0},{3,1},{4,6},{5,7},{6,4},{7,5},{8,10},{9,11},{10,... | collective-permute-start | bytes 786440 | tf_op jit(solution)/shard_map/panel_cols/ppermute | solution.py:420
  83.8 19.3 %collective-permute-start.18 = (f16[64,16,128]{2,1,0:T(8,128)(2,1)S(1)}, f16[64,16,128]{2,1,0:T(8,128)(2,1)S(1)}, u32[]{:S(2)}, u32[]{:S(2)}) collective-permute-start(f16[64,16,128]{2,1,0:T(8,128)(2,1)S(1)} %get-tuple-element.48), channel_id=1, source_target_pairs={{0,1},{1,0},{2,3},{3,2},{4,5},{5,4},{6,7},{7,6},{8,9},{9,8},{10,11... | collective-permute-start | bytes 786440 | tf_op jit(solution)/shard_map/panel_cols/ppermute | solution.py:420
  99.5 6.7 %collective-permute-start.21 = (f16[64,16,128]{2,1,0:T(8,128)(2,1)S(1)}, f16[64,16,128]{2,1,0:T(8,128)(2,1)S(1)}, u32[]{:S(2)}, u32[]{:S(2)}) collective-permute-start(f16[64,16,128]{2,1,0:T(8,128)(2,1)S(1)} %get-tuple-element.48), channel_id=1, source_target_pairs={{0,4},{4,0},{8,12},{12,8},{16,20},{20,16},{24,28},{28,24},{1,5},{5... | collective-permute-start | bytes 786440 | tf_op jit(solution)/shard_map/panel_cols/ppermute | solution.py:414
  102.4 15.5 %copy-start.1 = (bf16[2048,1024]{1,0:T(8,128)(2,1)S(1)}, bf16[2048,1024]{1,0:T(8,128)(2,1)}, u32[]{:S(2)}) copy-start(bf16[2048,1024]{1,0:T(8,128)(2,1)} %mix_tiles.2.after_ref.early_ref) | copy-start | bytes 12582916
  102.5 15.5 %copy-start.3 = (bf16[2048,1024]{1,0:T(8,128)(2,1)S(1)}, bf16[2048,1024]{1,0:T(8,128)(2,1)}, u32[]{:S(2)}) copy-start(bf16[2048,1024]{1,0:T(8,128)(2,1)} %mix_tiles.3.after_ref.late_ref) | copy-start | bytes 12582916
  102.5 10.1 %collective-permute-start.27 = (f16[64,16,128]{2,1,0:T(8,128)(2,1)S(1)}, f16[64,16,128]{2,1,0:T(8,128)(2,1)S(1)}, u32[]{:S(2)}, u32[]{:S(2)}) collective-permute-start(f16[64,16,128]{2,1,0:T(8,128)(2,1)S(1)} %get-tuple-element.46), channel_id=1, source_target_pairs={{0,3},{1,2},{2,1},{3,0},{4,7},{5,6},{6,5},{7,4},{8,11},{9,10},{10,... | collective-permute-start | bytes 786440 | tf_op jit(solution)/shard_map/panel_cols/ppermute | solution.py:420
  102.6 10.0 %collective-permute-start.28 = (f16[64,16,128]{2,1,0:T(8,128)(2,1)S(1)}, f16[64,16,128]{2,1,0:T(8,128)(2,1)S(1)}, u32[]{:S(2)}, u32[]{:S(2)}) collective-permute-start(f16[64,16,128]{2,1,0:T(8,128)(2,1)S(1)} %get-tuple-element.46), channel_id=1, source_target_pairs={{0,4},{4,0},{8,12},{12,8},{16,20},{20,16},{24,28},{28,24},{1,5},{5... | collective-permute-start | bytes 786440 | tf_op jit(solution)/shard_map/panel_cols/ppermute | solution.py:414
  103.1 13.9 %collective-permute-start.26 = (f16[64,16,128]{2,1,0:T(8,128)(2,1)S(1)}, f16[64,16,128]{2,1,0:T(8,128)(2,1)S(1)}, u32[]{:S(2)}, u32[]{:S(2)}) collective-permute-start(f16[64,16,128]{2,1,0:T(8,128)(2,1)S(1)} %get-tuple-element.46), channel_id=1, source_target_pairs={{0,2},{1,3},{2,0},{3,1},{4,6},{5,7},{6,4},{7,5},{8,10},{9,11},{10,... | collective-permute-start | bytes 786440 | tf_op jit(solution)/shard_map/panel_cols/ppermute | solution.py:420
  103.1 14.0 %collective-permute-start.25 = (f16[64,16,128]{2,1,0:T(8,128)(2,1)S(1)}, f16[64,16,128]{2,1,0:T(8,128)(2,1)S(1)}, u32[]{:S(2)}, u32[]{:S(2)}) collective-permute-start(f16[64,16,128]{2,1,0:T(8,128)(2,1)S(1)} %get-tuple-element.46), channel_id=1, source_target_pairs={{0,1},{1,0},{2,3},{3,2},{4,5},{5,4},{6,7},{7,6},{8,9},{9,8},{10,11... | collective-permute-start | bytes 786440 | tf_op jit(solution)/shard_map/panel_cols/ppermute | solution.py:420
  106.3 11.5 %collective-permute-start.24 = (f16[64,16,128]{2,1,0:T(8,128)(2,1)S(1)}, f16[64,16,128]{2,1,0:T(8,128)(2,1)S(1)}, u32[]{:S(2)}, u32[]{:S(2)}) collective-permute-start(f16[64,16,128]{2,1,0:T(8,128)(2,1)S(1)} %collective-permute-done.20), channel_id=1, source_target_pairs={{0,4},{4,0},{8,12},{12,8},{16,20},{20,16},{24,28},{28,24},{1,5},{5... | collective-permute-start | bytes 786440 | tf_op jit(solution)/shard_map/panel_cols/ppermute | solution.py:414
  112.6 5.3 %collective-permute-start.23 = (f16[64,16,128]{2,1,0:T(8,128)(2,1)S(1)}, f16[64,16,128]{2,1,0:T(8,128)(2,1)S(1)}, u32[]{:S(2)}, u32[]{:S(2)}) collective-permute-start(f16[64,16,128]{2,1,0:T(8,128)(2,1)S(1)} %collective-permute-done.19), channel_id=1, source_target_pairs={{0,4},{4,0},{8,12},{12,8},{16,20},{20,16},{24,28},{28,24},{1,5},{5... | collective-permute-start | bytes 786440 | tf_op jit(solution)/shard_map/panel_cols/ppermute | solution.py:414
  112.6 5.3 %collective-permute-start.22 = (f16[64,16,128]{2,1,0:T(8,128)(2,1)S(1)}, f16[64,16,128]{2,1,0:T(8,128)(2,1)S(1)}, u32[]{:S(2)}, u32[]{:S(2)}) collective-permute-start(f16[64,16,128]{2,1,0:T(8,128)(2,1)S(1)} %collective-permute-done.18), channel_id=1, source_target_pairs={{0,4},{4,0},{8,12},{12,8},{16,20},{20,16},{24,28},{28,24},{1,5},{5... | collective-permute-start | bytes 786440 | tf_op jit(solution)/shard_map/panel_cols/ppermute | solution.py:414
  117.0 19.7 %collective-permute-start.31 = (f16[64,16,128]{2,1,0:T(8,128)(2,1)S(1)}, f16[64,16,128]{2,1,0:T(8,128)(2,1)S(1)}, u32[]{:S(2)}, u32[]{:S(2)}) collective-permute-start(f16[64,16,128]{2,1,0:T(8,128)(2,1)S(1)} %collective-permute-done.27), channel_id=1, source_target_pairs={{0,4},{4,0},{8,12},{12,8},{16,20},{20,16},{24,28},{28,24},{1,5},{5... | collective-permute-start | bytes 786440 | tf_op jit(solution)/shard_map/panel_cols/ppermute | solution.py:414
  117.1 19.7 %collective-permute-start.30 = (f16[64,16,128]{2,1,0:T(8,128)(2,1)S(1)}, f16[64,16,128]{2,1,0:T(8,128)(2,1)S(1)}, u32[]{:S(2)}, u32[]{:S(2)}) collective-permute-start(f16[64,16,128]{2,1,0:T(8,128)(2,1)S(1)} %collective-permute-done.26), channel_id=1, source_target_pairs={{0,4},{4,0},{8,12},{12,8},{16,20},{20,16},{24,28},{28,24},{1,5},{5... | collective-permute-start | bytes 786440 | tf_op jit(solution)/shard_map/panel_cols/ppermute | solution.py:414
  117.7 19.2 %collective-permute-start.29 = (f16[64,16,128]{2,1,0:T(8,128)(2,1)S(1)}, f16[64,16,128]{2,1,0:T(8,128)(2,1)S(1)}, u32[]{:S(2)}, u32[]{:S(2)}) collective-permute-start(f16[64,16,128]{2,1,0:T(8,128)(2,1)S(1)} %collective-permute-done.25), channel_id=1, source_target_pairs={{0,4},{4,0},{8,12},{12,8},{16,20},{20,16},{24,28},{28,24},{1,5},{5... | collective-permute-start | bytes 786440 | tf_op jit(solution)/shard_map/panel_cols/ppermute | solution.py:414
  124.6 16.5 %collective-permute-start.33 = (f32[4,128,128]{2,1,0:T(8,128)S(1)}, f32[4,128,128]{2,1,0:T(8,128)S(1)}, u32[]{:S(2)}, u32[]{:S(2)}) collective-permute-start(f32[4,128,128]{2,1,0:T(8,128)S(1)} %get-tuple-element.44), channel_id=1, source_target_pairs={{0,4},{4,0},{8,12},{12,8},{16,20},{20,16},{24,28},{28,24},{1,5},{5... | collective-permute-start | bytes 786440 | tf_op jit(solution)/shard_map/cross_sum/ppermute | solution.py:414
  141.0 10.3 %collective-permute-start.32 = (f32[4,128,128]{2,1,0:T(8,128)S(1)}, f32[4,128,128]{2,1,0:T(8,128)S(1)}, u32[]{:S(2)}, u32[]{:S(2)}) collective-permute-start(f32[4,128,128]{2,1,0:T(8,128)S(1)} %get-tuple-element.39), channel_id=1, source_target_pairs={{0,4},{4,0},{8,12},{12,8},{16,20},{20,16},{24,28},{28,24},{1,5},{5... | collective-permute-start | bytes 786440 | tf_op jit(solution)/shard_map/cross_sum/ppermute | solution.py:414
  141.1 7.3 %collective-permute-start.34 = (f32[128,128]{1,0:T(8,128)S(1)}, f32[128,128]{1,0:T(8,128)S(1)}, u32[]{:S(2)}, u32[]{:S(2)}) collective-permute-start(f32[128,128]{1,0:T(8,128)S(1)} %get-tuple-element.49), channel_id=1, source_target_pairs={{0,8},{4,12},{8,16},{12,20},{16,24},{20,28},{24,0},{28,4},{1,9},{5... | collective-permute-start | bytes 196616 | tf_op jit(solution)/shard_map/cross_sum/ppermute | solution.py:417
  141.2 7.3 %collective-permute-start.36 = (f32[128,128]{1,0:T(8,128)S(1)}, f32[128,128]{1,0:T(8,128)S(1)}, u32[]{:S(2)}, u32[]{:S(2)}) collective-permute-start(f32[128,128]{1,0:T(8,128)S(1)} %get-tuple-element.50), channel_id=1, source_target_pairs={{0,24},{4,28},{8,0},{12,4},{16,8},{20,12},{24,16},{28,20},{1,25},{... | collective-permute-start | bytes 196616 | tf_op jit(solution)/shard_map/cross_sum/ppermute | solution.py:417
  145.0 6.2 %collective-permute-start.35 = (f32[128,128]{1,0:T(8,128)S(1)}, f32[128,128]{1,0:T(8,128)S(1)}, u32[]{:S(2)}, u32[]{:S(2)}) collective-permute-start(f32[128,128]{1,0:T(8,128)S(1)} %get-tuple-element.51), channel_id=1, source_target_pairs={{0,16},{4,20},{8,24},{12,28},{16,0},{20,4},{24,8},{28,12},{1,17},{... | collective-permute-start | bytes 196616 | tf_op jit(solution)/shard_map/cross_sum/ppermute | solution.py:417
  151.3 16.2 %collective-permute-start.37 = (f32[128,128]{1,0:T(8,128)S(1)}, f32[128,128]{1,0:T(8,128)S(1)}, u32[]{:S(2)}, u32[]{:S(2)}) collective-permute-start(f32[128,128]{1,0:T(8,128)S(1)} %get-tuple-element.52), channel_id=1, source_target_pairs={{0,8},{4,12},{8,16},{12,20},{16,24},{20,28},{24,0},{28,4},{1,9},{5... | collective-permute-start | bytes 196616 | tf_op jit(solution)/shard_map/cross_sum/ppermute | solution.py:417
  151.4 16.2 %collective-permute-start.39 = (f32[128,128]{1,0:T(8,128)S(1)}, f32[128,128]{1,0:T(8,128)S(1)}, u32[]{:S(2)}, u32[]{:S(2)}) collective-permute-start(f32[128,128]{1,0:T(8,128)S(1)} %get-tuple-element.53), channel_id=1, source_target_pairs={{0,24},{4,28},{8,0},{12,4},{16,8},{20,12},{24,16},{28,20},{1,25},{... | collective-permute-start | bytes 196616 | tf_op jit(solution)/shard_map/cross_sum/ppermute | solution.py:417
  155.2 12.4 %collective-permute-start.38 = (f32[128,128]{1,0:T(8,128)S(1)}, f32[128,128]{1,0:T(8,128)S(1)}, u32[]{:S(2)}, u32[]{:S(2)}) collective-permute-start(f32[128,128]{1,0:T(8,128)S(1)} %get-tuple-element.54), channel_id=1, source_target_pairs={{0,16},{4,20},{8,24},{12,28},{16,0},{20,4},{24,8},{28,12},{1,17},{... | collective-permute-start | bytes 196616 | tf_op jit(solution)/shard_map/cross_sum/ppermute | solution.py:417

commit v3 on v2

v3 whole, which is shorter than its diff:
```python
import functools
import jax
import jax.numpy as jnp
from jax import lax
from jax.experimental import pallas as pl
from jax.experimental.pallas import tpu as pltpu
from jax.sharding import PartitionSpec as P

TILE = 128
P_SIZE = 256
NB = 64
CHUNKS = 2
WIDTH = 16
HALF = P_SIZE // CHUNKS
SLICES = HALF // (2 * WIDTH)
BASE = 64
STEP = 8
F32, BF16, F16 = jnp.float32, jnp.bfloat16, jnp.float16
HI = lax.Precision.HIGHEST
MIB = 1 << 20


def vmem():
    return pl.BlockSpec(memory_space=pltpu.VMEM)


def smem():
    return pl.BlockSpec(memory_space=pltpu.SMEM)


def anywhere():
    return pl.BlockSpec(memory_space=pl.ANY)


def params(mib):
    return pltpu.CompilerParams(vmem_limit_bytes=mib * MIB)


def cost(flops, bytes_accessed):
    return pl.CostEstimate(flops=flops, bytes_accessed=bytes_accessed, transcendentals=0)


LIGHT = cost(10**6, 10**5)


def signed_mixer(mixers_ref, names_ref, tile):
    position = lax.broadcasted_iota(jnp.int32, (1, TILE), 1)
    hashed = (names_ref[4, tile] ^ position * 40503) * 69069
    sign = (1 - 2 * (hashed >> 16 & 1)).astype(F32)
    return mixers_ref[names_ref[3, tile]] * sign


def split(value):
    high = value.astype(BF16)
    return high, (value - high.astype(F32)).astype(BF16)


def product(mixer, block):
    mixer_high, mixer_low = split(mixer)
    block_high, block_low = split(block)
    wide = jnp.dot(jnp.concatenate([mixer_high, mixer_low], axis=0), block_high, preferred_element_type=F32)
    low = jnp.dot(mixer_high, block_low, preferred_element_type=F32)
    return wide[:TILE] + (wide[TILE:] + low)


def panel_kernel(per_step, names_ref, order_ref, matrix_ref, mixers_ref, *refs):
    outs, turned = refs[:-1], refs[-1]
    first = pl.program_id(0) * per_step
    core = order_ref[2 * SLICES + 1]
    for u in range(per_step):
        mixer = signed_mixer(mixers_ref, names_ref, first + u)
        block = matrix_ref[u * TILE : (u + 1) * TILE, :]
        turned[u] = product(mixer, block).T
        for h in range(CHUNKS):
            for c in range(SLICES):
                for s in range(2):
                    who = core if s == 0 else 1 - core
                    start = pl.multiple_of(h * HALF + who * (HALF // 2) + c * WIDTH, WIDTH)
                    outs[h * SLICES + c][s, u] = turned[u, pl.ds(start, WIDTH), :].astype(BF16)


def mix_panel(matrix, mixers, names, order):
    tiles = names.shape[1]
    per_step = 8
    spec = pl.BlockSpec((2, per_step, WIDTH, TILE), lambda i, *_: (0, i, 0, 0))
    return pl.pallas_call(
        functools.partial(panel_kernel, per_step),
        grid_spec=pltpu.PrefetchScalarGridSpec(
            num_scalar_prefetch=2,
            grid=(tiles // per_step,),
            in_specs=[
                pl.BlockSpec((per_step * TILE, P_SIZE), lambda i, *_: (i, 0)),
                pl.BlockSpec(mixers.shape, lambda i, *_: (0, 0, 0)),
            ],
            out_specs=[spec] * (CHUNKS * SLICES),
            scratch_shapes=[pltpu.VMEM((per_step, P_SIZE, TILE), F32)],
        ),
        out_shape=[jax.ShapeDtypeStruct((2, tiles, WIDTH, TILE), BF16)] * (CHUNKS * SLICES),
        compiler_params=params(52),
        cost_estimate=LIGHT,
        name="mix_panel",
    )(names, order, matrix, mixers)


def mix_kernel(per_step, start, names_ref, matrix_ref, mixers_ref, after_ref, out_ref):
    first = start + pl.program_id(0) * per_step
    for u in range(per_step):
        mixer = signed_mixer(mixers_ref, names_ref, first + u)
        block = matrix_ref[u * TILE : (u + 1) * TILE, :]
        out_ref[u * TILE : (u + 1) * TILE, :] = product(mixer, block).astype(BF16)


def mix_tiles(matrix, mixers, names, after, start, count):
    cols = matrix.shape[1]
    per_step = 4
    return pl.pallas_call(
        functools.partial(mix_kernel, per_step, start),
        grid_spec=pltpu.PrefetchScalarGridSpec(
            num_scalar_prefetch=1,
            grid=(count // per_step,),
            in_specs=[
                pl.BlockSpec((per_step * TILE, cols), lambda i, *_: (i + start // per_step, 0)),
                pl.BlockSpec(mixers.shape, lambda i, *_: (0, 0, 0)),
                anywhere(),
            ],
            out_specs=pl.BlockSpec((per_step * TILE, cols), lambda i, *_: (i, 0)),
        ),
        out_shape=jax.ShapeDtypeStruct((count * TILE, cols), BF16),
        compiler_params=params(52),
        cost_estimate=LIGHT,
        name="mix_tiles",
    )(names, matrix, mixers, after)


def pick_kernel(count, order_ref, *refs):
    extra, sources, (keep_ref, give_ref) = refs[:count], refs[count:-2], refs[-2:]
    part = order_ref[2 * SLICES + 2]
    tiles = sources[0].shape[1]
    for j, source in enumerate(sources):
        taken = part == j if j else (part == 0) | (part >= len(sources))

        @pl.when(taken)
        def copy(source=source):
            keep_ref[:tiles] = source[0]
            give_ref[:tiles] = source[1]

    for i, ref in enumerate(extra):
        keep_ref[tiles + i] = ref[...]
        give_ref[tiles + i] = ref[...]


def pick(order, extra, sources):
    tiles = sources[0].shape[1] + len(extra)
    return pl.pallas_call(
        functools.partial(pick_kernel, len(extra)),
        in_specs=[smem()] + [vmem()] * (len(extra) + len(sources)),
        out_specs=[vmem()] * 2,
        out_shape=[jax.ShapeDtypeStruct((tiles, WIDTH, TILE), BF16)] * 2,
        compiler_params=params(16),
        cost_estimate=LIGHT,
        name="pick",
    )(order, *extra, *sources)


def add_tiles(names, stride, tiles, pieces, out_ref, total):
    total[...] = jnp.zeros_like(total)
    for j, piece in enumerate(pieces):
        for s in range(2):

            def add(i, carry, j=j, s=s, piece=piece):
                value = piece[s * stride + i].astype(F32)
                one, two = names[2 * j + s, 0, i], names[2 * j + s, 1, i]
                total[one] = total[one] + value
                total[two] = total[two] + names[2 * j + s, 2, i].astype(F32) * value
                return carry

            lax.fori_loop(0, tiles, add, 0, unroll=8)
    summed = total[...]
    largest = jnp.max(jnp.max(jnp.abs(summed), axis=0), axis=1, keepdims=True)
    out_ref[...] = summed * jnp.where(largest > 1e-37, 1.0 / largest, 1.0)


def first_sum_kernel(after_ref, *refs):
    pieces, (out_ref, names_ref, total, names, sem) = refs[:-5], refs[-5:]
    tiles = pieces[0].shape[0] // 2 - 1
    for j, piece in enumerate(pieces):
        for s in range(2):
            names_ref[2 * j + s] = piece[s * (tiles + 1) + tiles].astype(F32)[:8].astype(jnp.int32)
    copy = pltpu.make_async_copy(names_ref, names, sem)
    copy.start()
    copy.wait()
    add_tiles(names, tiles + 1, tiles, pieces, out_ref, total)


def first_sum(after, pieces):
    names = (2 * len(pieces), 8, TILE)
    return pl.pallas_call(
        first_sum_kernel,
        in_specs=[anywhere()] + [vmem()] * len(pieces),
        out_specs=[vmem()] * 2,
        out_shape=[jax.ShapeDtypeStruct((NB, WIDTH, TILE), F32), jax.ShapeDtypeStruct(names, jnp.int32)],
        scratch_shapes=[pltpu.VMEM((NB, WIDTH, TILE), F32), pltpu.SMEM(names, jnp.int32), pltpu.SemaphoreType.DMA],
        compiler_params=params(24),
        cost_estimate=LIGHT,
        name="first_sum",
    )(after, *pieces)


def next_sum_kernel(names, after_ref, *refs):
    pieces, (out_ref, total) = refs[:-2], refs[-2:]
    tiles = pieces[0].shape[0] // 2
    add_tiles(names, tiles, tiles, pieces, out_ref, total)


def next_sum(names, after, pieces):
    return pl.pallas_call(
        next_sum_kernel,
        in_specs=[smem(), anywhere()] + [vmem()] * len(pieces),
        out_specs=vmem(),
        out_shape=jax.ShapeDtypeStruct((NB, WIDTH, TILE), F32),
        scratch_shapes=[pltpu.VMEM((NB, WIDTH, TILE), F32)],
        compiler_params=params(24),
        cost_estimate=LIGHT,
        name="next_sum",
    )(names, after, *pieces)


def nt(a, b, precision=None):
    return lax.dot_general(a, b, (((1,), (1,)), ((), ())), precision=precision, preferred_element_type=F32)


def nn(a, b):
    return jnp.dot(a, b, precision=HI, preferred_element_type=F32)


def join(order_ref, pieces, panel):
    for q, piece in enumerate(pieces):
        panel[:, pl.ds(pl.multiple_of(order_ref[q] * WIDTH, WIDTH), WIDTH), :] = piece[...]


def cross_kernel(steps, chips, earlier, fast, names_ref, order_ref, after_ref, *refs):
    mixed, refs = refs[: len(steps)], refs[len(steps) :]
    pieces, refs = refs[: 2 * SLICES], refs[2 * SLICES :]
    before, refs = refs[:earlier], refs[earlier:]
    panel, outs, total = refs[0], refs[1:-1], refs[-1]
    step = pl.program_id(0)

    @pl.when(step == 0)
    def start():
        total[...] = jnp.zeros_like(total)
        join(order_ref, pieces, panel)

    high, low = [], []
    for u in range(STEP):
        t = STEP * step + u
        one, two = split(panel[names_ref[0, t]] + names_ref[2, t].astype(F32) * panel[names_ref[1, t]])
        high.append(one)
        low.append(two)
    weights = jnp.concatenate([jnp.concatenate(high, axis=1), jnp.concatenate(low, axis=1)], axis=0)

    begin = 0
    for count, mixed_ref in zip(steps, mixed):

        @pl.when((step >= begin) & (step < begin + count))
        def add(mixed_ref=mixed_ref):
            total[...] += jnp.dot(weights, mixed_ref[...], preferred_element_type=F32)

        begin += count

    @pl.when(step == pl.num_programs(0) - 1)
    def finish():
        total[:HALF, :] = total[:HALF, :] + total[HALF:, :]
        rows = earlier and HALF
        for ref, out in zip(before, outs):
            out[..., :HALF, :] = ref[...]
        if not fast:
            outs[0][rows:, :] = total[:HALF, :]
        else:
            chip, core = order_ref[2 * SLICES], order_ref[2 * SLICES + 1]
            for s in range(2):
                who = core if s == 0 else 1 - core
                for j in range(chips):
                    at = (2 * lax.rem(chip + j, chips) + who) * TILE
                    outs[s][j, rows:, :] = total[:HALF, pl.ds(pl.multiple_of(at, TILE), TILE)]


def cross_parts(names, order, after, mixed, pieces, before, chips, fast):
    cols = mixed[0].shape[1]
    steps = [v.shape[0] // (STEP * TILE) for v in mixed]
    rows = 2 * HALF if before else HALF
    if fast:
        outs = [jax.ShapeDtypeStruct((chips, rows, TILE), F32)] * 2
    else:
        outs = [jax.ShapeDtypeStruct((rows, cols), F32)]
    outs = [jax.ShapeDtypeStruct((NB, HALF, TILE), F32)] + outs
    begins = [sum(steps[:i]) for i in range(len(steps))]
    blocks = [
        pl.BlockSpec((STEP * TILE, cols), lambda i, b=begin, n=count: (jnp.clip(i - b, 0, n - 1), 0))
        for begin, count in zip(begins, steps)
    ]
    return pl.pallas_call(
        functools.partial(cross_kernel, steps, chips, len(before), fast),
        grid=(sum(steps),),
        in_specs=[smem(), smem(), anywhere()] + blocks + [vmem()] * (len(pieces) + len(before)),
        out_specs=[vmem()] * len(outs),
        out_shape=outs,
        scratch_shapes=[pltpu.VMEM((2 * HALF, cols), F32)],
        compiler_params=params(32),
        cost_estimate=LIGHT,
        name="cross_parts",
    )(names, order, after, *mixed, *pieces, *before)


def above(value):
    return jnp.concatenate([value[:1], value[:-1]], axis=0)


def factor_inverse(block):
    row = lax.broadcasted_iota(jnp.int32, (BASE, BASE), 0)
    lane = lax.broadcasted_iota(jnp.int32, (BASE, BASE), 1)
    eye = (row == lane).astype(F32)
    wide = jnp.concatenate([block, eye], axis=1)
    slabs = [wide[8 * g : 8 * g + 8, :] for g in range(BASE // 8)]
    place = lax.broadcasted_iota(jnp.int32, (8, 2 * BASE), 0)

    def full(value):
        return jnp.broadcast_to(value, (8, 2 * BASE))

    for j in range(0, BASE, 2):
        own, at = j // 8, j % 8
        slab = slabs[own]
        col0, col1 = full(slab[:, j : j + 1]), full(slab[:, j + 1 : j + 2])
        row0, row1 = full(slab[at : at + 1, :]), full(slab[at + 1 : at + 2, :])
        first, cross, second = full(col0[at : at + 1, :]), full(col1[at : at + 1, :]), full(col1[at + 1 : at + 2, :])
        scale = 1.0 / (first * second - cross * cross)
        solved0 = (second * row0 - cross * row1) * scale
        solved1 = (first * row1 - cross * row0) * scale
        for g in range(own, BASE // 8):
            if g == own:
                col0, col1 = jnp.where(place > at + 1, col0, 0.0), jnp.where(place > at + 1, col1, 0.0)
            else:
                col0, col1 = slabs[g][:, j : j + 1], slabs[g][:, j + 1 : j + 2]
            slabs[g] = slabs[g] - col0 * solved0 - col1 * solved1
    wide = jnp.concatenate(slabs, axis=0)
    diagonal = jnp.sum(wide[:, :BASE] * eye, axis=1, keepdims=True)
    beside = jnp.sum(jnp.where(lane == row + 1, wide[:, :BASE], 0.0), axis=1, keepdims=True)
    odd = row[:, :1] % 2 == 1
    ratio = jnp.where(odd, above(beside) / above(diagonal), 0.0)
    pivots = jnp.where(odd, diagonal - above(beside) * ratio, diagonal)
    return (wide - ratio * above(wide))[:, BASE:] * lax.rsqrt(pivots)


def factor_inverse_pair(block):
    first = factor_inverse(block[:BASE, :BASE])
    side = nt(block[BASE:, :BASE], first, HI)
    second = factor_inverse(block[BASE:, BASE:] - nt(side, side, HI))
    corner = -nn(second, nn(side, first))
    top = jnp.concatenate([first, jnp.zeros_like(first)], axis=1)
    return jnp.concatenate([top, jnp.concatenate([corner, second], axis=1)], axis=0)


GROUP = 8


def wide_buckets(panel, i):
    return jnp.concatenate([panel[GROUP * i + u] for u in range(GROUP)], axis=1)


def first_kernel(after_ref, panel, out_ref, acc):
    acc[...] = jnp.zeros_like(acc)

    def step(i, carry):
        one, two = split(wide_buckets(panel, i))
        acc[...] += nt(jnp.concatenate([one, two], axis=0), one)
        return carry

    lax.fori_loop(0, NB // GROUP, step, 0)
    mixed = acc[HALF:, :]
    out_ref[...] = acc[:HALF, :] + (mixed + mixed.T)


def first_gram(after, panel):
    return pl.pallas_call(
        first_kernel,
        in_specs=[anywhere(), vmem()],
        out_specs=vmem(),
        out_shape=jax.ShapeDtypeStruct((HALF, HALF), F32),
        scratch_shapes=[pltpu.VMEM((2 * HALF, HALF), F32)],
        compiler_params=params(32),
        cost_estimate=LIGHT,
        name="first_gram",
    )(after, panel)


def factor_kernel(block_ref, out_ref):
    out_ref[...] = factor_inverse_pair(block_ref[...])


def first_factor(block):
    return pl.pallas_call(
        factor_kernel,
        in_specs=[vmem()],
        out_specs=vmem(),
        out_shape=jax.ShapeDtypeStruct((HALF, HALF), F32),
        compiler_params=params(16),
        cost_estimate=LIGHT,
        name="first_factor",
    )(block)


def second_kernel(after_ref, panel0, panel1, side_ref, block_ref, acc, extra):
    acc[...] = jnp.zeros_like(acc)
    extra[...] = jnp.zeros_like(extra)

    def step(i, carry):
        one0, two0 = split(wide_buckets(panel0, i))
        one1, two1 = split(wide_buckets(panel1, i))
        acc[...] += nt(jnp.concatenate([one1, two1], axis=0), jnp.concatenate([one0, one1], axis=0))
        extra[...] += nt(one1, two0)
        return carry

    lax.fori_loop(0, NB // GROUP, step, 0)
    side_ref[...] = acc[:HALF, :HALF] + (acc[HALF:, :HALF] + extra[...])
    mixed = acc[HALF:, HALF:]
    block_ref[...] = acc[:HALF, HALF:] + (mixed + mixed.T)


def second_gram(after, panel0, panel1):
    return pl.pallas_call(
        second_kernel,
        in_specs=[anywhere()] + [vmem()] * 2,
        out_specs=[vmem()] * 2,
        out_shape=[jax.ShapeDtypeStruct((HALF, HALF), F32)] * 2,
        scratch_shapes=[pltpu.VMEM((2 * HALF, 2 * HALF), F32), pltpu.VMEM((HALF, HALF), F32)],
        compiler_params=params(32),
        cost_estimate=LIGHT,
        name="second_gram",
    )(after, panel0, panel1)


def last_kernel(after_ref, side_ref, block_ref, inverse_ref, out_ref):
    first = inverse_ref[...]
    side = nt(side_ref[...], first, HI)
    second = factor_inverse_pair(block_ref[...] - nt(side, side, HI))
    out_ref[:HALF, :HALF] = first
    out_ref[:HALF, HALF:] = jnp.zeros_like(first)
    out_ref[HALF:, :HALF] = -nn(second, nn(side, first))
    out_ref[HALF:, HALF:] = second


def second_factor(after, side, block, inverse):
    return pl.pallas_call(
        last_kernel,
        in_specs=[anywhere()] + [vmem()] * 3,
        out_specs=vmem(),
        out_shape=jax.ShapeDtypeStruct((P_SIZE, P_SIZE), F32),
        compiler_params=params(32),
        cost_estimate=LIGHT,
        name="second_factor",
    )(after, side, block, inverse)


def local(matrix, mixers, bucket_pair, mixer_index, sign_seed):
    cols = matrix.shape[1]
    rows_n, parts = lax.axis_size("rows"), lax.axis_size("cols")
    chips = rows_n // 2
    row, part = lax.axis_index("rows"), lax.axis_index("cols")
    core, chip = row % 2, row // 2

    def swap(value):
        return lax.ppermute(value, "rows", [(i, i ^ 1) for i in range(rows_n)])

    def shift(value, j):
        return lax.ppermute(value, "rows", [(i, (i + 2 * j) % rows_n) for i in range(rows_n)])

    def beside(value, j):
        return lax.ppermute(value, "rows", [(i, i ^ 2 * j) for i in range(rows_n)])

    def across(value, j):
        return lax.ppermute(value, "cols", [(i, i ^ j) for i in range(parts)])

    fast = cols % (TILE * rows_n) == 0
    with jax.named_scope("names"):
        flips = 1 - 2 * (sign_seed >> 29 & 1)
        names = jnp.stack([bucket_pair[:, 0], bucket_pair[:, 1], flips, mixer_index, sign_seed])
        place = [part ^ j if parts == SLICES else j for j in range(SLICES)]
        order = [who * SLICES + c for who in (core, 1 - core) for c in place]
        order = jnp.stack([jnp.asarray(v, jnp.int32) for v in order + [chip, core, part]])
    with jax.named_scope("panel_mix"):
        tiles = mix_panel(matrix, mixers, names, order)
    with jax.named_scope("names"):
        carried = jnp.pad(names[:3].astype(BF16), ((0, WIDTH - 3), (0, TILE - names.shape[1])))

    def spread(h, *extra):
        with jax.named_scope("panel_spread"):
            slices = tiles[h * SLICES : (h + 1) * SLICES]
            got = [slices[0]] + [lax.ppermute(slices[j], "cols", [(0, j)]) for j in range(1, SLICES)]
            keep, give = pick(order, extra, got)
            return jnp.concatenate([keep, swap(give)])

    def gather_rows(held):
        with jax.named_scope("panel_rows"):
            if chips != 4:
                return [held] + [shift(held, j) for j in range(1, chips)]
            far, near = beside(held, 2), beside(held, 1)
            return [held, far, near, beside(far, 1)]

    def gather_cols(summed):
        with jax.named_scope("panel_cols"):
            sent = summed.astype(F16)
            if parts == SLICES:
                return [sent] + [across(sent, j) for j in range(1, parts)]
            return list(lax.all_gather(sent, "cols")[:SLICES])

    def both_cores(mine):
        with jax.named_scope("panel_cores"):
            return [v.astype(F32) for v in mine + [swap(v) for v in mine]]

    def before(values, *others):
        return lax.optimization_barrier((values, others))[0]

    held0 = spread(0, carried)
    arrived0 = gather_rows(held0)
    with jax.named_scope("mix"):
        mixed = [mix_tiles(matrix, mixers, names, held0, 0, names.shape[1])]
    held1 = spread(1)
    arrived1 = gather_rows(held1)
    with jax.named_scope("panel_sum"):
        summed0, all_names = first_sum(mixed[0], arrived0)
    pieces0 = both_cores(gather_cols(summed0))
    with jax.named_scope("panel_sum"):
        summed1 = next_sum(all_names, summed0, arrived1)
    mine1 = gather_cols(summed1)
    with jax.named_scope("cross0"):
        panel0, *crossed0 = cross_parts(names, order, summed1, mixed, pieces0, [], chips, fast)
    with jax.named_scope("factor0"):
        inverse0 = first_factor(first_gram(crossed0[0], panel0))
    pieces1 = both_cores(before(mine1, inverse0, crossed0[0]))
    with jax.named_scope("cross1"):
        panel1, *crossed = cross_parts(names, order, inverse0, mixed, pieces1, crossed0, chips, fast)
    with jax.named_scope("gram1"):
        side, block = second_gram(crossed[0], panel0, panel1)

    if not fast:
        inverse = second_factor(side, side, block, inverse0)
        total = lax.psum(crossed[0], "rows")
        share = P_SIZE // rows_n
        return lax.dynamic_slice_in_dim(nn(inverse, total), row * share, share, 0)
    with jax.named_scope("cross_sum"):
        keep, give = crossed
        on_chip = keep + before(swap(give), side)
    with jax.named_scope("factor1"):
        inverse = second_factor(on_chip, side, block, inverse0)
    with jax.named_scope("cross_sum"):
        total = on_chip[0]
        for j in range(1, chips):
            total = total + shift(on_chip[j], j)
    with jax.named_scope("solve"):
        solved = nn(inverse, total)
        return lax.all_to_all(solved, "rows", split_axis=0, concat_axis=1, tiled=True)


def solution(mesh):
    in_specs = (P("rows", "cols"), P(), P("rows", None), P("rows"), P("rows"))
    out_specs = P("rows", "cols")
    return jax.shard_map(local, mesh=mesh, in_specs=in_specs, out_specs=out_specs, check_vma=False)
```

time: 180 us -> 148 us (0.82)
  starting transfers between devices: 49.7 us -> 38 us
  waiting for transfers between devices: 35.9 us -> 27.3 us
  Pallas kernels: 73.3 us -> 64.7 us
  local copies, waits for them, and re-layouts: 7.35 us -> 4.92 us
    ppermute x15 -> x3, starting transfers between devices: 29 us -> 3.89 us  [shift(): lax.ppermute(value, 'rows', [(i, (i + 2 * j) % rows_n) for i in range(row...]
    ppermute x15 -> x3, waiting for transfers between devices: 25.8 us -> 0.99 us  [shift(): lax.ppermute(value, 'rows', [(i, (i + 2 * j) % rows_n) for i in range(row...]
    ppermute x0 -> x6, starting transfers between devices: none -> 10.4 us  [beside(): return lax.ppermute(value, 'rows', [(i, i ^ 2 * j) for i in range(rows_n)])]
    ppermute x6, waiting for transfers between devices: 0.02 us -> 8.51 us  [spread(): lax.ppermute(slices[j], 'cols', [(0, j)])]
    pallas_call x2 -> x1, Pallas kernels: 20.1 us -> 14.5 us  [mix_tiles(): pl.pallas_call(functools.partial(mix_kernel, per_step, start), grid_spec=...]
    ppermute x0 -> x6, waiting for transfers between devices: none -> 4.44 us  [beside(): return lax.ppermute(value, 'rows', [(i, i ^ 2 * j) for i in range(rows_n)])]
    ppermute x13 -> x11, waiting for transfers between devices: 0.03 us -> 3.99 us  [swap(): return lax.ppermute(value, 'rows', [(i, i ^ 1) for i in range(rows_n)])]
    ppermute x6, starting transfers between devices: 5.1 us -> 7.65 us  [across(): return lax.ppermute(value, 'cols', [(i, i ^ j) for i in range(parts)])]
  transfers between devices with their start and end apart: 40 -> 32, of which waited for: 8 -> 13; matrix products, arithmetic and copies ran while one was open for 1% -> 0% of each run, Pallas kernels for 36% -> 36%
where the time goes in v3:
time: 148 us
  Pallas kernels  64.7 us (44%)
  starting transfers between devices  38 us (26%)
  waiting for transfers between devices  27.3 us (18%)
  blocking collectives  9.81 us (7%)
  local copies, waits for them, and re-layouts  4.92 us (3%)
  other arithmetic  2.14 us (1%)
    pallas_call x1, Pallas kernels, mix_tiles(): pl.pallas_call(functools.partial(mix_kernel, per_step, start), grid_spec=...  14.5 us
    ppermute x6, starting transfers between devices, spread(): lax.ppermute(slices[j], 'cols', [(0, j)])  14.1 us
    pallas_call x1, Pallas kernels, second_factor(): pl.pallas_call(last_kernel, in_specs=[anywhere()] + [vmem()] * 3, out_spe...  10.7 us
    ppermute x6, starting transfers between devices, beside(): return lax.ppermute(value, 'rows', [(i, i ^ 2 * j) for i in range(rows_n)])  10.4 us
    pallas_call x1, Pallas kernels, first_factor(): pl.pallas_call(factor_kernel, in_specs=[vmem()], out_specs=vmem(), out_sh...  9.91 us
    all_to_all x1, blocking collectives, local(): lax.all_to_all(solved, 'rows', split_axis=0, concat_axis=1, tiled=True)  9.81 us
    ppermute x6, waiting for transfers between devices, across(): return lax.ppermute(value, 'cols', [(i, i ^ j) for i in range(parts)])  9.37 us
    pallas_call x2, Pallas kernels, cross_parts(): pl.pallas_call(functools.partial(cross_kernel, steps, chips, len(before),...  8.98 us
  transfers between devices with their start and end apart: 32, of which 13 were waited for; matrix products, arithmetic and copies ran while one was open for 0% of the time, Pallas kernels for 36%

profile of v3, /device:TPU:0, one launch (start us, length us, event | category | flops | bytes accessed | tf_op | source)
XLA Modules:
  0.0 147.7 jit_solution(16545345025087045462)
XLA Ops:
  0.0 0.7 fusion.16
  0.7 0.8 fusion.14
  1.4 0.7 stack.53.names_ref
  2.2 6.3 %mix_panel.1 = (bf16[2,32,16,128]{3,2,1,0:T(8,128)(2,1)S(1)}, bf16[2,32,16,128]{3,2,1,0:T(8,128)(2,1)S(1)}, bf16[2,32,16,128]{3,2,1,0:T(8,128)(2,1)S(1)}, bf16[2...) custom-call(s32[5,32]{1,0:T(8,128)S(1)} %stack.53.names_ref, ...), custom_call_target="tpu_custom_call" | custom-call | flops 1000000 | bytes 100000 | tf_op jit(solution)/shard_map/panel_mix/mix_panel/pallas_call | solution.py:86
  8.5 4.8 %collective-permute-start = (bf16[2,32,16,128]{3,2,1,0:T(8,128)(2,1)S(1)}, bf16[2,32,16,128]{3,2,1,0:T(8,128)(2,1)S(1)}, u32[]{:S(2)}, u32[]{:S(2)}) collective-permute-start(bf16[2,32,16,128]{3,2,1,0:T(8,128)(2,1)S(1)} %get-tuple-element.33), channel_id=1, source_target_pairs={{0,1},{4,5},{8,9},{12,13},{16,17},{20,21},{24,25},{28,29}} | collective-permute-start | bytes 786440 | tf_op jit(solution)/shard_map/panel_spread/ppermute | solution.py:497
  13.4 1.3 collective-permute-start.1
  14.7 1.3 collective-permute-start.2
  16.0 4.0 %collective-permute-done.refs_2_ = bf16[2,32,16,128]{3,2,1,0:T(8,128)(2,1)S(1)} collective-permute-done((bf16[2,32,16,128]{3,2,1,0:T(8,128)(2,1)S(1)}, bf16[2,32,16,128]{3,2,1,0:T(8,128)(2,1)S(1)}, u32[]{:S(2)}, u32[]{:S(2)}) %collective-permute-start) | collective-permute-done | bytes 262176 | tf_op jit(solution)/shard_map/panel_spread/ppermute | solution.py:497
  20.3 4.3 %collective-permute-done.2.refs_4_ = bf16[2,32,16,128]{3,2,1,0:T(8,128)(2,1)S(1)} collective-permute-done((bf16[2,32,16,128]{3,2,1,0:T(8,128)(2,1)S(1)}, bf16[2,32,16,128]{3,2,1,0:T(8,128)(2,1)S(1)}, u32[]{:S(2)}, u32[]{:S(2)}) %collective-permute-start.2) | collective-permute-done | bytes 262176 | tf_op jit(solution)/shard_map/panel_spread/ppermute | solution.py:497
  24.6 0.6 pick.2
  25.2 1.3 collective-permute-done.3
  26.6 2.7 %collective-permute-start.4 = (bf16[66,16,128]{2,1,0:T(8,128)(2,1)S(1)}, bf16[66,16,128]{2,1,0:T(8,128)(2,1)S(1)}, u32[]{:S(2)}, u32[]{:S(2)}) collective-permute-start(bf16[66,16,128]{2,1,0:T(8,128)(2,1)S(1)} %constant_dynamic-update-slice_fusion.after_ref.refs_0_), channel_id=1, source_target_pairs={{0,16},{4,20},{8,24},{12,28},{16,0},{20,4},{24,8},{28,12},{1,17},{... | collective-permute-start | bytes 811016 | tf_op jit(solution)/shard_map/panel_rows/ppermute | solution.py:477
  29.2 1.3 collective-permute-start.7
  30.5 1.3 collective-permute-start.8
  31.9 4.0 %collective-permute-start.9 = (bf16[2,32,16,128]{3,2,1,0:T(8,128)(2,1)}, bf16[2,32,16,128]{3,2,1,0:T(8,128)(2,1)S(1)}, u32[]{:S(2)}, u32[]{:S(2)}) collective-permute-start(bf16[2,32,16,128]{3,2,1,0:T(8,128)(2,1)} %get-tuple-element.43), channel_id=1, source_target_pairs={{0,3},{4,7},{8,11},{12,15},{16,19},{20,23},{24,27},{28,31}} | collective-permute-start | bytes 786440 | tf_op jit(solution)/shard_map/panel_spread/ppermute | solution.py:497
  35.9 1.6 %collective-permute-start.5 = (bf16[66,16,128]{2,1,0:T(8,128)(2,1)S(1)}, bf16[66,16,128]{2,1,0:T(8,128)(2,1)S(1)}, u32[]{:S(2)}, u32[]{:S(2)}) collective-permute-start(bf16[66,16,128]{2,1,0:T(8,128)(2,1)S(1)} %constant_dynamic-update-slice_fusion.after_ref.refs_0_), channel_id=1, source_target_pairs={{0,8},{4,12},{8,0},{12,4},{16,24},{20,28},{24,16},{28,20},{1,9},{5... | collective-permute-start | bytes 811016 | tf_op jit(solution)/shard_map/panel_rows/ppermute | solution.py:477
  37.5 4.4 %collective-permute-done.4.refs_1_ = bf16[66,16,128]{2,1,0:T(8,128)(2,1)S(1)} collective-permute-done((bf16[66,16,128]{2,1,0:T(8,128)(2,1)S(1)}, bf16[66,16,128]{2,1,0:T(8,128)(2,1)S(1)}, u32[]{:S(2)}, u32[]{:S(2)}) %collective-permute-start.4) | collective-permute-done | bytes 270368 | tf_op jit(solution)/shard_map/panel_rows/ppermute | solution.py:477
  42.0 0.6 collective-permute-start.6
  42.6 0.6 pick.3
  43.3 1.3 collective-permute-done.10
  44.6 1.5 collective-permute-start.12
  46.1 2.1 %collective-permute-start.11 = (bf16[64,16,128]{2,1,0:T(8,128)(2,1)S(1)}, bf16[64,16,128]{2,1,0:T(8,128)(2,1)S(1)}, u32[]{:S(2)}, u32[]{:S(2)}) collective-permute-start(bf16[64,16,128]{2,1,0:T(8,128)(2,1)S(1)} %constant_dynamic-update-slice_fusion.2.refs_0_), channel_id=1, source_target_pairs={{0,16},{4,20},{8,24},{12,28},{16,0},{20,4},{24,8},{28,12},{1,17},{... | collective-permute-start | bytes 786440 | tf_op jit(solution)/shard_map/panel_rows/ppermute | solution.py:477
  48.2 14.5 %mix_tiles.1.after_ref.refs_0_ = bf16[4096,1024]{1,0:T(8,128)(2,1)} custom-call(s32[5,32]{1,0:T(8,128)S(1)} %stack.53.names_ref, f32[4096,1024]{1,0:T(8,128)} %matrix_ref.3, f32[8,128,128]{2,1,0:T(8,128)S(1)} %copy-done.1, bf16[66,16,128]{2,1,0:T(8,128)(2,1)S(1)} %constant_dynamic-update-slice_fusion.after_ref.refs_0_), custom_call_target="tpu_custom_call" | custom-call | flops 1000000 | bytes 100000 | tf_op jit(solution)/shard_map/mix/mix_tiles/pallas_call | solution.py:116
  62.8 3.4 %copy-done = bf16[4096,1024]{1,0:T(8,128)(2,1)S(1)} copy-done((bf16[4096,1024]{1,0:T(8,128)(2,1)S(1)}, bf16[4096,1024]{1,0:T(8,128)(2,1)}, u32[]{:S(2)}) %copy-start) | copy-done | bytes 8388632
  66.1 3.5 %first_sum.1 = (f32[64,16,128]{2,1,0:T(8,128)S(1)}, s32[8,8,128]{2,1,0:T(8,128)S(1)}) custom-call(bf16[4096,1024]{1,0:T(8,128)(2,1)S(1)} %copy-done, bf16[66,16,128]{2,1,0:T(8,128)(2,1)S(1)} %constant_dynamic-update-slice_fusion.after_ref.refs_0_, bf16[66,16,128]{2,1,0:T(8,128)(2,1)S(1)} %collective-permute-done.4.refs_1_, ...), custom_call_target="tpu_custom_call" | custom-call | flops 1000000 | bytes 100000 | tf_op jit(solution)/shard_map/panel_sum/first_sum/pallas_call | solution.py:197
  69.8 3.5 %collective-permute-start.16 = (f16[64,16,128]{2,1,0:T(8,128)(2,1)S(1)}, f16[64,16,128]{2,1,0:T(8,128)(2,1)S(1)}, u32[]{:S(2)}, u32[]{:S(2)}) collective-permute-start(f16[64,16,128]{2,1,0:T(8,128)(2,1)S(1)} %get-tuple-element.60), channel_id=1, source_target_pairs={{0,3},{1,2},{2,1},{3,0},{4,7},{5,6},{6,5},{7,4},{8,11},{9,10},{10,... | collective-permute-start | bytes 786440 | tf_op jit(solution)/shard_map/panel_cols/ppermute | solution.py:480
  73.2 0.6 collective-permute-start.14
  73.9 1.9 %collective-permute-start.13 = (bf16[64,16,128]{2,1,0:T(8,128)(2,1)S(1)}, bf16[64,16,128]{2,1,0:T(8,128)(2,1)S(1)}, u32[]{:S(2)}, u32[]{:S(2)}) collective-permute-start(bf16[64,16,128]{2,1,0:T(8,128)(2,1)S(1)} %collective-permute-done.11.refs_1_), channel_id=1, source_target_pairs={{0,8},{4,12},{8,0},{12,4},{16,24},{20,28},{24,16},{28,20},{1,9},{5... | collective-permute-start | bytes 786440 | tf_op jit(solution)/shard_map/panel_rows/ppermute | solution.py:477
  75.8 4.6 %collective-permute-done.16 = f16[64,16,128]{2,1,0:T(8,128)(2,1)S(1)} collective-permute-done((f16[64,16,128]{2,1,0:T(8,128)(2,1)S(1)}, f16[64,16,128]{2,1,0:T(8,128)(2,1)S(1)}, u32[]{:S(2)}, u32[]{:S(2)}) %collective-permute-start.16) | collective-permute-done | bytes 262176 | tf_op jit(solution)/shard_map/panel_cols/ppermute | solution.py:480
  80.4 4.8 %collective-permute-done.15 = f16[64,16,128]{2,1,0:T(8,128)(2,1)S(1)} collective-permute-done((f16[64,16,128]{2,1,0:T(8,128)(2,1)S(1)}, f16[64,16,128]{2,1,0:T(8,128)(2,1)S(1)}, u32[]{:S(2)}, u32[]{:S(2)}) %collective-permute-start.15) | collective-permute-done | bytes 262176 | tf_op jit(solution)/shard_map/panel_cols/ppermute | solution.py:480
  85.2 0.5 collective-permute-start.18
  85.7 3.5 %next_sum.1.after_ref = f32[64,16,128]{2,1,0:T(8,128)S(1)} custom-call(s32[8,8,128]{2,1,0:T(8,128)S(1)} %get-tuple-element.38.names, f32[64,16,128]{2,1,0:T(8,128)S(1)} %get-tuple-element.39.after_ref, bf16[64,16,128]{2,1,0:T(8,128)(2,1)S(1)} %constant_dynamic-update-slice_fusion.2.refs_0_, bf16[64,16,128]{2,1,0:T(8,128)(2,1)S(1)} %collective-permute-done.11.refs_1_, ...), custom_call_target="tpu_custom_call" | custom-call | flops 1000000 | bytes 100000 | tf_op jit(solution)/shard_map/panel_sum/next_sum/pallas_call | solution.py:216
  89.3 1.9 %collective-permute-start.23 = (f16[64,16,128]{2,1,0:T(8,128)(2,1)S(1)}, f16[64,16,128]{2,1,0:T(8,128)(2,1)S(1)}, u32[]{:S(2)}, u32[]{:S(2)}) collective-permute-start(f16[64,16,128]{2,1,0:T(8,128)(2,1)S(1)} %convert_element_type.66), channel_id=1, source_target_pairs={{0,3},{1,2},{2,1},{3,0},{4,7},{5,6},{6,5},{7,4},{8,11},{9,10},{10,... | collective-permute-start | bytes 786440 | tf_op jit(solution)/shard_map/panel_cols/ppermute | solution.py:480
  91.2 0.9 collective-permute-start.22
  92.1 0.8 collective-permute-start.21
  93.2 4.5 %cross_parts.2 = (f32[64,128,128]{2,1,0:T(8,128)S(1)}, f32[4,128,128]{2,1,0:T(8,128)S(1)}, f32[4,128,128]{2,1,0:T(8,128)S(1)}) custom-call(s32[5,32]{1,0:T(8,128)S(1)} %stack.53.names_ref, s32[11]{0:T(128)S(1)} %stack.65.order_ref, f32[64,16,128]{2,1,0:T(8,128)S(1)} %next_sum.1.after_ref, bf16[4096,1024]{1,0:T(8,128)(2,1)S(1)} %bitcast.49, ...), custom_call_target="tpu_custom_call" | custom-call | flops 1000000 | bytes 100000 | tf_op jit(solution)/shard_map/cross0/cross_parts/pallas_call | solution.py:301
  97.7 2.5 %first_gram.1.block_ref = f32[128,128]{1,0:T(8,128)S(1)} custom-call(f32[4,128,128]{2,1,0:T(8,128)S(1)} %get-tuple-element.46.after_ref.refs_9_, f32[64,128,128]{2,1,0:T(8,128)S(1)} %get-tuple-element.47.panel.panel0), custom_call_target="tpu_custom_call" | custom-call | flops 1000000 | bytes 100000 | tf_op jit(solution)/shard_map/factor0/first_gram/pallas_call | solution.py:383
  100.2 9.9 %first_factor.1.after_ref.inverse_ref = f32[128,128]{1,0:T(8,128)S(1)} custom-call(f32[128,128]{1,0:T(8,128)S(1)} %first_gram.1.block_ref), custom_call_target="tpu_custom_call" | custom-call | flops 1000000 | bytes 100000 | tf_op jit(solution)/shard_map/factor0/first_factor/pallas_call | solution.py:400
  110.3 0.5 collective-permute-start.25
  110.8 0.4 collective-permute-start.27
  113.0 4.5 %cross_parts.3 = (f32[64,128,128]{2,1,0:T(8,128)S(1)}, f32[4,256,128]{2,1,0:T(8,128)S(1)}, f32[4,256,128]{2,1,0:T(8,128)S(1)}) custom-call(s32[5,32]{1,0:T(8,128)S(1)} %stack.53.names_ref, s32[11]{0:T(128)S(1)} %stack.65.order_ref, f32[128,128]{1,0:T(8,128)S(1)} %first_factor.1.after_ref.inverse_ref, bf16[4096,1024]{1,0:T(8,128)(2,1)S(1)} %bitcast.49, ...), custom_call_target="tpu_custom_call" | custom-call | flops 1000000 | bytes 100000 | tf_op jit(solution)/shard_map/cross1/cross_parts/pallas_call | solution.py:301
  117.7 3.5 %second_gram.1 = (f32[128,128]{1,0:T(8,128)S(1)}, f32[128,128]{1,0:T(8,128)S(1)}) custom-call(f32[4,256,128]{2,1,0:T(8,128)S(1)} %get-tuple-element.53.after_ref, f32[64,128,128]{2,1,0:T(8,128)S(1)} %get-tuple-element.47.panel.panel0, f32[64,128,128]{2,1,0:T(8,128)S(1)} %get-tuple-element.55.panel1), custom_call_target="tpu_custom_call" | custom-call | flops 1000000 | bytes 100000 | tf_op jit(solution)/shard_map/gram1/second_gram/pallas_call | solution.py:429
  121.2 1.7 %collective-permute-start.29 = (f32[256,128]{1,0:T(8,128)S(1)}, f32[256,128]{1,0:T(8,128)S(1)}, u32[]{:S(2)}, u32[]{:S(2)}) collective-permute-start(f32[256,128]{1,0:T(8,128)S(1)} %get-tuple-element.61), channel_id=1, source_target_pairs={{0,8},{4,12},{8,16},{12,20},{16,24},{20,28},{24,0},{28,4},{1,9},{5... | collective-permute-start | bytes 393224 | tf_op jit(solution)/shard_map/cross_sum/ppermute | solution.py:474
  123.0 2.2 %collective-permute-start.31 = (f32[256,128]{1,0:T(8,128)S(1)}, f32[256,128]{1,0:T(8,128)S(1)}, u32[]{:S(2)}, u32[]{:S(2)}) collective-permute-start(f32[256,128]{1,0:T(8,128)S(1)} %get-tuple-element.62), channel_id=1, source_target_pairs={{0,24},{4,28},{8,0},{12,4},{16,8},{20,12},{24,16},{28,20},{1,25},{... | collective-permute-start | bytes 393224 | tf_op jit(solution)/shard_map/cross_sum/ppermute | solution.py:474
  125.1 10.7 %second_factor.1 = f32[256,256]{1,0:T(8,128)S(1)} custom-call(f32[4,256,128]{2,1,0:T(8,128)S(1)} %add.52.after_ref, f32[128,128]{1,0:T(8,128)S(1)} %get-tuple-element.56.side_ref, f32[128,128]{1,0:T(8,128)S(1)} %get-tuple-element.58.block_ref, f32[128,128]{1,0:T(8,128)S(1)} %first_factor.1.after_ref.inverse_ref), custom_call_target="tpu_custom_call" | custom-call | flops 1000000 | bytes 100000 | tf_op jit(solution)/shard_map/factor1/second_factor/pallas_call | solution.py:452
  135.9 1.0 collective-permute-done.30
  137.2 9.8 %all_to_all.19 = f32[8,32,128]{2,1,0:T(8,128)S(1)} all-to-all(f32[8,32,128]{2,1,0:T(8,128)S(1)} %bitcast.50), channel_id=1, replica_groups=mesh['rows'=8,'cols'=4] {'rows'}, dimensions={0} | all-to-all | bytes 262144 | tf_op jit(solution)/shard_map/solve/all_to_all | solution.py:560
  147.0 0.7 copy_bitcast_fusion
  (68 shorter events, 3.4 us)
Async XLA Ops:
  2.2 46.0 %copy-start.1 = (f32[8,128,128]{2,1,0:T(8,128)S(1)}, f32[8,128,128]{2,1,0:T(8,128)}, u32[]{:S(2)}) copy-start(f32[8,128,128]{2,1,0:T(8,128)} %mixers_ref.3) | copy-start | bytes 1572868
  8.5 11.5 %collective-permute-start = (bf16[2,32,16,128]{3,2,1,0:T(8,128)(2,1)S(1)}, bf16[2,32,16,128]{3,2,1,0:T(8,128)(2,1)S(1)}, u32[]{:S(2)}, u32[]{:S(2)}) collective-permute-start(bf16[2,32,16,128]{3,2,1,0:T(8,128)(2,1)S(1)} %get-tuple-element.33), channel_id=1, source_target_pairs={{0,1},{4,5},{8,9},{12,13},{16,17},{20,21},{24,25},{28,29}} | collective-permute-start | bytes 786440 | tf_op jit(solution)/shard_map/panel_spread/ppermute | solution.py:497
  13.4 6.8 %collective-permute-start.1 = (bf16[2,32,16,128]{3,2,1,0:T(8,128)(2,1)S(1)}, bf16[2,32,16,128]{3,2,1,0:T(8,128)(2,1)S(1)}, u32[]{:S(2)}, u32[]{:S(2)}) collective-permute-start(bf16[2,32,16,128]{3,2,1,0:T(8,128)(2,1)S(1)} %get-tuple-element.34), channel_id=1, source_target_pairs={{0,2},{4,6},{8,10},{12,14},{16,18},{20,22},{24,26},{28,30}} | collective-permute-start | bytes 786440 | tf_op jit(solution)/shard_map/panel_spread/ppermute | solution.py:497
  14.7 9.8 %collective-permute-start.2 = (bf16[2,32,16,128]{3,2,1,0:T(8,128)(2,1)S(1)}, bf16[2,32,16,128]{3,2,1,0:T(8,128)(2,1)S(1)}, u32[]{:S(2)}, u32[]{:S(2)}) collective-permute-start(bf16[2,32,16,128]{3,2,1,0:T(8,128)(2,1)S(1)} %get-tuple-element.35), channel_id=1, source_target_pairs={{0,3},{4,7},{8,11},{12,15},{16,19},{20,23},{24,27},{28,31}} | collective-permute-start | bytes 786440 | tf_op jit(solution)/shard_map/panel_spread/ppermute | solution.py:497
  25.1 1.4 collective-permute-start.3
  26.6 15.4 %collective-permute-start.4 = (bf16[66,16,128]{2,1,0:T(8,128)(2,1)S(1)}, bf16[66,16,128]{2,1,0:T(8,128)(2,1)S(1)}, u32[]{:S(2)}, u32[]{:S(2)}) collective-permute-start(bf16[66,16,128]{2,1,0:T(8,128)(2,1)S(1)} %constant_dynamic-update-slice_fusion.after_ref.refs_0_), channel_id=1, source_target_pairs={{0,16},{4,20},{8,24},{12,28},{16,0},{20,4},{24,8},{28,12},{1,17},{... | collective-permute-start | bytes 811016 | tf_op jit(solution)/shard_map/panel_rows/ppermute | solution.py:477
  29.2 13.4 %collective-permute-start.7 = (bf16[2,32,16,128]{3,2,1,0:T(8,128)(2,1)S(1)}, bf16[2,32,16,128]{3,2,1,0:T(8,128)(2,1)S(1)}, u32[]{:S(2)}, u32[]{:S(2)}) collective-permute-start(bf16[2,32,16,128]{3,2,1,0:T(8,128)(2,1)S(1)} %get-tuple-element.41), channel_id=1, source_target_pairs={{0,1},{4,5},{8,9},{12,13},{16,17},{20,21},{24,25},{28,29}} | collective-permute-start | bytes 786440 | tf_op jit(solution)/shard_map/panel_spread/ppermute | solution.py:497
  30.5 12.1 %collective-permute-start.8 = (bf16[2,32,16,128]{3,2,1,0:T(8,128)(2,1)S(1)}, bf16[2,32,16,128]{3,2,1,0:T(8,128)(2,1)S(1)}, u32[]{:S(2)}, u32[]{:S(2)}) collective-permute-start(bf16[2,32,16,128]{3,2,1,0:T(8,128)(2,1)S(1)} %get-tuple-element.42), channel_id=1, source_target_pairs={{0,2},{4,6},{8,10},{12,14},{16,18},{20,22},{24,26},{28,30}} | collective-permute-start | bytes 786440 | tf_op jit(solution)/shard_map/panel_spread/ppermute | solution.py:497
  31.9 10.8 %collective-permute-start.9 = (bf16[2,32,16,128]{3,2,1,0:T(8,128)(2,1)}, bf16[2,32,16,128]{3,2,1,0:T(8,128)(2,1)S(1)}, u32[]{:S(2)}, u32[]{:S(2)}) collective-permute-start(bf16[2,32,16,128]{3,2,1,0:T(8,128)(2,1)} %get-tuple-element.43), channel_id=1, source_target_pairs={{0,3},{4,7},{8,11},{12,15},{16,19},{20,23},{24,27},{28,31}} | collective-permute-start | bytes 786440 | tf_op jit(solution)/shard_map/panel_spread/ppermute | solution.py:497
  35.9 26.8 %collective-permute-start.5 = (bf16[66,16,128]{2,1,0:T(8,128)(2,1)S(1)}, bf16[66,16,128]{2,1,0:T(8,128)(2,1)S(1)}, u32[]{:S(2)}, u32[]{:S(2)}) collective-permute-start(bf16[66,16,128]{2,1,0:T(8,128)(2,1)S(1)} %constant_dynamic-update-slice_fusion.after_ref.refs_0_), channel_id=1, source_target_pairs={{0,8},{4,12},{8,0},{12,4},{16,24},{20,28},{24,16},{28,20},{1,9},{5... | collective-permute-start | bytes 811016 | tf_op jit(solution)/shard_map/panel_rows/ppermute | solution.py:477
  42.0 20.8 %collective-permute-start.6 = (bf16[66,16,128]{2,1,0:T(8,128)(2,1)S(1)}, bf16[66,16,128]{2,1,0:T(8,128)(2,1)S(1)}, u32[]{:S(2)}, u32[]{:S(2)}) collective-permute-start(bf16[66,16,128]{2,1,0:T(8,128)(2,1)S(1)} %collective-permute-done.4.refs_1_), channel_id=1, source_target_pairs={{0,8},{4,12},{8,0},{12,4},{16,24},{20,28},{24,16},{28,20},{1,9},{5... | collective-permute-start | bytes 811016 | tf_op jit(solution)/shard_map/panel_rows/ppermute | solution.py:477
  43.2 1.4 collective-permute-start.10
  44.6 31.2 %collective-permute-start.12 = (bf16[64,16,128]{2,1,0:T(8,128)(2,1)S(1)}, bf16[64,16,128]{2,1,0:T(8,128)(2,1)S(1)}, u32[]{:S(2)}, u32[]{:S(2)}) collective-permute-start(bf16[64,16,128]{2,1,0:T(8,128)(2,1)S(1)} %constant_dynamic-update-slice_fusion.2.refs_0_), channel_id=1, source_target_pairs={{0,8},{4,12},{8,0},{12,4},{16,24},{20,28},{24,16},{28,20},{1,9},{5... | collective-permute-start | bytes 786440 | tf_op jit(solution)/shard_map/panel_rows/ppermute | solution.py:477
  46.1 27.8 %collective-permute-start.11 = (bf16[64,16,128]{2,1,0:T(8,128)(2,1)S(1)}, bf16[64,16,128]{2,1,0:T(8,128)(2,1)S(1)}, u32[]{:S(2)}, u32[]{:S(2)}) collective-permute-start(bf16[64,16,128]{2,1,0:T(8,128)(2,1)S(1)} %constant_dynamic-update-slice_fusion.2.refs_0_), channel_id=1, source_target_pairs={{0,16},{4,20},{8,24},{12,28},{16,0},{20,4},{24,8},{28,12},{1,17},{... | collective-permute-start | bytes 786440 | tf_op jit(solution)/shard_map/panel_rows/ppermute | solution.py:477
  62.7 3.4 %copy-start = (bf16[4096,1024]{1,0:T(8,128)(2,1)S(1)}, bf16[4096,1024]{1,0:T(8,128)(2,1)}, u32[]{:S(2)}) copy-start(bf16[4096,1024]{1,0:T(8,128)(2,1)} %mix_tiles.1.after_ref.refs_0_) | copy-start | bytes 25165828
  66.1 27.1 %slice-start = ((s8[8388608]{0:T(1024)(128)(4,1)}), s8[4194304]{0:T(1024)(128)(4,1)S(1)}, s32[]{:S(2)}) async-start(s8[8388608]{0:T(1024)(128)(4,1)} %bitcast.48), calls=%async_computation.1 | async-start | bytes 8388608
  69.7 23.5 %slice-start.1 = ((s8[8388608]{0:T(1024)(128)(4,1)}), s8[4194304]{0:T(1024)(128)(4,1)S(1)}, s32[]{:S(2)}) async-start(s8[8388608]{0:T(1024)(128)(4,1)} %bitcast.48), calls=%async_computation.2 | async-start | bytes 8388608
  69.8 10.6 %collective-permute-start.16 = (f16[64,16,128]{2,1,0:T(8,128)(2,1)S(1)}, f16[64,16,128]{2,1,0:T(8,128)(2,1)S(1)}, u32[]{:S(2)}, u32[]{:S(2)}) collective-permute-start(f16[64,16,128]{2,1,0:T(8,128)(2,1)S(1)} %get-tuple-element.60), channel_id=1, source_target_pairs={{0,3},{1,2},{2,1},{3,0},{4,7},{5,6},{6,5},{7,4},{8,11},{9,10},{10,... | collective-permute-start | bytes 786440 | tf_op jit(solution)/shard_map/panel_cols/ppermute | solution.py:480
  73.2 12.0 %collective-permute-start.15 = (f16[64,16,128]{2,1,0:T(8,128)(2,1)S(1)}, f16[64,16,128]{2,1,0:T(8,128)(2,1)S(1)}, u32[]{:S(2)}, u32[]{:S(2)}) collective-permute-start(f16[64,16,128]{2,1,0:T(8,128)(2,1)S(1)} %get-tuple-element.60), channel_id=1, source_target_pairs={{0,2},{1,3},{2,0},{3,1},{4,6},{5,7},{6,4},{7,5},{8,10},{9,11},{10,... | collective-permute-start | bytes 786440 | tf_op jit(solution)/shard_map/panel_cols/ppermute | solution.py:480
  73.2 12.0 %collective-permute-start.14 = (f16[64,16,128]{2,1,0:T(8,128)(2,1)S(1)}, f16[64,16,128]{2,1,0:T(8,128)(2,1)S(1)}, u32[]{:S(2)}, u32[]{:S(2)}) collective-permute-start(f16[64,16,128]{2,1,0:T(8,128)(2,1)S(1)} %get-tuple-element.60), channel_id=1, source_target_pairs={{0,1},{1,0},{2,3},{3,2},{4,5},{5,4},{6,7},{7,6},{8,9},{9,8},{10,11... | collective-permute-start | bytes 786440 | tf_op jit(solution)/shard_map/panel_cols/ppermute | solution.py:480
  73.9 11.8 %collective-permute-start.13 = (bf16[64,16,128]{2,1,0:T(8,128)(2,1)S(1)}, bf16[64,16,128]{2,1,0:T(8,128)(2,1)S(1)}, u32[]{:S(2)}, u32[]{:S(2)}) collective-permute-start(bf16[64,16,128]{2,1,0:T(8,128)(2,1)S(1)} %collective-permute-done.11.refs_1_), channel_id=1, source_target_pairs={{0,8},{4,12},{8,0},{12,4},{16,24},{20,28},{24,16},{28,20},{1,9},{5... | collective-permute-start | bytes 786440 | tf_op jit(solution)/shard_map/panel_rows/ppermute | solution.py:477
  75.8 15.4 %collective-permute-start.17 = (f16[64,16,128]{2,1,0:T(8,128)(2,1)S(1)}, f16[64,16,128]{2,1,0:T(8,128)(2,1)S(1)}, u32[]{:S(2)}, u32[]{:S(2)}) collective-permute-start(f16[64,16,128]{2,1,0:T(8,128)(2,1)S(1)} %get-tuple-element.60), channel_id=1, source_target_pairs={{0,4},{4,0},{8,12},{12,8},{16,20},{20,16},{24,28},{28,24},{1,5},{5... | collective-permute-start | bytes 786440 | tf_op jit(solution)/shard_map/panel_cores/ppermute | solution.py:471
  80.4 11.7 %collective-permute-start.20 = (f16[64,16,128]{2,1,0:T(8,128)(2,1)S(1)}, f16[64,16,128]{2,1,0:T(8,128)(2,1)S(1)}, u32[]{:S(2)}, u32[]{:S(2)}) collective-permute-start(f16[64,16,128]{2,1,0:T(8,128)(2,1)S(1)} %collective-permute-done.16), channel_id=1, source_target_pairs={{0,4},{4,0},{8,12},{12,8},{16,20},{20,16},{24,28},{28,24},{1,5},{5... | collective-permute-start | bytes 786440 | tf_op jit(solution)/shard_map/panel_cores/ppermute | solution.py:471
  85.2 7.9 %collective-permute-start.19 = (f16[64,16,128]{2,1,0:T(8,128)(2,1)S(1)}, f16[64,16,128]{2,1,0:T(8,128)(2,1)S(1)}, u32[]{:S(2)}, u32[]{:S(2)}) collective-permute-start(f16[64,16,128]{2,1,0:T(8,128)(2,1)S(1)} %collective-permute-done.15), channel_id=1, source_target_pairs={{0,4},{4,0},{8,12},{12,8},{16,20},{20,16},{24,28},{28,24},{1,5},{5... | collective-permute-start | bytes 786440 | tf_op jit(solution)/shard_map/panel_cores/ppermute | solution.py:471
  85.2 7.9 %collective-permute-start.18 = (f16[64,16,128]{2,1,0:T(8,128)(2,1)S(1)}, f16[64,16,128]{2,1,0:T(8,128)(2,1)S(1)}, u32[]{:S(2)}, u32[]{:S(2)}) collective-permute-start(f16[64,16,128]{2,1,0:T(8,128)(2,1)S(1)} %collective-permute-done.14), channel_id=1, source_target_pairs={{0,4},{4,0},{8,12},{12,8},{16,20},{20,16},{24,28},{28,24},{1,5},{5... | collective-permute-start | bytes 786440 | tf_op jit(solution)/shard_map/panel_cores/ppermute | solution.py:471
  89.3 20.9 %collective-permute-start.23 = (f16[64,16,128]{2,1,0:T(8,128)(2,1)S(1)}, f16[64,16,128]{2,1,0:T(8,128)(2,1)S(1)}, u32[]{:S(2)}, u32[]{:S(2)}) collective-permute-start(f16[64,16,128]{2,1,0:T(8,128)(2,1)S(1)} %convert_element_type.66), channel_id=1, source_target_pairs={{0,3},{1,2},{2,1},{3,0},{4,7},{5,6},{6,5},{7,4},{8,11},{9,10},{10,... | collective-permute-start | bytes 786440 | tf_op jit(solution)/shard_map/panel_cols/ppermute | solution.py:480
  91.2 19.0 %collective-permute-start.22 = (f16[64,16,128]{2,1,0:T(8,128)(2,1)S(1)}, f16[64,16,128]{2,1,0:T(8,128)(2,1)S(1)}, u32[]{:S(2)}, u32[]{:S(2)}) collective-permute-start(f16[64,16,128]{2,1,0:T(8,128)(2,1)S(1)} %convert_element_type.66), channel_id=1, source_target_pairs={{0,2},{1,3},{2,0},{3,1},{4,6},{5,7},{6,4},{7,5},{8,10},{9,11},{10,... | collective-permute-start | bytes 786440 | tf_op jit(solution)/shard_map/panel_cols/ppermute | solution.py:480
  92.1 18.1 %collective-permute-start.21 = (f16[64,16,128]{2,1,0:T(8,128)(2,1)S(1)}, f16[64,16,128]{2,1,0:T(8,128)(2,1)S(1)}, u32[]{:S(2)}, u32[]{:S(2)}) collective-permute-start(f16[64,16,128]{2,1,0:T(8,128)(2,1)S(1)} %convert_element_type.66), channel_id=1, source_target_pairs={{0,1},{1,0},{2,3},{3,2},{4,5},{5,4},{6,7},{7,6},{8,9},{9,8},{10,11... | collective-permute-start | bytes 786440 | tf_op jit(solution)/shard_map/panel_cols/ppermute | solution.py:480
  110.2 1.6 %collective-permute-start.24 = (f16[64,16,128]{2,1,0:T(8,128)(2,1)S(1)}, f16[64,16,128]{2,1,0:T(8,128)(2,1)S(1)}, u32[]{:S(2)}, u32[]{:S(2)}) collective-permute-start(f16[64,16,128]{2,1,0:T(8,128)(2,1)S(1)} %convert_element_type.66), channel_id=1, source_target_pairs={{0,4},{4,0},{8,12},{12,8},{16,20},{20,16},{24,28},{28,24},{1,5},{5... | collective-permute-start | bytes 786440 | tf_op jit(solution)/shard_map/panel_cores/ppermute | solution.py:471
  110.3 1.9 %collective-permute-start.25 = (f16[64,16,128]{2,1,0:T(8,128)(2,1)S(1)}, f16[64,16,128]{2,1,0:T(8,128)(2,1)S(1)}, u32[]{:S(2)}, u32[]{:S(2)}) collective-permute-start(f16[64,16,128]{2,1,0:T(8,128)(2,1)S(1)} %collective-permute-done.21), channel_id=1, source_target_pairs={{0,4},{4,0},{8,12},{12,8},{16,20},{20,16},{24,28},{28,24},{1,5},{5... | collective-permute-start | bytes 786440 | tf_op jit(solution)/shard_map/panel_cores/ppermute | solution.py:471
  110.8 1.8 %collective-permute-start.26 = (f16[64,16,128]{2,1,0:T(8,128)(2,1)S(1)}, f16[64,16,128]{2,1,0:T(8,128)(2,1)S(1)}, u32[]{:S(2)}, u32[]{:S(2)}) collective-permute-start(f16[64,16,128]{2,1,0:T(8,128)(2,1)S(1)} %collective-permute-done.22), channel_id=1, source_target_pairs={{0,4},{4,0},{8,12},{12,8},{16,20},{20,16},{24,28},{28,24},{1,5},{5... | collective-permute-start | bytes 786440 | tf_op jit(solution)/shard_map/panel_cores/ppermute | solution.py:471
  110.8 2.1 %collective-permute-start.27 = (f16[64,16,128]{2,1,0:T(8,128)(2,1)S(1)}, f16[64,16,128]{2,1,0:T(8,128)(2,1)S(1)}, u32[]{:S(2)}, u32[]{:S(2)}) collective-permute-start(f16[64,16,128]{2,1,0:T(8,128)(2,1)S(1)} %collective-permute-done.23), channel_id=1, source_target_pairs={{0,4},{4,0},{8,12},{12,8},{16,20},{20,16},{24,28},{28,24},{1,5},{5... | collective-permute-start | bytes 786440 | tf_op jit(solution)/shard_map/panel_cores/ppermute | solution.py:471
  117.5 3.7 %collective-permute-start.28 = (f32[4,256,128]{2,1,0:T(8,128)S(1)}, f32[4,256,128]{2,1,0:T(8,128)S(1)}, u32[]{:S(2)}, u32[]{:S(2)}) collective-permute-start(f32[4,256,128]{2,1,0:T(8,128)S(1)} %get-tuple-element.54), channel_id=1, source_target_pairs={{0,4},{4,0},{8,12},{12,8},{16,20},{20,16},{24,28},{28,24},{1,5},{5... | collective-permute-start | bytes 1572872 | tf_op jit(solution)/shard_map/cross_sum/ppermute | solution.py:471
  121.2 14.6 %collective-permute-start.29 = (f32[256,128]{1,0:T(8,128)S(1)}, f32[256,128]{1,0:T(8,128)S(1)}, u32[]{:S(2)}, u32[]{:S(2)}) collective-permute-start(f32[256,128]{1,0:T(8,128)S(1)} %get-tuple-element.61), channel_id=1, source_target_pairs={{0,8},{4,12},{8,16},{12,20},{16,24},{20,28},{24,0},{28,4},{1,9},{5... | collective-permute-start | bytes 393224 | tf_op jit(solution)/shard_map/cross_sum/ppermute | solution.py:474
  123.0 12.9 %collective-permute-start.31 = (f32[256,128]{1,0:T(8,128)S(1)}, f32[256,128]{1,0:T(8,128)S(1)}, u32[]{:S(2)}, u32[]{:S(2)}) collective-permute-start(f32[256,128]{1,0:T(8,128)S(1)} %get-tuple-element.62), channel_id=1, source_target_pairs={{0,24},{4,28},{8,0},{12,4},{16,8},{20,12},{24,16},{28,20},{1,25},{... | collective-permute-start | bytes 393224 | tf_op jit(solution)/shard_map/cross_sum/ppermute | solution.py:474
  125.1 11.7 %collective-permute-start.30 = (f32[256,128]{1,0:T(8,128)S(1)}, f32[256,128]{1,0:T(8,128)S(1)}, u32[]{:S(2)}, u32[]{:S(2)}) collective-permute-start(f32[256,128]{1,0:T(8,128)S(1)} %get-tuple-element.63), channel_id=1, source_target_pairs={{0,16},{4,20},{8,24},{12,28},{16,0},{20,4},{24,8},{28,12},{1,17},{... | collective-permute-start | bytes 393224 | tf_op jit(solution)/shard_map/cross_sum/ppermute | solution.py:474

commit v4 on v3

--- a/solution.py
+++ b/solution.py
@@ -96,18 +96,19 @@
             scratch_shapes=[pltpu.VMEM((per_step, P_SIZE, TILE), F32)],
         ),
         out_shape=[jax.ShapeDtypeStruct((2, tiles, WIDTH, TILE), BF16)] * (CHUNKS * SLICES),
-        compiler_params=params(52),
+        compiler_params=params(49),
         cost_estimate=LIGHT,
         name="mix_panel",
     )(names, order, matrix, mixers)
 
 
-def mix_kernel(per_step, start, names_ref, matrix_ref, mixers_ref, after_ref, out_ref):
+def mix_kernel(per_step, start, names_ref, matrix_ref, mixers_ref, after_ref, out_ref, token_ref):
     first = start + pl.program_id(0) * per_step
     for u in range(per_step):
         mixer = signed_mixer(mixers_ref, names_ref, first + u)
         block = matrix_ref[u * TILE : (u + 1) * TILE, :]
         out_ref[u * TILE : (u + 1) * TILE, :] = product(mixer, block).astype(BF16)
+    token_ref[...] = jnp.zeros_like(token_ref)
 
 
 def mix_tiles(matrix, mixers, names, after, start, count):
@@ -123,16 +124,19 @@
                 pl.BlockSpec(mixers.shape, lambda i, *_: (0, 0, 0)),
                 anywhere(),
             ],
-            out_specs=pl.BlockSpec((per_step * TILE, cols), lambda i, *_: (i, 0)),
+            out_specs=[
+                pl.BlockSpec((per_step * TILE, cols), lambda i, *_: (i, 0)),
+                pl.BlockSpec((8, TILE), lambda i, *_: (0, 0)),
+            ],
         ),
-        out_shape=jax.ShapeDtypeStruct((count * TILE, cols), BF16),
-        compiler_params=params(52),
+        out_shape=[jax.ShapeDtypeStruct((count * TILE, cols), BF16), jax.ShapeDtypeStruct((8, TILE), F32)],
+        compiler_params=params(49),
         cost_estimate=LIGHT,
         name="mix_tiles",
     )(names, matrix, mixers, after)
 
 
-def pick_kernel(count, order_ref, *refs):
+def pick_kernel(count, order_ref, after_ref, *refs):
     extra, sources, (keep_ref, give_ref) = refs[:count], refs[count:-2], refs[-2:]
     part = order_ref[2 * SLICES + 2]
     tiles = sources[0].shape[1]
@@ -149,17 +153,17 @@
         give_ref[tiles + i] = ref[...]
 
 
-def pick(order, extra, sources):
+def pick(order, after, extra, sources):
     tiles = sources[0].shape[1] + len(extra)
     return pl.pallas_call(
         functools.partial(pick_kernel, len(extra)),
-        in_specs=[smem()] + [vmem()] * (len(extra) + len(sources)),
+        in_specs=[smem(), anywhere()] + [vmem()] * (len(extra) + len(sources)),
         out_specs=[vmem()] * 2,
         out_shape=[jax.ShapeDtypeStruct((tiles, WIDTH, TILE), BF16)] * 2,
         compiler_params=params(16),
         cost_estimate=LIGHT,
         name="pick",
-    )(order, *extra, *sources)
+    )(order, after, *extra, *sources)
 
 
 def add_tiles(names, stride, tiles, pieces, out_ref, total):
@@ -491,11 +495,17 @@
     with jax.named_scope("names"):
         carried = jnp.pad(names[:3].astype(BF16), ((0, WIDTH - 3), (0, TILE - names.shape[1])))
 
-    def spread(h, *extra):
+    def before(values, *others):
+        return lax.optimization_barrier((values, others))[0]
+
+    def scatter(h):
         with jax.named_scope("panel_spread"):
             slices = tiles[h * SLICES : (h + 1) * SLICES]
-            got = [slices[0]] + [lax.ppermute(slices[j], "cols", [(0, j)]) for j in range(1, SLICES)]
-            keep, give = pick(order, extra, got)
+            return [slices[0]] + [lax.ppermute(slices[j], "cols", [(0, j)]) for j in range(1, SLICES)]
+
+    def spread(got, after, *extra):
+        with jax.named_scope("panel_spread"):
+            keep, give = pick(order, after, extra, got)
             return jnp.concatenate([keep, swap(give)])
 
     def gather_rows(held):
@@ -516,21 +526,28 @@
         with jax.named_scope("panel_cores"):
             return [v.astype(F32) for v in mine + [swap(v) for v in mine]]
 
-    def before(values, *others):
-        return lax.optimization_barrier((values, others))[0]
-
-    held0 = spread(0, carried)
-    arrived0 = gather_rows(held0)
-    with jax.named_scope("mix"):
-        mixed = [mix_tiles(matrix, mixers, names, held0, 0, names.shape[1])]
-    held1 = spread(1)
-    arrived1 = gather_rows(held1)
+    mixed = []
+
+    def mix_next(after, count):
+        for _ in range(count):
+            with jax.named_scope("mix"):
+                more, after = mix_tiles(matrix, mixers, names, after, len(mixed) * STEP, STEP)
+            mixed.append(more)
+        return after
+
+    early = names.shape[1] // STEP // 2
+    token = mix_next(tiles[0], early)
+    held0 = spread(scatter(0), token, carried)
+    held1 = spread(scatter(1), token)
+    arrived0, arrived1 = gather_rows(held0), gather_rows(held1)
+    token = mix_next(held1, names.shape[1] // STEP - early)
     with jax.named_scope("panel_sum"):
-        summed0, all_names = first_sum(mixed[0], arrived0)
-    pieces0 = both_cores(gather_cols(summed0))
+        summed0, all_names = first_sum(token, arrived0)
+    mine0 = gather_cols(summed0)
     with jax.named_scope("panel_sum"):
         summed1 = next_sum(all_names, summed0, arrived1)
     mine1 = gather_cols(summed1)
+    pieces0 = both_cores(before(mine0, summed1))
     with jax.named_scope("cross0"):
         panel0, *crossed0 = cross_parts(names, order, summed1, mixed, pieces0, [], chips, fast)
     with jax.named_scope("factor0"):

time: 148 us -> 143 us (0.966)
  waiting for transfers between devices: 27.3 us -> 23.3 us
  local copies, waits for them, and re-layouts: 4.92 us -> 2.57 us
  Pallas kernels: 64.7 us -> 66.5 us
    ppermute x6, waiting for transfers between devices: 4.44 us -> 13.3 us  [beside(): return lax.ppermute(value, 'rows', [(i, i ^ 2 * j) for i in range(rows_n)])]
    ppermute x6, waiting for transfers between devices: 9.37 us -> 3.16 us  [across(): return lax.ppermute(value, 'cols', [(i, i ^ j) for i in range(parts)])]
    ppermute x6, waiting for transfers between devices: 8.51 us -> 4.11 us  [scatter(): lax.ppermute(slices[j], 'cols', [(0, j)])]
    ppermute x11, waiting for transfers between devices: 3.99 us -> 1.36 us  [swap(): return lax.ppermute(value, 'rows', [(i, i ^ 1) for i in range(rows_n)])]
    pallas_call x1 -> x4, Pallas kernels: 14.5 us -> 16.9 us  [mix_tiles(): pl.pallas_call(functools.partial(mix_kernel, per_step, start), grid_spec=...]
    unnamed x10 -> x6, local copies, waits for them, and re-layouts: 3.41 us -> 1.07 us
  transfers between devices with their start and end apart: 32 -> 32, of which waited for: 13 -> 12; matrix products, arithmetic and copies ran while one was open for 0% -> 0% of each run, Pallas kernels for 36% -> 39%
where the time goes in v4:
time: 143 us; the launch traced here: 142 us
  Pallas kernels  66.5 us (47%)
  starting transfers between devices  37.6 us (26%)
  waiting for transfers between devices  23.3 us (16%)
  blocking collectives  9.36 us (7%)
  local copies, waits for them, and re-layouts  2.57 us (2%)
  other arithmetic  2.16 us (2%)
    pallas_call x4, Pallas kernels, mix_tiles(): pl.pallas_call(functools.partial(mix_kernel, per_step, start), grid_spec=...  16.9 us
    ppermute x6, starting transfers between devices, scatter(): lax.ppermute(slices[j], 'cols', [(0, j)])  14.1 us
    ppermute x6, waiting for transfers between devices, beside(): return lax.ppermute(value, 'rows', [(i, i ^ 2 * j) for i in range(rows_n)])  13.3 us
    pallas_call x1, Pallas kernels, second_factor(): pl.pallas_call(last_kernel, in_specs=[anywhere()] + [vmem()] * 3, out_spe...  10.7 us
    pallas_call x1, Pallas kernels, first_factor(): pl.pallas_call(factor_kernel, in_specs=[vmem()], out_specs=vmem(), out_sh...  9.91 us
    ppermute x6, starting transfers between devices, beside(): return lax.ppermute(value, 'rows', [(i, i ^ 2 * j) for i in range(rows_n)])  9.88 us
    all_to_all x1, blocking collectives, local(): lax.all_to_all(solved, 'rows', split_axis=0, concat_axis=1, tiled=True)  9.36 us
    pallas_call x2, Pallas kernels, cross_parts(): pl.pallas_call(functools.partial(cross_kernel, steps, chips, len(before),...  9.36 us
  transfers between devices with their start and end apart: 32, of which 12 were waited for; matrix products, arithmetic and copies ran while one was open for 0% of the time, Pallas kernels for 39%

profile of v4, /device:TPU:0, one launch (start us, length us, event | category | flops | bytes accessed | tf_op | source)
XLA Modules:
  0.0 142.3 jit_solution(9407669746964990973)
XLA Ops:
  0.0 0.7 fusion.16
  0.7 0.8 fusion.14
  1.4 0.7 stack.53.names_ref
  2.2 1.0 copy-done
  3.2 5.4 %mix_panel.1 = (bf16[2,32,16,128]{3,2,1,0:T(8,128)(2,1)S(1)}, bf16[2,32,16,128]{3,2,1,0:T(8,128)(2,1)S(1)}, bf16[2,32,16,128]{3,2,1,0:T(8,128)(2,1)S(1)}, bf16[2...) custom-call(s32[5,32]{1,0:T(8,128)S(1)} %stack.53.names_ref, ...), custom_call_target="tpu_custom_call" | custom-call | flops 1000000 | bytes 100000 | tf_op jit(solution)/shard_map/panel_mix/mix_panel/pallas_call | solution.py:86
  8.6 4.9 %collective-permute-start.4 = (bf16[2,32,16,128]{3,2,1,0:T(8,128)(2,1)S(1)}, bf16[2,32,16,128]{3,2,1,0:T(8,128)(2,1)S(1)}, u32[]{:S(2)}, u32[]{:S(2)}) collective-permute-start(bf16[2,32,16,128]{3,2,1,0:T(8,128)(2,1)S(1)} %get-tuple-element.55), channel_id=1, source_target_pairs={{0,1},{4,5},{8,9},{12,13},{16,17},{20,21},{24,25},{28,29}} | collective-permute-start | bytes 786440 | tf_op jit(solution)/shard_map/panel_spread/ppermute | solution.py:504
  13.5 1.3 collective-permute-start.5
  14.8 1.3 collective-permute-start.6
  16.1 4.2 %mix_tiles.4 = (bf16[1024,1024]{1,0:T(8,128)(2,1)S(1)}, f32[8,128]{1,0:T(8,128)S(1)}) custom-call(s32[5,32]{1,0:T(8,128)S(1)} %stack.53.names_ref, f32[4096,1024]{1,0:T(8,128)} %matrix_ref.9, f32[8,128,128]{2,1,0:T(8,128)S(1)} %copy-done.1, bf16[2,32,16,128]{3,2,1,0:T(8,128)(2,1)S(1)} %get-tuple-element.44.after_ref.refs_1_), custom_call_target="tpu_custom_call" | custom-call | flops 1000000 | bytes 100000 | tf_op jit(solution)/shard_map/mix/mix_tiles/pallas_call | solution.py:117
  20.3 4.2 %mix_tiles.5 = (bf16[1024,1024]{1,0:T(8,128)(2,1)S(1)}, f32[8,128]{1,0:T(8,128)S(1)}) custom-call(s32[5,32]{1,0:T(8,128)S(1)} %stack.53.names_ref, f32[4096,1024]{1,0:T(8,128)} %matrix_ref.9, f32[8,128,128]{2,1,0:T(8,128)S(1)} %copy-done.1, f32[8,128]{1,0:T(8,128)S(1)} %get-tuple-element.45.after_ref), custom_call_target="tpu_custom_call" | custom-call | flops 1000000 | bytes 100000 | tf_op jit(solution)/shard_map/mix/mix_tiles/pallas_call | solution.py:117
  24.7 0.6 pick.3
  25.3 1.3 collective-permute-start
  26.6 1.3 collective-permute-start.1
  27.9 4.0 %collective-permute-start.2 = (bf16[2,32,16,128]{3,2,1,0:T(8,128)(2,1)S(1)}, bf16[2,32,16,128]{3,2,1,0:T(8,128)(2,1)S(1)}, u32[]{:S(2)}, u32[]{:S(2)}) collective-permute-start(bf16[2,32,16,128]{3,2,1,0:T(8,128)(2,1)S(1)} %get-tuple-element.50), channel_id=1, source_target_pairs={{0,3},{4,7},{8,11},{12,15},{16,19},{20,23},{24,27},{28,31}} | collective-permute-start | bytes 786440 | tf_op jit(solution)/shard_map/panel_spread/ppermute | solution.py:504
  32.1 2.7 %collective-permute-start.8 = (bf16[66,16,128]{2,1,0:T(8,128)(2,1)S(1)}, bf16[66,16,128]{2,1,0:T(8,128)(2,1)S(1)}, u32[]{:S(2)}, u32[]{:S(2)}) collective-permute-start(bf16[66,16,128]{2,1,0:T(8,128)(2,1)S(1)} %constant_dynamic-update-slice_fusion.2.refs_0_), channel_id=1, source_target_pairs={{0,16},{4,20},{8,24},{12,28},{16,0},{20,4},{24,8},{28,12},{1,17},{... | collective-permute-start | bytes 811016 | tf_op jit(solution)/shard_map/panel_rows/ppermute | solution.py:481
  34.7 4.0 %collective-permute-done.2.refs_3_ = bf16[2,32,16,128]{3,2,1,0:T(8,128)(2,1)S(1)} collective-permute-done((bf16[2,32,16,128]{3,2,1,0:T(8,128)(2,1)S(1)}, bf16[2,32,16,128]{3,2,1,0:T(8,128)(2,1)S(1)}, u32[]{:S(2)}, u32[]{:S(2)}) %collective-permute-start.2) | collective-permute-done | bytes 262176 | tf_op jit(solution)/shard_map/panel_spread/ppermute | solution.py:504
  38.7 0.6 pick.2
  39.4 1.6 %collective-permute-start.9 = (bf16[66,16,128]{2,1,0:T(8,128)(2,1)S(1)}, bf16[66,16,128]{2,1,0:T(8,128)(2,1)S(1)}, u32[]{:S(2)}, u32[]{:S(2)}) collective-permute-start(bf16[66,16,128]{2,1,0:T(8,128)(2,1)S(1)} %constant_dynamic-update-slice_fusion.2.refs_0_), channel_id=1, source_target_pairs={{0,8},{4,12},{8,0},{12,4},{16,24},{20,28},{24,16},{28,20},{1,9},{5... | collective-permute-start | bytes 811016 | tf_op jit(solution)/shard_map/panel_rows/ppermute | solution.py:481
  41.0 6.5 %collective-permute-done.8.refs_1_ = bf16[66,16,128]{2,1,0:T(8,128)(2,1)S(1)} collective-permute-done((bf16[66,16,128]{2,1,0:T(8,128)(2,1)S(1)}, bf16[66,16,128]{2,1,0:T(8,128)(2,1)S(1)}, u32[]{:S(2)}, u32[]{:S(2)}) %collective-permute-start.8) | collective-permute-done | bytes 270368 | tf_op jit(solution)/shard_map/panel_rows/ppermute | solution.py:481
  47.5 0.6 collective-permute-start.10
  48.1 3.5 %collective-permute-start.11 = (bf16[64,16,128]{2,1,0:T(8,128)(2,1)S(1)}, bf16[64,16,128]{2,1,0:T(8,128)(2,1)S(1)}, u32[]{:S(2)}, u32[]{:S(2)}) collective-permute-start(bf16[64,16,128]{2,1,0:T(8,128)(2,1)S(1)} %constant_dynamic-update-slice_fusion.after_ref.refs_0_), channel_id=1, source_target_pairs={{0,16},{4,20},{8,24},{12,28},{16,0},{20,4},{24,8},{28,12},{1,17},{... | collective-permute-start | bytes 786440 | tf_op jit(solution)/shard_map/panel_rows/ppermute | solution.py:481
  51.7 4.4 %mix_tiles.6 = (bf16[1024,1024]{1,0:T(8,128)(2,1)S(1)}, f32[8,128]{1,0:T(8,128)S(1)}) custom-call(s32[5,32]{1,0:T(8,128)S(1)} %stack.53.names_ref, f32[4096,1024]{1,0:T(8,128)} %matrix_ref.9, f32[8,128,128]{2,1,0:T(8,128)S(1)} %copy-done.1, bf16[64,16,128]{2,1,0:T(8,128)(2,1)S(1)} %constant_dynamic-update-slice_fusion.after_ref.refs_0_), custom_call_target="tpu_custom_call" | custom-call | flops 1000000 | bytes 100000 | tf_op jit(solution)/shard_map/mix/mix_tiles/pallas_call | solution.py:117
  56.0 4.2 %mix_tiles.7 = (bf16[1024,1024]{1,0:T(8,128)(2,1)S(1)}, f32[8,128]{1,0:T(8,128)S(1)}) custom-call(s32[5,32]{1,0:T(8,128)S(1)} %stack.53.names_ref, f32[4096,1024]{1,0:T(8,128)} %matrix_ref.9, f32[8,128,128]{2,1,0:T(8,128)S(1)} %copy-done.1, f32[8,128]{1,0:T(8,128)S(1)} %get-tuple-element.53.after_ref), custom_call_target="tpu_custom_call" | custom-call | flops 1000000 | bytes 100000 | tf_op jit(solution)/shard_map/mix/mix_tiles/pallas_call | solution.py:117
  60.2 2.8 %collective-permute-done.11.refs_1_ = bf16[64,16,128]{2,1,0:T(8,128)(2,1)S(1)} collective-permute-done((bf16[64,16,128]{2,1,0:T(8,128)(2,1)S(1)}, bf16[64,16,128]{2,1,0:T(8,128)(2,1)S(1)}, u32[]{:S(2)}, u32[]{:S(2)}) %collective-permute-start.11) | collective-permute-done | bytes 262176 | tf_op jit(solution)/shard_map/panel_rows/ppermute | solution.py:481
  63.0 1.5 %collective-permute-start.13 = (bf16[64,16,128]{2,1,0:T(8,128)(2,1)S(1)}, bf16[64,16,128]{2,1,0:T(8,128)(2,1)S(1)}, u32[]{:S(2)}, u32[]{:S(2)}) collective-permute-start(bf16[64,16,128]{2,1,0:T(8,128)(2,1)S(1)} %collective-permute-done.11.refs_1_), channel_id=1, source_target_pairs={{0,8},{4,12},{8,0},{12,4},{16,24},{20,28},{24,16},{28,20},{1,9},{5... | collective-permute-start | bytes 786440 | tf_op jit(solution)/shard_map/panel_rows/ppermute | solution.py:481
  64.7 3.6 %first_sum.1 = (f32[64,16,128]{2,1,0:T(8,128)S(1)}, s32[8,8,128]{2,1,0:T(8,128)S(1)}) custom-call(f32[8,128]{1,0:T(8,128)S(1)} %get-tuple-element.54.after_ref, bf16[66,16,128]{2,1,0:T(8,128)(2,1)S(1)} %constant_dynamic-update-slice_fusion.2.refs_0_, bf16[66,16,128]{2,1,0:T(8,128)(2,1)S(1)} %collective-permute-done.8.refs_1_, ...), custom_call_target="tpu_custom_call" | custom-call | flops 1000000 | bytes 100000 | tf_op jit(solution)/shard_map/panel_sum/first_sum/pallas_call | solution.py:201
  68.3 1.5 %collective-permute-start.16 = (f16[64,16,128]{2,1,0:T(8,128)(2,1)S(1)}, f16[64,16,128]{2,1,0:T(8,128)(2,1)S(1)}, u32[]{:S(2)}, u32[]{:S(2)}) collective-permute-start(f16[64,16,128]{2,1,0:T(8,128)(2,1)S(1)} %convert_element_type.57), channel_id=1, source_target_pairs={{0,3},{1,2},{2,1},{3,0},{4,7},{5,6},{6,5},{7,4},{8,11},{9,10},{10,... | collective-permute-start | bytes 786440 | tf_op jit(solution)/shard_map/panel_cols/ppermute | solution.py:484
  69.8 2.1 %collective-permute-start.14 = (f16[64,16,128]{2,1,0:T(8,128)(2,1)S(1)}, f16[64,16,128]{2,1,0:T(8,128)(2,1)S(1)}, u32[]{:S(2)}, u32[]{:S(2)}) collective-permute-start(f16[64,16,128]{2,1,0:T(8,128)(2,1)S(1)} %convert_element_type.57), channel_id=1, source_target_pairs={{0,1},{1,0},{2,3},{3,2},{4,5},{5,4},{6,7},{7,6},{8,9},{9,8},{10,11... | collective-permute-start | bytes 786440 | tf_op jit(solution)/shard_map/panel_cols/ppermute | solution.py:484
  71.9 3.8 %collective-permute-done.13.refs_3_ = bf16[64,16,128]{2,1,0:T(8,128)(2,1)S(1)} collective-permute-done((bf16[64,16,128]{2,1,0:T(8,128)(2,1)S(1)}, bf16[64,16,128]{2,1,0:T(8,128)(2,1)S(1)}, u32[]{:S(2)}, u32[]{:S(2)}) %collective-permute-start.13) | collective-permute-done | bytes 262176 | tf_op jit(solution)/shard_map/panel_rows/ppermute | solution.py:481
  75.7 3.5 %next_sum.1.after_ref = f32[64,16,128]{2,1,0:T(8,128)S(1)} custom-call(s32[8,8,128]{2,1,0:T(8,128)S(1)} %get-tuple-element.60.names, f32[64,16,128]{2,1,0:T(8,128)S(1)} %get-tuple-element.61.after_ref, bf16[64,16,128]{2,1,0:T(8,128)(2,1)S(1)} %constant_dynamic-update-slice_fusion.after_ref.refs_0_, bf16[64,16,128]{2,1,0:T(8,128)(2,1)S(1)} %collective-permute-done.11.refs_1_, ...), custom_call_target="tpu_custom_call" | custom-call | flops 1000000 | bytes 100000 | tf_op jit(solution)/shard_map/panel_sum/next_sum/pallas_call | solution.py:220
  79.2 3.1 %collective-permute-done.15 = f16[64,16,128]{2,1,0:T(8,128)(2,1)S(1)} collective-permute-done((f16[64,16,128]{2,1,0:T(8,128)(2,1)S(1)}, f16[64,16,128]{2,1,0:T(8,128)(2,1)S(1)}, u32[]{:S(2)}, u32[]{:S(2)}) %collective-permute-start.15) | collective-permute-done | bytes 262176 | tf_op jit(solution)/shard_map/panel_cols/ppermute | solution.py:484
  82.4 0.5 collective-permute-start.18
  82.9 0.5 collective-permute-start.20
  83.4 1.2 collective-permute-start.23
  84.7 0.6 collective-permute-start.22
  85.3 1.7 %collective-permute-start.21 = (f16[64,16,128]{2,1,0:T(8,128)(2,1)S(1)}, f16[64,16,128]{2,1,0:T(8,128)(2,1)S(1)}, u32[]{:S(2)}, u32[]{:S(2)}) collective-permute-start(f16[64,16,128]{2,1,0:T(8,128)(2,1)S(1)} %convert_element_type.66), channel_id=1, source_target_pairs={{0,1},{1,0},{2,3},{3,2},{4,5},{5,4},{6,7},{7,6},{8,9},{9,8},{10,11... | collective-permute-start | bytes 786440 | tf_op jit(solution)/shard_map/panel_cols/ppermute | solution.py:484
  87.4 4.6 %cross_parts.2 = (f32[64,128,128]{2,1,0:T(8,128)S(1)}, f32[4,128,128]{2,1,0:T(8,128)S(1)}, f32[4,128,128]{2,1,0:T(8,128)S(1)}) custom-call(s32[5,32]{1,0:T(8,128)S(1)} %stack.53.names_ref, s32[11]{0:T(128)S(1)} %stack.65.order_ref, f32[64,16,128]{2,1,0:T(8,128)S(1)} %next_sum.1.after_ref, bf16[1024,1024]{1,0:T(8,128)(2,1)S(1)} %get-tuple-element.62.refs_0_, ...), custom_call_target="tpu_custom_call" | custom-call | flops 1000000 | bytes 100000 | tf_op jit(solution)/shard_map/cross0/cross_parts/pallas_call | solution.py:305
  91.9 2.5 %first_gram.1.block_ref = f32[128,128]{1,0:T(8,128)S(1)} custom-call(f32[4,128,128]{2,1,0:T(8,128)S(1)} %get-tuple-element.70.after_ref.refs_12_, f32[64,128,128]{2,1,0:T(8,128)S(1)} %get-tuple-element.71.panel.panel0), custom_call_target="tpu_custom_call" | custom-call | flops 1000000 | bytes 100000 | tf_op jit(solution)/shard_map/factor0/first_gram/pallas_call | solution.py:387
  94.5 9.9 %first_factor.1.after_ref.inverse_ref = f32[128,128]{1,0:T(8,128)S(1)} custom-call(f32[128,128]{1,0:T(8,128)S(1)} %first_gram.1.block_ref), custom_call_target="tpu_custom_call" | custom-call | flops 1000000 | bytes 100000 | tf_op jit(solution)/shard_map/factor0/first_factor/pallas_call | solution.py:404
  104.5 0.5 collective-permute-start.25
  105.1 0.4 collective-permute-start.27
  107.2 4.8 %cross_parts.3 = (f32[64,128,128]{2,1,0:T(8,128)S(1)}, f32[4,256,128]{2,1,0:T(8,128)S(1)}, f32[4,256,128]{2,1,0:T(8,128)S(1)}) custom-call(s32[5,32]{1,0:T(8,128)S(1)} %stack.53.names_ref, s32[11]{0:T(128)S(1)} %stack.65.order_ref, f32[128,128]{1,0:T(8,128)S(1)} %first_factor.1.after_ref.inverse_ref, bf16[1024,1024]{1,0:T(8,128)(2,1)S(1)} %get-tuple-element.62.refs_0_, ...), custom_call_target="tpu_custom_call" | custom-call | flops 1000000 | bytes 100000 | tf_op jit(solution)/shard_map/cross1/cross_parts/pallas_call | solution.py:305
  112.2 3.5 %second_gram.1 = (f32[128,128]{1,0:T(8,128)S(1)}, f32[128,128]{1,0:T(8,128)S(1)}) custom-call(f32[4,256,128]{2,1,0:T(8,128)S(1)} %get-tuple-element.77.after_ref, f32[64,128,128]{2,1,0:T(8,128)S(1)} %get-tuple-element.71.panel.panel0, f32[64,128,128]{2,1,0:T(8,128)S(1)} %get-tuple-element.79.panel1), custom_call_target="tpu_custom_call" | custom-call | flops 1000000 | bytes 100000 | tf_op jit(solution)/shard_map/gram1/second_gram/pallas_call | solution.py:433
  115.9 3.8 %collective-permute-start.31 = (f32[256,128]{1,0:T(8,128)S(1)}, f32[256,128]{1,0:T(8,128)S(1)}, u32[]{:S(2)}, u32[]{:S(2)}) collective-permute-start(f32[256,128]{1,0:T(8,128)S(1)} %get-tuple-element.84), channel_id=1, source_target_pairs={{0,24},{4,28},{8,0},{12,4},{16,8},{20,12},{24,16},{28,20},{1,25},{... | collective-permute-start | bytes 393224 | tf_op jit(solution)/shard_map/cross_sum/ppermute | solution.py:478
  119.8 10.7 %second_factor.1 = f32[256,256]{1,0:T(8,128)S(1)} custom-call(f32[4,256,128]{2,1,0:T(8,128)S(1)} %add.52.after_ref, f32[128,128]{1,0:T(8,128)S(1)} %get-tuple-element.80.side_ref, f32[128,128]{1,0:T(8,128)S(1)} %get-tuple-element.82.block_ref, f32[128,128]{1,0:T(8,128)S(1)} %first_factor.1.after_ref.inverse_ref), custom_call_target="tpu_custom_call" | custom-call | flops 1000000 | bytes 100000 | tf_op jit(solution)/shard_map/factor1/second_factor/pallas_call | solution.py:456
  130.5 1.3 collective-permute-done.30
  132.2 9.4 %all_to_all.19 = f32[8,32,128]{2,1,0:T(8,128)S(1)} all-to-all(f32[8,32,128]{2,1,0:T(8,128)S(1)} %bitcast.48), channel_id=1, replica_groups=mesh['rows'=8,'cols'=4] {'rows'}, dimensions={0} | all-to-all | bytes 262144 | tf_op jit(solution)/shard_map/solve/all_to_all | solution.py:577
  141.6 0.7 copy_bitcast_fusion
  (67 shorter events, 3.7 us)
Async XLA Ops:
  2.2 1.0 copy-start
  3.2 12.9 %copy-start.1 = (f32[8,128,128]{2,1,0:T(8,128)S(1)}, f32[8,128,128]{2,1,0:T(8,128)}, u32[]{:S(2)}) copy-start(f32[8,128,128]{2,1,0:T(8,128)} %mixers_ref.9) | copy-start | bytes 1572868
  8.6 15.9 %collective-permute-start.4 = (bf16[2,32,16,128]{3,2,1,0:T(8,128)(2,1)S(1)}, bf16[2,32,16,128]{3,2,1,0:T(8,128)(2,1)S(1)}, u32[]{:S(2)}, u32[]{:S(2)}) collective-permute-start(bf16[2,32,16,128]{3,2,1,0:T(8,128)(2,1)S(1)} %get-tuple-element.55), channel_id=1, source_target_pairs={{0,1},{4,5},{8,9},{12,13},{16,17},{20,21},{24,25},{28,29}} | collective-permute-start | bytes 786440 | tf_op jit(solution)/shard_map/panel_spread/ppermute | solution.py:504
  13.5 11.0 %collective-permute-start.5 = (bf16[2,32,16,128]{3,2,1,0:T(8,128)(2,1)S(1)}, bf16[2,32,16,128]{3,2,1,0:T(8,128)(2,1)S(1)}, u32[]{:S(2)}, u32[]{:S(2)}) collective-permute-start(bf16[2,32,16,128]{3,2,1,0:T(8,128)(2,1)S(1)} %get-tuple-element.56), channel_id=1, source_target_pairs={{0,2},{4,6},{8,10},{12,14},{16,18},{20,22},{24,26},{28,30}} | collective-permute-start | bytes 786440 | tf_op jit(solution)/shard_map/panel_spread/ppermute | solution.py:504
  14.8 9.8 %collective-permute-start.6 = (bf16[2,32,16,128]{3,2,1,0:T(8,128)(2,1)S(1)}, bf16[2,32,16,128]{3,2,1,0:T(8,128)(2,1)S(1)}, u32[]{:S(2)}, u32[]{:S(2)}) collective-permute-start(bf16[2,32,16,128]{3,2,1,0:T(8,128)(2,1)S(1)} %get-tuple-element.57), channel_id=1, source_target_pairs={{0,3},{4,7},{8,11},{12,15},{16,19},{20,23},{24,27},{28,31}} | collective-permute-start | bytes 786440 | tf_op jit(solution)/shard_map/panel_spread/ppermute | solution.py:504
  25.2 6.8 %collective-permute-start.7 = (bf16[33,16,128]{2,1,0:T(8,128)(2,1)S(1)}, bf16[33,16,128]{2,1,0:T(8,128)(2,1)S(1)}, u32[]{:S(2)}, u32[]{:S(2)}) collective-permute-start(bf16[33,16,128]{2,1,0:T(8,128)(2,1)S(1)} %get-tuple-element.59), channel_id=1, source_target_pairs={{0,4},{4,0},{8,12},{12,8},{16,20},{20,16},{24,28},{28,24},{1,5},{5... | collective-permute-start | bytes 405512 | tf_op jit(solution)/shard_map/panel_spread/ppermute | solution.py:475
  25.3 9.4 %collective-permute-start = (bf16[2,32,16,128]{3,2,1,0:T(8,128)(2,1)S(1)}, bf16[2,32,16,128]{3,2,1,0:T(8,128)(2,1)S(1)}, u32[]{:S(2)}, u32[]{:S(2)}) collective-permute-start(bf16[2,32,16,128]{3,2,1,0:T(8,128)(2,1)S(1)} %get-tuple-element.48), channel_id=1, source_target_pairs={{0,1},{4,5},{8,9},{12,13},{16,17},{20,21},{24,25},{28,29}} | collective-permute-start | bytes 786440 | tf_op jit(solution)/shard_map/panel_spread/ppermute | solution.py:504
  26.6 8.1 %collective-permute-start.1 = (bf16[2,32,16,128]{3,2,1,0:T(8,128)(2,1)S(1)}, bf16[2,32,16,128]{3,2,1,0:T(8,128)(2,1)S(1)}, u32[]{:S(2)}, u32[]{:S(2)}) collective-permute-start(bf16[2,32,16,128]{3,2,1,0:T(8,128)(2,1)S(1)} %get-tuple-element.49), channel_id=1, source_target_pairs={{0,2},{4,6},{8,10},{12,14},{16,18},{20,22},{24,26},{28,30}} | collective-permute-start | bytes 786440 | tf_op jit(solution)/shard_map/panel_spread/ppermute | solution.py:504
  27.9 10.8 %collective-permute-start.2 = (bf16[2,32,16,128]{3,2,1,0:T(8,128)(2,1)S(1)}, bf16[2,32,16,128]{3,2,1,0:T(8,128)(2,1)S(1)}, u32[]{:S(2)}, u32[]{:S(2)}) collective-permute-start(bf16[2,32,16,128]{3,2,1,0:T(8,128)(2,1)S(1)} %get-tuple-element.50), channel_id=1, source_target_pairs={{0,3},{4,7},{8,11},{12,15},{16,19},{20,23},{24,27},{28,31}} | collective-permute-start | bytes 786440 | tf_op jit(solution)/shard_map/panel_spread/ppermute | solution.py:504
  32.1 15.5 %collective-permute-start.8 = (bf16[66,16,128]{2,1,0:T(8,128)(2,1)S(1)}, bf16[66,16,128]{2,1,0:T(8,128)(2,1)S(1)}, u32[]{:S(2)}, u32[]{:S(2)}) collective-permute-start(bf16[66,16,128]{2,1,0:T(8,128)(2,1)S(1)} %constant_dynamic-update-slice_fusion.2.refs_0_), channel_id=1, source_target_pairs={{0,16},{4,20},{8,24},{12,28},{16,0},{20,4},{24,8},{28,12},{1,17},{... | collective-permute-start | bytes 811016 | tf_op jit(solution)/shard_map/panel_rows/ppermute | solution.py:481
  39.3 8.8 %collective-permute-start.3 = (bf16[32,16,128]{2,1,0:T(8,128)(2,1)S(1)}, bf16[32,16,128]{2,1,0:T(8,128)(2,1)S(1)}, u32[]{:S(2)}, u32[]{:S(2)}) collective-permute-start(bf16[32,16,128]{2,1,0:T(8,128)(2,1)S(1)} %get-tuple-element.52), channel_id=1, source_target_pairs={{0,4},{4,0},{8,12},{12,8},{16,20},{20,16},{24,28},{28,24},{1,5},{5... | collective-permute-start | bytes 393224 | tf_op jit(solution)/shard_map/panel_spread/ppermute | solution.py:475
  39.4 25.1 %collective-permute-start.9 = (bf16[66,16,128]{2,1,0:T(8,128)(2,1)S(1)}, bf16[66,16,128]{2,1,0:T(8,128)(2,1)S(1)}, u32[]{:S(2)}, u32[]{:S(2)}) collective-permute-start(bf16[66,16,128]{2,1,0:T(8,128)(2,1)S(1)} %constant_dynamic-update-slice_fusion.2.refs_0_), channel_id=1, source_target_pairs={{0,8},{4,12},{8,0},{12,4},{16,24},{20,28},{24,16},{28,20},{1,9},{5... | collective-permute-start | bytes 811016 | tf_op jit(solution)/shard_map/panel_rows/ppermute | solution.py:481
  47.5 17.2 %collective-permute-start.10 = (bf16[66,16,128]{2,1,0:T(8,128)(2,1)S(1)}, bf16[66,16,128]{2,1,0:T(8,128)(2,1)S(1)}, u32[]{:S(2)}, u32[]{:S(2)}) collective-permute-start(bf16[66,16,128]{2,1,0:T(8,128)(2,1)S(1)} %collective-permute-done.8.refs_1_), channel_id=1, source_target_pairs={{0,8},{4,12},{8,0},{12,4},{16,24},{20,28},{24,16},{28,20},{1,9},{5... | collective-permute-start | bytes 811016 | tf_op jit(solution)/shard_map/panel_rows/ppermute | solution.py:481
  48.1 14.9 %collective-permute-start.11 = (bf16[64,16,128]{2,1,0:T(8,128)(2,1)S(1)}, bf16[64,16,128]{2,1,0:T(8,128)(2,1)S(1)}, u32[]{:S(2)}, u32[]{:S(2)}) collective-permute-start(bf16[64,16,128]{2,1,0:T(8,128)(2,1)S(1)} %constant_dynamic-update-slice_fusion.after_ref.refs_0_), channel_id=1, source_target_pairs={{0,16},{4,20},{8,24},{12,28},{16,0},{20,4},{24,8},{28,12},{1,17},{... | collective-permute-start | bytes 786440 | tf_op jit(solution)/shard_map/panel_rows/ppermute | solution.py:481
  51.6 20.2 %collective-permute-start.12 = (bf16[64,16,128]{2,1,0:T(8,128)(2,1)S(1)}, bf16[64,16,128]{2,1,0:T(8,128)(2,1)S(1)}, u32[]{:S(2)}, u32[]{:S(2)}) collective-permute-start(bf16[64,16,128]{2,1,0:T(8,128)(2,1)S(1)} %constant_dynamic-update-slice_fusion.after_ref.refs_0_), channel_id=1, source_target_pairs={{0,8},{4,12},{8,0},{12,4},{16,24},{20,28},{24,16},{28,20},{1,9},{5... | collective-permute-start | bytes 786440 | tf_op jit(solution)/shard_map/panel_rows/ppermute | solution.py:481
  63.0 12.6 %collective-permute-start.13 = (bf16[64,16,128]{2,1,0:T(8,128)(2,1)S(1)}, bf16[64,16,128]{2,1,0:T(8,128)(2,1)S(1)}, u32[]{:S(2)}, u32[]{:S(2)}) collective-permute-start(bf16[64,16,128]{2,1,0:T(8,128)(2,1)S(1)} %collective-permute-done.11.refs_1_), channel_id=1, source_target_pairs={{0,8},{4,12},{8,0},{12,4},{16,24},{20,28},{24,16},{28,20},{1,9},{5... | collective-permute-start | bytes 786440 | tf_op jit(solution)/shard_map/panel_rows/ppermute | solution.py:481
  68.3 10.9 %collective-permute-start.16 = (f16[64,16,128]{2,1,0:T(8,128)(2,1)S(1)}, f16[64,16,128]{2,1,0:T(8,128)(2,1)S(1)}, u32[]{:S(2)}, u32[]{:S(2)}) collective-permute-start(f16[64,16,128]{2,1,0:T(8,128)(2,1)S(1)} %convert_element_type.57), channel_id=1, source_target_pairs={{0,3},{1,2},{2,1},{3,0},{4,7},{5,6},{6,5},{7,4},{8,11},{9,10},{10,... | collective-permute-start | bytes 786440 | tf_op jit(solution)/shard_map/panel_cols/ppermute | solution.py:484
  69.8 12.6 %collective-permute-start.15 = (f16[64,16,128]{2,1,0:T(8,128)(2,1)S(1)}, f16[64,16,128]{2,1,0:T(8,128)(2,1)S(1)}, u32[]{:S(2)}, u32[]{:S(2)}) collective-permute-start(f16[64,16,128]{2,1,0:T(8,128)(2,1)S(1)} %convert_element_type.57), channel_id=1, source_target_pairs={{0,2},{1,3},{2,0},{3,1},{4,6},{5,7},{6,4},{7,5},{8,10},{9,11},{10,... | collective-permute-start | bytes 786440 | tf_op jit(solution)/shard_map/panel_cols/ppermute | solution.py:484
  69.8 12.6 %collective-permute-start.14 = (f16[64,16,128]{2,1,0:T(8,128)(2,1)S(1)}, f16[64,16,128]{2,1,0:T(8,128)(2,1)S(1)}, u32[]{:S(2)}, u32[]{:S(2)}) collective-permute-start(f16[64,16,128]{2,1,0:T(8,128)(2,1)S(1)} %convert_element_type.57), channel_id=1, source_target_pairs={{0,1},{1,0},{2,3},{3,2},{4,5},{5,4},{6,7},{7,6},{8,9},{9,8},{10,11... | collective-permute-start | bytes 786440 | tf_op jit(solution)/shard_map/panel_cols/ppermute | solution.py:484
  82.4 2.3 %collective-permute-start.17 = (f16[64,16,128]{2,1,0:T(8,128)(2,1)S(1)}, f16[64,16,128]{2,1,0:T(8,128)(2,1)S(1)}, u32[]{:S(2)}, u32[]{:S(2)}) collective-permute-start(f16[64,16,128]{2,1,0:T(8,128)(2,1)S(1)} %convert_element_type.57), channel_id=1, source_target_pairs={{0,4},{4,0},{8,12},{12,8},{16,20},{20,16},{24,28},{28,24},{1,5},{5... | collective-permute-start | bytes 786440 | tf_op jit(solution)/shard_map/panel_cores/ppermute | solution.py:475
  82.4 2.9 %collective-permute-start.18 = (f16[64,16,128]{2,1,0:T(8,128)(2,1)S(1)}, f16[64,16,128]{2,1,0:T(8,128)(2,1)S(1)}, u32[]{:S(2)}, u32[]{:S(2)}) collective-permute-start(f16[64,16,128]{2,1,0:T(8,128)(2,1)S(1)} %collective-permute-done.14), channel_id=1, source_target_pairs={{0,4},{4,0},{8,12},{12,8},{16,20},{20,16},{24,28},{28,24},{1,5},{5... | collective-permute-start | bytes 786440 | tf_op jit(solution)/shard_map/panel_cores/ppermute | solution.py:475
  82.9 4.4 %collective-permute-start.19 = (f16[64,16,128]{2,1,0:T(8,128)(2,1)S(1)}, f16[64,16,128]{2,1,0:T(8,128)(2,1)S(1)}, u32[]{:S(2)}, u32[]{:S(2)}) collective-permute-start(f16[64,16,128]{2,1,0:T(8,128)(2,1)S(1)} %collective-permute-done.15), channel_id=1, source_target_pairs={{0,4},{4,0},{8,12},{12,8},{16,20},{20,16},{24,28},{28,24},{1,5},{5... | collective-permute-start | bytes 786440 | tf_op jit(solution)/shard_map/panel_cores/ppermute | solution.py:475
  82.9 4.4 %collective-permute-start.20 = (f16[64,16,128]{2,1,0:T(8,128)(2,1)S(1)}, f16[64,16,128]{2,1,0:T(8,128)(2,1)S(1)}, u32[]{:S(2)}, u32[]{:S(2)}) collective-permute-start(f16[64,16,128]{2,1,0:T(8,128)(2,1)S(1)} %collective-permute-done.16), channel_id=1, source_target_pairs={{0,4},{4,0},{8,12},{12,8},{16,20},{20,16},{24,28},{28,24},{1,5},{5... | collective-permute-start | bytes 786440 | tf_op jit(solution)/shard_map/panel_cores/ppermute | solution.py:475
  83.4 21.0 %collective-permute-start.23 = (f16[64,16,128]{2,1,0:T(8,128)(2,1)S(1)}, f16[64,16,128]{2,1,0:T(8,128)(2,1)S(1)}, u32[]{:S(2)}, u32[]{:S(2)}) collective-permute-start(f16[64,16,128]{2,1,0:T(8,128)(2,1)S(1)} %convert_element_type.66), channel_id=1, source_target_pairs={{0,3},{1,2},{2,1},{3,0},{4,7},{5,6},{6,5},{7,4},{8,11},{9,10},{10,... | collective-permute-start | bytes 786440 | tf_op jit(solution)/shard_map/panel_cols/ppermute | solution.py:484
  84.7 19.7 %collective-permute-start.22 = (f16[64,16,128]{2,1,0:T(8,128)(2,1)S(1)}, f16[64,16,128]{2,1,0:T(8,128)(2,1)S(1)}, u32[]{:S(2)}, u32[]{:S(2)}) collective-permute-start(f16[64,16,128]{2,1,0:T(8,128)(2,1)S(1)} %convert_element_type.66), channel_id=1, source_target_pairs={{0,2},{1,3},{2,0},{3,1},{4,6},{5,7},{6,4},{7,5},{8,10},{9,11},{10,... | collective-permute-start | bytes 786440 | tf_op jit(solution)/shard_map/panel_cols/ppermute | solution.py:484
  85.3 19.1 %collective-permute-start.21 = (f16[64,16,128]{2,1,0:T(8,128)(2,1)S(1)}, f16[64,16,128]{2,1,0:T(8,128)(2,1)S(1)}, u32[]{:S(2)}, u32[]{:S(2)}) collective-permute-start(f16[64,16,128]{2,1,0:T(8,128)(2,1)S(1)} %convert_element_type.66), channel_id=1, source_target_pairs={{0,1},{1,0},{2,3},{3,2},{4,5},{5,4},{6,7},{7,6},{8,9},{9,8},{10,11... | collective-permute-start | bytes 786440 | tf_op jit(solution)/shard_map/panel_cols/ppermute | solution.py:484
  104.4 1.6 %collective-permute-start.24 = (f16[64,16,128]{2,1,0:T(8,128)(2,1)S(1)}, f16[64,16,128]{2,1,0:T(8,128)(2,1)S(1)}, u32[]{:S(2)}, u32[]{:S(2)}) collective-permute-start(f16[64,16,128]{2,1,0:T(8,128)(2,1)S(1)} %convert_element_type.66), channel_id=1, source_target_pairs={{0,4},{4,0},{8,12},{12,8},{16,20},{20,16},{24,28},{28,24},{1,5},{5... | collective-permute-start | bytes 786440 | tf_op jit(solution)/shard_map/panel_cores/ppermute | solution.py:475
  104.5 1.9 %collective-permute-start.25 = (f16[64,16,128]{2,1,0:T(8,128)(2,1)S(1)}, f16[64,16,128]{2,1,0:T(8,128)(2,1)S(1)}, u32[]{:S(2)}, u32[]{:S(2)}) collective-permute-start(f16[64,16,128]{2,1,0:T(8,128)(2,1)S(1)} %collective-permute-done.21), channel_id=1, source_target_pairs={{0,4},{4,0},{8,12},{12,8},{16,20},{20,16},{24,28},{28,24},{1,5},{5... | collective-permute-start | bytes 786440 | tf_op jit(solution)/shard_map/panel_cores/ppermute | solution.py:475
  105.0 1.8 %collective-permute-start.26 = (f16[64,16,128]{2,1,0:T(8,128)(2,1)S(1)}, f16[64,16,128]{2,1,0:T(8,128)(2,1)S(1)}, u32[]{:S(2)}, u32[]{:S(2)}) collective-permute-start(f16[64,16,128]{2,1,0:T(8,128)(2,1)S(1)} %collective-permute-done.22), channel_id=1, source_target_pairs={{0,4},{4,0},{8,12},{12,8},{16,20},{20,16},{24,28},{28,24},{1,5},{5... | collective-permute-start | bytes 786440 | tf_op jit(solution)/shard_map/panel_cores/ppermute | solution.py:475
  105.1 2.1 %collective-permute-start.27 = (f16[64,16,128]{2,1,0:T(8,128)(2,1)S(1)}, f16[64,16,128]{2,1,0:T(8,128)(2,1)S(1)}, u32[]{:S(2)}, u32[]{:S(2)}) collective-permute-start(f16[64,16,128]{2,1,0:T(8,128)(2,1)S(1)} %collective-permute-done.23), channel_id=1, source_target_pairs={{0,4},{4,0},{8,12},{12,8},{16,20},{20,16},{24,28},{28,24},{1,5},{5... | collective-permute-start | bytes 786440 | tf_op jit(solution)/shard_map/panel_cores/ppermute | solution.py:475
  112.0 3.7 %collective-permute-start.28 = (f32[4,256,128]{2,1,0:T(8,128)S(1)}, f32[4,256,128]{2,1,0:T(8,128)S(1)}, u32[]{:S(2)}, u32[]{:S(2)}) collective-permute-start(f32[4,256,128]{2,1,0:T(8,128)S(1)} %get-tuple-element.78), channel_id=1, source_target_pairs={{0,4},{4,0},{8,12},{12,8},{16,20},{20,16},{24,28},{28,24},{1,5},{5... | collective-permute-start | bytes 1572872 | tf_op jit(solution)/shard_map/cross_sum/ppermute | solution.py:475
  115.8 14.7 %collective-permute-start.29 = (f32[256,128]{1,0:T(8,128)S(1)}, f32[256,128]{1,0:T(8,128)S(1)}, u32[]{:S(2)}, u32[]{:S(2)}) collective-permute-start(f32[256,128]{1,0:T(8,128)S(1)} %get-tuple-element.83), channel_id=1, source_target_pairs={{0,8},{4,12},{8,16},{12,20},{16,24},{20,28},{24,0},{28,4},{1,9},{5... | collective-permute-start | bytes 393224 | tf_op jit(solution)/shard_map/cross_sum/ppermute | solution.py:478
  115.9 14.6 %collective-permute-start.31 = (f32[256,128]{1,0:T(8,128)S(1)}, f32[256,128]{1,0:T(8,128)S(1)}, u32[]{:S(2)}, u32[]{:S(2)}) collective-permute-start(f32[256,128]{1,0:T(8,128)S(1)} %get-tuple-element.84), channel_id=1, source_target_pairs={{0,24},{4,28},{8,0},{12,4},{16,8},{20,12},{24,16},{28,20},{1,25},{... | collective-permute-start | bytes 393224 | tf_op jit(solution)/shard_map/cross_sum/ppermute | solution.py:478
  119.7 12.2 %collective-permute-start.30 = (f32[256,128]{1,0:T(8,128)S(1)}, f32[256,128]{1,0:T(8,128)S(1)}, u32[]{:S(2)}, u32[]{:S(2)}) collective-permute-start(f32[256,128]{1,0:T(8,128)S(1)} %get-tuple-element.85), channel_id=1, source_target_pairs={{0,16},{4,20},{8,24},{12,28},{16,0},{20,4},{24,8},{28,12},{1,17},{... | collective-permute-start | bytes 393224 | tf_op jit(solution)/shard_map/cross_sum/ppermute | solution.py:478

commit v5 on v4

--- a/solution.py
+++ b/solution.py
@@ -45,9 +45,9 @@
 
 def signed_mixer(mixers_ref, names_ref, tile):
     position = lax.broadcasted_iota(jnp.int32, (1, TILE), 1)
-    hashed = (names_ref[4, tile] ^ position * 40503) * 69069
+    hashed = (names_ref[1, tile] ^ position * 40503) * 69069
     sign = (1 - 2 * (hashed >> 16 & 1)).astype(F32)
-    return mixers_ref[names_ref[3, tile]] * sign
+    return mixers_ref[names_ref[0, tile]] * sign
 
 
 def split(value):
@@ -315,43 +315,46 @@
     )(names, order, after, *mixed, *pieces, *before)
 
 
-def above(value):
-    return jnp.concatenate([value[:1], value[:-1]], axis=0)
-
-
 def factor_inverse(block):
     row = lax.broadcasted_iota(jnp.int32, (BASE, BASE), 0)
     lane = lax.broadcasted_iota(jnp.int32, (BASE, BASE), 1)
-    eye = (row == lane).astype(F32)
-    wide = jnp.concatenate([block, eye], axis=1)
+    wide = jnp.concatenate([block, (row == lane).astype(F32)], axis=1)
     slabs = [wide[8 * g : 8 * g + 8, :] for g in range(BASE // 8)]
     place = lax.broadcasted_iota(jnp.int32, (8, 2 * BASE), 0)
 
     def full(value):
         return jnp.broadcast_to(value, (8, 2 * BASE))
 
-    for j in range(0, BASE, 2):
-        own, at = j // 8, j % 8
-        slab = slabs[own]
-        col0, col1 = full(slab[:, j : j + 1]), full(slab[:, j + 1 : j + 2])
-        row0, row1 = full(slab[at : at + 1, :]), full(slab[at + 1 : at + 2, :])
-        first, cross, second = full(col0[at : at + 1, :]), full(col1[at : at + 1, :]), full(col1[at + 1 : at + 2, :])
-        scale = 1.0 / (first * second - cross * cross)
-        solved0 = (second * row0 - cross * row1) * scale
-        solved1 = (first * row1 - cross * row0) * scale
-        for g in range(own, BASE // 8):
-            if g == own:
-                col0, col1 = jnp.where(place > at + 1, col0, 0.0), jnp.where(place > at + 1, col1, 0.0)
-            else:
-                col0, col1 = slabs[g][:, j : j + 1], slabs[g][:, j + 1 : j + 2]
-            slabs[g] = slabs[g] - col0 * solved0 - col1 * solved1
-    wide = jnp.concatenate(slabs, axis=0)
-    diagonal = jnp.sum(wide[:, :BASE] * eye, axis=1, keepdims=True)
-    beside = jnp.sum(jnp.where(lane == row + 1, wide[:, :BASE], 0.0), axis=1, keepdims=True)
-    odd = row[:, :1] % 2 == 1
-    ratio = jnp.where(odd, above(beside) / above(diagonal), 0.0)
-    pivots = jnp.where(odd, diagonal - above(beside) * ratio, diagonal)
-    return (wide - ratio * above(wide))[:, BASE:] * lax.rsqrt(pivots)
+    done = []
+    for own in range(BASE // 8):
+        slab, first = slabs[own], 8 * own
+        cols = [full(slab[:, first + k : first + k + 1]) for k in range(8)]
+        rows = [full(slab[k : k + 1, :]) for k in range(8)]
+        entry = {(a, b): full(cols[b][a : a + 1, :]) for a in range(8) for b in range(a, 8)}
+        factor, scale = {}, []
+        for k in range(8):
+            scale.append(1.0 / entry[k, k])
+            for a in range(k + 1, 8):
+                factor[a, k] = entry[k, a] * scale[k]
+            for a in range(k + 1, 8):
+                for b in range(a, 8):
+                    entry[a, b] = entry[a, b] - factor[a, k] * entry[k, b]
+                rows[a] = rows[a] - factor[a, k] * rows[k]
+        solved = [None] * 8
+        for k in reversed(range(8)):
+            value = rows[k] * scale[k]
+            for m in range(k + 1, 8):
+                value = value - factor[m, k] * solved[m]
+            solved[k] = value
+        for g in range(own + 1, BASE // 8):
+            before = slabs[g]
+            for k in range(8):
+                slabs[g] = slabs[g] - before[:, first + k : first + k + 1] * solved[k]
+        out = jnp.zeros((8, 2 * BASE), F32)
+        for k in range(8):
+            out = jnp.where(place == k, rows[k] * lax.rsqrt(entry[k, k]), out)
+        done.append(out)
+    return jnp.concatenate(done, axis=0)[:, BASE:]
 
 
 def factor_inverse_pair(block):
@@ -486,14 +489,15 @@
     fast = cols % (TILE * rows_n) == 0
     with jax.named_scope("names"):
         flips = 1 - 2 * (sign_seed >> 29 & 1)
-        names = jnp.stack([bucket_pair[:, 0], bucket_pair[:, 1], flips, mixer_index, sign_seed])
+        names = jnp.concatenate([bucket_pair.T, flips[None]])
+        kinds = jnp.stack([mixer_index, sign_seed])
         place = [part ^ j if parts == SLICES else j for j in range(SLICES)]
         order = [who * SLICES + c for who in (core, 1 - core) for c in place]
         order = jnp.stack([jnp.asarray(v, jnp.int32) for v in order + [chip, core, part]])
     with jax.named_scope("panel_mix"):
-        tiles = mix_panel(matrix, mixers, names, order)
+        tiles = mix_panel(matrix, mixers, kinds, order)
     with jax.named_scope("names"):
-        carried = jnp.pad(names[:3].astype(BF16), ((0, WIDTH - 3), (0, TILE - names.shape[1])))
+        carried = jnp.pad(names.astype(BF16), ((0, WIDTH - 3), (0, TILE - names.shape[1])))
 
     def before(values, *others):
         return lax.optimization_barrier((values, others))[0]
@@ -531,15 +535,16 @@
     def mix_next(after, count):
         for _ in range(count):
             with jax.named_scope("mix"):
-                more, after = mix_tiles(matrix, mixers, names, after, len(mixed) * STEP, STEP)
+                more, after = mix_tiles(matrix, mixers, kinds, after, len(mixed) * STEP, STEP)
             mixed.append(more)
         return after
 
     early = names.shape[1] // STEP // 2
     token = mix_next(tiles[0], early)
     held0 = spread(scatter(0), token, carried)
-    held1 = spread(scatter(1), token)
-    arrived0, arrived1 = gather_rows(held0), gather_rows(held1)
+    arrived0 = gather_rows(held0)
+    held1 = spread(scatter(1), arrived0[1])
+    arrived1 = gather_rows(held1)
     token = mix_next(held1, names.shape[1] // STEP - early)
     with jax.named_scope("panel_sum"):
         summed0, all_names = first_sum(token, arrived0)
@@ -547,7 +552,7 @@
     with jax.named_scope("panel_sum"):
         summed1 = next_sum(all_names, summed0, arrived1)
     mine1 = gather_cols(summed1)
-    pieces0 = both_cores(before(mine0, summed1))
+    pieces0 = both_cores(mine0[:2] + list(before(mine0[2:], summed1)))
     with jax.named_scope("cross0"):
         panel0, *crossed0 = cross_parts(names, order, summed1, mixed, pieces0, [], chips, fast)
     with jax.named_scope("factor0"):
@@ -565,7 +570,7 @@
         return lax.dynamic_slice_in_dim(nn(inverse, total), row * share, share, 0)
     with jax.named_scope("cross_sum"):
         keep, give = crossed
-        on_chip = keep + before(swap(give), side)
+        on_chip = keep + swap(give)
     with jax.named_scope("factor1"):
         inverse = second_factor(on_chip, side, block, inverse0)
     with jax.named_scope("cross_sum"):

time: 143 us -> 132 us (0.923)
  Pallas kernels: 66.5 us -> 58.5 us
    ppermute x6, waiting for transfers between devices: 13.3 us -> 6.94 us  [beside(): return lax.ppermute(value, 'rows', [(i, i ^ 2 * j) for i in range(rows_n)])]
    ppermute x6, waiting for transfers between devices: 3.16 us -> 9.08 us  [across(): return lax.ppermute(value, 'cols', [(i, i ^ j) for i in range(parts)])]
    ppermute x11, waiting for transfers between devices: 1.36 us -> 5.76 us  [swap(): return lax.ppermute(value, 'rows', [(i, i ^ 1) for i in range(rows_n)])]
    ppermute x6, waiting for transfers between devices: 4.11 us -> 0.18 us  [scatter(): lax.ppermute(slices[j], 'cols', [(0, j)])]
    pallas_call x1, Pallas kernels: 9.91 us -> 6.07 us  [first_factor(): pl.pallas_call(factor_kernel, in_specs=[vmem()], out_specs=vmem(), out_sh...]
    pallas_call x1, Pallas kernels: 10.7 us -> 6.86 us  [second_factor(): pl.pallas_call(last_kernel, in_specs=[anywhere()] + [vmem()] * 3, out_spe...]
  transfers between devices with their start and end apart: 32 -> 32, of which waited for: 12 -> 14; matrix products, arithmetic and copies ran while one was open for 0% -> 1% of each run, Pallas kernels for 39% -> 36%
where the time goes in v5:
time: 132 us
  Pallas kernels  58.5 us (44%)
  starting transfers between devices  36.4 us (28%)
  waiting for transfers between devices  22.7 us (17%)
  blocking collectives  10 us (8%)
  local copies, waits for them, and re-layouts  1.9 us (1%)
  other arithmetic  1.41 us (1%)
    pallas_call x4, Pallas kernels, mix_tiles(): pl.pallas_call(functools.partial(mix_kernel, per_step, start), grid_spec=...  16.5 us
    ppermute x6, starting transfers between devices, scatter(): lax.ppermute(slices[j], 'cols', [(0, j)])  14.1 us
    all_to_all x1, blocking collectives, local(): lax.all_to_all(solved, 'rows', split_axis=0, concat_axis=1, tiled=True)  10 us
    ppermute x6, starting transfers between devices, beside(): return lax.ppermute(value, 'rows', [(i, i ^ 2 * j) for i in range(rows_n)])  9.49 us
    pallas_call x2, Pallas kernels, cross_parts(): pl.pallas_call(functools.partial(cross_kernel, steps, chips, len(before),...  9.3 us
    ppermute x6, waiting for transfers between devices, across(): return lax.ppermute(value, 'cols', [(i, i ^ j) for i in range(parts)])  9.08 us
    ppermute x6, starting transfers between devices, across(): return lax.ppermute(value, 'cols', [(i, i ^ j) for i in range(parts)])  7.01 us
    ppermute x6, waiting for transfers between devices, beside(): return lax.ppermute(value, 'rows', [(i, i ^ 2 * j) for i in range(rows_n)])  6.94 us
  transfers between devices with their start and end apart: 32, of which 14 were waited for; matrix products, arithmetic and copies ran while one was open for 1% of the time, Pallas kernels for 36%

profile of v5, /device:TPU:0, one launch (start us, length us, event | category | flops | bytes accessed | tf_op | source)
XLA Modules:
  0.0 131.8 jit_solution(5897663065337063033)
XLA Ops:
  0.0 0.7 pad_add_fusion.1.names_ref
  0.8 1.0 copy-done
  1.8 5.3 %mix_panel.1 = (bf16[2,32,16,128]{3,2,1,0:T(8,128)(2,1)S(1)}, bf16[2,32,16,128]{3,2,1,0:T(8,128)(2,1)S(1)}, bf16[2,32,16,128]{3,2,1,0:T(8,128)(2,1)S(1)}, bf16[2...) custom-call(s32[2,32]{1,0:T(2,128)S(1)} %pad_add_fusion.1.names_ref,, ...), custom_call_target="tpu_custom_call" | custom-call | flops 1000000 | bytes 100000 | tf_op jit(solution)/shard_map/panel_mix/mix_panel/pallas_call | solution.py:86
  7.2 4.9 %collective-permute-start = (bf16[2,32,16,128]{3,2,1,0:T(8,128)(2,1)S(1)}, bf16[2,32,16,128]{3,2,1,0:T(8,128)(2,1)S(1)}, u32[]{:S(2)}, u32[]{:S(2)}) collective-permute-start(bf16[2,32,16,128]{3,2,1,0:T(8,128)(2,1)S(1)} %get-tuple-element.44), channel_id=1, source_target_pairs={{0,1},{4,5},{8,9},{12,13},{16,17},{20,21},{24,25},{28,29}} | collective-permute-start | bytes 786440 | tf_op jit(solution)/shard_map/panel_spread/ppermute | solution.py:508
  12.0 1.3 collective-permute-start.1
  13.3 1.3 collective-permute-start.2
  14.7 4.1 %mix_tiles.4 = (bf16[1024,1024]{1,0:T(8,128)(2,1)S(1)}, f32[8,128]{1,0:T(8,128)S(1)}) custom-call(s32[2,32]{1,0:T(2,128)S(1)} %pad_add_fusion.1.names_ref, f32[4096,1024]{1,0:T(8,128)} %matrix_ref.9, f32[8,128,128]{2,1,0:T(8,128)S(1)} %copy-done.1, bf16[2,32,16,128]{3,2,1,0:T(8,128)(2,1)S(1)} %get-tuple-element.41.after_ref.refs_1_), custom_call_target="tpu_custom_call" | custom-call | flops 1000000 | bytes 100000 | tf_op jit(solution)/shard_map/mix/mix_tiles/pallas_call | solution.py:117
  18.9 4.1 %mix_tiles.5 = (bf16[1024,1024]{1,0:T(8,128)(2,1)S(1)}, f32[8,128]{1,0:T(8,128)S(1)}) custom-call(s32[2,32]{1,0:T(2,128)S(1)} %pad_add_fusion.1.names_ref, f32[4096,1024]{1,0:T(8,128)} %matrix_ref.9, f32[8,128,128]{2,1,0:T(8,128)S(1)} %copy-done.1, f32[8,128]{1,0:T(8,128)S(1)} %get-tuple-element.42.after_ref), custom_call_target="tpu_custom_call" | custom-call | flops 1000000 | bytes 100000 | tf_op jit(solution)/shard_map/mix/mix_tiles/pallas_call | solution.py:117
  23.2 0.6 pick.2
  23.9 1.3 %collective-permute-done.3 = bf16[33,16,128]{2,1,0:T(8,128)(2,1)S(1)} collective-permute-done((bf16[33,16,128]{2,1,0:T(8,128)(2,1)S(1)}, bf16[33,16,128]{2,1,0:T(8,128)(2,1)S(1)}, u32[]{:S(2)}, u32[]{:S(2)}) %collective-permute-start.3) | collective-permute-done | bytes 135200 | tf_op jit(solution)/shard_map/panel_spread/ppermute | solution.py:478
  25.2 2.7 %collective-permute-start.4 = (bf16[66,16,128]{2,1,0:T(8,128)(2,1)S(1)}, bf16[66,16,128]{2,1,0:T(8,128)(2,1)S(1)}, u32[]{:S(2)}, u32[]{:S(2)}) collective-permute-start(bf16[66,16,128]{2,1,0:T(8,128)(2,1)S(1)} %constant_dynamic-update-slice_fusion.refs_0_), channel_id=1, source_target_pairs={{0,16},{4,20},{8,24},{12,28},{16,0},{20,4},{24,8},{28,12},{1,17},{... | collective-permute-start | bytes 811016 | tf_op jit(solution)/shard_map/panel_rows/ppermute | solution.py:484
  27.9 1.3 collective-permute-start.5
  29.2 1.3 collective-permute-start.6
  30.5 4.0 %collective-permute-start.7 = (bf16[2,32,16,128]{3,2,1,0:T(8,128)(2,1)S(1)}, bf16[2,32,16,128]{3,2,1,0:T(8,128)(2,1)S(1)}, u32[]{:S(2)}, u32[]{:S(2)}) collective-permute-start(bf16[2,32,16,128]{3,2,1,0:T(8,128)(2,1)S(1)} %get-tuple-element.52), channel_id=1, source_target_pairs={{0,3},{4,7},{8,11},{12,15},{16,19},{20,23},{24,27},{28,31}} | collective-permute-start | bytes 786440 | tf_op jit(solution)/shard_map/panel_spread/ppermute | solution.py:508
  34.5 1.6 %collective-permute-start.9 = (bf16[66,16,128]{2,1,0:T(8,128)(2,1)S(1)}, bf16[66,16,128]{2,1,0:T(8,128)(2,1)S(1)}, u32[]{:S(2)}, u32[]{:S(2)}) collective-permute-start(bf16[66,16,128]{2,1,0:T(8,128)(2,1)S(1)} %constant_dynamic-update-slice_fusion.refs_0_), channel_id=1, source_target_pairs={{0,8},{4,12},{8,0},{12,4},{16,24},{20,28},{24,16},{28,20},{1,9},{5... | collective-permute-start | bytes 811016 | tf_op jit(solution)/shard_map/panel_rows/ppermute | solution.py:484
  36.2 4.4 %collective-permute-done.4.after_ref.refs_1_ = bf16[66,16,128]{2,1,0:T(8,128)(2,1)S(1)} collective-permute-done((bf16[66,16,128]{2,1,0:T(8,128)(2,1)S(1)}, bf16[66,16,128]{2,1,0:T(8,128)(2,1)S(1)}, u32[]{:S(2)}, u32[]{:S(2)}) %collective-permute-start.4) | collective-permute-done | bytes 270368 | tf_op jit(solution)/shard_map/panel_rows/ppermute | solution.py:484
  40.6 0.6 collective-permute-start.10
  41.2 0.8 pick.3
  42.1 1.3 collective-permute-done.8
  43.4 1.5 %collective-permute-start.12 = (bf16[64,16,128]{2,1,0:T(8,128)(2,1)S(1)}, bf16[64,16,128]{2,1,0:T(8,128)(2,1)S(1)}, u32[]{:S(2)}, u32[]{:S(2)}) collective-permute-start(bf16[64,16,128]{2,1,0:T(8,128)(2,1)S(1)} %constant_dynamic-update-slice_fusion.2.after_ref.refs_0_), channel_id=1, source_target_pairs={{0,8},{4,12},{8,0},{12,4},{16,24},{20,28},{24,16},{28,20},{1,9},{5... | collective-permute-start | bytes 786440 | tf_op jit(solution)/shard_map/panel_rows/ppermute | solution.py:484
  44.9 2.1 %collective-permute-start.11 = (bf16[64,16,128]{2,1,0:T(8,128)(2,1)S(1)}, bf16[64,16,128]{2,1,0:T(8,128)(2,1)S(1)}, u32[]{:S(2)}, u32[]{:S(2)}) collective-permute-start(bf16[64,16,128]{2,1,0:T(8,128)(2,1)S(1)} %constant_dynamic-update-slice_fusion.2.after_ref.refs_0_), channel_id=1, source_target_pairs={{0,16},{4,20},{8,24},{12,28},{16,0},{20,4},{24,8},{28,12},{1,17},{... | collective-permute-start | bytes 786440 | tf_op jit(solution)/shard_map/panel_rows/ppermute | solution.py:484
  47.0 4.1 %mix_tiles.6 = (bf16[1024,1024]{1,0:T(8,128)(2,1)S(1)}, f32[8,128]{1,0:T(8,128)S(1)}) custom-call(s32[2,32]{1,0:T(2,128)S(1)} %pad_add_fusion.1.names_ref, f32[4096,1024]{1,0:T(8,128)} %matrix_ref.9, f32[8,128,128]{2,1,0:T(8,128)S(1)} %copy-done.1, bf16[64,16,128]{2,1,0:T(8,128)(2,1)S(1)} %constant_dynamic-update-slice_fusion.2.after_ref.refs_0_), custom_call_target="tpu_custom_call" | custom-call | flops 1000000 | bytes 100000 | tf_op jit(solution)/shard_map/mix/mix_tiles/pallas_call | solution.py:117
  51.1 4.1 %mix_tiles.7 = (bf16[1024,1024]{1,0:T(8,128)(2,1)S(1)}, f32[8,128]{1,0:T(8,128)S(1)}) custom-call(s32[2,32]{1,0:T(2,128)S(1)} %pad_add_fusion.1.names_ref, f32[4096,1024]{1,0:T(8,128)} %matrix_ref.9, f32[8,128,128]{2,1,0:T(8,128)S(1)} %copy-done.1, f32[8,128]{1,0:T(8,128)S(1)} %get-tuple-element.55.after_ref), custom_call_target="tpu_custom_call" | custom-call | flops 1000000 | bytes 100000 | tf_op jit(solution)/shard_map/mix/mix_tiles/pallas_call | solution.py:117
  55.3 2.5 %collective-permute-done.10.refs_3_ = bf16[66,16,128]{2,1,0:T(8,128)(2,1)S(1)} collective-permute-done((bf16[66,16,128]{2,1,0:T(8,128)(2,1)S(1)}, bf16[66,16,128]{2,1,0:T(8,128)(2,1)S(1)}, u32[]{:S(2)}, u32[]{:S(2)}) %collective-permute-start.10) | collective-permute-done | bytes 270368 | tf_op jit(solution)/shard_map/panel_rows/ppermute | solution.py:484
  57.8 3.6 %first_sum.1 = (f32[64,16,128]{2,1,0:T(8,128)S(1)}, s32[8,8,128]{2,1,0:T(8,128)S(1)}) custom-call(f32[8,128]{1,0:T(8,128)S(1)} %get-tuple-element.56.after_ref, bf16[66,16,128]{2,1,0:T(8,128)(2,1)S(1)} %constant_dynamic-update-slice_fusion.refs_0_, bf16[66,16,128]{2,1,0:T(8,128)(2,1)S(1)} %collective-permute-done.4.after_ref.refs_1_, ...), custom_call_target="tpu_custom_call" | custom-call | flops 1000000 | bytes 100000 | tf_op jit(solution)/shard_map/panel_sum/first_sum/pallas_call | solution.py:201
  61.5 1.0 collective-permute-start.13
  62.5 3.4 %collective-permute-start.16 = (f16[64,16,128]{2,1,0:T(8,128)(2,1)S(1)}, f16[64,16,128]{2,1,0:T(8,128)(2,1)S(1)}, u32[]{:S(2)}, u32[]{:S(2)}) collective-permute-start(f16[64,16,128]{2,1,0:T(8,128)(2,1)S(1)} %get-tuple-element.78), channel_id=1, source_target_pairs={{0,3},{1,2},{2,1},{3,0},{4,7},{5,6},{6,5},{7,4},{8,11},{9,10},{10,... | collective-permute-start | bytes 786440 | tf_op jit(solution)/shard_map/panel_cols/ppermute | solution.py:487
  65.9 4.8 %collective-permute-done.14 = f16[64,16,128]{2,1,0:T(8,128)(2,1)S(1)} collective-permute-done((f16[64,16,128]{2,1,0:T(8,128)(2,1)S(1)}, f16[64,16,128]{2,1,0:T(8,128)(2,1)S(1)}, u32[]{:S(2)}, u32[]{:S(2)}) %collective-permute-start.14) | collective-permute-done | bytes 262176 | tf_op jit(solution)/shard_map/panel_cols/ppermute | solution.py:487
  70.7 3.5 %next_sum.1.after_ref = f32[64,16,128]{2,1,0:T(8,128)S(1)} custom-call(s32[8,8,128]{2,1,0:T(8,128)S(1)} %get-tuple-element.57.names, f32[64,16,128]{2,1,0:T(8,128)S(1)} %get-tuple-element.58.after_ref, bf16[64,16,128]{2,1,0:T(8,128)(2,1)S(1)} %constant_dynamic-update-slice_fusion.2.after_ref.refs_0_, ...), custom_call_target="tpu_custom_call" | custom-call | flops 1000000 | bytes 100000 | tf_op jit(solution)/shard_map/panel_sum/next_sum/pallas_call | solution.py:220
  74.4 4.1 %collective-permute-done.15 = f16[64,16,128]{2,1,0:T(8,128)(2,1)S(1)} collective-permute-done((f16[64,16,128]{2,1,0:T(8,128)(2,1)S(1)}, f16[64,16,128]{2,1,0:T(8,128)(2,1)S(1)}, u32[]{:S(2)}, u32[]{:S(2)}) %collective-permute-start.15) | collective-permute-done | bytes 262176 | tf_op jit(solution)/shard_map/panel_cols/ppermute | solution.py:487
  78.5 0.5 collective-permute-start.20
  79.1 0.4 collective-permute-start.23
  79.5 1.5 %collective-permute-start.22 = (f16[64,16,128]{2,1,0:T(8,128)(2,1)S(1)}, f16[64,16,128]{2,1,0:T(8,128)(2,1)S(1)}, u32[]{:S(2)}, u32[]{:S(2)}) collective-permute-start(f16[64,16,128]{2,1,0:T(8,128)(2,1)S(1)} %convert_element_type.69), channel_id=1, source_target_pairs={{0,2},{1,3},{2,0},{3,1},{4,6},{5,7},{6,4},{7,5},{8,10},{9,11},{10,... | collective-permute-start | bytes 786440 | tf_op jit(solution)/shard_map/panel_cols/ppermute | solution.py:487
  81.0 1.6 %collective-permute-start.21 = (f16[64,16,128]{2,1,0:T(8,128)(2,1)S(1)}, f16[64,16,128]{2,1,0:T(8,128)(2,1)S(1)}, u32[]{:S(2)}, u32[]{:S(2)}) collective-permute-start(f16[64,16,128]{2,1,0:T(8,128)(2,1)S(1)} %convert_element_type.69), channel_id=1, source_target_pairs={{0,1},{1,0},{2,3},{3,2},{4,5},{5,4},{6,7},{7,6},{8,9},{9,8},{10,11... | collective-permute-start | bytes 786440 | tf_op jit(solution)/shard_map/panel_cols/ppermute | solution.py:487
  83.0 4.5 %cross_parts.2 = (f32[64,128,128]{2,1,0:T(8,128)S(1)}, f32[4,128,128]{2,1,0:T(8,128)S(1)}, f32[4,128,128]{2,1,0:T(8,128)S(1)}) custom-call(s32[3,32]{1,0:T(4,128)S(1)} %get-tuple-element.83.names_ref, s32[11]{0:T(128)S(1)} %stack.56.order_ref, f32[64,16,128]{2,1,0:T(8,128)S(1)} %next_sum.1.after_ref, bf16[1024,1024]{1,0:T(8,128)(2,1)S(1)} %get-tuple-element.59.refs_0_, ...), custom_call_target="tpu_custom_call" | custom-call | flops 1000000 | bytes 100000 | tf_op jit(solution)/shard_map/cross0/cross_parts/pallas_call | solution.py:305
  87.5 2.5 %first_gram.1.block_ref = f32[128,128]{1,0:T(8,128)S(1)} custom-call(f32[4,128,128]{2,1,0:T(8,128)S(1)} %get-tuple-element.65.after_ref.refs_12_, f32[64,128,128]{2,1,0:T(8,128)S(1)} %get-tuple-element.66.panel.panel0), custom_call_target="tpu_custom_call" | custom-call | flops 1000000 | bytes 100000 | tf_op jit(solution)/shard_map/factor0/first_gram/pallas_call | solution.py:390
  90.0 6.1 %first_factor.1.after_ref.inverse_ref = f32[128,128]{1,0:T(8,128)S(1)} custom-call(f32[128,128]{1,0:T(8,128)S(1)} %first_gram.1.block_ref), custom_call_target="tpu_custom_call" | custom-call | flops 1000000 | bytes 100000 | tf_op jit(solution)/shard_map/factor0/first_factor/pallas_call | solution.py:407
  96.2 0.5 collective-permute-start.25
  96.8 0.4 collective-permute-start.27
  98.9 4.8 %cross_parts.3 = (f32[64,128,128]{2,1,0:T(8,128)S(1)}, f32[4,256,128]{2,1,0:T(8,128)S(1)}, f32[4,256,128]{2,1,0:T(8,128)S(1)}) custom-call(s32[3,32]{1,0:T(4,128)S(1)} %get-tuple-element.83.names_ref, s32[11]{0:T(128)S(1)} %stack.56.order_ref, f32[128,128]{1,0:T(8,128)S(1)} %first_factor.1.after_ref.inverse_ref, ...), custom_call_target="tpu_custom_call" | custom-call | flops 1000000 | bytes 100000 | tf_op jit(solution)/shard_map/cross1/cross_parts/pallas_call | solution.py:305
  103.9 1.8 %collective-permute-done.28 = f32[4,256,128]{2,1,0:T(8,128)S(1)} collective-permute-done((f32[4,256,128]{2,1,0:T(8,128)S(1)}, f32[4,256,128]{2,1,0:T(8,128)S(1)}, u32[]{:S(2)}, u32[]{:S(2)}) %collective-permute-start.28) | collective-permute-done | bytes 524320 | tf_op jit(solution)/shard_map/cross_sum/ppermute | solution.py:478
  105.8 0.4 collective-permute-start.29
  106.2 3.5 %collective-permute-start.31 = (f32[256,128]{1,0:T(8,128)S(1)}, f32[256,128]{1,0:T(8,128)S(1)}, u32[]{:S(2)}, u32[]{:S(2)}) collective-permute-start(f32[256,128]{1,0:T(8,128)S(1)} %get-tuple-element.80), channel_id=1, source_target_pairs={{0,24},{4,28},{8,0},{12,4},{16,8},{20,12},{24,16},{28,20},{1,25},{... | collective-permute-start | bytes 393224 | tf_op jit(solution)/shard_map/cross_sum/ppermute | solution.py:481
  109.7 3.5 %second_gram.1 = (f32[128,128]{1,0:T(8,128)S(1)}, f32[128,128]{1,0:T(8,128)S(1)}) custom-call(f32[4,256,128]{2,1,0:T(8,128)S(1)} %get-tuple-element.72.after_ref, f32[64,128,128]{2,1,0:T(8,128)S(1)} %get-tuple-element.66.panel.panel0, f32[64,128,128]{2,1,0:T(8,128)S(1)} %get-tuple-element.74.panel1), custom_call_target="tpu_custom_call" | custom-call | flops 1000000 | bytes 100000 | tf_op jit(solution)/shard_map/gram1/second_gram/pallas_call | solution.py:436
  113.1 6.9 %second_factor.1 = f32[256,256]{1,0:T(8,128)S(1)} custom-call(f32[4,256,128]{2,1,0:T(8,128)S(1)} %add.52.after_ref, f32[128,128]{1,0:T(8,128)S(1)} %get-tuple-element.75.side_ref, f32[128,128]{1,0:T(8,128)S(1)} %get-tuple-element.76.block_ref, f32[128,128]{1,0:T(8,128)S(1)} %first_factor.1.after_ref.inverse_ref), custom_call_target="tpu_custom_call" | custom-call | flops 1000000 | bytes 100000 | tf_op jit(solution)/shard_map/factor1/second_factor/pallas_call | solution.py:459
  120.0 0.8 collective-permute-done.30
  121.2 10.0 %all_to_all.19 = f32[8,32,128]{2,1,0:T(8,128)S(1)} all-to-all(f32[8,32,128]{2,1,0:T(8,128)S(1)} %bitcast.39), channel_id=1, replica_groups=mesh['rows'=8,'cols'=4] {'rows'}, dimensions={0} | all-to-all | bytes 262144 | tf_op jit(solution)/shard_map/solve/all_to_all | solution.py:582
  131.2 0.7 copy_bitcast_fusion
  (70 shorter events, 3.6 us)
Async XLA Ops:
  0.8 1.0 copy-start
  1.8 12.8 %copy-start.3 = (s32[32]{0:T(128)S(1)}, s32[32]{0:T(128)}, u32[]{:S(2)}) copy-start(s32[32]{0:T(128)} %param.9) | copy-start | bytes 388
  1.8 12.9 %copy-start.2 = (s32[32,2]{0,1:T(2,128)S(1)}, s32[32,2]{0,1:T(2,128)}, u32[]{:S(2)}) copy-start(s32[32,2]{0,1:T(2,128)} %param.7) | copy-start | bytes 772
  1.8 12.9 %copy-start.1 = (f32[8,128,128]{2,1,0:T(8,128)S(1)}, f32[8,128,128]{2,1,0:T(8,128)}, u32[]{:S(2)}) copy-start(f32[8,128,128]{2,1,0:T(8,128)} %mixers_ref.9) | copy-start | bytes 1572868
  7.2 15.8 %collective-permute-start = (bf16[2,32,16,128]{3,2,1,0:T(8,128)(2,1)S(1)}, bf16[2,32,16,128]{3,2,1,0:T(8,128)(2,1)S(1)}, u32[]{:S(2)}, u32[]{:S(2)}) collective-permute-start(bf16[2,32,16,128]{3,2,1,0:T(8,128)(2,1)S(1)} %get-tuple-element.44), channel_id=1, source_target_pairs={{0,1},{4,5},{8,9},{12,13},{16,17},{20,21},{24,25},{28,29}} | collective-permute-start | bytes 786440 | tf_op jit(solution)/shard_map/panel_spread/ppermute | solution.py:508
  12.0 11.0 %collective-permute-start.1 = (bf16[2,32,16,128]{3,2,1,0:T(8,128)(2,1)S(1)}, bf16[2,32,16,128]{3,2,1,0:T(8,128)(2,1)S(1)}, u32[]{:S(2)}, u32[]{:S(2)}) collective-permute-start(bf16[2,32,16,128]{3,2,1,0:T(8,128)(2,1)S(1)} %get-tuple-element.45), channel_id=1, source_target_pairs={{0,2},{4,6},{8,10},{12,14},{16,18},{20,22},{24,26},{28,30}} | collective-permute-start | bytes 786440 | tf_op jit(solution)/shard_map/panel_spread/ppermute | solution.py:508
  13.3 9.8 %collective-permute-start.2 = (bf16[2,32,16,128]{3,2,1,0:T(8,128)(2,1)S(1)}, bf16[2,32,16,128]{3,2,1,0:T(8,128)(2,1)S(1)}, u32[]{:S(2)}, u32[]{:S(2)}) collective-permute-start(bf16[2,32,16,128]{3,2,1,0:T(8,128)(2,1)S(1)} %get-tuple-element.46), channel_id=1, source_target_pairs={{0,3},{4,7},{8,11},{12,15},{16,19},{20,23},{24,27},{28,31}} | collective-permute-start | bytes 786440 | tf_op jit(solution)/shard_map/panel_spread/ppermute | solution.py:508
  23.8 1.4 %collective-permute-start.3 = (bf16[33,16,128]{2,1,0:T(8,128)(2,1)S(1)}, bf16[33,16,128]{2,1,0:T(8,128)(2,1)S(1)}, u32[]{:S(2)}, u32[]{:S(2)}) collective-permute-start(bf16[33,16,128]{2,1,0:T(8,128)(2,1)S(1)} %get-tuple-element.48), channel_id=1, source_target_pairs={{0,4},{4,0},{8,12},{12,8},{16,20},{20,16},{24,28},{28,24},{1,5},{5... | collective-permute-start | bytes 405512 | tf_op jit(solution)/shard_map/panel_spread/ppermute | solution.py:478
  25.2 15.4 %collective-permute-start.4 = (bf16[66,16,128]{2,1,0:T(8,128)(2,1)S(1)}, bf16[66,16,128]{2,1,0:T(8,128)(2,1)S(1)}, u32[]{:S(2)}, u32[]{:S(2)}) collective-permute-start(bf16[66,16,128]{2,1,0:T(8,128)(2,1)S(1)} %constant_dynamic-update-slice_fusion.refs_0_), channel_id=1, source_target_pairs={{0,16},{4,20},{8,24},{12,28},{16,0},{20,4},{24,8},{28,12},{1,17},{... | collective-permute-start | bytes 811016 | tf_op jit(solution)/shard_map/panel_rows/ppermute | solution.py:484
  27.9 13.4 %collective-permute-start.5 = (bf16[2,32,16,128]{3,2,1,0:T(8,128)(2,1)S(1)}, bf16[2,32,16,128]{3,2,1,0:T(8,128)(2,1)S(1)}, u32[]{:S(2)}, u32[]{:S(2)}) collective-permute-start(bf16[2,32,16,128]{3,2,1,0:T(8,128)(2,1)S(1)} %get-tuple-element.50), channel_id=1, source_target_pairs={{0,1},{4,5},{8,9},{12,13},{16,17},{20,21},{24,25},{28,29}} | collective-permute-start | bytes 786440 | tf_op jit(solution)/shard_map/panel_spread/ppermute | solution.py:508
  29.2 12.1 %collective-permute-start.6 = (bf16[2,32,16,128]{3,2,1,0:T(8,128)(2,1)S(1)}, bf16[2,32,16,128]{3,2,1,0:T(8,128)(2,1)S(1)}, u32[]{:S(2)}, u32[]{:S(2)}) collective-permute-start(bf16[2,32,16,128]{3,2,1,0:T(8,128)(2,1)S(1)} %get-tuple-element.51), channel_id=1, source_target_pairs={{0,2},{4,6},{8,10},{12,14},{16,18},{20,22},{24,26},{28,30}} | collective-permute-start | bytes 786440 | tf_op jit(solution)/shard_map/panel_spread/ppermute | solution.py:508
  30.5 10.8 %collective-permute-start.7 = (bf16[2,32,16,128]{3,2,1,0:T(8,128)(2,1)S(1)}, bf16[2,32,16,128]{3,2,1,0:T(8,128)(2,1)S(1)}, u32[]{:S(2)}, u32[]{:S(2)}) collective-permute-start(bf16[2,32,16,128]{3,2,1,0:T(8,128)(2,1)S(1)} %get-tuple-element.52), channel_id=1, source_target_pairs={{0,3},{4,7},{8,11},{12,15},{16,19},{20,23},{24,27},{28,31}} | collective-permute-start | bytes 786440 | tf_op jit(solution)/shard_map/panel_spread/ppermute | solution.py:508
  34.5 20.8 %collective-permute-start.9 = (bf16[66,16,128]{2,1,0:T(8,128)(2,1)S(1)}, bf16[66,16,128]{2,1,0:T(8,128)(2,1)S(1)}, u32[]{:S(2)}, u32[]{:S(2)}) collective-permute-start(bf16[66,16,128]{2,1,0:T(8,128)(2,1)S(1)} %constant_dynamic-update-slice_fusion.refs_0_), channel_id=1, source_target_pairs={{0,8},{4,12},{8,0},{12,4},{16,24},{20,28},{24,16},{28,20},{1,9},{5... | collective-permute-start | bytes 811016 | tf_op jit(solution)/shard_map/panel_rows/ppermute | solution.py:484
  40.6 17.2 %collective-permute-start.10 = (bf16[66,16,128]{2,1,0:T(8,128)(2,1)S(1)}, bf16[66,16,128]{2,1,0:T(8,128)(2,1)S(1)}, u32[]{:S(2)}, u32[]{:S(2)}) collective-permute-start(bf16[66,16,128]{2,1,0:T(8,128)(2,1)S(1)} %collective-permute-done.4.after_ref.refs_1_), channel_id=1, source_target_pairs={{0,8},{4,12},{8,0},{12,4},{16,24},{20,28},{24,16},{28,20},{1,9},{5... | collective-permute-start | bytes 811016 | tf_op jit(solution)/shard_map/panel_rows/ppermute | solution.py:484
  42.0 1.4 %collective-permute-start.8 = (bf16[32,16,128]{2,1,0:T(8,128)(2,1)S(1)}, bf16[32,16,128]{2,1,0:T(8,128)(2,1)S(1)}, u32[]{:S(2)}, u32[]{:S(2)}) collective-permute-start(bf16[32,16,128]{2,1,0:T(8,128)(2,1)S(1)} %get-tuple-element.54), channel_id=1, source_target_pairs={{0,4},{4,0},{8,12},{12,8},{16,20},{20,16},{24,28},{28,24},{1,5},{5... | collective-permute-start | bytes 393224 | tf_op jit(solution)/shard_map/panel_spread/ppermute | solution.py:478
  43.4 22.5 %collective-permute-start.12 = (bf16[64,16,128]{2,1,0:T(8,128)(2,1)S(1)}, bf16[64,16,128]{2,1,0:T(8,128)(2,1)S(1)}, u32[]{:S(2)}, u32[]{:S(2)}) collective-permute-start(bf16[64,16,128]{2,1,0:T(8,128)(2,1)S(1)} %constant_dynamic-update-slice_fusion.2.after_ref.refs_0_), channel_id=1, source_target_pairs={{0,8},{4,12},{8,0},{12,4},{16,24},{20,28},{24,16},{28,20},{1,9},{5... | collective-permute-start | bytes 786440 | tf_op jit(solution)/shard_map/panel_rows/ppermute | solution.py:484
  44.9 16.6 %collective-permute-start.11 = (bf16[64,16,128]{2,1,0:T(8,128)(2,1)S(1)}, bf16[64,16,128]{2,1,0:T(8,128)(2,1)S(1)}, u32[]{:S(2)}, u32[]{:S(2)}) collective-permute-start(bf16[64,16,128]{2,1,0:T(8,128)(2,1)S(1)} %constant_dynamic-update-slice_fusion.2.after_ref.refs_0_), channel_id=1, source_target_pairs={{0,16},{4,20},{8,24},{12,28},{16,0},{20,4},{24,8},{28,12},{1,17},{... | collective-permute-start | bytes 786440 | tf_op jit(solution)/shard_map/panel_rows/ppermute | solution.py:484
  61.4 9.2 %collective-permute-start.14 = (f16[64,16,128]{2,1,0:T(8,128)(2,1)S(1)}, f16[64,16,128]{2,1,0:T(8,128)(2,1)S(1)}, u32[]{:S(2)}, u32[]{:S(2)}) collective-permute-start(f16[64,16,128]{2,1,0:T(8,128)(2,1)S(1)} %get-tuple-element.78), channel_id=1, source_target_pairs={{0,1},{1,0},{2,3},{3,2},{4,5},{5,4},{6,7},{7,6},{8,9},{9,8},{10,11... | collective-permute-start | bytes 786440 | tf_op jit(solution)/shard_map/panel_cols/ppermute | solution.py:487
  61.5 9.2 %collective-permute-start.13 = (bf16[64,16,128]{2,1,0:T(8,128)(2,1)S(1)}, bf16[64,16,128]{2,1,0:T(8,128)(2,1)S(1)}, u32[]{:S(2)}, u32[]{:S(2)}) collective-permute-start(bf16[64,16,128]{2,1,0:T(8,128)(2,1)S(1)} %collective-permute-done.11.refs_1_), channel_id=1, source_target_pairs={{0,8},{4,12},{8,0},{12,4},{16,24},{20,28},{24,16},{28,20},{1,9},{5... | collective-permute-start | bytes 786440 | tf_op jit(solution)/shard_map/panel_rows/ppermute | solution.py:484
  62.5 11.9 %collective-permute-start.16 = (f16[64,16,128]{2,1,0:T(8,128)(2,1)S(1)}, f16[64,16,128]{2,1,0:T(8,128)(2,1)S(1)}, u32[]{:S(2)}, u32[]{:S(2)}) collective-permute-start(f16[64,16,128]{2,1,0:T(8,128)(2,1)S(1)} %get-tuple-element.78), channel_id=1, source_target_pairs={{0,3},{1,2},{2,1},{3,0},{4,7},{5,6},{6,5},{7,4},{8,11},{9,10},{10,... | collective-permute-start | bytes 786440 | tf_op jit(solution)/shard_map/panel_cols/ppermute | solution.py:487
  65.9 12.6 %collective-permute-start.15 = (f16[64,16,128]{2,1,0:T(8,128)(2,1)S(1)}, f16[64,16,128]{2,1,0:T(8,128)(2,1)S(1)}, u32[]{:S(2)}, u32[]{:S(2)}) collective-permute-start(f16[64,16,128]{2,1,0:T(8,128)(2,1)S(1)} %get-tuple-element.78), channel_id=1, source_target_pairs={{0,2},{1,3},{2,0},{3,1},{4,6},{5,7},{6,4},{7,5},{8,10},{9,11},{10,... | collective-permute-start | bytes 786440 | tf_op jit(solution)/shard_map/panel_cols/ppermute | solution.py:487
  65.9 13.6 %collective-permute-start.17 = (f16[64,16,128]{2,1,0:T(8,128)(2,1)S(1)}, f16[64,16,128]{2,1,0:T(8,128)(2,1)S(1)}, u32[]{:S(2)}, u32[]{:S(2)}) collective-permute-start(f16[64,16,128]{2,1,0:T(8,128)(2,1)S(1)} %get-tuple-element.78), channel_id=1, source_target_pairs={{0,4},{4,0},{8,12},{12,8},{16,20},{20,16},{24,28},{28,24},{1,5},{5... | collective-permute-start | bytes 786440 | tf_op jit(solution)/shard_map/panel_cores/ppermute | solution.py:478
  70.7 10.4 %collective-permute-start.18 = (f16[64,16,128]{2,1,0:T(8,128)(2,1)S(1)}, f16[64,16,128]{2,1,0:T(8,128)(2,1)S(1)}, u32[]{:S(2)}, u32[]{:S(2)}) collective-permute-start(f16[64,16,128]{2,1,0:T(8,128)(2,1)S(1)} %collective-permute-done.14), channel_id=1, source_target_pairs={{0,4},{4,0},{8,12},{12,8},{16,20},{20,16},{24,28},{28,24},{1,5},{5... | collective-permute-start | bytes 786440 | tf_op jit(solution)/shard_map/panel_cores/ppermute | solution.py:478
  78.5 4.3 %collective-permute-start.19 = (f16[64,16,128]{2,1,0:T(8,128)(2,1)S(1)}, f16[64,16,128]{2,1,0:T(8,128)(2,1)S(1)}, u32[]{:S(2)}, u32[]{:S(2)}) collective-permute-start(f16[64,16,128]{2,1,0:T(8,128)(2,1)S(1)} %collective-permute-done.15), channel_id=1, source_target_pairs={{0,4},{4,0},{8,12},{12,8},{16,20},{20,16},{24,28},{28,24},{1,5},{5... | collective-permute-start | bytes 786440 | tf_op jit(solution)/shard_map/panel_cores/ppermute | solution.py:478
  78.5 4.4 %collective-permute-start.20 = (f16[64,16,128]{2,1,0:T(8,128)(2,1)S(1)}, f16[64,16,128]{2,1,0:T(8,128)(2,1)S(1)}, u32[]{:S(2)}, u32[]{:S(2)}) collective-permute-start(f16[64,16,128]{2,1,0:T(8,128)(2,1)S(1)} %collective-permute-done.16), channel_id=1, source_target_pairs={{0,4},{4,0},{8,12},{12,8},{16,20},{20,16},{24,28},{28,24},{1,5},{5... | collective-permute-start | bytes 786440 | tf_op jit(solution)/shard_map/panel_cores/ppermute | solution.py:478
  79.1 17.0 %collective-permute-start.23 = (f16[64,16,128]{2,1,0:T(8,128)(2,1)S(1)}, f16[64,16,128]{2,1,0:T(8,128)(2,1)S(1)}, u32[]{:S(2)}, u32[]{:S(2)}) collective-permute-start(f16[64,16,128]{2,1,0:T(8,128)(2,1)S(1)} %convert_element_type.69), channel_id=1, source_target_pairs={{0,3},{1,2},{2,1},{3,0},{4,7},{5,6},{6,5},{7,4},{8,11},{9,10},{10,... | collective-permute-start | bytes 786440 | tf_op jit(solution)/shard_map/panel_cols/ppermute | solution.py:487
  79.5 16.6 %collective-permute-start.22 = (f16[64,16,128]{2,1,0:T(8,128)(2,1)S(1)}, f16[64,16,128]{2,1,0:T(8,128)(2,1)S(1)}, u32[]{:S(2)}, u32[]{:S(2)}) collective-permute-start(f16[64,16,128]{2,1,0:T(8,128)(2,1)S(1)} %convert_element_type.69), channel_id=1, source_target_pairs={{0,2},{1,3},{2,0},{3,1},{4,6},{5,7},{6,4},{7,5},{8,10},{9,11},{10,... | collective-permute-start | bytes 786440 | tf_op jit(solution)/shard_map/panel_cols/ppermute | solution.py:487
  81.0 15.1 %collective-permute-start.21 = (f16[64,16,128]{2,1,0:T(8,128)(2,1)S(1)}, f16[64,16,128]{2,1,0:T(8,128)(2,1)S(1)}, u32[]{:S(2)}, u32[]{:S(2)}) collective-permute-start(f16[64,16,128]{2,1,0:T(8,128)(2,1)S(1)} %convert_element_type.69), channel_id=1, source_target_pairs={{0,1},{1,0},{2,3},{3,2},{4,5},{5,4},{6,7},{7,6},{8,9},{9,8},{10,11... | collective-permute-start | bytes 786440 | tf_op jit(solution)/shard_map/panel_cols/ppermute | solution.py:487
  96.2 1.6 %collective-permute-start.24 = (f16[64,16,128]{2,1,0:T(8,128)(2,1)S(1)}, f16[64,16,128]{2,1,0:T(8,128)(2,1)S(1)}, u32[]{:S(2)}, u32[]{:S(2)}) collective-permute-start(f16[64,16,128]{2,1,0:T(8,128)(2,1)S(1)} %convert_element_type.69), channel_id=1, source_target_pairs={{0,4},{4,0},{8,12},{12,8},{16,20},{20,16},{24,28},{28,24},{1,5},{5... | collective-permute-start | bytes 786440 | tf_op jit(solution)/shard_map/panel_cores/ppermute | solution.py:478
  96.2 1.9 %collective-permute-start.25 = (f16[64,16,128]{2,1,0:T(8,128)(2,1)S(1)}, f16[64,16,128]{2,1,0:T(8,128)(2,1)S(1)}, u32[]{:S(2)}, u32[]{:S(2)}) collective-permute-start(f16[64,16,128]{2,1,0:T(8,128)(2,1)S(1)} %collective-permute-done.21), channel_id=1, source_target_pairs={{0,4},{4,0},{8,12},{12,8},{16,20},{20,16},{24,28},{28,24},{1,5},{5... | collective-permute-start | bytes 786440 | tf_op jit(solution)/shard_map/panel_cores/ppermute | solution.py:478
  96.7 1.8 %collective-permute-start.26 = (f16[64,16,128]{2,1,0:T(8,128)(2,1)S(1)}, f16[64,16,128]{2,1,0:T(8,128)(2,1)S(1)}, u32[]{:S(2)}, u32[]{:S(2)}) collective-permute-start(f16[64,16,128]{2,1,0:T(8,128)(2,1)S(1)} %collective-permute-done.22), channel_id=1, source_target_pairs={{0,4},{4,0},{8,12},{12,8},{16,20},{20,16},{24,28},{28,24},{1,5},{5... | collective-permute-start | bytes 786440 | tf_op jit(solution)/shard_map/panel_cores/ppermute | solution.py:478
  96.8 2.1 %collective-permute-start.27 = (f16[64,16,128]{2,1,0:T(8,128)(2,1)S(1)}, f16[64,16,128]{2,1,0:T(8,128)(2,1)S(1)}, u32[]{:S(2)}, u32[]{:S(2)}) collective-permute-start(f16[64,16,128]{2,1,0:T(8,128)(2,1)S(1)} %collective-permute-done.23), channel_id=1, source_target_pairs={{0,4},{4,0},{8,12},{12,8},{16,20},{20,16},{24,28},{28,24},{1,5},{5... | collective-permute-start | bytes 786440 | tf_op jit(solution)/shard_map/panel_cores/ppermute | solution.py:478
  103.7 2.0 %collective-permute-start.28 = (f32[4,256,128]{2,1,0:T(8,128)S(1)}, f32[4,256,128]{2,1,0:T(8,128)S(1)}, u32[]{:S(2)}, u32[]{:S(2)}) collective-permute-start(f32[4,256,128]{2,1,0:T(8,128)S(1)} %get-tuple-element.73), channel_id=1, source_target_pairs={{0,4},{4,0},{8,12},{12,8},{16,20},{20,16},{24,28},{28,24},{1,5},{5... | collective-permute-start | bytes 1572872 | tf_op jit(solution)/shard_map/cross_sum/ppermute | solution.py:478
  105.8 14.2 %collective-permute-start.29 = (f32[256,128]{1,0:T(8,128)S(1)}, f32[256,128]{1,0:T(8,128)S(1)}, u32[]{:S(2)}, u32[]{:S(2)}) collective-permute-start(f32[256,128]{1,0:T(8,128)S(1)} %get-tuple-element.79), channel_id=1, source_target_pairs={{0,8},{4,12},{8,16},{12,20},{16,24},{20,28},{24,0},{28,4},{1,9},{5... | collective-permute-start | bytes 393224 | tf_op jit(solution)/shard_map/cross_sum/ppermute | solution.py:481
  106.2 13.8 %collective-permute-start.31 = (f32[256,128]{1,0:T(8,128)S(1)}, f32[256,128]{1,0:T(8,128)S(1)}, u32[]{:S(2)}, u32[]{:S(2)}) collective-permute-start(f32[256,128]{1,0:T(8,128)S(1)} %get-tuple-element.80), channel_id=1, source_target_pairs={{0,24},{4,28},{8,0},{12,4},{16,8},{20,12},{24,16},{28,20},{1,25},{... | collective-permute-start | bytes 393224 | tf_op jit(solution)/shard_map/cross_sum/ppermute | solution.py:481
  109.7 11.1 %collective-permute-start.30 = (f32[256,128]{1,0:T(8,128)S(1)}, f32[256,128]{1,0:T(8,128)S(1)}, u32[]{:S(2)}, u32[]{:S(2)}) collective-permute-start(f32[256,128]{1,0:T(8,128)S(1)} %get-tuple-element.81), channel_id=1, source_target_pairs={{0,16},{4,20},{8,24},{12,28},{16,0},{20,4},{24,8},{28,12},{1,17},{... | collective-permute-start | bytes 393224 | tf_op jit(solution)/shard_map/cross_sum/ppermute | solution.py:481

commit v6 on v5

--- a/solution.py
+++ b/solution.py
@@ -81,7 +81,7 @@
 
 def mix_panel(matrix, mixers, names, order):
     tiles = names.shape[1]
-    per_step = 8
+    per_step = 16
     spec = pl.BlockSpec((2, per_step, WIDTH, TILE), lambda i, *_: (0, i, 0, 0))
     return pl.pallas_call(
         functools.partial(panel_kernel, per_step),
@@ -552,7 +552,7 @@
     with jax.named_scope("panel_sum"):
         summed1 = next_sum(all_names, summed0, arrived1)
     mine1 = gather_cols(summed1)
-    pieces0 = both_cores(mine0[:2] + list(before(mine0[2:], summed1)))
+    pieces0 = both_cores(mine0[:-1] + list(before(mine0[-1:], summed1)))
     with jax.named_scope("cross0"):
         panel0, *crossed0 = cross_parts(names, order, summed1, mixed, pieces0, [], chips, fast)
     with jax.named_scope("factor0"):

time: 132 us -> 129 us (0.977)
    ppermute x6, waiting for transfers between devices: 9.08 us -> 6.98 us  [across(): return lax.ppermute(value, 'cols', [(i, i ^ j) for i in range(parts)])]
  transfers between devices with their start and end apart: 32 -> 32, of which waited for: 14 -> 14; matrix products, arithmetic and copies ran while one was open for 1% -> 1% of each run, Pallas kernels for 36% -> 37%
where the time goes in v6:
time: 129 us
  Pallas kernels  57.8 us (45%)
  starting transfers between devices  35.9 us (28%)
  waiting for transfers between devices  21.4 us (17%)
  blocking collectives  9.31 us (7%)
  local copies, waits for them, and re-layouts  1.9 us (1%)
  other arithmetic  1.41 us (1%)
    pallas_call x4, Pallas kernels, mix_tiles(): pl.pallas_call(functools.partial(mix_kernel, per_step, start), grid_spec=...  16.5 us
    ppermute x6, starting transfers between devices, scatter(): lax.ppermute(slices[j], 'cols', [(0, j)])  14.1 us
    ppermute x6, starting transfers between devices, beside(): return lax.ppermute(value, 'rows', [(i, i ^ 2 * j) for i in range(rows_n)])  9.82 us
    all_to_all x1, blocking collectives, local(): lax.all_to_all(solved, 'rows', split_axis=0, concat_axis=1, tiled=True)  9.31 us
    pallas_call x2, Pallas kernels, cross_parts(): pl.pallas_call(functools.partial(cross_kernel, steps, chips, len(before),...  9.3 us
    ppermute x6, waiting for transfers between devices, across(): return lax.ppermute(value, 'cols', [(i, i ^ j) for i in range(parts)])  6.98 us
    ppermute x6, waiting for transfers between devices, beside(): return lax.ppermute(value, 'rows', [(i, i ^ 2 * j) for i in range(rows_n)])  6.95 us
    pallas_call x1, Pallas kernels, second_factor(): pl.pallas_call(last_kernel, in_specs=[anywhere()] + [vmem()] * 3, out_spe...  6.85 us
  transfers between devices with their start and end apart: 32, of which 14 were waited for; matrix products, arithmetic and copies ran while one was open for 1% of the time, Pallas kernels for 37%

profile of v6, /device:TPU:0, one launch (start us, length us, event | category | flops | bytes accessed | tf_op | source)
XLA Modules:
  0.0 128.5 jit_solution(5190141239615592893)
XLA Ops:
  0.0 0.7 pad_add_fusion.1.names_ref
  0.8 1.0 copy-done
  1.8 4.6 %mix_panel.1 = (bf16[2,32,16,128]{3,2,1,0:T(8,128)(2,1)S(1)}, bf16[2,32,16,128]{3,2,1,0:T(8,128)(2,1)S(1)}, bf16[2,32,16,128]{3,2,1,0:T(8,128)(2,1)S(1)}, bf16[2...) custom-call(s32[2,32]{1,0:T(2,128)S(1)} %pad_add_fusion.1.names_ref,, ...), custom_call_target="tpu_custom_call" | custom-call | flops 1000000 | bytes 100000 | tf_op jit(solution)/shard_map/panel_mix/mix_panel/pallas_call | solution.py:86
  6.5 4.9 %collective-permute-start = (bf16[2,32,16,128]{3,2,1,0:T(8,128)(2,1)S(1)}, bf16[2,32,16,128]{3,2,1,0:T(8,128)(2,1)S(1)}, u32[]{:S(2)}, u32[]{:S(2)}) collective-permute-start(bf16[2,32,16,128]{3,2,1,0:T(8,128)(2,1)S(1)} %get-tuple-element.43), channel_id=1, source_target_pairs={{0,1},{4,5},{8,9},{12,13},{16,17},{20,21},{24,25},{28,29}} | collective-permute-start | bytes 786440 | tf_op jit(solution)/shard_map/panel_spread/ppermute | solution.py:508
  11.3 1.3 %collective-permute-start.1 = (bf16[2,32,16,128]{3,2,1,0:T(8,128)(2,1)S(1)}, bf16[2,32,16,128]{3,2,1,0:T(8,128)(2,1)S(1)}, u32[]{:S(2)}, u32[]{:S(2)}) collective-permute-start(bf16[2,32,16,128]{3,2,1,0:T(8,128)(2,1)S(1)} %get-tuple-element.44), channel_id=1, source_target_pairs={{0,2},{4,6},{8,10},{12,14},{16,18},{20,22},{24,26},{28,30}} | collective-permute-start | bytes 786440 | tf_op jit(solution)/shard_map/panel_spread/ppermute | solution.py:508
  12.6 1.3 %collective-permute-start.2 = (bf16[2,32,16,128]{3,2,1,0:T(8,128)(2,1)S(1)}, bf16[2,32,16,128]{3,2,1,0:T(8,128)(2,1)S(1)}, u32[]{:S(2)}, u32[]{:S(2)}) collective-permute-start(bf16[2,32,16,128]{3,2,1,0:T(8,128)(2,1)S(1)} %get-tuple-element.45), channel_id=1, source_target_pairs={{0,3},{4,7},{8,11},{12,15},{16,19},{20,23},{24,27},{28,31}} | collective-permute-start | bytes 786440 | tf_op jit(solution)/shard_map/panel_spread/ppermute | solution.py:508
  14.0 4.1 %mix_tiles.4 = (bf16[1024,1024]{1,0:T(8,128)(2,1)S(1)}, f32[8,128]{1,0:T(8,128)S(1)}) custom-call(s32[2,32]{1,0:T(2,128)S(1)} %pad_add_fusion.1.names_ref, f32[4096,1024]{1,0:T(8,128)} %matrix_ref.9, f32[8,128,128]{2,1,0:T(8,128)S(1)} %copy-done.1, bf16[2,32,16,128]{3,2,1,0:T(8,128)(2,1)S(1)} %get-tuple-element.40.after_ref.refs_1_), custom_call_target="tpu_custom_call" | custom-call | flops 1000000 | bytes 100000 | tf_op jit(solution)/shard_map/mix/mix_tiles/pallas_call | solution.py:117
  18.2 4.1 %mix_tiles.5 = (bf16[1024,1024]{1,0:T(8,128)(2,1)S(1)}, f32[8,128]{1,0:T(8,128)S(1)}) custom-call(s32[2,32]{1,0:T(2,128)S(1)} %pad_add_fusion.1.names_ref, f32[4096,1024]{1,0:T(8,128)} %matrix_ref.9, f32[8,128,128]{2,1,0:T(8,128)S(1)} %copy-done.1, f32[8,128]{1,0:T(8,128)S(1)} %get-tuple-element.41.after_ref), custom_call_target="tpu_custom_call" | custom-call | flops 1000000 | bytes 100000 | tf_op jit(solution)/shard_map/mix/mix_tiles/pallas_call | solution.py:117
  22.5 0.6 pick.2
  23.2 1.3 %collective-permute-done.3 = bf16[33,16,128]{2,1,0:T(8,128)(2,1)S(1)} collective-permute-done((bf16[33,16,128]{2,1,0:T(8,128)(2,1)S(1)}, bf16[33,16,128]{2,1,0:T(8,128)(2,1)S(1)}, u32[]{:S(2)}, u32[]{:S(2)}) %collective-permute-start.3) | collective-permute-done | bytes 135200 | tf_op jit(solution)/shard_map/panel_spread/ppermute | solution.py:478
  24.5 2.7 %collective-permute-start.4 = (bf16[66,16,128]{2,1,0:T(8,128)(2,1)S(1)}, bf16[66,16,128]{2,1,0:T(8,128)(2,1)S(1)}, u32[]{:S(2)}, u32[]{:S(2)}) collective-permute-start(bf16[66,16,128]{2,1,0:T(8,128)(2,1)S(1)} %constant_dynamic-update-slice_fusion.refs_0_), channel_id=1, source_target_pairs={{0,16},{4,20},{8,24},{12,28},{16,0},{20,4},{24,8},{28,12},{1,17},{... | collective-permute-start | bytes 811016 | tf_op jit(solution)/shard_map/panel_rows/ppermute | solution.py:484
  27.2 1.3 %collective-permute-start.5 = (bf16[2,32,16,128]{3,2,1,0:T(8,128)(2,1)S(1)}, bf16[2,32,16,128]{3,2,1,0:T(8,128)(2,1)S(1)}, u32[]{:S(2)}, u32[]{:S(2)}) collective-permute-start(bf16[2,32,16,128]{3,2,1,0:T(8,128)(2,1)S(1)} %get-tuple-element.49), channel_id=1, source_target_pairs={{0,1},{4,5},{8,9},{12,13},{16,17},{20,21},{24,25},{28,29}} | collective-permute-start | bytes 786440 | tf_op jit(solution)/shard_map/panel_spread/ppermute | solution.py:508
  28.5 1.3 %collective-permute-start.6 = (bf16[2,32,16,128]{3,2,1,0:T(8,128)(2,1)S(1)}, bf16[2,32,16,128]{3,2,1,0:T(8,128)(2,1)S(1)}, u32[]{:S(2)}, u32[]{:S(2)}) collective-permute-start(bf16[2,32,16,128]{3,2,1,0:T(8,128)(2,1)S(1)} %get-tuple-element.50), channel_id=1, source_target_pairs={{0,2},{4,6},{8,10},{12,14},{16,18},{20,22},{24,26},{28,30}} | collective-permute-start | bytes 786440 | tf_op jit(solution)/shard_map/panel_spread/ppermute | solution.py:508
  29.8 4.0 %collective-permute-start.7 = (bf16[2,32,16,128]{3,2,1,0:T(8,128)(2,1)S(1)}, bf16[2,32,16,128]{3,2,1,0:T(8,128)(2,1)S(1)}, u32[]{:S(2)}, u32[]{:S(2)}) collective-permute-start(bf16[2,32,16,128]{3,2,1,0:T(8,128)(2,1)S(1)} %get-tuple-element.51), channel_id=1, source_target_pairs={{0,3},{4,7},{8,11},{12,15},{16,19},{20,23},{24,27},{28,31}} | collective-permute-start | bytes 786440 | tf_op jit(solution)/shard_map/panel_spread/ppermute | solution.py:508
  33.8 1.6 %collective-permute-start.9 = (bf16[66,16,128]{2,1,0:T(8,128)(2,1)S(1)}, bf16[66,16,128]{2,1,0:T(8,128)(2,1)S(1)}, u32[]{:S(2)}, u32[]{:S(2)}) collective-permute-start(bf16[66,16,128]{2,1,0:T(8,128)(2,1)S(1)} %constant_dynamic-update-slice_fusion.refs_0_), channel_id=1, source_target_pairs={{0,8},{4,12},{8,0},{12,4},{16,24},{20,28},{24,16},{28,20},{1,9},{5... | collective-permute-start | bytes 811016 | tf_op jit(solution)/shard_map/panel_rows/ppermute | solution.py:484
  35.5 4.4 %collective-permute-done.4.after_ref.refs_1_ = bf16[66,16,128]{2,1,0:T(8,128)(2,1)S(1)} collective-permute-done((bf16[66,16,128]{2,1,0:T(8,128)(2,1)S(1)}, bf16[66,16,128]{2,1,0:T(8,128)(2,1)S(1)}, u32[]{:S(2)}, u32[]{:S(2)}) %collective-permute-start.4) | collective-permute-done | bytes 270368 | tf_op jit(solution)/shard_map/panel_rows/ppermute | solution.py:484
  39.9 0.6 collective-permute-start.10
  40.5 0.8 pick.3
  41.4 1.3 %collective-permute-done.8 = bf16[32,16,128]{2,1,0:T(8,128)(2,1)S(1)} collective-permute-done((bf16[32,16,128]{2,1,0:T(8,128)(2,1)S(1)}, bf16[32,16,128]{2,1,0:T(8,128)(2,1)S(1)}, u32[]{:S(2)}, u32[]{:S(2)}) %collective-permute-start.8) | collective-permute-done | bytes 131104 | tf_op jit(solution)/shard_map/panel_spread/ppermute | solution.py:478
  42.7 1.5 %collective-permute-start.12 = (bf16[64,16,128]{2,1,0:T(8,128)(2,1)S(1)}, bf16[64,16,128]{2,1,0:T(8,128)(2,1)S(1)}, u32[]{:S(2)}, u32[]{:S(2)}) collective-permute-start(bf16[64,16,128]{2,1,0:T(8,128)(2,1)S(1)} %constant_dynamic-update-slice_fusion.2.after_ref.refs_0_), channel_id=1, source_target_pairs={{0,8},{4,12},{8,0},{12,4},{16,24},{20,28},{24,16},{28,20},{1,9},{5... | collective-permute-start | bytes 786440 | tf_op jit(solution)/shard_map/panel_rows/ppermute | solution.py:484
  44.2 2.1 %collective-permute-start.11 = (bf16[64,16,128]{2,1,0:T(8,128)(2,1)S(1)}, bf16[64,16,128]{2,1,0:T(8,128)(2,1)S(1)}, u32[]{:S(2)}, u32[]{:S(2)}) collective-permute-start(bf16[64,16,128]{2,1,0:T(8,128)(2,1)S(1)} %constant_dynamic-update-slice_fusion.2.after_ref.refs_0_), channel_id=1, source_target_pairs={{0,16},{4,20},{8,24},{12,28},{16,0},{20,4},{24,8},{28,12},{1,17},{... | collective-permute-start | bytes 786440 | tf_op jit(solution)/shard_map/panel_rows/ppermute | solution.py:484
  46.3 4.1 %mix_tiles.6 = (bf16[1024,1024]{1,0:T(8,128)(2,1)S(1)}, f32[8,128]{1,0:T(8,128)S(1)}) custom-call(s32[2,32]{1,0:T(2,128)S(1)} %pad_add_fusion.1.names_ref, f32[4096,1024]{1,0:T(8,128)} %matrix_ref.9, f32[8,128,128]{2,1,0:T(8,128)S(1)} %copy-done.1, bf16[64,16,128]{2,1,0:T(8,128)(2,1)S(1)} %constant_dynamic-update-slice_fusion.2.after_ref.refs_0_), custom_call_target="tpu_custom_call" | custom-call | flops 1000000 | bytes 100000 | tf_op jit(solution)/shard_map/mix/mix_tiles/pallas_call | solution.py:117
  50.4 4.1 %mix_tiles.7 = (bf16[1024,1024]{1,0:T(8,128)(2,1)S(1)}, f32[8,128]{1,0:T(8,128)S(1)}) custom-call(s32[2,32]{1,0:T(2,128)S(1)} %pad_add_fusion.1.names_ref, f32[4096,1024]{1,0:T(8,128)} %matrix_ref.9, f32[8,128,128]{2,1,0:T(8,128)S(1)} %copy-done.1, f32[8,128]{1,0:T(8,128)S(1)} %get-tuple-element.54.after_ref), custom_call_target="tpu_custom_call" | custom-call | flops 1000000 | bytes 100000 | tf_op jit(solution)/shard_map/mix/mix_tiles/pallas_call | solution.py:117
  54.6 2.5 %collective-permute-done.10.refs_3_ = bf16[66,16,128]{2,1,0:T(8,128)(2,1)S(1)} collective-permute-done((bf16[66,16,128]{2,1,0:T(8,128)(2,1)S(1)}, bf16[66,16,128]{2,1,0:T(8,128)(2,1)S(1)}, u32[]{:S(2)}, u32[]{:S(2)}) %collective-permute-start.10) | collective-permute-done | bytes 270368 | tf_op jit(solution)/shard_map/panel_rows/ppermute | solution.py:484
  57.1 3.6 %first_sum.1 = (f32[64,16,128]{2,1,0:T(8,128)S(1)}, s32[8,8,128]{2,1,0:T(8,128)S(1)}) custom-call(f32[8,128]{1,0:T(8,128)S(1)} %get-tuple-element.55.after_ref, bf16[66,16,128]{2,1,0:T(8,128)(2,1)S(1)} %constant_dynamic-update-slice_fusion.refs_0_, bf16[66,16,128]{2,1,0:T(8,128)(2,1)S(1)} %collective-permute-done.4.after_ref.refs_1_, ...), custom_call_target="tpu_custom_call" | custom-call | flops 1000000 | bytes 100000 | tf_op jit(solution)/shard_map/panel_sum/first_sum/pallas_call | solution.py:201
  60.8 2.0 %collective-permute-start.14 = (f16[64,16,128]{2,1,0:T(8,128)(2,1)S(1)}, f16[64,16,128]{2,1,0:T(8,128)(2,1)S(1)}, u32[]{:S(2)}, u32[]{:S(2)}) collective-permute-start(f16[64,16,128]{2,1,0:T(8,128)(2,1)S(1)} %get-tuple-element.76), channel_id=1, source_target_pairs={{0,1},{1,0},{2,3},{3,2},{4,5},{5,4},{6,7},{7,6},{8,9},{9,8},{10,11... | collective-permute-start | bytes 786440 | tf_op jit(solution)/shard_map/panel_cols/ppermute | solution.py:487
  62.9 1.3 %collective-permute-start.13 = (bf16[64,16,128]{2,1,0:T(8,128)(2,1)S(1)}, bf16[64,16,128]{2,1,0:T(8,128)(2,1)S(1)}, u32[]{:S(2)}, u32[]{:S(2)}) collective-permute-start(bf16[64,16,128]{2,1,0:T(8,128)(2,1)S(1)} %collective-permute-done.11.refs_1_), channel_id=1, source_target_pairs={{0,8},{4,12},{8,0},{12,4},{16,24},{20,28},{24,16},{28,20},{1,9},{5... | collective-permute-start | bytes 786440 | tf_op jit(solution)/shard_map/panel_rows/ppermute | solution.py:484
  64.2 1.0 collective-permute-start.16
  65.2 3.9 %collective-permute-done.15 = f16[64,16,128]{2,1,0:T(8,128)(2,1)S(1)} collective-permute-done((f16[64,16,128]{2,1,0:T(8,128)(2,1)S(1)}, f16[64,16,128]{2,1,0:T(8,128)(2,1)S(1)}, u32[]{:S(2)}, u32[]{:S(2)}) %collective-permute-start.15) | collective-permute-done | bytes 262176 | tf_op jit(solution)/shard_map/panel_cols/ppermute | solution.py:487
  69.1 0.9 collective-permute-done.14
  70.1 3.5 %next_sum.1.after_ref = f32[64,16,128]{2,1,0:T(8,128)S(1)} custom-call(s32[8,8,128]{2,1,0:T(8,128)S(1)} %get-tuple-element.56.names, f32[64,16,128]{2,1,0:T(8,128)S(1)} %get-tuple-element.57.after_ref, bf16[64,16,128]{2,1,0:T(8,128)(2,1)S(1)} %constant_dynamic-update-slice_fusion.2.after_ref.refs_0_, ...), custom_call_target="tpu_custom_call" | custom-call | flops 1000000 | bytes 100000 | tf_op jit(solution)/shard_map/panel_sum/next_sum/pallas_call | solution.py:220
  73.6 2.1 %collective-permute-done.16 = f16[64,16,128]{2,1,0:T(8,128)(2,1)S(1)} collective-permute-done((f16[64,16,128]{2,1,0:T(8,128)(2,1)S(1)}, f16[64,16,128]{2,1,0:T(8,128)(2,1)S(1)}, u32[]{:S(2)}, u32[]{:S(2)}) %collective-permute-start.16) | collective-permute-done | bytes 262176 | tf_op jit(solution)/shard_map/panel_cols/ppermute | solution.py:487
  75.8 0.9 collective-permute-start.23
  76.7 1.1 collective-permute-start.22
  77.8 1.5 %collective-permute-start.21 = (f16[64,16,128]{2,1,0:T(8,128)(2,1)S(1)}, f16[64,16,128]{2,1,0:T(8,128)(2,1)S(1)}, u32[]{:S(2)}, u32[]{:S(2)}) collective-permute-start(f16[64,16,128]{2,1,0:T(8,128)(2,1)S(1)} %convert_element_type.69), channel_id=1, source_target_pairs={{0,1},{1,0},{2,3},{3,2},{4,5},{5,4},{6,7},{7,6},{8,9},{9,8},{10,11... | collective-permute-start | bytes 786440 | tf_op jit(solution)/shard_map/panel_cols/ppermute | solution.py:487
  79.7 4.5 %cross_parts.2 = (f32[64,128,128]{2,1,0:T(8,128)S(1)}, f32[4,128,128]{2,1,0:T(8,128)S(1)}, f32[4,128,128]{2,1,0:T(8,128)S(1)}) custom-call(s32[3,32]{1,0:T(4,128)S(1)} %get-tuple-element.81.names_ref, s32[11]{0:T(128)S(1)} %stack.56.order_ref, f32[64,16,128]{2,1,0:T(8,128)S(1)} %next_sum.1.after_ref, bf16[1024,1024]{1,0:T(8,128)(2,1)S(1)} %get-tuple-element.58.refs_0_, ...), custom_call_target="tpu_custom_call" | custom-call | flops 1000000 | bytes 100000 | tf_op jit(solution)/shard_map/cross0/cross_parts/pallas_call | solution.py:305
  84.2 2.5 %first_gram.1.block_ref = f32[128,128]{1,0:T(8,128)S(1)} custom-call(f32[4,128,128]{2,1,0:T(8,128)S(1)} %get-tuple-element.63.after_ref.refs_12_, f32[64,128,128]{2,1,0:T(8,128)S(1)} %get-tuple-element.64.panel.panel0), custom_call_target="tpu_custom_call" | custom-call | flops 1000000 | bytes 100000 | tf_op jit(solution)/shard_map/factor0/first_gram/pallas_call | solution.py:390
  86.7 6.1 %first_factor.1.after_ref.inverse_ref = f32[128,128]{1,0:T(8,128)S(1)} custom-call(f32[128,128]{1,0:T(8,128)S(1)} %first_gram.1.block_ref), custom_call_target="tpu_custom_call" | custom-call | flops 1000000 | bytes 100000 | tf_op jit(solution)/shard_map/factor0/first_factor/pallas_call | solution.py:407
  92.9 0.5 collective-permute-start.25
  93.5 0.4 collective-permute-start.27
  95.6 4.8 %cross_parts.3 = (f32[64,128,128]{2,1,0:T(8,128)S(1)}, f32[4,256,128]{2,1,0:T(8,128)S(1)}, f32[4,256,128]{2,1,0:T(8,128)S(1)}) custom-call(s32[3,32]{1,0:T(4,128)S(1)} %get-tuple-element.81.names_ref, s32[11]{0:T(128)S(1)} %stack.56.order_ref, f32[128,128]{1,0:T(8,128)S(1)} %first_factor.1.after_ref.inverse_ref, ...), custom_call_target="tpu_custom_call" | custom-call | flops 1000000 | bytes 100000 | tf_op jit(solution)/shard_map/cross1/cross_parts/pallas_call | solution.py:305
  100.6 1.8 %collective-permute-done.28 = f32[4,256,128]{2,1,0:T(8,128)S(1)} collective-permute-done((f32[4,256,128]{2,1,0:T(8,128)S(1)}, f32[4,256,128]{2,1,0:T(8,128)S(1)}, u32[]{:S(2)}, u32[]{:S(2)}) %collective-permute-start.28) | collective-permute-done | bytes 524320 | tf_op jit(solution)/shard_map/cross_sum/ppermute | solution.py:478
  102.5 3.8 %collective-permute-start.31 = (f32[256,128]{1,0:T(8,128)S(1)}, f32[256,128]{1,0:T(8,128)S(1)}, u32[]{:S(2)}, u32[]{:S(2)}) collective-permute-start(f32[256,128]{1,0:T(8,128)S(1)} %get-tuple-element.78), channel_id=1, source_target_pairs={{0,24},{4,28},{8,0},{12,4},{16,8},{20,12},{24,16},{28,20},{1,25},{... | collective-permute-start | bytes 393224 | tf_op jit(solution)/shard_map/cross_sum/ppermute | solution.py:481
  106.3 3.5 %second_gram.1 = (f32[128,128]{1,0:T(8,128)S(1)}, f32[128,128]{1,0:T(8,128)S(1)}) custom-call(f32[4,256,128]{2,1,0:T(8,128)S(1)} %get-tuple-element.70.after_ref, f32[64,128,128]{2,1,0:T(8,128)S(1)} %get-tuple-element.64.panel.panel0, f32[64,128,128]{2,1,0:T(8,128)S(1)} %get-tuple-element.72.panel1), custom_call_target="tpu_custom_call" | custom-call | flops 1000000 | bytes 100000 | tf_op jit(solution)/shard_map/gram1/second_gram/pallas_call | solution.py:436
  109.8 6.9 %second_factor.1 = f32[256,256]{1,0:T(8,128)S(1)} custom-call(f32[4,256,128]{2,1,0:T(8,128)S(1)} %add.52.after_ref, f32[128,128]{1,0:T(8,128)S(1)} %get-tuple-element.73.side_ref, f32[128,128]{1,0:T(8,128)S(1)} %get-tuple-element.74.block_ref, f32[128,128]{1,0:T(8,128)S(1)} %first_factor.1.after_ref.inverse_ref), custom_call_target="tpu_custom_call" | custom-call | flops 1000000 | bytes 100000 | tf_op jit(solution)/shard_map/factor1/second_factor/pallas_call | solution.py:459
  116.7 1.5 %collective-permute-done.30 = f32[256,128]{1,0:T(8,128)S(1)} collective-permute-done((f32[256,128]{1,0:T(8,128)S(1)}, f32[256,128]{1,0:T(8,128)S(1)}, u32[]{:S(2)}, u32[]{:S(2)}) %collective-permute-start.30) | collective-permute-done | bytes 131104 | tf_op jit(solution)/shard_map/cross_sum/ppermute | solution.py:481
  118.6 9.3 %all_to_all.19 = f32[8,32,128]{2,1,0:T(8,128)S(1)} all-to-all(f32[8,32,128]{2,1,0:T(8,128)S(1)} %bitcast.39), channel_id=1, replica_groups=mesh['rows'=8,'cols'=4] {'rows'}, dimensions={0} | all-to-all | bytes 262144 | tf_op jit(solution)/shard_map/solve/all_to_all | solution.py:582
  127.9 0.7 copy_bitcast_fusion
  (70 shorter events, 3.5 us)
Async XLA Ops:
  0.8 1.0 copy-start
  1.8 12.1 %copy-start.3 = (s32[32]{0:T(128)S(1)}, s32[32]{0:T(128)}, u32[]{:S(2)}) copy-start(s32[32]{0:T(128)} %param.9) | copy-start | bytes 388
  1.8 12.2 %copy-start.2 = (s32[32,2]{0,1:T(2,128)S(1)}, s32[32,2]{0,1:T(2,128)}, u32[]{:S(2)}) copy-start(s32[32,2]{0,1:T(2,128)} %param.7) | copy-start | bytes 772
  1.8 12.2 %copy-start.1 = (f32[8,128,128]{2,1,0:T(8,128)S(1)}, f32[8,128,128]{2,1,0:T(8,128)}, u32[]{:S(2)}) copy-start(f32[8,128,128]{2,1,0:T(8,128)} %mixers_ref.9) | copy-start | bytes 1572868
  6.5 15.8 %collective-permute-start = (bf16[2,32,16,128]{3,2,1,0:T(8,128)(2,1)S(1)}, bf16[2,32,16,128]{3,2,1,0:T(8,128)(2,1)S(1)}, u32[]{:S(2)}, u32[]{:S(2)}) collective-permute-start(bf16[2,32,16,128]{3,2,1,0:T(8,128)(2,1)S(1)} %get-tuple-element.43), channel_id=1, source_target_pairs={{0,1},{4,5},{8,9},{12,13},{16,17},{20,21},{24,25},{28,29}} | collective-permute-start | bytes 786440 | tf_op jit(solution)/shard_map/panel_spread/ppermute | solution.py:508
  11.3 11.0 %collective-permute-start.1 = (bf16[2,32,16,128]{3,2,1,0:T(8,128)(2,1)S(1)}, bf16[2,32,16,128]{3,2,1,0:T(8,128)(2,1)S(1)}, u32[]{:S(2)}, u32[]{:S(2)}) collective-permute-start(bf16[2,32,16,128]{3,2,1,0:T(8,128)(2,1)S(1)} %get-tuple-element.44), channel_id=1, source_target_pairs={{0,2},{4,6},{8,10},{12,14},{16,18},{20,22},{24,26},{28,30}} | collective-permute-start | bytes 786440 | tf_op jit(solution)/shard_map/panel_spread/ppermute | solution.py:508
  12.6 9.8 %collective-permute-start.2 = (bf16[2,32,16,128]{3,2,1,0:T(8,128)(2,1)S(1)}, bf16[2,32,16,128]{3,2,1,0:T(8,128)(2,1)S(1)}, u32[]{:S(2)}, u32[]{:S(2)}) collective-permute-start(bf16[2,32,16,128]{3,2,1,0:T(8,128)(2,1)S(1)} %get-tuple-element.45), channel_id=1, source_target_pairs={{0,3},{4,7},{8,11},{12,15},{16,19},{20,23},{24,27},{28,31}} | collective-permute-start | bytes 786440 | tf_op jit(solution)/shard_map/panel_spread/ppermute | solution.py:508
  23.1 1.4 %collective-permute-start.3 = (bf16[33,16,128]{2,1,0:T(8,128)(2,1)S(1)}, bf16[33,16,128]{2,1,0:T(8,128)(2,1)S(1)}, u32[]{:S(2)}, u32[]{:S(2)}) collective-permute-start(bf16[33,16,128]{2,1,0:T(8,128)(2,1)S(1)} %get-tuple-element.47), channel_id=1, source_target_pairs={{0,4},{4,0},{8,12},{12,8},{16,20},{20,16},{24,28},{28,24},{1,5},{5... | collective-permute-start | bytes 405512 | tf_op jit(solution)/shard_map/panel_spread/ppermute | solution.py:478
  24.5 15.4 %collective-permute-start.4 = (bf16[66,16,128]{2,1,0:T(8,128)(2,1)S(1)}, bf16[66,16,128]{2,1,0:T(8,128)(2,1)S(1)}, u32[]{:S(2)}, u32[]{:S(2)}) collective-permute-start(bf16[66,16,128]{2,1,0:T(8,128)(2,1)S(1)} %constant_dynamic-update-slice_fusion.refs_0_), channel_id=1, source_target_pairs={{0,16},{4,20},{8,24},{12,28},{16,0},{20,4},{24,8},{28,12},{1,17},{... | collective-permute-start | bytes 811016 | tf_op jit(solution)/shard_map/panel_rows/ppermute | solution.py:484
  27.2 13.4 %collective-permute-start.5 = (bf16[2,32,16,128]{3,2,1,0:T(8,128)(2,1)S(1)}, bf16[2,32,16,128]{3,2,1,0:T(8,128)(2,1)S(1)}, u32[]{:S(2)}, u32[]{:S(2)}) collective-permute-start(bf16[2,32,16,128]{3,2,1,0:T(8,128)(2,1)S(1)} %get-tuple-element.49), channel_id=1, source_target_pairs={{0,1},{4,5},{8,9},{12,13},{16,17},{20,21},{24,25},{28,29}} | collective-permute-start | bytes 786440 | tf_op jit(solution)/shard_map/panel_spread/ppermute | solution.py:508
  28.5 12.1 %collective-permute-start.6 = (bf16[2,32,16,128]{3,2,1,0:T(8,128)(2,1)S(1)}, bf16[2,32,16,128]{3,2,1,0:T(8,128)(2,1)S(1)}, u32[]{:S(2)}, u32[]{:S(2)}) collective-permute-start(bf16[2,32,16,128]{3,2,1,0:T(8,128)(2,1)S(1)} %get-tuple-element.50), channel_id=1, source_target_pairs={{0,2},{4,6},{8,10},{12,14},{16,18},{20,22},{24,26},{28,30}} | collective-permute-start | bytes 786440 | tf_op jit(solution)/shard_map/panel_spread/ppermute | solution.py:508
  29.8 10.8 %collective-permute-start.7 = (bf16[2,32,16,128]{3,2,1,0:T(8,128)(2,1)S(1)}, bf16[2,32,16,128]{3,2,1,0:T(8,128)(2,1)S(1)}, u32[]{:S(2)}, u32[]{:S(2)}) collective-permute-start(bf16[2,32,16,128]{3,2,1,0:T(8,128)(2,1)S(1)} %get-tuple-element.51), channel_id=1, source_target_pairs={{0,3},{4,7},{8,11},{12,15},{16,19},{20,23},{24,27},{28,31}} | collective-permute-start | bytes 786440 | tf_op jit(solution)/shard_map/panel_spread/ppermute | solution.py:508
  33.8 20.8 %collective-permute-start.9 = (bf16[66,16,128]{2,1,0:T(8,128)(2,1)S(1)}, bf16[66,16,128]{2,1,0:T(8,128)(2,1)S(1)}, u32[]{:S(2)}, u32[]{:S(2)}) collective-permute-start(bf16[66,16,128]{2,1,0:T(8,128)(2,1)S(1)} %constant_dynamic-update-slice_fusion.refs_0_), channel_id=1, source_target_pairs={{0,8},{4,12},{8,0},{12,4},{16,24},{20,28},{24,16},{28,20},{1,9},{5... | collective-permute-start | bytes 811016 | tf_op jit(solution)/shard_map/panel_rows/ppermute | solution.py:484
  39.9 17.2 %collective-permute-start.10 = (bf16[66,16,128]{2,1,0:T(8,128)(2,1)S(1)}, bf16[66,16,128]{2,1,0:T(8,128)(2,1)S(1)}, u32[]{:S(2)}, u32[]{:S(2)}) collective-permute-start(bf16[66,16,128]{2,1,0:T(8,128)(2,1)S(1)} %collective-permute-done.4.after_ref.refs_1_), channel_id=1, source_target_pairs={{0,8},{4,12},{8,0},{12,4},{16,24},{20,28},{24,16},{28,20},{1,9},{5... | collective-permute-start | bytes 811016 | tf_op jit(solution)/shard_map/panel_rows/ppermute | solution.py:484
  41.3 1.4 %collective-permute-start.8 = (bf16[32,16,128]{2,1,0:T(8,128)(2,1)S(1)}, bf16[32,16,128]{2,1,0:T(8,128)(2,1)S(1)}, u32[]{:S(2)}, u32[]{:S(2)}) collective-permute-start(bf16[32,16,128]{2,1,0:T(8,128)(2,1)S(1)} %get-tuple-element.53), channel_id=1, source_target_pairs={{0,4},{4,0},{8,12},{12,8},{16,20},{20,16},{24,28},{28,24},{1,5},{5... | collective-permute-start | bytes 393224 | tf_op jit(solution)/shard_map/panel_spread/ppermute | solution.py:478
  42.7 22.5 %collective-permute-start.12 = (bf16[64,16,128]{2,1,0:T(8,128)(2,1)S(1)}, bf16[64,16,128]{2,1,0:T(8,128)(2,1)S(1)}, u32[]{:S(2)}, u32[]{:S(2)}) collective-permute-start(bf16[64,16,128]{2,1,0:T(8,128)(2,1)S(1)} %constant_dynamic-update-slice_fusion.2.after_ref.refs_0_), channel_id=1, source_target_pairs={{0,8},{4,12},{8,0},{12,4},{16,24},{20,28},{24,16},{28,20},{1,9},{5... | collective-permute-start | bytes 786440 | tf_op jit(solution)/shard_map/panel_rows/ppermute | solution.py:484
  44.2 18.7 %collective-permute-start.11 = (bf16[64,16,128]{2,1,0:T(8,128)(2,1)S(1)}, bf16[64,16,128]{2,1,0:T(8,128)(2,1)S(1)}, u32[]{:S(2)}, u32[]{:S(2)}) collective-permute-start(bf16[64,16,128]{2,1,0:T(8,128)(2,1)S(1)} %constant_dynamic-update-slice_fusion.2.after_ref.refs_0_), channel_id=1, source_target_pairs={{0,16},{4,20},{8,24},{12,28},{16,0},{20,4},{24,8},{28,12},{1,17},{... | collective-permute-start | bytes 786440 | tf_op jit(solution)/shard_map/panel_rows/ppermute | solution.py:484
  60.7 8.4 %collective-permute-start.15 = (f16[64,16,128]{2,1,0:T(8,128)(2,1)S(1)}, f16[64,16,128]{2,1,0:T(8,128)(2,1)S(1)}, u32[]{:S(2)}, u32[]{:S(2)}) collective-permute-start(f16[64,16,128]{2,1,0:T(8,128)(2,1)S(1)} %get-tuple-element.76), channel_id=1, source_target_pairs={{0,2},{1,3},{2,0},{3,1},{4,6},{5,7},{6,4},{7,5},{8,10},{9,11},{10,... | collective-permute-start | bytes 786440 | tf_op jit(solution)/shard_map/panel_cols/ppermute | solution.py:487
  60.8 9.2 %collective-permute-start.14 = (f16[64,16,128]{2,1,0:T(8,128)(2,1)S(1)}, f16[64,16,128]{2,1,0:T(8,128)(2,1)S(1)}, u32[]{:S(2)}, u32[]{:S(2)}) collective-permute-start(f16[64,16,128]{2,1,0:T(8,128)(2,1)S(1)} %get-tuple-element.76), channel_id=1, source_target_pairs={{0,1},{1,0},{2,3},{3,2},{4,5},{5,4},{6,7},{7,6},{8,9},{9,8},{10,11... | collective-permute-start | bytes 786440 | tf_op jit(solution)/shard_map/panel_cols/ppermute | solution.py:487
  62.9 7.2 %collective-permute-start.13 = (bf16[64,16,128]{2,1,0:T(8,128)(2,1)S(1)}, bf16[64,16,128]{2,1,0:T(8,128)(2,1)S(1)}, u32[]{:S(2)}, u32[]{:S(2)}) collective-permute-start(bf16[64,16,128]{2,1,0:T(8,128)(2,1)S(1)} %collective-permute-done.11.refs_1_), channel_id=1, source_target_pairs={{0,8},{4,12},{8,0},{12,4},{16,24},{20,28},{24,16},{28,20},{1,9},{5... | collective-permute-start | bytes 786440 | tf_op jit(solution)/shard_map/panel_rows/ppermute | solution.py:484
  64.2 11.5 %collective-permute-start.16 = (f16[64,16,128]{2,1,0:T(8,128)(2,1)S(1)}, f16[64,16,128]{2,1,0:T(8,128)(2,1)S(1)}, u32[]{:S(2)}, u32[]{:S(2)}) collective-permute-start(f16[64,16,128]{2,1,0:T(8,128)(2,1)S(1)} %get-tuple-element.76), channel_id=1, source_target_pairs={{0,3},{1,2},{2,1},{3,0},{4,7},{5,6},{6,5},{7,4},{8,11},{9,10},{10,... | collective-permute-start | bytes 786440 | tf_op jit(solution)/shard_map/panel_cols/ppermute | solution.py:487
  65.2 11.5 %collective-permute-start.17 = (f16[64,16,128]{2,1,0:T(8,128)(2,1)S(1)}, f16[64,16,128]{2,1,0:T(8,128)(2,1)S(1)}, u32[]{:S(2)}, u32[]{:S(2)}) collective-permute-start(f16[64,16,128]{2,1,0:T(8,128)(2,1)S(1)} %get-tuple-element.76), channel_id=1, source_target_pairs={{0,4},{4,0},{8,12},{12,8},{16,20},{20,16},{24,28},{28,24},{1,5},{5... | collective-permute-start | bytes 786440 | tf_op jit(solution)/shard_map/panel_cores/ppermute | solution.py:478
  69.1 8.7 %collective-permute-start.19 = (f16[64,16,128]{2,1,0:T(8,128)(2,1)S(1)}, f16[64,16,128]{2,1,0:T(8,128)(2,1)S(1)}, u32[]{:S(2)}, u32[]{:S(2)}) collective-permute-start(f16[64,16,128]{2,1,0:T(8,128)(2,1)S(1)} %collective-permute-done.15), channel_id=1, source_target_pairs={{0,4},{4,0},{8,12},{12,8},{16,20},{20,16},{24,28},{28,24},{1,5},{5... | collective-permute-start | bytes 786440 | tf_op jit(solution)/shard_map/panel_cores/ppermute | solution.py:478
  70.1 9.5 %collective-permute-start.18 = (f16[64,16,128]{2,1,0:T(8,128)(2,1)S(1)}, f16[64,16,128]{2,1,0:T(8,128)(2,1)S(1)}, u32[]{:S(2)}, u32[]{:S(2)}) collective-permute-start(f16[64,16,128]{2,1,0:T(8,128)(2,1)S(1)} %collective-permute-done.14), channel_id=1, source_target_pairs={{0,4},{4,0},{8,12},{12,8},{16,20},{20,16},{24,28},{28,24},{1,5},{5... | collective-permute-start | bytes 786440 | tf_op jit(solution)/shard_map/panel_cores/ppermute | solution.py:478
  75.7 3.9 %collective-permute-start.20 = (f16[64,16,128]{2,1,0:T(8,128)(2,1)S(1)}, f16[64,16,128]{2,1,0:T(8,128)(2,1)S(1)}, u32[]{:S(2)}, u32[]{:S(2)}) collective-permute-start(f16[64,16,128]{2,1,0:T(8,128)(2,1)S(1)} %collective-permute-done.16), channel_id=1, source_target_pairs={{0,4},{4,0},{8,12},{12,8},{16,20},{20,16},{24,28},{28,24},{1,5},{5... | collective-permute-start | bytes 786440 | tf_op jit(solution)/shard_map/panel_cores/ppermute | solution.py:478
  75.8 17.0 %collective-permute-start.23 = (f16[64,16,128]{2,1,0:T(8,128)(2,1)S(1)}, f16[64,16,128]{2,1,0:T(8,128)(2,1)S(1)}, u32[]{:S(2)}, u32[]{:S(2)}) collective-permute-start(f16[64,16,128]{2,1,0:T(8,128)(2,1)S(1)} %convert_element_type.69), channel_id=1, source_target_pairs={{0,3},{1,2},{2,1},{3,0},{4,7},{5,6},{6,5},{7,4},{8,11},{9,10},{10,... | collective-permute-start | bytes 786440 | tf_op jit(solution)/shard_map/panel_cols/ppermute | solution.py:487
  76.7 16.2 %collective-permute-start.22 = (f16[64,16,128]{2,1,0:T(8,128)(2,1)S(1)}, f16[64,16,128]{2,1,0:T(8,128)(2,1)S(1)}, u32[]{:S(2)}, u32[]{:S(2)}) collective-permute-start(f16[64,16,128]{2,1,0:T(8,128)(2,1)S(1)} %convert_element_type.69), channel_id=1, source_target_pairs={{0,2},{1,3},{2,0},{3,1},{4,6},{5,7},{6,4},{7,5},{8,10},{9,11},{10,... | collective-permute-start | bytes 786440 | tf_op jit(solution)/shard_map/panel_cols/ppermute | solution.py:487
  77.8 15.0 %collective-permute-start.21 = (f16[64,16,128]{2,1,0:T(8,128)(2,1)S(1)}, f16[64,16,128]{2,1,0:T(8,128)(2,1)S(1)}, u32[]{:S(2)}, u32[]{:S(2)}) collective-permute-start(f16[64,16,128]{2,1,0:T(8,128)(2,1)S(1)} %convert_element_type.69), channel_id=1, source_target_pairs={{0,1},{1,0},{2,3},{3,2},{4,5},{5,4},{6,7},{7,6},{8,9},{9,8},{10,11... | collective-permute-start | bytes 786440 | tf_op jit(solution)/shard_map/panel_cols/ppermute | solution.py:487
  92.8 1.6 %collective-permute-start.24 = (f16[64,16,128]{2,1,0:T(8,128)(2,1)S(1)}, f16[64,16,128]{2,1,0:T(8,128)(2,1)S(1)}, u32[]{:S(2)}, u32[]{:S(2)}) collective-permute-start(f16[64,16,128]{2,1,0:T(8,128)(2,1)S(1)} %convert_element_type.69), channel_id=1, source_target_pairs={{0,4},{4,0},{8,12},{12,8},{16,20},{20,16},{24,28},{28,24},{1,5},{5... | collective-permute-start | bytes 786440 | tf_op jit(solution)/shard_map/panel_cores/ppermute | solution.py:478
  92.9 1.9 %collective-permute-start.25 = (f16[64,16,128]{2,1,0:T(8,128)(2,1)S(1)}, f16[64,16,128]{2,1,0:T(8,128)(2,1)S(1)}, u32[]{:S(2)}, u32[]{:S(2)}) collective-permute-start(f16[64,16,128]{2,1,0:T(8,128)(2,1)S(1)} %collective-permute-done.21), channel_id=1, source_target_pairs={{0,4},{4,0},{8,12},{12,8},{16,20},{20,16},{24,28},{28,24},{1,5},{5... | collective-permute-start | bytes 786440 | tf_op jit(solution)/shard_map/panel_cores/ppermute | solution.py:478
  93.4 1.8 %collective-permute-start.26 = (f16[64,16,128]{2,1,0:T(8,128)(2,1)S(1)}, f16[64,16,128]{2,1,0:T(8,128)(2,1)S(1)}, u32[]{:S(2)}, u32[]{:S(2)}) collective-permute-start(f16[64,16,128]{2,1,0:T(8,128)(2,1)S(1)} %collective-permute-done.22), channel_id=1, source_target_pairs={{0,4},{4,0},{8,12},{12,8},{16,20},{20,16},{24,28},{28,24},{1,5},{5... | collective-permute-start | bytes 786440 | tf_op jit(solution)/shard_map/panel_cores/ppermute | solution.py:478
  93.5 2.1 %collective-permute-start.27 = (f16[64,16,128]{2,1,0:T(8,128)(2,1)S(1)}, f16[64,16,128]{2,1,0:T(8,128)(2,1)S(1)}, u32[]{:S(2)}, u32[]{:S(2)}) collective-permute-start(f16[64,16,128]{2,1,0:T(8,128)(2,1)S(1)} %collective-permute-done.23), channel_id=1, source_target_pairs={{0,4},{4,0},{8,12},{12,8},{16,20},{20,16},{24,28},{28,24},{1,5},{5... | collective-permute-start | bytes 786440 | tf_op jit(solution)/shard_map/panel_cores/ppermute | solution.py:478
  100.4 2.0 %collective-permute-start.28 = (f32[4,256,128]{2,1,0:T(8,128)S(1)}, f32[4,256,128]{2,1,0:T(8,128)S(1)}, u32[]{:S(2)}, u32[]{:S(2)}) collective-permute-start(f32[4,256,128]{2,1,0:T(8,128)S(1)} %get-tuple-element.71), channel_id=1, source_target_pairs={{0,4},{4,0},{8,12},{12,8},{16,20},{20,16},{24,28},{28,24},{1,5},{5... | collective-permute-start | bytes 1572872 | tf_op jit(solution)/shard_map/cross_sum/ppermute | solution.py:478
  102.5 14.2 %collective-permute-start.29 = (f32[256,128]{1,0:T(8,128)S(1)}, f32[256,128]{1,0:T(8,128)S(1)}, u32[]{:S(2)}, u32[]{:S(2)}) collective-permute-start(f32[256,128]{1,0:T(8,128)S(1)} %get-tuple-element.77), channel_id=1, source_target_pairs={{0,8},{4,12},{8,16},{12,20},{16,24},{20,28},{24,0},{28,4},{1,9},{5... | collective-permute-start | bytes 393224 | tf_op jit(solution)/shard_map/cross_sum/ppermute | solution.py:481
  102.5 14.2 %collective-permute-start.31 = (f32[256,128]{1,0:T(8,128)S(1)}, f32[256,128]{1,0:T(8,128)S(1)}, u32[]{:S(2)}, u32[]{:S(2)}) collective-permute-start(f32[256,128]{1,0:T(8,128)S(1)} %get-tuple-element.78), channel_id=1, source_target_pairs={{0,24},{4,28},{8,0},{12,4},{16,8},{20,12},{24,16},{28,20},{1,25},{... | collective-permute-start | bytes 393224 | tf_op jit(solution)/shard_map/cross_sum/ppermute | solution.py:481
  106.3 11.8 %collective-permute-start.30 = (f32[256,128]{1,0:T(8,128)S(1)}, f32[256,128]{1,0:T(8,128)S(1)}, u32[]{:S(2)}, u32[]{:S(2)}) collective-permute-start(f32[256,128]{1,0:T(8,128)S(1)} %get-tuple-element.79), channel_id=1, source_target_pairs={{0,16},{4,20},{8,24},{12,28},{16,0},{20,4},{24,8},{28,12},{1,17},{... | collective-permute-start | bytes 393224 | tf_op jit(solution)/shard_map/cross_sum/ppermute | solution.py:481

commit v7 on v6

--- a/solution.py
+++ b/solution.py
@@ -63,7 +63,7 @@
     return wide[:TILE] + (wide[TILE:] + low)
 
 
-def panel_kernel(per_step, names_ref, order_ref, matrix_ref, mixers_ref, *refs):
+def panel_kernel(per_step, names_ref, order_ref, matrix_ref, mixers_ref, after_ref, *refs):
     outs, turned = refs[:-1], refs[-1]
     first = pl.program_id(0) * per_step
     core = order_ref[2 * SLICES + 1]
@@ -71,15 +71,14 @@
         mixer = signed_mixer(mixers_ref, names_ref, first + u)
         block = matrix_ref[u * TILE : (u + 1) * TILE, :]
         turned[u] = product(mixer, block).T
-        for h in range(CHUNKS):
-            for c in range(SLICES):
-                for s in range(2):
-                    who = core if s == 0 else 1 - core
-                    start = pl.multiple_of(h * HALF + who * (HALF // 2) + c * WIDTH, WIDTH)
-                    outs[h * SLICES + c][s, u] = turned[u, pl.ds(start, WIDTH), :].astype(BF16)
-
-
-def mix_panel(matrix, mixers, names, order):
+        for c in range(SLICES):
+            for s in range(2):
+                who = core if s == 0 else 1 - core
+                start = pl.multiple_of(who * (HALF // 2) + c * WIDTH, WIDTH)
+                outs[c][s, u] = turned[u, pl.ds(start, WIDTH), :].astype(BF16)
+
+
+def mix_panel(matrix, mixers, names, order, after, chunk):
     tiles = names.shape[1]
     per_step = 16
     spec = pl.BlockSpec((2, per_step, WIDTH, TILE), lambda i, *_: (0, i, 0, 0))
@@ -89,17 +88,18 @@
             num_scalar_prefetch=2,
             grid=(tiles // per_step,),
             in_specs=[
-                pl.BlockSpec((per_step * TILE, P_SIZE), lambda i, *_: (i, 0)),
+                pl.BlockSpec((per_step * TILE, HALF), lambda i, *_: (i, chunk)),
                 pl.BlockSpec(mixers.shape, lambda i, *_: (0, 0, 0)),
+                anywhere(),
             ],
-            out_specs=[spec] * (CHUNKS * SLICES),
-            scratch_shapes=[pltpu.VMEM((per_step, P_SIZE, TILE), F32)],
+            out_specs=[spec] * SLICES,
+            scratch_shapes=[pltpu.VMEM((per_step, HALF, TILE), F32)],
         ),
-        out_shape=[jax.ShapeDtypeStruct((2, tiles, WIDTH, TILE), BF16)] * (CHUNKS * SLICES),
+        out_shape=[jax.ShapeDtypeStruct((2, tiles, WIDTH, TILE), BF16)] * SLICES,
         compiler_params=params(49),
         cost_estimate=LIGHT,
         name="mix_panel",
-    )(names, order, matrix, mixers)
+    )(names, order, matrix, mixers, after)
 
 
 def mix_kernel(per_step, start, names_ref, matrix_ref, mixers_ref, after_ref, out_ref, token_ref):
@@ -495,7 +495,8 @@
         order = [who * SLICES + c for who in (core, 1 - core) for c in place]
         order = jnp.stack([jnp.asarray(v, jnp.int32) for v in order + [chip, core, part]])
     with jax.named_scope("panel_mix"):
-        tiles = mix_panel(matrix, mixers, kinds, order)
+        tiles = mix_panel(matrix, mixers, kinds, order, order, 0)
+        tiles = tiles + mix_panel(matrix, mixers, kinds, order, tiles[0], 1)
     with jax.named_scope("names"):
         carried = jnp.pad(names.astype(BF16), ((0, WIDTH - 3), (0, TILE - names.shape[1])))
 

time: 129 us -> 128 us (level)
  Pallas kernels: 57.8 us -> 59.7 us
  starting transfers between devices: 35.9 us -> 34 us
    ppermute x6, waiting for transfers between devices: 6.95 us -> 3.83 us  [beside(): return lax.ppermute(value, 'rows', [(i, i ^ 2 * j) for i in range(rows_n)])]
    ppermute x6, starting transfers between devices: 9.82 us -> 6.96 us  [beside(): return lax.ppermute(value, 'rows', [(i, i ^ 2 * j) for i in range(rows_n)])]
    ppermute x6, waiting for transfers between devices: 0.18 us -> 2.85 us  [scatter(): lax.ppermute(slices[j], 'cols', [(0, j)])]
    pallas_call x1 -> x2, Pallas kernels: 4.63 us -> 6.53 us  [mix_panel(): pl.pallas_call(functools.partial(panel_kernel, per_step), grid_spec=pltpu...]
  transfers between devices with their start and end apart: 32 -> 32, of which waited for: 14 -> 16; matrix products, arithmetic and copies ran while one was open for 1% -> 1% of each run, Pallas kernels for 37% -> 40%
where the time goes in v7:
time: 128 us; the launch traced here: 127 us
  Pallas kernels  59.7 us (47%)
  starting transfers between devices  34 us (27%)
  waiting for transfers between devices  20.4 us (16%)
  blocking collectives  9.17 us (7%)
  local copies, waits for them, and re-layouts  1.9 us (1%)
  other arithmetic  1.41 us (1%)
    pallas_call x4, Pallas kernels, mix_tiles(): pl.pallas_call(functools.partial(mix_kernel, per_step, start), grid_spec=...  16.5 us
    ppermute x6, starting transfers between devices, scatter(): lax.ppermute(slices[j], 'cols', [(0, j)])  14.1 us
    pallas_call x2, Pallas kernels, cross_parts(): pl.pallas_call(functools.partial(cross_kernel, steps, chips, len(before),...  9.29 us
    all_to_all x1, blocking collectives, local(): lax.all_to_all(solved, 'rows', split_axis=0, concat_axis=1, tiled=True)  9.17 us
    ppermute x6, starting transfers between devices, across(): return lax.ppermute(value, 'cols', [(i, i ^ j) for i in range(parts)])  7.22 us
    ppermute x6, starting transfers between devices, beside(): return lax.ppermute(value, 'rows', [(i, i ^ 2 * j) for i in range(rows_n)])  6.96 us
    pallas_call x1, Pallas kernels, second_factor(): pl.pallas_call(last_kernel, in_specs=[anywhere()] + [vmem()] * 3, out_spe...  6.85 us
    ppermute x6, waiting for transfers between devices, across(): return lax.ppermute(value, 'cols', [(i, i ^ j) for i in range(parts)])  6.66 us
  transfers between devices with their start and end apart: 32, of which 16 were waited for; matrix products, arithmetic and copies ran while one was open for 1% of the time, Pallas kernels for 40%

profile of v7, /device:TPU:0, one launch (start us, length us, event | category | flops | bytes accessed | tf_op | source)
XLA Modules:
  0.0 127.5 jit_solution(5215674346311493296)
XLA Ops:
  0.0 0.7 pad_add_fusion.1.names_ref
  0.8 1.0 copy-done
  1.8 3.3 %mix_panel.2 = (bf16[2,32,16,128]{3,2,1,0:T(8,128)(2,1)S(1)}, bf16[2,32,16,128]{3,2,1,0:T(8,128)(2,1)S(1)}, bf16[2,32,16,128]{3,2,1,0:T(8,128)(2,1)S(1)}, bf16[2,32,16,128]{3,2,1,0:T(8,128)(2,1)S(1)}) custom-call(s32[2,32]{1,0:T(2,128)S(1)} %pad_add_fusion.1.names_ref, s32[11]{0:T(128)S(1)} %stack.56.order_ref.after_ref, f32[4096,1024]{1,0:T(8,128)} %matrix_ref.11, ...), custom_call_target="tpu_custom_call" | custom-call | flops 1000000 | bytes 100000 | tf_op jit(solution)/shard_map/panel_mix/mix_panel/pallas_call | solution.py:85
  5.1 4.9 %collective-permute-start = (bf16[2,32,16,128]{3,2,1,0:T(8,128)(2,1)S(1)}, bf16[2,32,16,128]{3,2,1,0:T(8,128)(2,1)S(1)}, u32[]{:S(2)}, u32[]{:S(2)}) collective-permute-start(bf16[2,32,16,128]{3,2,1,0:T(8,128)(2,1)S(1)} %get-tuple-element.43), channel_id=1, source_target_pairs={{0,1},{4,5},{8,9},{12,13},{16,17},{20,21},{24,25},{28,29}} | collective-permute-start | bytes 786440 | tf_op jit(solution)/shard_map/panel_spread/ppermute | solution.py:509
  10.0 1.3 %collective-permute-start.1 = (bf16[2,32,16,128]{3,2,1,0:T(8,128)(2,1)S(1)}, bf16[2,32,16,128]{3,2,1,0:T(8,128)(2,1)S(1)}, u32[]{:S(2)}, u32[]{:S(2)}) collective-permute-start(bf16[2,32,16,128]{3,2,1,0:T(8,128)(2,1)S(1)} %get-tuple-element.44), channel_id=1, source_target_pairs={{0,2},{4,6},{8,10},{12,14},{16,18},{20,22},{24,26},{28,30}} | collective-permute-start | bytes 786440 | tf_op jit(solution)/shard_map/panel_spread/ppermute | solution.py:509
  11.3 1.3 %collective-permute-start.2 = (bf16[2,32,16,128]{3,2,1,0:T(8,128)(2,1)S(1)}, bf16[2,32,16,128]{3,2,1,0:T(8,128)(2,1)S(1)}, u32[]{:S(2)}, u32[]{:S(2)}) collective-permute-start(bf16[2,32,16,128]{3,2,1,0:T(8,128)(2,1)S(1)} %get-tuple-element.45), channel_id=1, source_target_pairs={{0,3},{4,7},{8,11},{12,15},{16,19},{20,23},{24,27},{28,31}} | collective-permute-start | bytes 786440 | tf_op jit(solution)/shard_map/panel_spread/ppermute | solution.py:509
  12.7 4.1 %mix_tiles.4 = (bf16[1024,1024]{1,0:T(8,128)(2,1)S(1)}, f32[8,128]{1,0:T(8,128)S(1)}) custom-call(s32[2,32]{1,0:T(2,128)S(1)} %pad_add_fusion.1.names_ref, f32[4096,1024]{1,0:T(8,128)} %matrix_ref.11, f32[8,128,128]{2,1,0:T(8,128)S(1)} %copy-done.1, bf16[2,32,16,128]{3,2,1,0:T(8,128)(2,1)S(1)} %get-tuple-element.40.after_ref.refs_1_), custom_call_target="tpu_custom_call" | custom-call | flops 1000000 | bytes 100000 | tf_op jit(solution)/shard_map/mix/mix_tiles/pallas_call | solution.py:117
  16.8 4.1 %mix_tiles.5 = (bf16[1024,1024]{1,0:T(8,128)(2,1)S(1)}, f32[8,128]{1,0:T(8,128)S(1)}) custom-call(s32[2,32]{1,0:T(2,128)S(1)} %pad_add_fusion.1.names_ref, f32[4096,1024]{1,0:T(8,128)} %matrix_ref.11, f32[8,128,128]{2,1,0:T(8,128)S(1)} %copy-done.1, f32[8,128]{1,0:T(8,128)S(1)} %get-tuple-element.41.after_ref), custom_call_target="tpu_custom_call" | custom-call | flops 1000000 | bytes 100000 | tf_op jit(solution)/shard_map/mix/mix_tiles/pallas_call | solution.py:117
  21.1 0.6 pick.2
  21.8 1.3 %collective-permute-done.3 = bf16[33,16,128]{2,1,0:T(8,128)(2,1)S(1)} collective-permute-done((bf16[33,16,128]{2,1,0:T(8,128)(2,1)S(1)}, bf16[33,16,128]{2,1,0:T(8,128)(2,1)S(1)}, u32[]{:S(2)}, u32[]{:S(2)}) %collective-permute-start.3) | collective-permute-done | bytes 135200 | tf_op jit(solution)/shard_map/panel_spread/ppermute | solution.py:478
  23.1 2.7 %collective-permute-start.4 = (bf16[66,16,128]{2,1,0:T(8,128)(2,1)S(1)}, bf16[66,16,128]{2,1,0:T(8,128)(2,1)S(1)}, u32[]{:S(2)}, u32[]{:S(2)}) collective-permute-start(bf16[66,16,128]{2,1,0:T(8,128)(2,1)S(1)} %constant_dynamic-update-slice_fusion.refs_0_), channel_id=1, source_target_pairs={{0,16},{4,20},{8,24},{12,28},{16,0},{20,4},{24,8},{28,12},{1,17},{... | collective-permute-start | bytes 811016 | tf_op jit(solution)/shard_map/panel_rows/ppermute | solution.py:484
  25.8 3.3 %mix_panel.3 = (bf16[2,32,16,128]{3,2,1,0:T(8,128)(2,1)S(1)}, bf16[2,32,16,128]{3,2,1,0:T(8,128)(2,1)S(1)}, bf16[2,32,16,128]{3,2,1,0:T(8,128)(2,1)S(1)}, bf16[2,32,16,128]{3,2,1,0:T(8,128)(2,1)S(1)}) custom-call(s32[2,32]{1,0:T(2,128)S(1)} %pad_add_fusion.1.names_ref, s32[11]{0:T(128)S(1)} %stack.56.order_ref.after_ref, f32[4096,1024]{1,0:T(8,128)} %matrix_ref.11, ...), custom_call_target="tpu_custom_call" | custom-call | flops 1000000 | bytes 100000 | tf_op jit(solution)/shard_map/panel_mix/mix_panel/pallas_call | solution.py:85
  29.1 1.3 %collective-permute-start.5 = (bf16[2,32,16,128]{3,2,1,0:T(8,128)(2,1)S(1)}, bf16[2,32,16,128]{3,2,1,0:T(8,128)(2,1)S(1)}, u32[]{:S(2)}, u32[]{:S(2)}) collective-permute-start(bf16[2,32,16,128]{3,2,1,0:T(8,128)(2,1)S(1)} %get-tuple-element.49), channel_id=1, source_target_pairs={{0,1},{4,5},{8,9},{12,13},{16,17},{20,21},{24,25},{28,29}} | collective-permute-start | bytes 786440 | tf_op jit(solution)/shard_map/panel_spread/ppermute | solution.py:509
  30.4 1.3 %collective-permute-start.6 = (bf16[2,32,16,128]{3,2,1,0:T(8,128)(2,1)S(1)}, bf16[2,32,16,128]{3,2,1,0:T(8,128)(2,1)S(1)}, u32[]{:S(2)}, u32[]{:S(2)}) collective-permute-start(bf16[2,32,16,128]{3,2,1,0:T(8,128)(2,1)S(1)} %get-tuple-element.50), channel_id=1, source_target_pairs={{0,2},{4,6},{8,10},{12,14},{16,18},{20,22},{24,26},{28,30}} | collective-permute-start | bytes 786440 | tf_op jit(solution)/shard_map/panel_spread/ppermute | solution.py:509
  31.7 4.0 %collective-permute-start.7 = (bf16[2,32,16,128]{3,2,1,0:T(8,128)(2,1)S(1)}, bf16[2,32,16,128]{3,2,1,0:T(8,128)(2,1)S(1)}, u32[]{:S(2)}, u32[]{:S(2)}) collective-permute-start(bf16[2,32,16,128]{3,2,1,0:T(8,128)(2,1)S(1)} %get-tuple-element.51), channel_id=1, source_target_pairs={{0,3},{4,7},{8,11},{12,15},{16,19},{20,23},{24,27},{28,31}} | collective-permute-start | bytes 786440 | tf_op jit(solution)/shard_map/panel_spread/ppermute | solution.py:509
  35.7 1.6 %collective-permute-start.9 = (bf16[66,16,128]{2,1,0:T(8,128)(2,1)S(1)}, bf16[66,16,128]{2,1,0:T(8,128)(2,1)S(1)}, u32[]{:S(2)}, u32[]{:S(2)}) collective-permute-start(bf16[66,16,128]{2,1,0:T(8,128)(2,1)S(1)} %constant_dynamic-update-slice_fusion.refs_0_), channel_id=1, source_target_pairs={{0,8},{4,12},{8,0},{12,4},{16,24},{20,28},{24,16},{28,20},{1,9},{5... | collective-permute-start | bytes 811016 | tf_op jit(solution)/shard_map/panel_rows/ppermute | solution.py:484
  37.4 1.1 collective-permute-done.4.after_ref.refs_1_
  38.5 0.7 collective-permute-start.10
  39.2 2.7 %collective-permute-done.7.refs_3_ = bf16[2,32,16,128]{3,2,1,0:T(8,128)(2,1)S(1)} collective-permute-done((bf16[2,32,16,128]{3,2,1,0:T(8,128)(2,1)S(1)}, bf16[2,32,16,128]{3,2,1,0:T(8,128)(2,1)S(1)}, u32[]{:S(2)}, u32[]{:S(2)}) %collective-permute-start.7) | collective-permute-done | bytes 262176 | tf_op jit(solution)/shard_map/panel_spread/ppermute | solution.py:509
  41.8 0.8 pick.3
  42.7 1.3 %collective-permute-done.8 = bf16[32,16,128]{2,1,0:T(8,128)(2,1)S(1)} collective-permute-done((bf16[32,16,128]{2,1,0:T(8,128)(2,1)S(1)}, bf16[32,16,128]{2,1,0:T(8,128)(2,1)S(1)}, u32[]{:S(2)}, u32[]{:S(2)}) %collective-permute-start.8) | collective-permute-done | bytes 131104 | tf_op jit(solution)/shard_map/panel_spread/ppermute | solution.py:478
  44.0 1.6 %collective-permute-start.12 = (bf16[64,16,128]{2,1,0:T(8,128)(2,1)S(1)}, bf16[64,16,128]{2,1,0:T(8,128)(2,1)S(1)}, u32[]{:S(2)}, u32[]{:S(2)}) collective-permute-start(bf16[64,16,128]{2,1,0:T(8,128)(2,1)S(1)} %constant_dynamic-update-slice_fusion.2.after_ref.refs_0_), channel_id=1, source_target_pairs={{0,8},{4,12},{8,0},{12,4},{16,24},{20,28},{24,16},{28,20},{1,9},{5... | collective-permute-start | bytes 786440 | tf_op jit(solution)/shard_map/panel_rows/ppermute | solution.py:484
  46.0 4.1 %mix_tiles.6 = (bf16[1024,1024]{1,0:T(8,128)(2,1)S(1)}, f32[8,128]{1,0:T(8,128)S(1)}) custom-call(s32[2,32]{1,0:T(2,128)S(1)} %pad_add_fusion.1.names_ref, f32[4096,1024]{1,0:T(8,128)} %matrix_ref.11, f32[8,128,128]{2,1,0:T(8,128)S(1)} %copy-done.1, bf16[64,16,128]{2,1,0:T(8,128)(2,1)S(1)} %constant_dynamic-update-slice_fusion.2.after_ref.refs_0_), custom_call_target="tpu_custom_call" | custom-call | flops 1000000 | bytes 100000 | tf_op jit(solution)/shard_map/mix/mix_tiles/pallas_call | solution.py:117
  50.2 4.1 %mix_tiles.7 = (bf16[1024,1024]{1,0:T(8,128)(2,1)S(1)}, f32[8,128]{1,0:T(8,128)S(1)}) custom-call(s32[2,32]{1,0:T(2,128)S(1)} %pad_add_fusion.1.names_ref, f32[4096,1024]{1,0:T(8,128)} %matrix_ref.11, f32[8,128,128]{2,1,0:T(8,128)S(1)} %copy-done.1, f32[8,128]{1,0:T(8,128)S(1)} %get-tuple-element.54.after_ref), custom_call_target="tpu_custom_call" | custom-call | flops 1000000 | bytes 100000 | tf_op jit(solution)/shard_map/mix/mix_tiles/pallas_call | solution.py:117
  54.3 2.3 %collective-permute-done.10.refs_3_ = bf16[66,16,128]{2,1,0:T(8,128)(2,1)S(1)} collective-permute-done((bf16[66,16,128]{2,1,0:T(8,128)(2,1)S(1)}, bf16[66,16,128]{2,1,0:T(8,128)(2,1)S(1)}, u32[]{:S(2)}, u32[]{:S(2)}) %collective-permute-start.10) | collective-permute-done | bytes 270368 | tf_op jit(solution)/shard_map/panel_rows/ppermute | solution.py:484
  56.6 3.5 %first_sum.1 = (f32[64,16,128]{2,1,0:T(8,128)S(1)}, s32[8,8,128]{2,1,0:T(8,128)S(1)}) custom-call(f32[8,128]{1,0:T(8,128)S(1)} %get-tuple-element.55.after_ref, bf16[66,16,128]{2,1,0:T(8,128)(2,1)S(1)} %constant_dynamic-update-slice_fusion.refs_0_, bf16[66,16,128]{2,1,0:T(8,128)(2,1)S(1)} %collective-permute-done.4.after_ref.refs_1_, ...), custom_call_target="tpu_custom_call" | custom-call | flops 1000000 | bytes 100000 | tf_op jit(solution)/shard_map/panel_sum/first_sum/pallas_call | solution.py:201
  60.3 2.7 %collective-permute-start.14 = (f16[64,16,128]{2,1,0:T(8,128)(2,1)S(1)}, f16[64,16,128]{2,1,0:T(8,128)(2,1)S(1)}, u32[]{:S(2)}, u32[]{:S(2)}) collective-permute-start(f16[64,16,128]{2,1,0:T(8,128)(2,1)S(1)} %get-tuple-element.76), channel_id=1, source_target_pairs={{0,1},{1,0},{2,3},{3,2},{4,5},{5,4},{6,7},{7,6},{8,9},{9,8},{10,11... | collective-permute-start | bytes 786440 | tf_op jit(solution)/shard_map/panel_cols/ppermute | solution.py:487
  63.0 0.9 collective-permute-start.16
  63.9 2.8 %collective-permute-done.15 = f16[64,16,128]{2,1,0:T(8,128)(2,1)S(1)} collective-permute-done((f16[64,16,128]{2,1,0:T(8,128)(2,1)S(1)}, f16[64,16,128]{2,1,0:T(8,128)(2,1)S(1)}, u32[]{:S(2)}, u32[]{:S(2)}) %collective-permute-start.15) | collective-permute-done | bytes 262176 | tf_op jit(solution)/shard_map/panel_cols/ppermute | solution.py:487
  66.7 3.5 %collective-permute-done.14 = f16[64,16,128]{2,1,0:T(8,128)(2,1)S(1)} collective-permute-done((f16[64,16,128]{2,1,0:T(8,128)(2,1)S(1)}, f16[64,16,128]{2,1,0:T(8,128)(2,1)S(1)}, u32[]{:S(2)}, u32[]{:S(2)}) %collective-permute-start.14) | collective-permute-done | bytes 262176 | tf_op jit(solution)/shard_map/panel_cols/ppermute | solution.py:487
  70.2 0.4 collective-permute-done.13.refs_3_
  70.6 3.5 %next_sum.1.after_ref = f32[64,16,128]{2,1,0:T(8,128)S(1)} custom-call(s32[8,8,128]{2,1,0:T(8,128)S(1)} %get-tuple-element.56.names, f32[64,16,128]{2,1,0:T(8,128)S(1)} %get-tuple-element.57.after_ref, bf16[64,16,128]{2,1,0:T(8,128)(2,1)S(1)} %constant_dynamic-update-slice_fusion.2.after_ref.refs_0_, ...), custom_call_target="tpu_custom_call" | custom-call | flops 1000000 | bytes 100000 | tf_op jit(solution)/shard_map/panel_sum/next_sum/pallas_call | solution.py:220
  74.6 2.9 %collective-permute-start.23 = (f16[64,16,128]{2,1,0:T(8,128)(2,1)S(1)}, f16[64,16,128]{2,1,0:T(8,128)(2,1)S(1)}, u32[]{:S(2)}, u32[]{:S(2)}) collective-permute-start(f16[64,16,128]{2,1,0:T(8,128)(2,1)S(1)} %convert_element_type.69), channel_id=1, source_target_pairs={{0,3},{1,2},{2,1},{3,0},{4,7},{5,6},{6,5},{7,4},{8,11},{9,10},{10,... | collective-permute-start | bytes 786440 | tf_op jit(solution)/shard_map/panel_cols/ppermute | solution.py:487
  77.5 0.4 collective-permute-start.22
  78.5 4.5 %cross_parts.2 = (f32[64,128,128]{2,1,0:T(8,128)S(1)}, f32[4,128,128]{2,1,0:T(8,128)S(1)}, f32[4,128,128]{2,1,0:T(8,128)S(1)}) custom-call(s32[3,32]{1,0:T(4,128)S(1)} %get-tuple-element.81.names_ref, s32[11]{0:T(128)S(1)} %stack.56.order_ref.after_ref, f32[64,16,128]{2,1,0:T(8,128)S(1)} %next_sum.1.after_ref, ...), custom_call_target="tpu_custom_call" | custom-call | flops 1000000 | bytes 100000 | tf_op jit(solution)/shard_map/cross0/cross_parts/pallas_call | solution.py:305
  83.0 2.5 %first_gram.1.block_ref = f32[128,128]{1,0:T(8,128)S(1)} custom-call(f32[4,128,128]{2,1,0:T(8,128)S(1)} %get-tuple-element.63.after_ref.refs_12_, f32[64,128,128]{2,1,0:T(8,128)S(1)} %get-tuple-element.64.panel.panel0), custom_call_target="tpu_custom_call" | custom-call | flops 1000000 | bytes 100000 | tf_op jit(solution)/shard_map/factor0/first_gram/pallas_call | solution.py:390
  85.6 6.1 %first_factor.1.after_ref.inverse_ref = f32[128,128]{1,0:T(8,128)S(1)} custom-call(f32[128,128]{1,0:T(8,128)S(1)} %first_gram.1.block_ref), custom_call_target="tpu_custom_call" | custom-call | flops 1000000 | bytes 100000 | tf_op jit(solution)/shard_map/factor0/first_factor/pallas_call | solution.py:407
  91.8 0.5 collective-permute-start.25
  92.3 0.4 collective-permute-start.27
  94.4 4.8 %cross_parts.3 = (f32[64,128,128]{2,1,0:T(8,128)S(1)}, f32[4,256,128]{2,1,0:T(8,128)S(1)}, f32[4,256,128]{2,1,0:T(8,128)S(1)}) custom-call(s32[3,32]{1,0:T(4,128)S(1)} %get-tuple-element.81.names_ref, s32[11]{0:T(128)S(1)} %stack.56.order_ref.after_ref, f32[128,128]{1,0:T(8,128)S(1)} %first_factor.1.after_ref.inverse_ref, ...), custom_call_target="tpu_custom_call" | custom-call | flops 1000000 | bytes 100000 | tf_op jit(solution)/shard_map/cross1/cross_parts/pallas_call | solution.py:305
  99.4 1.8 %collective-permute-done.28 = f32[4,256,128]{2,1,0:T(8,128)S(1)} collective-permute-done((f32[4,256,128]{2,1,0:T(8,128)S(1)}, f32[4,256,128]{2,1,0:T(8,128)S(1)}, u32[]{:S(2)}, u32[]{:S(2)}) %collective-permute-start.28) | collective-permute-done | bytes 524320 | tf_op jit(solution)/shard_map/cross_sum/ppermute | solution.py:478
  101.4 3.8 %collective-permute-start.31 = (f32[256,128]{1,0:T(8,128)S(1)}, f32[256,128]{1,0:T(8,128)S(1)}, u32[]{:S(2)}, u32[]{:S(2)}) collective-permute-start(f32[256,128]{1,0:T(8,128)S(1)} %get-tuple-element.78), channel_id=1, source_target_pairs={{0,24},{4,28},{8,0},{12,4},{16,8},{20,12},{24,16},{28,20},{1,25},{... | collective-permute-start | bytes 393224 | tf_op jit(solution)/shard_map/cross_sum/ppermute | solution.py:481
  105.2 0.4 collective-permute-start.30
  105.6 3.5 %second_gram.1 = (f32[128,128]{1,0:T(8,128)S(1)}, f32[128,128]{1,0:T(8,128)S(1)}) custom-call(f32[4,256,128]{2,1,0:T(8,128)S(1)} %get-tuple-element.70.after_ref, f32[64,128,128]{2,1,0:T(8,128)S(1)} %get-tuple-element.64.panel.panel0, f32[64,128,128]{2,1,0:T(8,128)S(1)} %get-tuple-element.72.panel1), custom_call_target="tpu_custom_call" | custom-call | flops 1000000 | bytes 100000 | tf_op jit(solution)/shard_map/gram1/second_gram/pallas_call | solution.py:436
  109.0 6.9 %second_factor.1 = f32[256,256]{1,0:T(8,128)S(1)} custom-call(f32[4,256,128]{2,1,0:T(8,128)S(1)} %add.52.after_ref, f32[128,128]{1,0:T(8,128)S(1)} %get-tuple-element.73.side_ref, f32[128,128]{1,0:T(8,128)S(1)} %get-tuple-element.74.block_ref, f32[128,128]{1,0:T(8,128)S(1)} %first_factor.1.after_ref.inverse_ref), custom_call_target="tpu_custom_call" | custom-call | flops 1000000 | bytes 100000 | tf_op jit(solution)/shard_map/factor1/second_factor/pallas_call | solution.py:459
  115.9 1.3 %collective-permute-done.30 = f32[256,128]{1,0:T(8,128)S(1)} collective-permute-done((f32[256,128]{1,0:T(8,128)S(1)}, f32[256,128]{1,0:T(8,128)S(1)}, u32[]{:S(2)}, u32[]{:S(2)}) %collective-permute-start.30) | collective-permute-done | bytes 131104 | tf_op jit(solution)/shard_map/cross_sum/ppermute | solution.py:481
  117.6 9.2 %all_to_all.19 = f32[8,32,128]{2,1,0:T(8,128)S(1)} all-to-all(f32[8,32,128]{2,1,0:T(8,128)S(1)} %bitcast.39), channel_id=1, replica_groups=mesh['rows'=8,'cols'=4] {'rows'}, dimensions={0} | all-to-all | bytes 262144 | tf_op jit(solution)/shard_map/solve/all_to_all | solution.py:583
  126.8 0.7 copy_bitcast_fusion
  (71 shorter events, 4.4 us)
Async XLA Ops:
  0.8 1.0 copy-start
  1.8 10.8 %copy-start.3 = (s32[32]{0:T(128)S(1)}, s32[32]{0:T(128)}, u32[]{:S(2)}) copy-start(s32[32]{0:T(128)} %param.9) | copy-start | bytes 388
  1.8 10.8 %copy-start.2 = (s32[32,2]{0,1:T(2,128)S(1)}, s32[32,2]{0,1:T(2,128)}, u32[]{:S(2)}) copy-start(s32[32,2]{0,1:T(2,128)} %param.7) | copy-start | bytes 772
  1.8 10.8 %copy-start.1 = (f32[8,128,128]{2,1,0:T(8,128)S(1)}, f32[8,128,128]{2,1,0:T(8,128)}, u32[]{:S(2)}) copy-start(f32[8,128,128]{2,1,0:T(8,128)} %mixers_ref.11) | copy-start | bytes 1572868
  5.1 15.8 %collective-permute-start = (bf16[2,32,16,128]{3,2,1,0:T(8,128)(2,1)S(1)}, bf16[2,32,16,128]{3,2,1,0:T(8,128)(2,1)S(1)}, u32[]{:S(2)}, u32[]{:S(2)}) collective-permute-start(bf16[2,32,16,128]{3,2,1,0:T(8,128)(2,1)S(1)} %get-tuple-element.43), channel_id=1, source_target_pairs={{0,1},{4,5},{8,9},{12,13},{16,17},{20,21},{24,25},{28,29}} | collective-permute-start | bytes 786440 | tf_op jit(solution)/shard_map/panel_spread/ppermute | solution.py:509
  10.0 11.0 %collective-permute-start.1 = (bf16[2,32,16,128]{3,2,1,0:T(8,128)(2,1)S(1)}, bf16[2,32,16,128]{3,2,1,0:T(8,128)(2,1)S(1)}, u32[]{:S(2)}, u32[]{:S(2)}) collective-permute-start(bf16[2,32,16,128]{3,2,1,0:T(8,128)(2,1)S(1)} %get-tuple-element.44), channel_id=1, source_target_pairs={{0,2},{4,6},{8,10},{12,14},{16,18},{20,22},{24,26},{28,30}} | collective-permute-start | bytes 786440 | tf_op jit(solution)/shard_map/panel_spread/ppermute | solution.py:509
  11.3 9.8 %collective-permute-start.2 = (bf16[2,32,16,128]{3,2,1,0:T(8,128)(2,1)S(1)}, bf16[2,32,16,128]{3,2,1,0:T(8,128)(2,1)S(1)}, u32[]{:S(2)}, u32[]{:S(2)}) collective-permute-start(bf16[2,32,16,128]{3,2,1,0:T(8,128)(2,1)S(1)} %get-tuple-element.45), channel_id=1, source_target_pairs={{0,3},{4,7},{8,11},{12,15},{16,19},{20,23},{24,27},{28,31}} | collective-permute-start | bytes 786440 | tf_op jit(solution)/shard_map/panel_spread/ppermute | solution.py:509
  21.7 1.4 %collective-permute-start.3 = (bf16[33,16,128]{2,1,0:T(8,128)(2,1)S(1)}, bf16[33,16,128]{2,1,0:T(8,128)(2,1)S(1)}, u32[]{:S(2)}, u32[]{:S(2)}) collective-permute-start(bf16[33,16,128]{2,1,0:T(8,128)(2,1)S(1)} %get-tuple-element.47), channel_id=1, source_target_pairs={{0,4},{4,0},{8,12},{12,8},{16,20},{20,16},{24,28},{28,24},{1,5},{5... | collective-permute-start | bytes 405512 | tf_op jit(solution)/shard_map/panel_spread/ppermute | solution.py:478
  23.1 15.3 %collective-permute-start.4 = (bf16[66,16,128]{2,1,0:T(8,128)(2,1)S(1)}, bf16[66,16,128]{2,1,0:T(8,128)(2,1)S(1)}, u32[]{:S(2)}, u32[]{:S(2)}) collective-permute-start(bf16[66,16,128]{2,1,0:T(8,128)(2,1)S(1)} %constant_dynamic-update-slice_fusion.refs_0_), channel_id=1, source_target_pairs={{0,16},{4,20},{8,24},{12,28},{16,0},{20,4},{24,8},{28,12},{1,17},{... | collective-permute-start | bytes 811016 | tf_op jit(solution)/shard_map/panel_rows/ppermute | solution.py:484
  29.1 10.1 %collective-permute-start.5 = (bf16[2,32,16,128]{3,2,1,0:T(8,128)(2,1)S(1)}, bf16[2,32,16,128]{3,2,1,0:T(8,128)(2,1)S(1)}, u32[]{:S(2)}, u32[]{:S(2)}) collective-permute-start(bf16[2,32,16,128]{3,2,1,0:T(8,128)(2,1)S(1)} %get-tuple-element.49), channel_id=1, source_target_pairs={{0,1},{4,5},{8,9},{12,13},{16,17},{20,21},{24,25},{28,29}} | collective-permute-start | bytes 786440 | tf_op jit(solution)/shard_map/panel_spread/ppermute | solution.py:509
  30.4 8.8 %collective-permute-start.6 = (bf16[2,32,16,128]{3,2,1,0:T(8,128)(2,1)S(1)}, bf16[2,32,16,128]{3,2,1,0:T(8,128)(2,1)S(1)}, u32[]{:S(2)}, u32[]{:S(2)}) collective-permute-start(bf16[2,32,16,128]{3,2,1,0:T(8,128)(2,1)S(1)} %get-tuple-element.50), channel_id=1, source_target_pairs={{0,2},{4,6},{8,10},{12,14},{16,18},{20,22},{24,26},{28,30}} | collective-permute-start | bytes 786440 | tf_op jit(solution)/shard_map/panel_spread/ppermute | solution.py:509
  31.7 10.2 %collective-permute-start.7 = (bf16[2,32,16,128]{3,2,1,0:T(8,128)(2,1)S(1)}, bf16[2,32,16,128]{3,2,1,0:T(8,128)(2,1)S(1)}, u32[]{:S(2)}, u32[]{:S(2)}) collective-permute-start(bf16[2,32,16,128]{3,2,1,0:T(8,128)(2,1)S(1)} %get-tuple-element.51), channel_id=1, source_target_pairs={{0,3},{4,7},{8,11},{12,15},{16,19},{20,23},{24,27},{28,31}} | collective-permute-start | bytes 786440 | tf_op jit(solution)/shard_map/panel_spread/ppermute | solution.py:509
  35.7 18.5 %collective-permute-start.9 = (bf16[66,16,128]{2,1,0:T(8,128)(2,1)S(1)}, bf16[66,16,128]{2,1,0:T(8,128)(2,1)S(1)}, u32[]{:S(2)}, u32[]{:S(2)}) collective-permute-start(bf16[66,16,128]{2,1,0:T(8,128)(2,1)S(1)} %constant_dynamic-update-slice_fusion.refs_0_), channel_id=1, source_target_pairs={{0,8},{4,12},{8,0},{12,4},{16,24},{20,28},{24,16},{28,20},{1,9},{5... | collective-permute-start | bytes 811016 | tf_op jit(solution)/shard_map/panel_rows/ppermute | solution.py:484
  38.5 18.1 %collective-permute-start.10 = (bf16[66,16,128]{2,1,0:T(8,128)(2,1)S(1)}, bf16[66,16,128]{2,1,0:T(8,128)(2,1)S(1)}, u32[]{:S(2)}, u32[]{:S(2)}) collective-permute-start(bf16[66,16,128]{2,1,0:T(8,128)(2,1)S(1)} %collective-permute-done.4.after_ref.refs_1_), channel_id=1, source_target_pairs={{0,8},{4,12},{8,0},{12,4},{16,24},{20,28},{24,16},{28,20},{1,9},{5... | collective-permute-start | bytes 811016 | tf_op jit(solution)/shard_map/panel_rows/ppermute | solution.py:484
  42.6 1.4 %collective-permute-start.8 = (bf16[32,16,128]{2,1,0:T(8,128)(2,1)S(1)}, bf16[32,16,128]{2,1,0:T(8,128)(2,1)S(1)}, u32[]{:S(2)}, u32[]{:S(2)}) collective-permute-start(bf16[32,16,128]{2,1,0:T(8,128)(2,1)S(1)} %get-tuple-element.53), channel_id=1, source_target_pairs={{0,4},{4,0},{8,12},{12,8},{16,20},{20,16},{24,28},{28,24},{1,5},{5... | collective-permute-start | bytes 393224 | tf_op jit(solution)/shard_map/panel_spread/ppermute | solution.py:478
  44.0 19.9 %collective-permute-start.12 = (bf16[64,16,128]{2,1,0:T(8,128)(2,1)S(1)}, bf16[64,16,128]{2,1,0:T(8,128)(2,1)S(1)}, u32[]{:S(2)}, u32[]{:S(2)}) collective-permute-start(bf16[64,16,128]{2,1,0:T(8,128)(2,1)S(1)} %constant_dynamic-update-slice_fusion.2.after_ref.refs_0_), channel_id=1, source_target_pairs={{0,8},{4,12},{8,0},{12,4},{16,24},{20,28},{24,16},{28,20},{1,9},{5... | collective-permute-start | bytes 786440 | tf_op jit(solution)/shard_map/panel_rows/ppermute | solution.py:484
  45.7 17.4 %collective-permute-start.11 = (bf16[64,16,128]{2,1,0:T(8,128)(2,1)S(1)}, bf16[64,16,128]{2,1,0:T(8,128)(2,1)S(1)}, u32[]{:S(2)}, u32[]{:S(2)}) collective-permute-start(bf16[64,16,128]{2,1,0:T(8,128)(2,1)S(1)} %constant_dynamic-update-slice_fusion.2.after_ref.refs_0_), channel_id=1, source_target_pairs={{0,16},{4,20},{8,24},{12,28},{16,0},{20,4},{24,8},{28,12},{1,17},{... | collective-permute-start | bytes 786440 | tf_op jit(solution)/shard_map/panel_rows/ppermute | solution.py:484
  60.3 6.4 %collective-permute-start.15 = (f16[64,16,128]{2,1,0:T(8,128)(2,1)S(1)}, f16[64,16,128]{2,1,0:T(8,128)(2,1)S(1)}, u32[]{:S(2)}, u32[]{:S(2)}) collective-permute-start(f16[64,16,128]{2,1,0:T(8,128)(2,1)S(1)} %get-tuple-element.76), channel_id=1, source_target_pairs={{0,2},{1,3},{2,0},{3,1},{4,6},{5,7},{6,4},{7,5},{8,10},{9,11},{10,... | collective-permute-start | bytes 786440 | tf_op jit(solution)/shard_map/panel_cols/ppermute | solution.py:487
  60.3 9.9 %collective-permute-start.14 = (f16[64,16,128]{2,1,0:T(8,128)(2,1)S(1)}, f16[64,16,128]{2,1,0:T(8,128)(2,1)S(1)}, u32[]{:S(2)}, u32[]{:S(2)}) collective-permute-start(f16[64,16,128]{2,1,0:T(8,128)(2,1)S(1)} %get-tuple-element.76), channel_id=1, source_target_pairs={{0,1},{1,0},{2,3},{3,2},{4,5},{5,4},{6,7},{7,6},{8,9},{9,8},{10,11... | collective-permute-start | bytes 786440 | tf_op jit(solution)/shard_map/panel_cols/ppermute | solution.py:487
  63.0 7.6 %collective-permute-start.13 = (bf16[64,16,128]{2,1,0:T(8,128)(2,1)S(1)}, bf16[64,16,128]{2,1,0:T(8,128)(2,1)S(1)}, u32[]{:S(2)}, u32[]{:S(2)}) collective-permute-start(bf16[64,16,128]{2,1,0:T(8,128)(2,1)S(1)} %collective-permute-done.11.refs_1_), channel_id=1, source_target_pairs={{0,8},{4,12},{8,0},{12,4},{16,24},{20,28},{24,16},{28,20},{1,9},{5... | collective-permute-start | bytes 786440 | tf_op jit(solution)/shard_map/panel_rows/ppermute | solution.py:484
  63.0 11.5 %collective-permute-start.16 = (f16[64,16,128]{2,1,0:T(8,128)(2,1)S(1)}, f16[64,16,128]{2,1,0:T(8,128)(2,1)S(1)}, u32[]{:S(2)}, u32[]{:S(2)}) collective-permute-start(f16[64,16,128]{2,1,0:T(8,128)(2,1)S(1)} %get-tuple-element.76), channel_id=1, source_target_pairs={{0,3},{1,2},{2,1},{3,0},{4,7},{5,6},{6,5},{7,4},{8,11},{9,10},{10,... | collective-permute-start | bytes 786440 | tf_op jit(solution)/shard_map/panel_cols/ppermute | solution.py:487
  63.9 13.6 %collective-permute-start.17 = (f16[64,16,128]{2,1,0:T(8,128)(2,1)S(1)}, f16[64,16,128]{2,1,0:T(8,128)(2,1)S(1)}, u32[]{:S(2)}, u32[]{:S(2)}) collective-permute-start(f16[64,16,128]{2,1,0:T(8,128)(2,1)S(1)} %get-tuple-element.76), channel_id=1, source_target_pairs={{0,4},{4,0},{8,12},{12,8},{16,20},{20,16},{24,28},{28,24},{1,5},{5... | collective-permute-start | bytes 786440 | tf_op jit(solution)/shard_map/panel_cores/ppermute | solution.py:478
  66.7 11.3 %collective-permute-start.19 = (f16[64,16,128]{2,1,0:T(8,128)(2,1)S(1)}, f16[64,16,128]{2,1,0:T(8,128)(2,1)S(1)}, u32[]{:S(2)}, u32[]{:S(2)}) collective-permute-start(f16[64,16,128]{2,1,0:T(8,128)(2,1)S(1)} %collective-permute-done.15), channel_id=1, source_target_pairs={{0,4},{4,0},{8,12},{12,8},{16,20},{20,16},{24,28},{28,24},{1,5},{5... | collective-permute-start | bytes 786440 | tf_op jit(solution)/shard_map/panel_cores/ppermute | solution.py:478
  70.2 8.2 %collective-permute-start.18 = (f16[64,16,128]{2,1,0:T(8,128)(2,1)S(1)}, f16[64,16,128]{2,1,0:T(8,128)(2,1)S(1)}, u32[]{:S(2)}, u32[]{:S(2)}) collective-permute-start(f16[64,16,128]{2,1,0:T(8,128)(2,1)S(1)} %collective-permute-done.14), channel_id=1, source_target_pairs={{0,4},{4,0},{8,12},{12,8},{16,20},{20,16},{24,28},{28,24},{1,5},{5... | collective-permute-start | bytes 786440 | tf_op jit(solution)/shard_map/panel_cores/ppermute | solution.py:478
  74.6 3.9 %collective-permute-start.20 = (f16[64,16,128]{2,1,0:T(8,128)(2,1)S(1)}, f16[64,16,128]{2,1,0:T(8,128)(2,1)S(1)}, u32[]{:S(2)}, u32[]{:S(2)}) collective-permute-start(f16[64,16,128]{2,1,0:T(8,128)(2,1)S(1)} %collective-permute-done.16), channel_id=1, source_target_pairs={{0,4},{4,0},{8,12},{12,8},{16,20},{20,16},{24,28},{28,24},{1,5},{5... | collective-permute-start | bytes 786440 | tf_op jit(solution)/shard_map/panel_cores/ppermute | solution.py:478
  74.6 17.0 %collective-permute-start.23 = (f16[64,16,128]{2,1,0:T(8,128)(2,1)S(1)}, f16[64,16,128]{2,1,0:T(8,128)(2,1)S(1)}, u32[]{:S(2)}, u32[]{:S(2)}) collective-permute-start(f16[64,16,128]{2,1,0:T(8,128)(2,1)S(1)} %convert_element_type.69), channel_id=1, source_target_pairs={{0,3},{1,2},{2,1},{3,0},{4,7},{5,6},{6,5},{7,4},{8,11},{9,10},{10,... | collective-permute-start | bytes 786440 | tf_op jit(solution)/shard_map/panel_cols/ppermute | solution.py:487
  77.5 14.1 %collective-permute-start.22 = (f16[64,16,128]{2,1,0:T(8,128)(2,1)S(1)}, f16[64,16,128]{2,1,0:T(8,128)(2,1)S(1)}, u32[]{:S(2)}, u32[]{:S(2)}) collective-permute-start(f16[64,16,128]{2,1,0:T(8,128)(2,1)S(1)} %convert_element_type.69), channel_id=1, source_target_pairs={{0,2},{1,3},{2,0},{3,1},{4,6},{5,7},{6,4},{7,5},{8,10},{9,11},{10,... | collective-permute-start | bytes 786440 | tf_op jit(solution)/shard_map/panel_cols/ppermute | solution.py:487
  78.0 13.7 %collective-permute-start.21 = (f16[64,16,128]{2,1,0:T(8,128)(2,1)S(1)}, f16[64,16,128]{2,1,0:T(8,128)(2,1)S(1)}, u32[]{:S(2)}, u32[]{:S(2)}) collective-permute-start(f16[64,16,128]{2,1,0:T(8,128)(2,1)S(1)} %convert_element_type.69), channel_id=1, source_target_pairs={{0,1},{1,0},{2,3},{3,2},{4,5},{5,4},{6,7},{7,6},{8,9},{9,8},{10,11... | collective-permute-start | bytes 786440 | tf_op jit(solution)/shard_map/panel_cols/ppermute | solution.py:487
  91.7 1.6 %collective-permute-start.24 = (f16[64,16,128]{2,1,0:T(8,128)(2,1)S(1)}, f16[64,16,128]{2,1,0:T(8,128)(2,1)S(1)}, u32[]{:S(2)}, u32[]{:S(2)}) collective-permute-start(f16[64,16,128]{2,1,0:T(8,128)(2,1)S(1)} %convert_element_type.69), channel_id=1, source_target_pairs={{0,4},{4,0},{8,12},{12,8},{16,20},{20,16},{24,28},{28,24},{1,5},{5... | collective-permute-start | bytes 786440 | tf_op jit(solution)/shard_map/panel_cores/ppermute | solution.py:478
  91.8 1.9 %collective-permute-start.25 = (f16[64,16,128]{2,1,0:T(8,128)(2,1)S(1)}, f16[64,16,128]{2,1,0:T(8,128)(2,1)S(1)}, u32[]{:S(2)}, u32[]{:S(2)}) collective-permute-start(f16[64,16,128]{2,1,0:T(8,128)(2,1)S(1)} %collective-permute-done.21), channel_id=1, source_target_pairs={{0,4},{4,0},{8,12},{12,8},{16,20},{20,16},{24,28},{28,24},{1,5},{5... | collective-permute-start | bytes 786440 | tf_op jit(solution)/shard_map/panel_cores/ppermute | solution.py:478
  92.3 1.8 %collective-permute-start.26 = (f16[64,16,128]{2,1,0:T(8,128)(2,1)S(1)}, f16[64,16,128]{2,1,0:T(8,128)(2,1)S(1)}, u32[]{:S(2)}, u32[]{:S(2)}) collective-permute-start(f16[64,16,128]{2,1,0:T(8,128)(2,1)S(1)} %collective-permute-done.22), channel_id=1, source_target_pairs={{0,4},{4,0},{8,12},{12,8},{16,20},{20,16},{24,28},{28,24},{1,5},{5... | collective-permute-start | bytes 786440 | tf_op jit(solution)/shard_map/panel_cores/ppermute | solution.py:478
  92.3 2.1 %collective-permute-start.27 = (f16[64,16,128]{2,1,0:T(8,128)(2,1)S(1)}, f16[64,16,128]{2,1,0:T(8,128)(2,1)S(1)}, u32[]{:S(2)}, u32[]{:S(2)}) collective-permute-start(f16[64,16,128]{2,1,0:T(8,128)(2,1)S(1)} %collective-permute-done.23), channel_id=1, source_target_pairs={{0,4},{4,0},{8,12},{12,8},{16,20},{20,16},{24,28},{28,24},{1,5},{5... | collective-permute-start | bytes 786440 | tf_op jit(solution)/shard_map/panel_cores/ppermute | solution.py:478
  99.2 2.0 %collective-permute-start.28 = (f32[4,256,128]{2,1,0:T(8,128)S(1)}, f32[4,256,128]{2,1,0:T(8,128)S(1)}, u32[]{:S(2)}, u32[]{:S(2)}) collective-permute-start(f32[4,256,128]{2,1,0:T(8,128)S(1)} %get-tuple-element.71), channel_id=1, source_target_pairs={{0,4},{4,0},{8,12},{12,8},{16,20},{20,16},{24,28},{28,24},{1,5},{5... | collective-permute-start | bytes 1572872 | tf_op jit(solution)/shard_map/cross_sum/ppermute | solution.py:478
  101.3 14.6 %collective-permute-start.29 = (f32[256,128]{1,0:T(8,128)S(1)}, f32[256,128]{1,0:T(8,128)S(1)}, u32[]{:S(2)}, u32[]{:S(2)}) collective-permute-start(f32[256,128]{1,0:T(8,128)S(1)} %get-tuple-element.77), channel_id=1, source_target_pairs={{0,8},{4,12},{8,16},{12,20},{16,24},{20,28},{24,0},{28,4},{1,9},{5... | collective-permute-start | bytes 393224 | tf_op jit(solution)/shard_map/cross_sum/ppermute | solution.py:481
  101.4 14.6 %collective-permute-start.31 = (f32[256,128]{1,0:T(8,128)S(1)}, f32[256,128]{1,0:T(8,128)S(1)}, u32[]{:S(2)}, u32[]{:S(2)}) collective-permute-start(f32[256,128]{1,0:T(8,128)S(1)} %get-tuple-element.78), channel_id=1, source_target_pairs={{0,24},{4,28},{8,0},{12,4},{16,8},{20,12},{24,16},{28,20},{1,25},{... | collective-permute-start | bytes 393224 | tf_op jit(solution)/shard_map/cross_sum/ppermute | solution.py:481
  105.2 12.1 %collective-permute-start.30 = (f32[256,128]{1,0:T(8,128)S(1)}, f32[256,128]{1,0:T(8,128)S(1)}, u32[]{:S(2)}, u32[]{:S(2)}) collective-permute-start(f32[256,128]{1,0:T(8,128)S(1)} %get-tuple-element.79), channel_id=1, source_target_pairs={{0,16},{4,20},{8,24},{12,28},{16,0},{20,4},{24,8},{28,12},{1,17},{... | collective-permute-start | bytes 393224 | tf_op jit(solution)/shard_map/cross_sum/ppermute | solution.py:481

commit v8 on v7

--- a/solution.py
+++ b/solution.py
@@ -513,12 +513,12 @@
             keep, give = pick(order, after, extra, got)
             return jnp.concatenate([keep, swap(give)])
 
-    def gather_rows(held):
+    def gather_rows(held, forward):
         with jax.named_scope("panel_rows"):
             if chips != 4:
                 return [held] + [shift(held, j) for j in range(1, chips)]
             far, near = beside(held, 2), beside(held, 1)
-            return [held, far, near, beside(far, 1)]
+            return [held, far, near, beside(far, 1) if forward else beside(held, 3)]
 
     def gather_cols(summed):
         with jax.named_scope("panel_cols"):
@@ -543,9 +543,9 @@
     early = names.shape[1] // STEP // 2
     token = mix_next(tiles[0], early)
     held0 = spread(scatter(0), token, carried)
-    arrived0 = gather_rows(held0)
+    arrived0 = gather_rows(held0, True)
     held1 = spread(scatter(1), arrived0[1])
-    arrived1 = gather_rows(held1)
+    arrived1 = gather_rows(held1, False)
     token = mix_next(held1, names.shape[1] // STEP - early)
     with jax.named_scope("panel_sum"):
         summed0, all_names = first_sum(token, arrived0)

time: 128 us -> 129 us (level)
  waiting for transfers between devices: 20.4 us -> 17 us
  starting transfers between devices: 34 us -> 37.1 us
  blocking collectives: 9.17 us -> 10.7 us
    ppermute x6, waiting for transfers between devices: 6.66 us -> 1.3 us  [across(): return lax.ppermute(value, 'cols', [(i, i ^ j) for i in range(parts)])]
    ppermute x6, waiting for transfers between devices: 3.83 us -> 6.91 us  [beside(): return lax.ppermute(value, 'rows', [(i, i ^ 2 * j) for i in range(rows_n)])]
    ppermute x6, starting transfers between devices: 6.96 us -> 9.43 us  [beside(): return lax.ppermute(value, 'rows', [(i, i ^ 2 * j) for i in range(rows_n)])]
    all_to_all x1, blocking collectives: 9.17 us -> 10.7 us  [local(): lax.all_to_all(solved, 'rows', split_axis=0, concat_axis=1, tiled=True)]
  transfers between devices with their start and end apart: 32 -> 32, of which waited for: 16 -> 13; matrix products, arithmetic and copies ran while one was open for 1% -> 1% of each run, Pallas kernels for 40% -> 40%
where the time goes in v8:
time: 129 us
  Pallas kernels  59.7 us (46%)
  starting transfers between devices  37.1 us (29%)
  waiting for transfers between devices  17 us (13%)
  blocking collectives  10.7 us (8%)
  local copies, waits for them, and re-layouts  1.9 us (1%)
  other arithmetic  1.41 us (1%)
    pallas_call x4, Pallas kernels, mix_tiles(): pl.pallas_call(functools.partial(mix_kernel, per_step, start), grid_spec=...  16.5 us
    ppermute x6, starting transfers between devices, scatter(): lax.ppermute(slices[j], 'cols', [(0, j)])  14.1 us
    all_to_all x1, blocking collectives, local(): lax.all_to_all(solved, 'rows', split_axis=0, concat_axis=1, tiled=True)  10.7 us
    ppermute x6, starting transfers between devices, beside(): return lax.ppermute(value, 'rows', [(i, i ^ 2 * j) for i in range(rows_n)])  9.43 us
    pallas_call x2, Pallas kernels, cross_parts(): pl.pallas_call(functools.partial(cross_kernel, steps, chips, len(before),...  9.31 us
    ppermute x6, starting transfers between devices, across(): return lax.ppermute(value, 'cols', [(i, i ^ j) for i in range(parts)])  7.64 us
    ppermute x6, waiting for transfers between devices, beside(): return lax.ppermute(value, 'rows', [(i, i ^ 2 * j) for i in range(rows_n)])  6.91 us
    pallas_call x1, Pallas kernels, second_factor(): pl.pallas_call(last_kernel, in_specs=[anywhere()] + [vmem()] * 3, out_spe...  6.86 us
  transfers between devices with their start and end apart: 32, of which 13 were waited for; matrix products, arithmetic and copies ran while one was open for 1% of the time, Pallas kernels for 40%

profile of v8, /device:TPU:0, one launch (start us, length us, event | category | flops | bytes accessed | tf_op | source)
XLA Modules:
  0.0 128.6 jit_solution(7026249756772048032)
XLA Ops:
  0.0 0.7 pad_add_fusion.1.names_ref
  0.8 1.0 copy-done
  1.8 3.3 %mix_panel.2 = (bf16[2,32,16,128]{3,2,1,0:T(8,128)(2,1)S(1)}, bf16[2,32,16,128]{3,2,1,0:T(8,128)(2,1)S(1)}, bf16[2,32,16,128]{3,2,1,0:T(8,128)(2,1)S(1)}, bf16[2,32,16,128]{3,2,1,0:T(8,128)(2,1)S(1)}) custom-call(s32[2,32]{1,0:T(2,128)S(1)} %pad_add_fusion.1.names_ref, s32[11]{0:T(128)S(1)} %stack.56.order_ref.after_ref, f32[4096,1024]{1,0:T(8,128)} %matrix_ref.11, ...), custom_call_target="tpu_custom_call" | custom-call | flops 1000000 | bytes 100000 | tf_op jit(solution)/shard_map/panel_mix/mix_panel/pallas_call | solution.py:85
  5.1 4.9 %collective-permute-start = (bf16[2,32,16,128]{3,2,1,0:T(8,128)(2,1)S(1)}, bf16[2,32,16,128]{3,2,1,0:T(8,128)(2,1)S(1)}, u32[]{:S(2)}, u32[]{:S(2)}) collective-permute-start(bf16[2,32,16,128]{3,2,1,0:T(8,128)(2,1)S(1)} %get-tuple-element.43), channel_id=1, source_target_pairs={{0,1},{4,5},{8,9},{12,13},{16,17},{20,21},{24,25},{28,29}} | collective-permute-start | bytes 786440 | tf_op jit(solution)/shard_map/panel_spread/ppermute | solution.py:509
  10.0 1.3 %collective-permute-start.1 = (bf16[2,32,16,128]{3,2,1,0:T(8,128)(2,1)S(1)}, bf16[2,32,16,128]{3,2,1,0:T(8,128)(2,1)S(1)}, u32[]{:S(2)}, u32[]{:S(2)}) collective-permute-start(bf16[2,32,16,128]{3,2,1,0:T(8,128)(2,1)S(1)} %get-tuple-element.44), channel_id=1, source_target_pairs={{0,2},{4,6},{8,10},{12,14},{16,18},{20,22},{24,26},{28,30}} | collective-permute-start | bytes 786440 | tf_op jit(solution)/shard_map/panel_spread/ppermute | solution.py:509
  11.3 1.3 %collective-permute-start.2 = (bf16[2,32,16,128]{3,2,1,0:T(8,128)(2,1)S(1)}, bf16[2,32,16,128]{3,2,1,0:T(8,128)(2,1)S(1)}, u32[]{:S(2)}, u32[]{:S(2)}) collective-permute-start(bf16[2,32,16,128]{3,2,1,0:T(8,128)(2,1)S(1)} %get-tuple-element.45), channel_id=1, source_target_pairs={{0,3},{4,7},{8,11},{12,15},{16,19},{20,23},{24,27},{28,31}} | collective-permute-start | bytes 786440 | tf_op jit(solution)/shard_map/panel_spread/ppermute | solution.py:509
  12.7 4.1 %mix_tiles.4 = (bf16[1024,1024]{1,0:T(8,128)(2,1)S(1)}, f32[8,128]{1,0:T(8,128)S(1)}) custom-call(s32[2,32]{1,0:T(2,128)S(1)} %pad_add_fusion.1.names_ref, f32[4096,1024]{1,0:T(8,128)} %matrix_ref.11, f32[8,128,128]{2,1,0:T(8,128)S(1)} %copy-done.1, bf16[2,32,16,128]{3,2,1,0:T(8,128)(2,1)S(1)} %get-tuple-element.40.after_ref.refs_1_), custom_call_target="tpu_custom_call" | custom-call | flops 1000000 | bytes 100000 | tf_op jit(solution)/shard_map/mix/mix_tiles/pallas_call | solution.py:117
  16.8 4.1 %mix_tiles.5 = (bf16[1024,1024]{1,0:T(8,128)(2,1)S(1)}, f32[8,128]{1,0:T(8,128)S(1)}) custom-call(s32[2,32]{1,0:T(2,128)S(1)} %pad_add_fusion.1.names_ref, f32[4096,1024]{1,0:T(8,128)} %matrix_ref.11, f32[8,128,128]{2,1,0:T(8,128)S(1)} %copy-done.1, f32[8,128]{1,0:T(8,128)S(1)} %get-tuple-element.41.after_ref), custom_call_target="tpu_custom_call" | custom-call | flops 1000000 | bytes 100000 | tf_op jit(solution)/shard_map/mix/mix_tiles/pallas_call | solution.py:117
  21.1 0.6 pick.2
  21.8 1.3 %collective-permute-done.3 = bf16[33,16,128]{2,1,0:T(8,128)(2,1)S(1)} collective-permute-done((bf16[33,16,128]{2,1,0:T(8,128)(2,1)S(1)}, bf16[33,16,128]{2,1,0:T(8,128)(2,1)S(1)}, u32[]{:S(2)}, u32[]{:S(2)}) %collective-permute-start.3) | collective-permute-done | bytes 135200 | tf_op jit(solution)/shard_map/panel_spread/ppermute | solution.py:478
  23.1 2.7 %collective-permute-start.4 = (bf16[66,16,128]{2,1,0:T(8,128)(2,1)S(1)}, bf16[66,16,128]{2,1,0:T(8,128)(2,1)S(1)}, u32[]{:S(2)}, u32[]{:S(2)}) collective-permute-start(bf16[66,16,128]{2,1,0:T(8,128)(2,1)S(1)} %constant_dynamic-update-slice_fusion.refs_0_), channel_id=1, source_target_pairs={{0,16},{4,20},{8,24},{12,28},{16,0},{20,4},{24,8},{28,12},{1,17},{... | collective-permute-start | bytes 811016 | tf_op jit(solution)/shard_map/panel_rows/ppermute | solution.py:484
  25.8 3.3 %mix_panel.3 = (bf16[2,32,16,128]{3,2,1,0:T(8,128)(2,1)S(1)}, bf16[2,32,16,128]{3,2,1,0:T(8,128)(2,1)S(1)}, bf16[2,32,16,128]{3,2,1,0:T(8,128)(2,1)S(1)}, bf16[2,32,16,128]{3,2,1,0:T(8,128)(2,1)S(1)}) custom-call(s32[2,32]{1,0:T(2,128)S(1)} %pad_add_fusion.1.names_ref, s32[11]{0:T(128)S(1)} %stack.56.order_ref.after_ref, f32[4096,1024]{1,0:T(8,128)} %matrix_ref.11, ...), custom_call_target="tpu_custom_call" | custom-call | flops 1000000 | bytes 100000 | tf_op jit(solution)/shard_map/panel_mix/mix_panel/pallas_call | solution.py:85
  29.1 1.3 %collective-permute-start.5 = (bf16[2,32,16,128]{3,2,1,0:T(8,128)(2,1)S(1)}, bf16[2,32,16,128]{3,2,1,0:T(8,128)(2,1)S(1)}, u32[]{:S(2)}, u32[]{:S(2)}) collective-permute-start(bf16[2,32,16,128]{3,2,1,0:T(8,128)(2,1)S(1)} %get-tuple-element.49), channel_id=1, source_target_pairs={{0,1},{4,5},{8,9},{12,13},{16,17},{20,21},{24,25},{28,29}} | collective-permute-start | bytes 786440 | tf_op jit(solution)/shard_map/panel_spread/ppermute | solution.py:509
  30.4 1.3 %collective-permute-start.6 = (bf16[2,32,16,128]{3,2,1,0:T(8,128)(2,1)S(1)}, bf16[2,32,16,128]{3,2,1,0:T(8,128)(2,1)S(1)}, u32[]{:S(2)}, u32[]{:S(2)}) collective-permute-start(bf16[2,32,16,128]{3,2,1,0:T(8,128)(2,1)S(1)} %get-tuple-element.50), channel_id=1, source_target_pairs={{0,2},{4,6},{8,10},{12,14},{16,18},{20,22},{24,26},{28,30}} | collective-permute-start | bytes 786440 | tf_op jit(solution)/shard_map/panel_spread/ppermute | solution.py:509
  31.7 4.0 %collective-permute-start.7 = (bf16[2,32,16,128]{3,2,1,0:T(8,128)(2,1)S(1)}, bf16[2,32,16,128]{3,2,1,0:T(8,128)(2,1)S(1)}, u32[]{:S(2)}, u32[]{:S(2)}) collective-permute-start(bf16[2,32,16,128]{3,2,1,0:T(8,128)(2,1)S(1)} %get-tuple-element.51), channel_id=1, source_target_pairs={{0,3},{4,7},{8,11},{12,15},{16,19},{20,23},{24,27},{28,31}} | collective-permute-start | bytes 786440 | tf_op jit(solution)/shard_map/panel_spread/ppermute | solution.py:509
  35.7 1.6 %collective-permute-start.9 = (bf16[66,16,128]{2,1,0:T(8,128)(2,1)S(1)}, bf16[66,16,128]{2,1,0:T(8,128)(2,1)S(1)}, u32[]{:S(2)}, u32[]{:S(2)}) collective-permute-start(bf16[66,16,128]{2,1,0:T(8,128)(2,1)S(1)} %constant_dynamic-update-slice_fusion.refs_0_), channel_id=1, source_target_pairs={{0,8},{4,12},{8,0},{12,4},{16,24},{20,28},{24,16},{28,20},{1,9},{5... | collective-permute-start | bytes 811016 | tf_op jit(solution)/shard_map/panel_rows/ppermute | solution.py:484
  37.4 1.1 collective-permute-done.4.after_ref.refs_1_
  38.5 0.7 collective-permute-start.10
  39.2 2.7 %collective-permute-done.7.refs_3_ = bf16[2,32,16,128]{3,2,1,0:T(8,128)(2,1)S(1)} collective-permute-done((bf16[2,32,16,128]{3,2,1,0:T(8,128)(2,1)S(1)}, bf16[2,32,16,128]{3,2,1,0:T(8,128)(2,1)S(1)}, u32[]{:S(2)}, u32[]{:S(2)}) %collective-permute-start.7) | collective-permute-done | bytes 262176 | tf_op jit(solution)/shard_map/panel_spread/ppermute | solution.py:509
  41.8 0.8 pick.3
  42.7 1.3 %collective-permute-done.8 = bf16[32,16,128]{2,1,0:T(8,128)(2,1)S(1)} collective-permute-done((bf16[32,16,128]{2,1,0:T(8,128)(2,1)S(1)}, bf16[32,16,128]{2,1,0:T(8,128)(2,1)S(1)}, u32[]{:S(2)}, u32[]{:S(2)}) %collective-permute-start.8) | collective-permute-done | bytes 131104 | tf_op jit(solution)/shard_map/panel_spread/ppermute | solution.py:478
  44.0 1.4 %collective-permute-start.13 = (bf16[64,16,128]{2,1,0:T(8,128)(2,1)S(1)}, bf16[64,16,128]{2,1,0:T(8,128)(2,1)S(1)}, u32[]{:S(2)}, u32[]{:S(2)}) collective-permute-start(bf16[64,16,128]{2,1,0:T(8,128)(2,1)S(1)} %constant_dynamic-update-slice_fusion.2.after_ref.refs_0_), channel_id=1, source_target_pairs={{0,24},{4,28},{8,16},{12,20},{16,8},{20,12},{24,0},{28,4},{1,25},{... | collective-permute-start | bytes 786440 | tf_op jit(solution)/shard_map/panel_rows/ppermute | solution.py:484
  45.8 2.7 %collective-permute-start.11 = (bf16[64,16,128]{2,1,0:T(8,128)(2,1)S(1)}, bf16[64,16,128]{2,1,0:T(8,128)(2,1)S(1)}, u32[]{:S(2)}, u32[]{:S(2)}) collective-permute-start(bf16[64,16,128]{2,1,0:T(8,128)(2,1)S(1)} %constant_dynamic-update-slice_fusion.2.after_ref.refs_0_), channel_id=1, source_target_pairs={{0,16},{4,20},{8,24},{12,28},{16,0},{20,4},{24,8},{28,12},{1,17},{... | collective-permute-start | bytes 786440 | tf_op jit(solution)/shard_map/panel_rows/ppermute | solution.py:484
  48.5 4.1 %mix_tiles.6 = (bf16[1024,1024]{1,0:T(8,128)(2,1)S(1)}, f32[8,128]{1,0:T(8,128)S(1)}) custom-call(s32[2,32]{1,0:T(2,128)S(1)} %pad_add_fusion.1.names_ref, f32[4096,1024]{1,0:T(8,128)} %matrix_ref.11, f32[8,128,128]{2,1,0:T(8,128)S(1)} %copy-done.1, bf16[64,16,128]{2,1,0:T(8,128)(2,1)S(1)} %constant_dynamic-update-slice_fusion.2.after_ref.refs_0_), custom_call_target="tpu_custom_call" | custom-call | flops 1000000 | bytes 100000 | tf_op jit(solution)/shard_map/mix/mix_tiles/pallas_call | solution.py:117
  52.6 4.1 %mix_tiles.7 = (bf16[1024,1024]{1,0:T(8,128)(2,1)S(1)}, f32[8,128]{1,0:T(8,128)S(1)}) custom-call(s32[2,32]{1,0:T(2,128)S(1)} %pad_add_fusion.1.names_ref, f32[4096,1024]{1,0:T(8,128)} %matrix_ref.11, f32[8,128,128]{2,1,0:T(8,128)S(1)} %copy-done.1, f32[8,128]{1,0:T(8,128)S(1)} %get-tuple-element.54.after_ref), custom_call_target="tpu_custom_call" | custom-call | flops 1000000 | bytes 100000 | tf_op jit(solution)/shard_map/mix/mix_tiles/pallas_call | solution.py:117
  56.8 3.6 %first_sum.1 = (f32[64,16,128]{2,1,0:T(8,128)S(1)}, s32[8,8,128]{2,1,0:T(8,128)S(1)}) custom-call(f32[8,128]{1,0:T(8,128)S(1)} %get-tuple-element.55.after_ref, bf16[66,16,128]{2,1,0:T(8,128)(2,1)S(1)} %constant_dynamic-update-slice_fusion.refs_0_, bf16[66,16,128]{2,1,0:T(8,128)(2,1)S(1)} %collective-permute-done.4.after_ref.refs_1_, ...), custom_call_target="tpu_custom_call" | custom-call | flops 1000000 | bytes 100000 | tf_op jit(solution)/shard_map/panel_sum/first_sum/pallas_call | solution.py:201
  60.4 3.4 %collective-permute-start.16 = (f16[64,16,128]{2,1,0:T(8,128)(2,1)S(1)}, f16[64,16,128]{2,1,0:T(8,128)(2,1)S(1)}, u32[]{:S(2)}, u32[]{:S(2)}) collective-permute-start(f16[64,16,128]{2,1,0:T(8,128)(2,1)S(1)} %get-tuple-element.76), channel_id=1, source_target_pairs={{0,3},{1,2},{2,1},{3,0},{4,7},{5,6},{6,5},{7,4},{8,11},{9,10},{10,... | collective-permute-start | bytes 786440 | tf_op jit(solution)/shard_map/panel_cols/ppermute | solution.py:487
  63.9 0.6 collective-permute-start.14
  64.5 5.8 %collective-permute-done.11.refs_1_ = bf16[64,16,128]{2,1,0:T(8,128)(2,1)S(1)} collective-permute-done((bf16[64,16,128]{2,1,0:T(8,128)(2,1)S(1)}, bf16[64,16,128]{2,1,0:T(8,128)(2,1)S(1)}, u32[]{:S(2)}, u32[]{:S(2)}) %collective-permute-start.11) | collective-permute-done | bytes 262176 | tf_op jit(solution)/shard_map/panel_rows/ppermute | solution.py:484
  70.3 3.5 %next_sum.1.after_ref = f32[64,16,128]{2,1,0:T(8,128)S(1)} custom-call(s32[8,8,128]{2,1,0:T(8,128)S(1)} %get-tuple-element.56.names, f32[64,16,128]{2,1,0:T(8,128)S(1)} %get-tuple-element.57.after_ref, bf16[64,16,128]{2,1,0:T(8,128)(2,1)S(1)} %constant_dynamic-update-slice_fusion.2.after_ref.refs_0_, ...), custom_call_target="tpu_custom_call" | custom-call | flops 1000000 | bytes 100000 | tf_op jit(solution)/shard_map/panel_sum/next_sum/pallas_call | solution.py:220
  74.0 1.3 %collective-permute-done.15 = f16[64,16,128]{2,1,0:T(8,128)(2,1)S(1)} collective-permute-done((f16[64,16,128]{2,1,0:T(8,128)(2,1)S(1)}, f16[64,16,128]{2,1,0:T(8,128)(2,1)S(1)}, u32[]{:S(2)}, u32[]{:S(2)}) %collective-permute-start.15) | collective-permute-done | bytes 262176 | tf_op jit(solution)/shard_map/panel_cols/ppermute | solution.py:487
  75.3 0.5 collective-permute-start.18
  75.8 2.2 %collective-permute-start.23 = (f16[64,16,128]{2,1,0:T(8,128)(2,1)S(1)}, f16[64,16,128]{2,1,0:T(8,128)(2,1)S(1)}, u32[]{:S(2)}, u32[]{:S(2)}) collective-permute-start(f16[64,16,128]{2,1,0:T(8,128)(2,1)S(1)} %convert_element_type.69), channel_id=1, source_target_pairs={{0,3},{1,2},{2,1},{3,0},{4,7},{5,6},{6,5},{7,4},{8,11},{9,10},{10,... | collective-permute-start | bytes 786440 | tf_op jit(solution)/shard_map/panel_cols/ppermute | solution.py:487
  78.1 0.6 collective-permute-start.22
  78.6 0.8 collective-permute-start.21
  79.7 4.5 %cross_parts.2 = (f32[64,128,128]{2,1,0:T(8,128)S(1)}, f32[4,128,128]{2,1,0:T(8,128)S(1)}, f32[4,128,128]{2,1,0:T(8,128)S(1)}) custom-call(s32[3,32]{1,0:T(4,128)S(1)} %get-tuple-element.81.names_ref, s32[11]{0:T(128)S(1)} %stack.56.order_ref.after_ref, f32[64,16,128]{2,1,0:T(8,128)S(1)} %next_sum.1.after_ref, ...), custom_call_target="tpu_custom_call" | custom-call | flops 1000000 | bytes 100000 | tf_op jit(solution)/shard_map/cross0/cross_parts/pallas_call | solution.py:305
  84.2 2.5 %first_gram.1.block_ref = f32[128,128]{1,0:T(8,128)S(1)} custom-call(f32[4,128,128]{2,1,0:T(8,128)S(1)} %get-tuple-element.63.after_ref.refs_12_, f32[64,128,128]{2,1,0:T(8,128)S(1)} %get-tuple-element.64.panel.panel0), custom_call_target="tpu_custom_call" | custom-call | flops 1000000 | bytes 100000 | tf_op jit(solution)/shard_map/factor0/first_gram/pallas_call | solution.py:390
  86.8 6.1 %first_factor.1.after_ref.inverse_ref = f32[128,128]{1,0:T(8,128)S(1)} custom-call(f32[128,128]{1,0:T(8,128)S(1)} %first_gram.1.block_ref), custom_call_target="tpu_custom_call" | custom-call | flops 1000000 | bytes 100000 | tf_op jit(solution)/shard_map/factor0/first_factor/pallas_call | solution.py:407
  93.0 0.5 collective-permute-start.25
  93.6 0.4 collective-permute-start.27
  95.7 4.8 %cross_parts.3 = (f32[64,128,128]{2,1,0:T(8,128)S(1)}, f32[4,256,128]{2,1,0:T(8,128)S(1)}, f32[4,256,128]{2,1,0:T(8,128)S(1)}) custom-call(s32[3,32]{1,0:T(4,128)S(1)} %get-tuple-element.81.names_ref, s32[11]{0:T(128)S(1)} %stack.56.order_ref.after_ref, f32[128,128]{1,0:T(8,128)S(1)} %first_factor.1.after_ref.inverse_ref, ...), custom_call_target="tpu_custom_call" | custom-call | flops 1000000 | bytes 100000 | tf_op jit(solution)/shard_map/cross1/cross_parts/pallas_call | solution.py:305
  100.7 1.8 %collective-permute-done.28 = f32[4,256,128]{2,1,0:T(8,128)S(1)} collective-permute-done((f32[4,256,128]{2,1,0:T(8,128)S(1)}, f32[4,256,128]{2,1,0:T(8,128)S(1)}, u32[]{:S(2)}, u32[]{:S(2)}) %collective-permute-start.28) | collective-permute-done | bytes 524320 | tf_op jit(solution)/shard_map/cross_sum/ppermute | solution.py:478
  102.5 0.7 collective-permute-start.29
  103.2 3.2 %collective-permute-start.31 = (f32[256,128]{1,0:T(8,128)S(1)}, f32[256,128]{1,0:T(8,128)S(1)}, u32[]{:S(2)}, u32[]{:S(2)}) collective-permute-start(f32[256,128]{1,0:T(8,128)S(1)} %get-tuple-element.78), channel_id=1, source_target_pairs={{0,24},{4,28},{8,0},{12,4},{16,8},{20,12},{24,16},{28,20},{1,25},{... | collective-permute-start | bytes 393224 | tf_op jit(solution)/shard_map/cross_sum/ppermute | solution.py:481
  106.4 3.5 %second_gram.1 = (f32[128,128]{1,0:T(8,128)S(1)}, f32[128,128]{1,0:T(8,128)S(1)}) custom-call(f32[4,256,128]{2,1,0:T(8,128)S(1)} %get-tuple-element.70.after_ref, f32[64,128,128]{2,1,0:T(8,128)S(1)} %get-tuple-element.64.panel.panel0, f32[64,128,128]{2,1,0:T(8,128)S(1)} %get-tuple-element.72.panel1), custom_call_target="tpu_custom_call" | custom-call | flops 1000000 | bytes 100000 | tf_op jit(solution)/shard_map/gram1/second_gram/pallas_call | solution.py:436
  109.9 6.9 %second_factor.1 = f32[256,256]{1,0:T(8,128)S(1)} custom-call(f32[4,256,128]{2,1,0:T(8,128)S(1)} %add.52.after_ref, f32[128,128]{1,0:T(8,128)S(1)} %get-tuple-element.73.side_ref, f32[128,128]{1,0:T(8,128)S(1)} %get-tuple-element.74.block_ref, f32[128,128]{1,0:T(8,128)S(1)} %first_factor.1.after_ref.inverse_ref), custom_call_target="tpu_custom_call" | custom-call | flops 1000000 | bytes 100000 | tf_op jit(solution)/shard_map/factor1/second_factor/pallas_call | solution.py:459
  117.3 10.7 %all_to_all.19 = f32[8,32,128]{2,1,0:T(8,128)S(1)} all-to-all(f32[8,32,128]{2,1,0:T(8,128)S(1)} %bitcast.39), channel_id=1, replica_groups=mesh['rows'=8,'cols'=4] {'rows'}, dimensions={0} | all-to-all | bytes 262144 | tf_op jit(solution)/shard_map/solve/all_to_all | solution.py:583
  127.9 0.7 copy_bitcast_fusion
  (71 shorter events, 3.9 us)
Async XLA Ops:
  0.8 1.0 copy-start
  1.8 10.8 %copy-start.3 = (s32[32]{0:T(128)S(1)}, s32[32]{0:T(128)}, u32[]{:S(2)}) copy-start(s32[32]{0:T(128)} %param.9) | copy-start | bytes 388
  1.8 10.8 %copy-start.2 = (s32[32,2]{0,1:T(2,128)S(1)}, s32[32,2]{0,1:T(2,128)}, u32[]{:S(2)}) copy-start(s32[32,2]{0,1:T(2,128)} %param.7) | copy-start | bytes 772
  1.8 10.8 %copy-start.1 = (f32[8,128,128]{2,1,0:T(8,128)S(1)}, f32[8,128,128]{2,1,0:T(8,128)}, u32[]{:S(2)}) copy-start(f32[8,128,128]{2,1,0:T(8,128)} %mixers_ref.11) | copy-start | bytes 1572868
  5.1 15.8 %collective-permute-start = (bf16[2,32,16,128]{3,2,1,0:T(8,128)(2,1)S(1)}, bf16[2,32,16,128]{3,2,1,0:T(8,128)(2,1)S(1)}, u32[]{:S(2)}, u32[]{:S(2)}) collective-permute-start(bf16[2,32,16,128]{3,2,1,0:T(8,128)(2,1)S(1)} %get-tuple-element.43), channel_id=1, source_target_pairs={{0,1},{4,5},{8,9},{12,13},{16,17},{20,21},{24,25},{28,29}} | collective-permute-start | bytes 786440 | tf_op jit(solution)/shard_map/panel_spread/ppermute | solution.py:509
  10.0 11.0 %collective-permute-start.1 = (bf16[2,32,16,128]{3,2,1,0:T(8,128)(2,1)S(1)}, bf16[2,32,16,128]{3,2,1,0:T(8,128)(2,1)S(1)}, u32[]{:S(2)}, u32[]{:S(2)}) collective-permute-start(bf16[2,32,16,128]{3,2,1,0:T(8,128)(2,1)S(1)} %get-tuple-element.44), channel_id=1, source_target_pairs={{0,2},{4,6},{8,10},{12,14},{16,18},{20,22},{24,26},{28,30}} | collective-permute-start | bytes 786440 | tf_op jit(solution)/shard_map/panel_spread/ppermute | solution.py:509
  11.3 9.8 %collective-permute-start.2 = (bf16[2,32,16,128]{3,2,1,0:T(8,128)(2,1)S(1)}, bf16[2,32,16,128]{3,2,1,0:T(8,128)(2,1)S(1)}, u32[]{:S(2)}, u32[]{:S(2)}) collective-permute-start(bf16[2,32,16,128]{3,2,1,0:T(8,128)(2,1)S(1)} %get-tuple-element.45), channel_id=1, source_target_pairs={{0,3},{4,7},{8,11},{12,15},{16,19},{20,23},{24,27},{28,31}} | collective-permute-start | bytes 786440 | tf_op jit(solution)/shard_map/panel_spread/ppermute | solution.py:509
  21.7 1.4 %collective-permute-start.3 = (bf16[33,16,128]{2,1,0:T(8,128)(2,1)S(1)}, bf16[33,16,128]{2,1,0:T(8,128)(2,1)S(1)}, u32[]{:S(2)}, u32[]{:S(2)}) collective-permute-start(bf16[33,16,128]{2,1,0:T(8,128)(2,1)S(1)} %get-tuple-element.47), channel_id=1, source_target_pairs={{0,4},{4,0},{8,12},{12,8},{16,20},{20,16},{24,28},{28,24},{1,5},{5... | collective-permute-start | bytes 405512 | tf_op jit(solution)/shard_map/panel_spread/ppermute | solution.py:478
  23.1 15.3 %collective-permute-start.4 = (bf16[66,16,128]{2,1,0:T(8,128)(2,1)S(1)}, bf16[66,16,128]{2,1,0:T(8,128)(2,1)S(1)}, u32[]{:S(2)}, u32[]{:S(2)}) collective-permute-start(bf16[66,16,128]{2,1,0:T(8,128)(2,1)S(1)} %constant_dynamic-update-slice_fusion.refs_0_), channel_id=1, source_target_pairs={{0,16},{4,20},{8,24},{12,28},{16,0},{20,4},{24,8},{28,12},{1,17},{... | collective-permute-start | bytes 811016 | tf_op jit(solution)/shard_map/panel_rows/ppermute | solution.py:484
  29.1 10.1 %collective-permute-start.5 = (bf16[2,32,16,128]{3,2,1,0:T(8,128)(2,1)S(1)}, bf16[2,32,16,128]{3,2,1,0:T(8,128)(2,1)S(1)}, u32[]{:S(2)}, u32[]{:S(2)}) collective-permute-start(bf16[2,32,16,128]{3,2,1,0:T(8,128)(2,1)S(1)} %get-tuple-element.49), channel_id=1, source_target_pairs={{0,1},{4,5},{8,9},{12,13},{16,17},{20,21},{24,25},{28,29}} | collective-permute-start | bytes 786440 | tf_op jit(solution)/shard_map/panel_spread/ppermute | solution.py:509
  30.4 8.8 %collective-permute-start.6 = (bf16[2,32,16,128]{3,2,1,0:T(8,128)(2,1)S(1)}, bf16[2,32,16,128]{3,2,1,0:T(8,128)(2,1)S(1)}, u32[]{:S(2)}, u32[]{:S(2)}) collective-permute-start(bf16[2,32,16,128]{3,2,1,0:T(8,128)(2,1)S(1)} %get-tuple-element.50), channel_id=1, source_target_pairs={{0,2},{4,6},{8,10},{12,14},{16,18},{20,22},{24,26},{28,30}} | collective-permute-start | bytes 786440 | tf_op jit(solution)/shard_map/panel_spread/ppermute | solution.py:509
  31.7 10.2 %collective-permute-start.7 = (bf16[2,32,16,128]{3,2,1,0:T(8,128)(2,1)S(1)}, bf16[2,32,16,128]{3,2,1,0:T(8,128)(2,1)S(1)}, u32[]{:S(2)}, u32[]{:S(2)}) collective-permute-start(bf16[2,32,16,128]{3,2,1,0:T(8,128)(2,1)S(1)} %get-tuple-element.51), channel_id=1, source_target_pairs={{0,3},{4,7},{8,11},{12,15},{16,19},{20,23},{24,27},{28,31}} | collective-permute-start | bytes 786440 | tf_op jit(solution)/shard_map/panel_spread/ppermute | solution.py:509
  35.7 21.0 %collective-permute-start.9 = (bf16[66,16,128]{2,1,0:T(8,128)(2,1)S(1)}, bf16[66,16,128]{2,1,0:T(8,128)(2,1)S(1)}, u32[]{:S(2)}, u32[]{:S(2)}) collective-permute-start(bf16[66,16,128]{2,1,0:T(8,128)(2,1)S(1)} %constant_dynamic-update-slice_fusion.refs_0_), channel_id=1, source_target_pairs={{0,8},{4,12},{8,0},{12,4},{16,24},{20,28},{24,16},{28,20},{1,9},{5... | collective-permute-start | bytes 811016 | tf_op jit(solution)/shard_map/panel_rows/ppermute | solution.py:484
  38.5 18.3 %collective-permute-start.10 = (bf16[66,16,128]{2,1,0:T(8,128)(2,1)S(1)}, bf16[66,16,128]{2,1,0:T(8,128)(2,1)S(1)}, u32[]{:S(2)}, u32[]{:S(2)}) collective-permute-start(bf16[66,16,128]{2,1,0:T(8,128)(2,1)S(1)} %collective-permute-done.4.after_ref.refs_1_), channel_id=1, source_target_pairs={{0,8},{4,12},{8,0},{12,4},{16,24},{20,28},{24,16},{28,20},{1,9},{5... | collective-permute-start | bytes 811016 | tf_op jit(solution)/shard_map/panel_rows/ppermute | solution.py:484
  42.6 1.4 %collective-permute-start.8 = (bf16[32,16,128]{2,1,0:T(8,128)(2,1)S(1)}, bf16[32,16,128]{2,1,0:T(8,128)(2,1)S(1)}, u32[]{:S(2)}, u32[]{:S(2)}) collective-permute-start(bf16[32,16,128]{2,1,0:T(8,128)(2,1)S(1)} %get-tuple-element.53), channel_id=1, source_target_pairs={{0,4},{4,0},{8,12},{12,8},{16,20},{20,16},{24,28},{28,24},{1,5},{5... | collective-permute-start | bytes 393224 | tf_op jit(solution)/shard_map/panel_spread/ppermute | solution.py:478
  44.0 19.8 %collective-permute-start.13 = (bf16[64,16,128]{2,1,0:T(8,128)(2,1)S(1)}, bf16[64,16,128]{2,1,0:T(8,128)(2,1)S(1)}, u32[]{:S(2)}, u32[]{:S(2)}) collective-permute-start(bf16[64,16,128]{2,1,0:T(8,128)(2,1)S(1)} %constant_dynamic-update-slice_fusion.2.after_ref.refs_0_), channel_id=1, source_target_pairs={{0,24},{4,28},{8,16},{12,20},{16,8},{20,12},{24,0},{28,4},{1,25},{... | collective-permute-start | bytes 786440 | tf_op jit(solution)/shard_map/panel_rows/ppermute | solution.py:484
  45.5 19.1 %collective-permute-start.12 = (bf16[64,16,128]{2,1,0:T(8,128)(2,1)S(1)}, bf16[64,16,128]{2,1,0:T(8,128)(2,1)S(1)}, u32[]{:S(2)}, u32[]{:S(2)}) collective-permute-start(bf16[64,16,128]{2,1,0:T(8,128)(2,1)S(1)} %constant_dynamic-update-slice_fusion.2.after_ref.refs_0_), channel_id=1, source_target_pairs={{0,8},{4,12},{8,0},{12,4},{16,24},{20,28},{24,16},{28,20},{1,9},{5... | collective-permute-start | bytes 786440 | tf_op jit(solution)/shard_map/panel_rows/ppermute | solution.py:484
  45.8 24.6 %collective-permute-start.11 = (bf16[64,16,128]{2,1,0:T(8,128)(2,1)S(1)}, bf16[64,16,128]{2,1,0:T(8,128)(2,1)S(1)}, u32[]{:S(2)}, u32[]{:S(2)}) collective-permute-start(bf16[64,16,128]{2,1,0:T(8,128)(2,1)S(1)} %constant_dynamic-update-slice_fusion.2.after_ref.refs_0_), channel_id=1, source_target_pairs={{0,16},{4,20},{8,24},{12,28},{16,0},{20,4},{24,8},{28,12},{1,17},{... | collective-permute-start | bytes 786440 | tf_op jit(solution)/shard_map/panel_rows/ppermute | solution.py:484
  60.4 13.5 %collective-permute-start.16 = (f16[64,16,128]{2,1,0:T(8,128)(2,1)S(1)}, f16[64,16,128]{2,1,0:T(8,128)(2,1)S(1)}, u32[]{:S(2)}, u32[]{:S(2)}) collective-permute-start(f16[64,16,128]{2,1,0:T(8,128)(2,1)S(1)} %get-tuple-element.76), channel_id=1, source_target_pairs={{0,3},{1,2},{2,1},{3,0},{4,7},{5,6},{6,5},{7,4},{8,11},{9,10},{10,... | collective-permute-start | bytes 786440 | tf_op jit(solution)/shard_map/panel_cols/ppermute | solution.py:487
  63.9 11.4 %collective-permute-start.15 = (f16[64,16,128]{2,1,0:T(8,128)(2,1)S(1)}, f16[64,16,128]{2,1,0:T(8,128)(2,1)S(1)}, u32[]{:S(2)}, u32[]{:S(2)}) collective-permute-start(f16[64,16,128]{2,1,0:T(8,128)(2,1)S(1)} %get-tuple-element.76), channel_id=1, source_target_pairs={{0,2},{1,3},{2,0},{3,1},{4,6},{5,7},{6,4},{7,5},{8,10},{9,11},{10,... | collective-permute-start | bytes 786440 | tf_op jit(solution)/shard_map/panel_cols/ppermute | solution.py:487
  63.9 11.4 %collective-permute-start.14 = (f16[64,16,128]{2,1,0:T(8,128)(2,1)S(1)}, f16[64,16,128]{2,1,0:T(8,128)(2,1)S(1)}, u32[]{:S(2)}, u32[]{:S(2)}) collective-permute-start(f16[64,16,128]{2,1,0:T(8,128)(2,1)S(1)} %get-tuple-element.76), channel_id=1, source_target_pairs={{0,1},{1,0},{2,3},{3,2},{4,5},{5,4},{6,7},{7,6},{8,9},{9,8},{10,11... | collective-permute-start | bytes 786440 | tf_op jit(solution)/shard_map/panel_cols/ppermute | solution.py:487
  64.5 13.5 %collective-permute-start.17 = (f16[64,16,128]{2,1,0:T(8,128)(2,1)S(1)}, f16[64,16,128]{2,1,0:T(8,128)(2,1)S(1)}, u32[]{:S(2)}, u32[]{:S(2)}) collective-permute-start(f16[64,16,128]{2,1,0:T(8,128)(2,1)S(1)} %get-tuple-element.76), channel_id=1, source_target_pairs={{0,4},{4,0},{8,12},{12,8},{16,20},{20,16},{24,28},{28,24},{1,5},{5... | collective-permute-start | bytes 786440 | tf_op jit(solution)/shard_map/panel_cores/ppermute | solution.py:478
  73.9 4.7 %collective-permute-start.20 = (f16[64,16,128]{2,1,0:T(8,128)(2,1)S(1)}, f16[64,16,128]{2,1,0:T(8,128)(2,1)S(1)}, u32[]{:S(2)}, u32[]{:S(2)}) collective-permute-start(f16[64,16,128]{2,1,0:T(8,128)(2,1)S(1)} %collective-permute-done.16), channel_id=1, source_target_pairs={{0,4},{4,0},{8,12},{12,8},{16,20},{20,16},{24,28},{28,24},{1,5},{5... | collective-permute-start | bytes 786440 | tf_op jit(solution)/shard_map/panel_cores/ppermute | solution.py:478
  75.3 4.3 %collective-permute-start.19 = (f16[64,16,128]{2,1,0:T(8,128)(2,1)S(1)}, f16[64,16,128]{2,1,0:T(8,128)(2,1)S(1)}, u32[]{:S(2)}, u32[]{:S(2)}) collective-permute-start(f16[64,16,128]{2,1,0:T(8,128)(2,1)S(1)} %collective-permute-done.15), channel_id=1, source_target_pairs={{0,4},{4,0},{8,12},{12,8},{16,20},{20,16},{24,28},{28,24},{1,5},{5... | collective-permute-start | bytes 786440 | tf_op jit(solution)/shard_map/panel_cores/ppermute | solution.py:478
  75.3 4.4 %collective-permute-start.18 = (f16[64,16,128]{2,1,0:T(8,128)(2,1)S(1)}, f16[64,16,128]{2,1,0:T(8,128)(2,1)S(1)}, u32[]{:S(2)}, u32[]{:S(2)}) collective-permute-start(f16[64,16,128]{2,1,0:T(8,128)(2,1)S(1)} %collective-permute-done.14), channel_id=1, source_target_pairs={{0,4},{4,0},{8,12},{12,8},{16,20},{20,16},{24,28},{28,24},{1,5},{5... | collective-permute-start | bytes 786440 | tf_op jit(solution)/shard_map/panel_cores/ppermute | solution.py:478
  75.8 17.1 %collective-permute-start.23 = (f16[64,16,128]{2,1,0:T(8,128)(2,1)S(1)}, f16[64,16,128]{2,1,0:T(8,128)(2,1)S(1)}, u32[]{:S(2)}, u32[]{:S(2)}) collective-permute-start(f16[64,16,128]{2,1,0:T(8,128)(2,1)S(1)} %convert_element_type.69), channel_id=1, source_target_pairs={{0,3},{1,2},{2,1},{3,0},{4,7},{5,6},{6,5},{7,4},{8,11},{9,10},{10,... | collective-permute-start | bytes 786440 | tf_op jit(solution)/shard_map/panel_cols/ppermute | solution.py:487
  78.1 14.8 %collective-permute-start.22 = (f16[64,16,128]{2,1,0:T(8,128)(2,1)S(1)}, f16[64,16,128]{2,1,0:T(8,128)(2,1)S(1)}, u32[]{:S(2)}, u32[]{:S(2)}) collective-permute-start(f16[64,16,128]{2,1,0:T(8,128)(2,1)S(1)} %convert_element_type.69), channel_id=1, source_target_pairs={{0,2},{1,3},{2,0},{3,1},{4,6},{5,7},{6,4},{7,5},{8,10},{9,11},{10,... | collective-permute-start | bytes 786440 | tf_op jit(solution)/shard_map/panel_cols/ppermute | solution.py:487
  78.6 14.3 %collective-permute-start.21 = (f16[64,16,128]{2,1,0:T(8,128)(2,1)S(1)}, f16[64,16,128]{2,1,0:T(8,128)(2,1)S(1)}, u32[]{:S(2)}, u32[]{:S(2)}) collective-permute-start(f16[64,16,128]{2,1,0:T(8,128)(2,1)S(1)} %convert_element_type.69), channel_id=1, source_target_pairs={{0,1},{1,0},{2,3},{3,2},{4,5},{5,4},{6,7},{7,6},{8,9},{9,8},{10,11... | collective-permute-start | bytes 786440 | tf_op jit(solution)/shard_map/panel_cols/ppermute | solution.py:487
  92.9 1.6 %collective-permute-start.24 = (f16[64,16,128]{2,1,0:T(8,128)(2,1)S(1)}, f16[64,16,128]{2,1,0:T(8,128)(2,1)S(1)}, u32[]{:S(2)}, u32[]{:S(2)}) collective-permute-start(f16[64,16,128]{2,1,0:T(8,128)(2,1)S(1)} %convert_element_type.69), channel_id=1, source_target_pairs={{0,4},{4,0},{8,12},{12,8},{16,20},{20,16},{24,28},{28,24},{1,5},{5... | collective-permute-start | bytes 786440 | tf_op jit(solution)/shard_map/panel_cores/ppermute | solution.py:478
  93.0 1.9 %collective-permute-start.25 = (f16[64,16,128]{2,1,0:T(8,128)(2,1)S(1)}, f16[64,16,128]{2,1,0:T(8,128)(2,1)S(1)}, u32[]{:S(2)}, u32[]{:S(2)}) collective-permute-start(f16[64,16,128]{2,1,0:T(8,128)(2,1)S(1)} %collective-permute-done.21), channel_id=1, source_target_pairs={{0,4},{4,0},{8,12},{12,8},{16,20},{20,16},{24,28},{28,24},{1,5},{5... | collective-permute-start | bytes 786440 | tf_op jit(solution)/shard_map/panel_cores/ppermute | solution.py:478
  93.5 1.8 %collective-permute-start.26 = (f16[64,16,128]{2,1,0:T(8,128)(2,1)S(1)}, f16[64,16,128]{2,1,0:T(8,128)(2,1)S(1)}, u32[]{:S(2)}, u32[]{:S(2)}) collective-permute-start(f16[64,16,128]{2,1,0:T(8,128)(2,1)S(1)} %collective-permute-done.22), channel_id=1, source_target_pairs={{0,4},{4,0},{8,12},{12,8},{16,20},{20,16},{24,28},{28,24},{1,5},{5... | collective-permute-start | bytes 786440 | tf_op jit(solution)/shard_map/panel_cores/ppermute | solution.py:478
  93.6 2.1 %collective-permute-start.27 = (f16[64,16,128]{2,1,0:T(8,128)(2,1)S(1)}, f16[64,16,128]{2,1,0:T(8,128)(2,1)S(1)}, u32[]{:S(2)}, u32[]{:S(2)}) collective-permute-start(f16[64,16,128]{2,1,0:T(8,128)(2,1)S(1)} %collective-permute-done.23), channel_id=1, source_target_pairs={{0,4},{4,0},{8,12},{12,8},{16,20},{20,16},{24,28},{28,24},{1,5},{5... | collective-permute-start | bytes 786440 | tf_op jit(solution)/shard_map/panel_cores/ppermute | solution.py:478
  100.5 2.0 %collective-permute-start.28 = (f32[4,256,128]{2,1,0:T(8,128)S(1)}, f32[4,256,128]{2,1,0:T(8,128)S(1)}, u32[]{:S(2)}, u32[]{:S(2)}) collective-permute-start(f32[4,256,128]{2,1,0:T(8,128)S(1)} %get-tuple-element.71), channel_id=1, source_target_pairs={{0,4},{4,0},{8,12},{12,8},{16,20},{20,16},{24,28},{28,24},{1,5},{5... | collective-permute-start | bytes 1572872 | tf_op jit(solution)/shard_map/cross_sum/ppermute | solution.py:478
  102.5 14.2 %collective-permute-start.29 = (f32[256,128]{1,0:T(8,128)S(1)}, f32[256,128]{1,0:T(8,128)S(1)}, u32[]{:S(2)}, u32[]{:S(2)}) collective-permute-start(f32[256,128]{1,0:T(8,128)S(1)} %get-tuple-element.77), channel_id=1, source_target_pairs={{0,8},{4,12},{8,16},{12,20},{16,24},{20,28},{24,0},{28,4},{1,9},{5... | collective-permute-start | bytes 393224 | tf_op jit(solution)/shard_map/cross_sum/ppermute | solution.py:481
  103.2 13.5 %collective-permute-start.31 = (f32[256,128]{1,0:T(8,128)S(1)}, f32[256,128]{1,0:T(8,128)S(1)}, u32[]{:S(2)}, u32[]{:S(2)}) collective-permute-start(f32[256,128]{1,0:T(8,128)S(1)} %get-tuple-element.78), channel_id=1, source_target_pairs={{0,24},{4,28},{8,0},{12,4},{16,8},{20,12},{24,16},{28,20},{1,25},{... | collective-permute-start | bytes 393224 | tf_op jit(solution)/shard_map/cross_sum/ppermute | solution.py:481
  106.4 10.5 %collective-permute-start.30 = (f32[256,128]{1,0:T(8,128)S(1)}, f32[256,128]{1,0:T(8,128)S(1)}, u32[]{:S(2)}, u32[]{:S(2)}) collective-permute-start(f32[256,128]{1,0:T(8,128)S(1)} %get-tuple-element.79), channel_id=1, source_target_pairs={{0,16},{4,20},{8,24},{12,28},{16,0},{20,4},{24,8},{28,12},{1,17},{... | collective-permute-start | bytes 393224 | tf_op jit(solution)/shard_map/cross_sum/ppermute | solution.py:481

commit v9 on v7

--- a/solution.py
+++ b/solution.py
@@ -513,12 +513,12 @@
             keep, give = pick(order, after, extra, got)
             return jnp.concatenate([keep, swap(give)])
 
-    def gather_rows(held):
+    def gather_rows(held, *after):
         with jax.named_scope("panel_rows"):
             if chips != 4:
                 return [held] + [shift(held, j) for j in range(1, chips)]
             far, near = beside(held, 2), beside(held, 1)
-            return [held, far, near, beside(far, 1)]
+            return [held, far, near, beside(before(far, *after) if after else far, 1)]
 
     def gather_cols(summed):
         with jax.named_scope("panel_cols"):
@@ -545,10 +545,10 @@
     held0 = spread(scatter(0), token, carried)
     arrived0 = gather_rows(held0)
     held1 = spread(scatter(1), arrived0[1])
-    arrived1 = gather_rows(held1)
     token = mix_next(held1, names.shape[1] // STEP - early)
     with jax.named_scope("panel_sum"):
         summed0, all_names = first_sum(token, arrived0)
+    arrived1 = gather_rows(held1, summed0)
     mine0 = gather_cols(summed0)
     with jax.named_scope("panel_sum"):
         summed1 = next_sum(all_names, summed0, arrived1)

time: 128 us -> 128 us (level)
  no operation moved by 1% of the time
where the time goes in v9:
time: 128 us; the launch traced here: 127 us
  Pallas kernels  59.7 us (47%)
  starting transfers between devices  34 us (27%)
  waiting for transfers between devices  20.4 us (16%)
  blocking collectives  9.17 us (7%)
  local copies, waits for them, and re-layouts  1.9 us (1%)
  other arithmetic  1.41 us (1%)
    pallas_call x4, Pallas kernels, mix_tiles(): pl.pallas_call(functools.partial(mix_kernel, per_step, start), grid_spec=...  16.5 us
    ppermute x6, starting transfers between devices, scatter(): lax.ppermute(slices[j], 'cols', [(0, j)])  14.1 us
    pallas_call x2, Pallas kernels, cross_parts(): pl.pallas_call(functools.partial(cross_kernel, steps, chips, len(before),...  9.3 us
    all_to_all x1, blocking collectives, local(): lax.all_to_all(solved, 'rows', split_axis=0, concat_axis=1, tiled=True)  9.17 us
    ppermute x6, starting transfers between devices, across(): return lax.ppermute(value, 'cols', [(i, i ^ j) for i in range(parts)])  7.22 us
    ppermute x6, starting transfers between devices, beside(): return lax.ppermute(value, 'rows', [(i, i ^ 2 * j) for i in range(rows_n)])  6.96 us
    pallas_call x1, Pallas kernels, second_factor(): pl.pallas_call(last_kernel, in_specs=[anywhere()] + [vmem()] * 3, out_spe...  6.86 us
    ppermute x6, waiting for transfers between devices, across(): return lax.ppermute(value, 'cols', [(i, i ^ j) for i in range(parts)])  6.66 us
  transfers between devices with their start and end apart: 32, of which 16 were waited for; matrix products, arithmetic and copies ran while one was open for 1% of the time, Pallas kernels for 40%

profile of v9, /device:TPU:0, one launch (start us, length us, event | category | flops | bytes accessed | tf_op | source)
XLA Modules:
  0.0 127.5 jit_solution(5215674346311493296)
XLA Ops:
  0.0 0.7 pad_add_fusion.1.names_ref
  0.8 1.0 copy-done
  1.8 3.3 %mix_panel.2 = (bf16[2,32,16,128]{3,2,1,0:T(8,128)(2,1)S(1)}, bf16[2,32,16,128]{3,2,1,0:T(8,128)(2,1)S(1)}, bf16[2,32,16,128]{3,2,1,0:T(8,128)(2,1)S(1)}, bf16[2,32,16,128]{3,2,1,0:T(8,128)(2,1)S(1)}) custom-call(s32[2,32]{1,0:T(2,128)S(1)} %pad_add_fusion.1.names_ref, s32[11]{0:T(128)S(1)} %stack.56.order_ref.after_ref, f32[4096,1024]{1,0:T(8,128)} %matrix_ref.11, ...), custom_call_target="tpu_custom_call" | custom-call | flops 1000000 | bytes 100000 | tf_op jit(solution)/shard_map/panel_mix/mix_panel/pallas_call | solution.py:85
  5.1 4.9 %collective-permute-start = (bf16[2,32,16,128]{3,2,1,0:T(8,128)(2,1)S(1)}, bf16[2,32,16,128]{3,2,1,0:T(8,128)(2,1)S(1)}, u32[]{:S(2)}, u32[]{:S(2)}) collective-permute-start(bf16[2,32,16,128]{3,2,1,0:T(8,128)(2,1)S(1)} %get-tuple-element.44), channel_id=1, source_target_pairs={{0,1},{4,5},{8,9},{12,13},{16,17},{20,21},{24,25},{28,29}} | collective-permute-start | bytes 786440 | tf_op jit(solution)/shard_map/panel_spread/ppermute | solution.py:509
  10.0 1.3 %collective-permute-start.1 = (bf16[2,32,16,128]{3,2,1,0:T(8,128)(2,1)S(1)}, bf16[2,32,16,128]{3,2,1,0:T(8,128)(2,1)S(1)}, u32[]{:S(2)}, u32[]{:S(2)}) collective-permute-start(bf16[2,32,16,128]{3,2,1,0:T(8,128)(2,1)S(1)} %get-tuple-element.45), channel_id=1, source_target_pairs={{0,2},{4,6},{8,10},{12,14},{16,18},{20,22},{24,26},{28,30}} | collective-permute-start | bytes 786440 | tf_op jit(solution)/shard_map/panel_spread/ppermute | solution.py:509
  11.3 1.3 %collective-permute-start.2 = (bf16[2,32,16,128]{3,2,1,0:T(8,128)(2,1)S(1)}, bf16[2,32,16,128]{3,2,1,0:T(8,128)(2,1)S(1)}, u32[]{:S(2)}, u32[]{:S(2)}) collective-permute-start(bf16[2,32,16,128]{3,2,1,0:T(8,128)(2,1)S(1)} %get-tuple-element.46), channel_id=1, source_target_pairs={{0,3},{4,7},{8,11},{12,15},{16,19},{20,23},{24,27},{28,31}} | collective-permute-start | bytes 786440 | tf_op jit(solution)/shard_map/panel_spread/ppermute | solution.py:509
  12.7 4.1 %mix_tiles.4 = (bf16[1024,1024]{1,0:T(8,128)(2,1)S(1)}, f32[8,128]{1,0:T(8,128)S(1)}) custom-call(s32[2,32]{1,0:T(2,128)S(1)} %pad_add_fusion.1.names_ref, f32[4096,1024]{1,0:T(8,128)} %matrix_ref.11, f32[8,128,128]{2,1,0:T(8,128)S(1)} %copy-done.1, bf16[2,32,16,128]{3,2,1,0:T(8,128)(2,1)S(1)} %get-tuple-element.41.after_ref.refs_1_), custom_call_target="tpu_custom_call" | custom-call | flops 1000000 | bytes 100000 | tf_op jit(solution)/shard_map/mix/mix_tiles/pallas_call | solution.py:117
  16.8 4.1 %mix_tiles.5 = (bf16[1024,1024]{1,0:T(8,128)(2,1)S(1)}, f32[8,128]{1,0:T(8,128)S(1)}) custom-call(s32[2,32]{1,0:T(2,128)S(1)} %pad_add_fusion.1.names_ref, f32[4096,1024]{1,0:T(8,128)} %matrix_ref.11, f32[8,128,128]{2,1,0:T(8,128)S(1)} %copy-done.1, f32[8,128]{1,0:T(8,128)S(1)} %get-tuple-element.42.after_ref), custom_call_target="tpu_custom_call" | custom-call | flops 1000000 | bytes 100000 | tf_op jit(solution)/shard_map/mix/mix_tiles/pallas_call | solution.py:117
  21.1 0.6 pick.2
  21.8 1.3 %collective-permute-done.3 = bf16[33,16,128]{2,1,0:T(8,128)(2,1)S(1)} collective-permute-done((bf16[33,16,128]{2,1,0:T(8,128)(2,1)S(1)}, bf16[33,16,128]{2,1,0:T(8,128)(2,1)S(1)}, u32[]{:S(2)}, u32[]{:S(2)}) %collective-permute-start.3) | collective-permute-done | bytes 135200 | tf_op jit(solution)/shard_map/panel_spread/ppermute | solution.py:478
  23.1 2.7 %collective-permute-start.4 = (bf16[66,16,128]{2,1,0:T(8,128)(2,1)S(1)}, bf16[66,16,128]{2,1,0:T(8,128)(2,1)S(1)}, u32[]{:S(2)}, u32[]{:S(2)}) collective-permute-start(bf16[66,16,128]{2,1,0:T(8,128)(2,1)S(1)} %constant_dynamic-update-slice_fusion.refs_0_), channel_id=1, source_target_pairs={{0,16},{4,20},{8,24},{12,28},{16,0},{20,4},{24,8},{28,12},{1,17},{... | collective-permute-start | bytes 811016 | tf_op jit(solution)/shard_map/panel_rows/ppermute | solution.py:484
  25.8 3.3 %mix_panel.3 = (bf16[2,32,16,128]{3,2,1,0:T(8,128)(2,1)S(1)}, bf16[2,32,16,128]{3,2,1,0:T(8,128)(2,1)S(1)}, bf16[2,32,16,128]{3,2,1,0:T(8,128)(2,1)S(1)}, bf16[2,32,16,128]{3,2,1,0:T(8,128)(2,1)S(1)}) custom-call(s32[2,32]{1,0:T(2,128)S(1)} %pad_add_fusion.1.names_ref, s32[11]{0:T(128)S(1)} %stack.56.order_ref.after_ref, f32[4096,1024]{1,0:T(8,128)} %matrix_ref.11, ...), custom_call_target="tpu_custom_call" | custom-call | flops 1000000 | bytes 100000 | tf_op jit(solution)/shard_map/panel_mix/mix_panel/pallas_call | solution.py:85
  29.1 1.3 %collective-permute-start.5 = (bf16[2,32,16,128]{3,2,1,0:T(8,128)(2,1)S(1)}, bf16[2,32,16,128]{3,2,1,0:T(8,128)(2,1)S(1)}, u32[]{:S(2)}, u32[]{:S(2)}) collective-permute-start(bf16[2,32,16,128]{3,2,1,0:T(8,128)(2,1)S(1)} %get-tuple-element.50), channel_id=1, source_target_pairs={{0,1},{4,5},{8,9},{12,13},{16,17},{20,21},{24,25},{28,29}} | collective-permute-start | bytes 786440 | tf_op jit(solution)/shard_map/panel_spread/ppermute | solution.py:509
  30.4 1.3 %collective-permute-start.6 = (bf16[2,32,16,128]{3,2,1,0:T(8,128)(2,1)S(1)}, bf16[2,32,16,128]{3,2,1,0:T(8,128)(2,1)S(1)}, u32[]{:S(2)}, u32[]{:S(2)}) collective-permute-start(bf16[2,32,16,128]{3,2,1,0:T(8,128)(2,1)S(1)} %get-tuple-element.51), channel_id=1, source_target_pairs={{0,2},{4,6},{8,10},{12,14},{16,18},{20,22},{24,26},{28,30}} | collective-permute-start | bytes 786440 | tf_op jit(solution)/shard_map/panel_spread/ppermute | solution.py:509
  31.7 4.0 %collective-permute-start.7 = (bf16[2,32,16,128]{3,2,1,0:T(8,128)(2,1)S(1)}, bf16[2,32,16,128]{3,2,1,0:T(8,128)(2,1)S(1)}, u32[]{:S(2)}, u32[]{:S(2)}) collective-permute-start(bf16[2,32,16,128]{3,2,1,0:T(8,128)(2,1)S(1)} %get-tuple-element.52), channel_id=1, source_target_pairs={{0,3},{4,7},{8,11},{12,15},{16,19},{20,23},{24,27},{28,31}} | collective-permute-start | bytes 786440 | tf_op jit(solution)/shard_map/panel_spread/ppermute | solution.py:509
  35.7 1.6 %collective-permute-start.9 = (bf16[66,16,128]{2,1,0:T(8,128)(2,1)S(1)}, bf16[66,16,128]{2,1,0:T(8,128)(2,1)S(1)}, u32[]{:S(2)}, u32[]{:S(2)}) collective-permute-start(bf16[66,16,128]{2,1,0:T(8,128)(2,1)S(1)} %constant_dynamic-update-slice_fusion.refs_0_), channel_id=1, source_target_pairs={{0,8},{4,12},{8,0},{12,4},{16,24},{20,28},{24,16},{28,20},{1,9},{5... | collective-permute-start | bytes 811016 | tf_op jit(solution)/shard_map/panel_rows/ppermute | solution.py:484
  37.4 1.1 collective-permute-done.4.after_ref.refs_1_
  38.5 0.7 collective-permute-start.10
  39.2 2.7 %collective-permute-done.7.refs_3_ = bf16[2,32,16,128]{3,2,1,0:T(8,128)(2,1)S(1)} collective-permute-done((bf16[2,32,16,128]{3,2,1,0:T(8,128)(2,1)S(1)}, bf16[2,32,16,128]{3,2,1,0:T(8,128)(2,1)S(1)}, u32[]{:S(2)}, u32[]{:S(2)}) %collective-permute-start.7) | collective-permute-done | bytes 262176 | tf_op jit(solution)/shard_map/panel_spread/ppermute | solution.py:509
  41.8 0.8 pick.3
  42.7 1.3 %collective-permute-done.8 = bf16[32,16,128]{2,1,0:T(8,128)(2,1)S(1)} collective-permute-done((bf16[32,16,128]{2,1,0:T(8,128)(2,1)S(1)}, bf16[32,16,128]{2,1,0:T(8,128)(2,1)S(1)}, u32[]{:S(2)}, u32[]{:S(2)}) %collective-permute-start.8) | collective-permute-done | bytes 131104 | tf_op jit(solution)/shard_map/panel_spread/ppermute | solution.py:478
  44.0 1.6 %collective-permute-start.12 = (bf16[64,16,128]{2,1,0:T(8,128)(2,1)S(1)}, bf16[64,16,128]{2,1,0:T(8,128)(2,1)S(1)}, u32[]{:S(2)}, u32[]{:S(2)}) collective-permute-start(bf16[64,16,128]{2,1,0:T(8,128)(2,1)S(1)} %constant_dynamic-update-slice_fusion.2.after_ref.refs_0_), channel_id=1, source_target_pairs={{0,8},{4,12},{8,0},{12,4},{16,24},{20,28},{24,16},{28,20},{1,9},{5... | collective-permute-start | bytes 786440 | tf_op jit(solution)/shard_map/panel_rows/ppermute | solution.py:484
  46.0 4.1 %mix_tiles.6 = (bf16[1024,1024]{1,0:T(8,128)(2,1)S(1)}, f32[8,128]{1,0:T(8,128)S(1)}) custom-call(s32[2,32]{1,0:T(2,128)S(1)} %pad_add_fusion.1.names_ref, f32[4096,1024]{1,0:T(8,128)} %matrix_ref.11, f32[8,128,128]{2,1,0:T(8,128)S(1)} %copy-done.1, bf16[64,16,128]{2,1,0:T(8,128)(2,1)S(1)} %constant_dynamic-update-slice_fusion.2.after_ref.refs_0_), custom_call_target="tpu_custom_call" | custom-call | flops 1000000 | bytes 100000 | tf_op jit(solution)/shard_map/mix/mix_tiles/pallas_call | solution.py:117
  50.2 4.1 %mix_tiles.7 = (bf16[1024,1024]{1,0:T(8,128)(2,1)S(1)}, f32[8,128]{1,0:T(8,128)S(1)}) custom-call(s32[2,32]{1,0:T(2,128)S(1)} %pad_add_fusion.1.names_ref, f32[4096,1024]{1,0:T(8,128)} %matrix_ref.11, f32[8,128,128]{2,1,0:T(8,128)S(1)} %copy-done.1, f32[8,128]{1,0:T(8,128)S(1)} %get-tuple-element.55.after_ref), custom_call_target="tpu_custom_call" | custom-call | flops 1000000 | bytes 100000 | tf_op jit(solution)/shard_map/mix/mix_tiles/pallas_call | solution.py:117
  54.3 2.3 %collective-permute-done.10.refs_3_ = bf16[66,16,128]{2,1,0:T(8,128)(2,1)S(1)} collective-permute-done((bf16[66,16,128]{2,1,0:T(8,128)(2,1)S(1)}, bf16[66,16,128]{2,1,0:T(8,128)(2,1)S(1)}, u32[]{:S(2)}, u32[]{:S(2)}) %collective-permute-start.10) | collective-permute-done | bytes 270368 | tf_op jit(solution)/shard_map/panel_rows/ppermute | solution.py:484
  56.6 3.5 %first_sum.1 = (f32[64,16,128]{2,1,0:T(8,128)S(1)}, s32[8,8,128]{2,1,0:T(8,128)S(1)}) custom-call(f32[8,128]{1,0:T(8,128)S(1)} %get-tuple-element.56.after_ref, bf16[66,16,128]{2,1,0:T(8,128)(2,1)S(1)} %constant_dynamic-update-slice_fusion.refs_0_, bf16[66,16,128]{2,1,0:T(8,128)(2,1)S(1)} %collective-permute-done.4.after_ref.refs_1_, ...), custom_call_target="tpu_custom_call" | custom-call | flops 1000000 | bytes 100000 | tf_op jit(solution)/shard_map/panel_sum/first_sum/pallas_call | solution.py:201
  60.3 2.7 %collective-permute-start.14 = (f16[64,16,128]{2,1,0:T(8,128)(2,1)S(1)}, f16[64,16,128]{2,1,0:T(8,128)(2,1)S(1)}, u32[]{:S(2)}, u32[]{:S(2)}) collective-permute-start(f16[64,16,128]{2,1,0:T(8,128)(2,1)S(1)} %get-tuple-element.78), channel_id=1, source_target_pairs={{0,1},{1,0},{2,3},{3,2},{4,5},{5,4},{6,7},{7,6},{8,9},{9,8},{10,11... | collective-permute-start | bytes 786440 | tf_op jit(solution)/shard_map/panel_cols/ppermute | solution.py:487
  63.0 0.9 collective-permute-start.16
  63.9 2.8 %collective-permute-done.15 = f16[64,16,128]{2,1,0:T(8,128)(2,1)S(1)} collective-permute-done((f16[64,16,128]{2,1,0:T(8,128)(2,1)S(1)}, f16[64,16,128]{2,1,0:T(8,128)(2,1)S(1)}, u32[]{:S(2)}, u32[]{:S(2)}) %collective-permute-start.15) | collective-permute-done | bytes 262176 | tf_op jit(solution)/shard_map/panel_cols/ppermute | solution.py:487
  66.7 3.5 %collective-permute-done.14 = f16[64,16,128]{2,1,0:T(8,128)(2,1)S(1)} collective-permute-done((f16[64,16,128]{2,1,0:T(8,128)(2,1)S(1)}, f16[64,16,128]{2,1,0:T(8,128)(2,1)S(1)}, u32[]{:S(2)}, u32[]{:S(2)}) %collective-permute-start.14) | collective-permute-done | bytes 262176 | tf_op jit(solution)/shard_map/panel_cols/ppermute | solution.py:487
  70.2 0.4 collective-permute-done.13.refs_3_
  70.6 3.5 %next_sum.1.after_ref = f32[64,16,128]{2,1,0:T(8,128)S(1)} custom-call(s32[8,8,128]{2,1,0:T(8,128)S(1)} %get-tuple-element.57.names, f32[64,16,128]{2,1,0:T(8,128)S(1)} %get-tuple-element.58.after_ref, bf16[64,16,128]{2,1,0:T(8,128)(2,1)S(1)} %constant_dynamic-update-slice_fusion.2.after_ref.refs_0_, ...), custom_call_target="tpu_custom_call" | custom-call | flops 1000000 | bytes 100000 | tf_op jit(solution)/shard_map/panel_sum/next_sum/pallas_call | solution.py:220
  74.6 2.9 %collective-permute-start.23 = (f16[64,16,128]{2,1,0:T(8,128)(2,1)S(1)}, f16[64,16,128]{2,1,0:T(8,128)(2,1)S(1)}, u32[]{:S(2)}, u32[]{:S(2)}) collective-permute-start(f16[64,16,128]{2,1,0:T(8,128)(2,1)S(1)} %convert_element_type.69), channel_id=1, source_target_pairs={{0,3},{1,2},{2,1},{3,0},{4,7},{5,6},{6,5},{7,4},{8,11},{9,10},{10,... | collective-permute-start | bytes 786440 | tf_op jit(solution)/shard_map/panel_cols/ppermute | solution.py:487
  77.5 0.4 collective-permute-start.22
  78.5 4.5 %cross_parts.2 = (f32[64,128,128]{2,1,0:T(8,128)S(1)}, f32[4,128,128]{2,1,0:T(8,128)S(1)}, f32[4,128,128]{2,1,0:T(8,128)S(1)}) custom-call(s32[3,32]{1,0:T(4,128)S(1)} %get-tuple-element.83.names_ref, s32[11]{0:T(128)S(1)} %stack.56.order_ref.after_ref, f32[64,16,128]{2,1,0:T(8,128)S(1)} %next_sum.1.after_ref, ...), custom_call_target="tpu_custom_call" | custom-call | flops 1000000 | bytes 100000 | tf_op jit(solution)/shard_map/cross0/cross_parts/pallas_call | solution.py:305
  83.0 2.5 %first_gram.1.block_ref = f32[128,128]{1,0:T(8,128)S(1)} custom-call(f32[4,128,128]{2,1,0:T(8,128)S(1)} %get-tuple-element.65.after_ref.refs_12_, f32[64,128,128]{2,1,0:T(8,128)S(1)} %get-tuple-element.66.panel.panel0), custom_call_target="tpu_custom_call" | custom-call | flops 1000000 | bytes 100000 | tf_op jit(solution)/shard_map/factor0/first_gram/pallas_call | solution.py:390
  85.6 6.1 %first_factor.1.after_ref.inverse_ref = f32[128,128]{1,0:T(8,128)S(1)} custom-call(f32[128,128]{1,0:T(8,128)S(1)} %first_gram.1.block_ref), custom_call_target="tpu_custom_call" | custom-call | flops 1000000 | bytes 100000 | tf_op jit(solution)/shard_map/factor0/first_factor/pallas_call | solution.py:407
  91.8 0.5 collective-permute-start.25
  92.3 0.4 collective-permute-start.27
  94.5 4.8 %cross_parts.3 = (f32[64,128,128]{2,1,0:T(8,128)S(1)}, f32[4,256,128]{2,1,0:T(8,128)S(1)}, f32[4,256,128]{2,1,0:T(8,128)S(1)}) custom-call(s32[3,32]{1,0:T(4,128)S(1)} %get-tuple-element.83.names_ref, s32[11]{0:T(128)S(1)} %stack.56.order_ref.after_ref, f32[128,128]{1,0:T(8,128)S(1)} %first_factor.1.after_ref.inverse_ref, ...), custom_call_target="tpu_custom_call" | custom-call | flops 1000000 | bytes 100000 | tf_op jit(solution)/shard_map/cross1/cross_parts/pallas_call | solution.py:305
  99.4 1.8 %collective-permute-done.28 = f32[4,256,128]{2,1,0:T(8,128)S(1)} collective-permute-done((f32[4,256,128]{2,1,0:T(8,128)S(1)}, f32[4,256,128]{2,1,0:T(8,128)S(1)}, u32[]{:S(2)}, u32[]{:S(2)}) %collective-permute-start.28) | collective-permute-done | bytes 524320 | tf_op jit(solution)/shard_map/cross_sum/ppermute | solution.py:478
  101.4 3.8 %collective-permute-start.31 = (f32[256,128]{1,0:T(8,128)S(1)}, f32[256,128]{1,0:T(8,128)S(1)}, u32[]{:S(2)}, u32[]{:S(2)}) collective-permute-start(f32[256,128]{1,0:T(8,128)S(1)} %get-tuple-element.80), channel_id=1, source_target_pairs={{0,24},{4,28},{8,0},{12,4},{16,8},{20,12},{24,16},{28,20},{1,25},{... | collective-permute-start | bytes 393224 | tf_op jit(solution)/shard_map/cross_sum/ppermute | solution.py:481
  105.2 0.4 collective-permute-start.30
  105.6 3.5 %second_gram.1 = (f32[128,128]{1,0:T(8,128)S(1)}, f32[128,128]{1,0:T(8,128)S(1)}) custom-call(f32[4,256,128]{2,1,0:T(8,128)S(1)} %get-tuple-element.72.after_ref, f32[64,128,128]{2,1,0:T(8,128)S(1)} %get-tuple-element.66.panel.panel0, f32[64,128,128]{2,1,0:T(8,128)S(1)} %get-tuple-element.74.panel1), custom_call_target="tpu_custom_call" | custom-call | flops 1000000 | bytes 100000 | tf_op jit(solution)/shard_map/gram1/second_gram/pallas_call | solution.py:436
  109.1 6.9 %second_factor.1 = f32[256,256]{1,0:T(8,128)S(1)} custom-call(f32[4,256,128]{2,1,0:T(8,128)S(1)} %add.52.after_ref, f32[128,128]{1,0:T(8,128)S(1)} %get-tuple-element.75.side_ref, f32[128,128]{1,0:T(8,128)S(1)} %get-tuple-element.76.block_ref, f32[128,128]{1,0:T(8,128)S(1)} %first_factor.1.after_ref.inverse_ref), custom_call_target="tpu_custom_call" | custom-call | flops 1000000 | bytes 100000 | tf_op jit(solution)/shard_map/factor1/second_factor/pallas_call | solution.py:459
  115.9 1.3 %collective-permute-done.30 = f32[256,128]{1,0:T(8,128)S(1)} collective-permute-done((f32[256,128]{1,0:T(8,128)S(1)}, f32[256,128]{1,0:T(8,128)S(1)}, u32[]{:S(2)}, u32[]{:S(2)}) %collective-permute-start.30) | collective-permute-done | bytes 131104 | tf_op jit(solution)/shard_map/cross_sum/ppermute | solution.py:481
  117.6 9.2 %all_to_all.19 = f32[8,32,128]{2,1,0:T(8,128)S(1)} all-to-all(f32[8,32,128]{2,1,0:T(8,128)S(1)} %bitcast.39), channel_id=1, replica_groups=mesh['rows'=8,'cols'=4] {'rows'}, dimensions={0} | all-to-all | bytes 262144 | tf_op jit(solution)/shard_map/solve/all_to_all | solution.py:583
  126.8 0.7 copy_bitcast_fusion
  (71 shorter events, 4.4 us)
Async XLA Ops:
  0.8 1.0 copy-start
  1.8 10.8 %copy-start.3 = (s32[32]{0:T(128)S(1)}, s32[32]{0:T(128)}, u32[]{:S(2)}) copy-start(s32[32]{0:T(128)} %param.9) | copy-start | bytes 388
  1.8 10.8 %copy-start.2 = (s32[32,2]{0,1:T(2,128)S(1)}, s32[32,2]{0,1:T(2,128)}, u32[]{:S(2)}) copy-start(s32[32,2]{0,1:T(2,128)} %param.7) | copy-start | bytes 772
  1.8 10.8 %copy-start.1 = (f32[8,128,128]{2,1,0:T(8,128)S(1)}, f32[8,128,128]{2,1,0:T(8,128)}, u32[]{:S(2)}) copy-start(f32[8,128,128]{2,1,0:T(8,128)} %mixers_ref.11) | copy-start | bytes 1572868
  5.1 15.8 %collective-permute-start = (bf16[2,32,16,128]{3,2,1,0:T(8,128)(2,1)S(1)}, bf16[2,32,16,128]{3,2,1,0:T(8,128)(2,1)S(1)}, u32[]{:S(2)}, u32[]{:S(2)}) collective-permute-start(bf16[2,32,16,128]{3,2,1,0:T(8,128)(2,1)S(1)} %get-tuple-element.44), channel_id=1, source_target_pairs={{0,1},{4,5},{8,9},{12,13},{16,17},{20,21},{24,25},{28,29}} | collective-permute-start | bytes 786440 | tf_op jit(solution)/shard_map/panel_spread/ppermute | solution.py:509
  10.0 11.0 %collective-permute-start.1 = (bf16[2,32,16,128]{3,2,1,0:T(8,128)(2,1)S(1)}, bf16[2,32,16,128]{3,2,1,0:T(8,128)(2,1)S(1)}, u32[]{:S(2)}, u32[]{:S(2)}) collective-permute-start(bf16[2,32,16,128]{3,2,1,0:T(8,128)(2,1)S(1)} %get-tuple-element.45), channel_id=1, source_target_pairs={{0,2},{4,6},{8,10},{12,14},{16,18},{20,22},{24,26},{28,30}} | collective-permute-start | bytes 786440 | tf_op jit(solution)/shard_map/panel_spread/ppermute | solution.py:509
  11.3 9.8 %collective-permute-start.2 = (bf16[2,32,16,128]{3,2,1,0:T(8,128)(2,1)S(1)}, bf16[2,32,16,128]{3,2,1,0:T(8,128)(2,1)S(1)}, u32[]{:S(2)}, u32[]{:S(2)}) collective-permute-start(bf16[2,32,16,128]{3,2,1,0:T(8,128)(2,1)S(1)} %get-tuple-element.46), channel_id=1, source_target_pairs={{0,3},{4,7},{8,11},{12,15},{16,19},{20,23},{24,27},{28,31}} | collective-permute-start | bytes 786440 | tf_op jit(solution)/shard_map/panel_spread/ppermute | solution.py:509
  21.7 1.4 %collective-permute-start.3 = (bf16[33,16,128]{2,1,0:T(8,128)(2,1)S(1)}, bf16[33,16,128]{2,1,0:T(8,128)(2,1)S(1)}, u32[]{:S(2)}, u32[]{:S(2)}) collective-permute-start(bf16[33,16,128]{2,1,0:T(8,128)(2,1)S(1)} %get-tuple-element.48), channel_id=1, source_target_pairs={{0,4},{4,0},{8,12},{12,8},{16,20},{20,16},{24,28},{28,24},{1,5},{5... | collective-permute-start | bytes 405512 | tf_op jit(solution)/shard_map/panel_spread/ppermute | solution.py:478
  23.1 15.3 %collective-permute-start.4 = (bf16[66,16,128]{2,1,0:T(8,128)(2,1)S(1)}, bf16[66,16,128]{2,1,0:T(8,128)(2,1)S(1)}, u32[]{:S(2)}, u32[]{:S(2)}) collective-permute-start(bf16[66,16,128]{2,1,0:T(8,128)(2,1)S(1)} %constant_dynamic-update-slice_fusion.refs_0_), channel_id=1, source_target_pairs={{0,16},{4,20},{8,24},{12,28},{16,0},{20,4},{24,8},{28,12},{1,17},{... | collective-permute-start | bytes 811016 | tf_op jit(solution)/shard_map/panel_rows/ppermute | solution.py:484
  29.1 10.1 %collective-permute-start.5 = (bf16[2,32,16,128]{3,2,1,0:T(8,128)(2,1)S(1)}, bf16[2,32,16,128]{3,2,1,0:T(8,128)(2,1)S(1)}, u32[]{:S(2)}, u32[]{:S(2)}) collective-permute-start(bf16[2,32,16,128]{3,2,1,0:T(8,128)(2,1)S(1)} %get-tuple-element.50), channel_id=1, source_target_pairs={{0,1},{4,5},{8,9},{12,13},{16,17},{20,21},{24,25},{28,29}} | collective-permute-start | bytes 786440 | tf_op jit(solution)/shard_map/panel_spread/ppermute | solution.py:509
  30.4 8.8 %collective-permute-start.6 = (bf16[2,32,16,128]{3,2,1,0:T(8,128)(2,1)S(1)}, bf16[2,32,16,128]{3,2,1,0:T(8,128)(2,1)S(1)}, u32[]{:S(2)}, u32[]{:S(2)}) collective-permute-start(bf16[2,32,16,128]{3,2,1,0:T(8,128)(2,1)S(1)} %get-tuple-element.51), channel_id=1, source_target_pairs={{0,2},{4,6},{8,10},{12,14},{16,18},{20,22},{24,26},{28,30}} | collective-permute-start | bytes 786440 | tf_op jit(solution)/shard_map/panel_spread/ppermute | solution.py:509
  31.7 10.2 %collective-permute-start.7 = (bf16[2,32,16,128]{3,2,1,0:T(8,128)(2,1)S(1)}, bf16[2,32,16,128]{3,2,1,0:T(8,128)(2,1)S(1)}, u32[]{:S(2)}, u32[]{:S(2)}) collective-permute-start(bf16[2,32,16,128]{3,2,1,0:T(8,128)(2,1)S(1)} %get-tuple-element.52), channel_id=1, source_target_pairs={{0,3},{4,7},{8,11},{12,15},{16,19},{20,23},{24,27},{28,31}} | collective-permute-start | bytes 786440 | tf_op jit(solution)/shard_map/panel_spread/ppermute | solution.py:509
  35.7 18.5 %collective-permute-start.9 = (bf16[66,16,128]{2,1,0:T(8,128)(2,1)S(1)}, bf16[66,16,128]{2,1,0:T(8,128)(2,1)S(1)}, u32[]{:S(2)}, u32[]{:S(2)}) collective-permute-start(bf16[66,16,128]{2,1,0:T(8,128)(2,1)S(1)} %constant_dynamic-update-slice_fusion.refs_0_), channel_id=1, source_target_pairs={{0,8},{4,12},{8,0},{12,4},{16,24},{20,28},{24,16},{28,20},{1,9},{5... | collective-permute-start | bytes 811016 | tf_op jit(solution)/shard_map/panel_rows/ppermute | solution.py:484
  38.5 18.1 %collective-permute-start.10 = (bf16[66,16,128]{2,1,0:T(8,128)(2,1)S(1)}, bf16[66,16,128]{2,1,0:T(8,128)(2,1)S(1)}, u32[]{:S(2)}, u32[]{:S(2)}) collective-permute-start(bf16[66,16,128]{2,1,0:T(8,128)(2,1)S(1)} %collective-permute-done.4.after_ref.refs_1_), channel_id=1, source_target_pairs={{0,8},{4,12},{8,0},{12,4},{16,24},{20,28},{24,16},{28,20},{1,9},{5... | collective-permute-start | bytes 811016 | tf_op jit(solution)/shard_map/panel_rows/ppermute | solution.py:484
  42.6 1.4 %collective-permute-start.8 = (bf16[32,16,128]{2,1,0:T(8,128)(2,1)S(1)}, bf16[32,16,128]{2,1,0:T(8,128)(2,1)S(1)}, u32[]{:S(2)}, u32[]{:S(2)}) collective-permute-start(bf16[32,16,128]{2,1,0:T(8,128)(2,1)S(1)} %get-tuple-element.54), channel_id=1, source_target_pairs={{0,4},{4,0},{8,12},{12,8},{16,20},{20,16},{24,28},{28,24},{1,5},{5... | collective-permute-start | bytes 393224 | tf_op jit(solution)/shard_map/panel_spread/ppermute | solution.py:478
  44.0 19.9 %collective-permute-start.12 = (bf16[64,16,128]{2,1,0:T(8,128)(2,1)S(1)}, bf16[64,16,128]{2,1,0:T(8,128)(2,1)S(1)}, u32[]{:S(2)}, u32[]{:S(2)}) collective-permute-start(bf16[64,16,128]{2,1,0:T(8,128)(2,1)S(1)} %constant_dynamic-update-slice_fusion.2.after_ref.refs_0_), channel_id=1, source_target_pairs={{0,8},{4,12},{8,0},{12,4},{16,24},{20,28},{24,16},{28,20},{1,9},{5... | collective-permute-start | bytes 786440 | tf_op jit(solution)/shard_map/panel_rows/ppermute | solution.py:484
  45.7 17.4 %collective-permute-start.11 = (bf16[64,16,128]{2,1,0:T(8,128)(2,1)S(1)}, bf16[64,16,128]{2,1,0:T(8,128)(2,1)S(1)}, u32[]{:S(2)}, u32[]{:S(2)}) collective-permute-start(bf16[64,16,128]{2,1,0:T(8,128)(2,1)S(1)} %constant_dynamic-update-slice_fusion.2.after_ref.refs_0_), channel_id=1, source_target_pairs={{0,16},{4,20},{8,24},{12,28},{16,0},{20,4},{24,8},{28,12},{1,17},{... | collective-permute-start | bytes 786440 | tf_op jit(solution)/shard_map/panel_rows/ppermute | solution.py:484
  60.3 6.4 %collective-permute-start.15 = (f16[64,16,128]{2,1,0:T(8,128)(2,1)S(1)}, f16[64,16,128]{2,1,0:T(8,128)(2,1)S(1)}, u32[]{:S(2)}, u32[]{:S(2)}) collective-permute-start(f16[64,16,128]{2,1,0:T(8,128)(2,1)S(1)} %get-tuple-element.78), channel_id=1, source_target_pairs={{0,2},{1,3},{2,0},{3,1},{4,6},{5,7},{6,4},{7,5},{8,10},{9,11},{10,... | collective-permute-start | bytes 786440 | tf_op jit(solution)/shard_map/panel_cols/ppermute | solution.py:487
  60.3 9.9 %collective-permute-start.14 = (f16[64,16,128]{2,1,0:T(8,128)(2,1)S(1)}, f16[64,16,128]{2,1,0:T(8,128)(2,1)S(1)}, u32[]{:S(2)}, u32[]{:S(2)}) collective-permute-start(f16[64,16,128]{2,1,0:T(8,128)(2,1)S(1)} %get-tuple-element.78), channel_id=1, source_target_pairs={{0,1},{1,0},{2,3},{3,2},{4,5},{5,4},{6,7},{7,6},{8,9},{9,8},{10,11... | collective-permute-start | bytes 786440 | tf_op jit(solution)/shard_map/panel_cols/ppermute | solution.py:487
  63.0 7.6 %collective-permute-start.13 = (bf16[64,16,128]{2,1,0:T(8,128)(2,1)S(1)}, bf16[64,16,128]{2,1,0:T(8,128)(2,1)S(1)}, u32[]{:S(2)}, u32[]{:S(2)}) collective-permute-start(bf16[64,16,128]{2,1,0:T(8,128)(2,1)S(1)} %collective-permute-done.11.refs_1_), channel_id=1, source_target_pairs={{0,8},{4,12},{8,0},{12,4},{16,24},{20,28},{24,16},{28,20},{1,9},{5... | collective-permute-start | bytes 786440 | tf_op jit(solution)/shard_map/panel_rows/ppermute | solution.py:484
  63.0 11.5 %collective-permute-start.16 = (f16[64,16,128]{2,1,0:T(8,128)(2,1)S(1)}, f16[64,16,128]{2,1,0:T(8,128)(2,1)S(1)}, u32[]{:S(2)}, u32[]{:S(2)}) collective-permute-start(f16[64,16,128]{2,1,0:T(8,128)(2,1)S(1)} %get-tuple-element.78), channel_id=1, source_target_pairs={{0,3},{1,2},{2,1},{3,0},{4,7},{5,6},{6,5},{7,4},{8,11},{9,10},{10,... | collective-permute-start | bytes 786440 | tf_op jit(solution)/shard_map/panel_cols/ppermute | solution.py:487
  63.9 13.6 %collective-permute-start.17 = (f16[64,16,128]{2,1,0:T(8,128)(2,1)S(1)}, f16[64,16,128]{2,1,0:T(8,128)(2,1)S(1)}, u32[]{:S(2)}, u32[]{:S(2)}) collective-permute-start(f16[64,16,128]{2,1,0:T(8,128)(2,1)S(1)} %get-tuple-element.78), channel_id=1, source_target_pairs={{0,4},{4,0},{8,12},{12,8},{16,20},{20,16},{24,28},{28,24},{1,5},{5... | collective-permute-start | bytes 786440 | tf_op jit(solution)/shard_map/panel_cores/ppermute | solution.py:478
  66.7 11.3 %collective-permute-start.19 = (f16[64,16,128]{2,1,0:T(8,128)(2,1)S(1)}, f16[64,16,128]{2,1,0:T(8,128)(2,1)S(1)}, u32[]{:S(2)}, u32[]{:S(2)}) collective-permute-start(f16[64,16,128]{2,1,0:T(8,128)(2,1)S(1)} %collective-permute-done.15), channel_id=1, source_target_pairs={{0,4},{4,0},{8,12},{12,8},{16,20},{20,16},{24,28},{28,24},{1,5},{5... | collective-permute-start | bytes 786440 | tf_op jit(solution)/shard_map/panel_cores/ppermute | solution.py:478
  70.2 8.2 %collective-permute-start.18 = (f16[64,16,128]{2,1,0:T(8,128)(2,1)S(1)}, f16[64,16,128]{2,1,0:T(8,128)(2,1)S(1)}, u32[]{:S(2)}, u32[]{:S(2)}) collective-permute-start(f16[64,16,128]{2,1,0:T(8,128)(2,1)S(1)} %collective-permute-done.14), channel_id=1, source_target_pairs={{0,4},{4,0},{8,12},{12,8},{16,20},{20,16},{24,28},{28,24},{1,5},{5... | collective-permute-start | bytes 786440 | tf_op jit(solution)/shard_map/panel_cores/ppermute | solution.py:478
  74.6 3.9 %collective-permute-start.20 = (f16[64,16,128]{2,1,0:T(8,128)(2,1)S(1)}, f16[64,16,128]{2,1,0:T(8,128)(2,1)S(1)}, u32[]{:S(2)}, u32[]{:S(2)}) collective-permute-start(f16[64,16,128]{2,1,0:T(8,128)(2,1)S(1)} %collective-permute-done.16), channel_id=1, source_target_pairs={{0,4},{4,0},{8,12},{12,8},{16,20},{20,16},{24,28},{28,24},{1,5},{5... | collective-permute-start | bytes 786440 | tf_op jit(solution)/shard_map/panel_cores/ppermute | solution.py:478
  74.6 17.1 %collective-permute-start.23 = (f16[64,16,128]{2,1,0:T(8,128)(2,1)S(1)}, f16[64,16,128]{2,1,0:T(8,128)(2,1)S(1)}, u32[]{:S(2)}, u32[]{:S(2)}) collective-permute-start(f16[64,16,128]{2,1,0:T(8,128)(2,1)S(1)} %convert_element_type.69), channel_id=1, source_target_pairs={{0,3},{1,2},{2,1},{3,0},{4,7},{5,6},{6,5},{7,4},{8,11},{9,10},{10,... | collective-permute-start | bytes 786440 | tf_op jit(solution)/shard_map/panel_cols/ppermute | solution.py:487
  77.5 14.1 %collective-permute-start.22 = (f16[64,16,128]{2,1,0:T(8,128)(2,1)S(1)}, f16[64,16,128]{2,1,0:T(8,128)(2,1)S(1)}, u32[]{:S(2)}, u32[]{:S(2)}) collective-permute-start(f16[64,16,128]{2,1,0:T(8,128)(2,1)S(1)} %convert_element_type.69), channel_id=1, source_target_pairs={{0,2},{1,3},{2,0},{3,1},{4,6},{5,7},{6,4},{7,5},{8,10},{9,11},{10,... | collective-permute-start | bytes 786440 | tf_op jit(solution)/shard_map/panel_cols/ppermute | solution.py:487
  78.0 13.7 %collective-permute-start.21 = (f16[64,16,128]{2,1,0:T(8,128)(2,1)S(1)}, f16[64,16,128]{2,1,0:T(8,128)(2,1)S(1)}, u32[]{:S(2)}, u32[]{:S(2)}) collective-permute-start(f16[64,16,128]{2,1,0:T(8,128)(2,1)S(1)} %convert_element_type.69), channel_id=1, source_target_pairs={{0,1},{1,0},{2,3},{3,2},{4,5},{5,4},{6,7},{7,6},{8,9},{9,8},{10,11... | collective-permute-start | bytes 786440 | tf_op jit(solution)/shard_map/panel_cols/ppermute | solution.py:487
  91.7 1.6 %collective-permute-start.24 = (f16[64,16,128]{2,1,0:T(8,128)(2,1)S(1)}, f16[64,16,128]{2,1,0:T(8,128)(2,1)S(1)}, u32[]{:S(2)}, u32[]{:S(2)}) collective-permute-start(f16[64,16,128]{2,1,0:T(8,128)(2,1)S(1)} %convert_element_type.69), channel_id=1, source_target_pairs={{0,4},{4,0},{8,12},{12,8},{16,20},{20,16},{24,28},{28,24},{1,5},{5... | collective-permute-start | bytes 786440 | tf_op jit(solution)/shard_map/panel_cores/ppermute | solution.py:478
  91.8 1.9 %collective-permute-start.25 = (f16[64,16,128]{2,1,0:T(8,128)(2,1)S(1)}, f16[64,16,128]{2,1,0:T(8,128)(2,1)S(1)}, u32[]{:S(2)}, u32[]{:S(2)}) collective-permute-start(f16[64,16,128]{2,1,0:T(8,128)(2,1)S(1)} %collective-permute-done.21), channel_id=1, source_target_pairs={{0,4},{4,0},{8,12},{12,8},{16,20},{20,16},{24,28},{28,24},{1,5},{5... | collective-permute-start | bytes 786440 | tf_op jit(solution)/shard_map/panel_cores/ppermute | solution.py:478
  92.3 1.8 %collective-permute-start.26 = (f16[64,16,128]{2,1,0:T(8,128)(2,1)S(1)}, f16[64,16,128]{2,1,0:T(8,128)(2,1)S(1)}, u32[]{:S(2)}, u32[]{:S(2)}) collective-permute-start(f16[64,16,128]{2,1,0:T(8,128)(2,1)S(1)} %collective-permute-done.22), channel_id=1, source_target_pairs={{0,4},{4,0},{8,12},{12,8},{16,20},{20,16},{24,28},{28,24},{1,5},{5... | collective-permute-start | bytes 786440 | tf_op jit(solution)/shard_map/panel_cores/ppermute | solution.py:478
  92.3 2.1 %collective-permute-start.27 = (f16[64,16,128]{2,1,0:T(8,128)(2,1)S(1)}, f16[64,16,128]{2,1,0:T(8,128)(2,1)S(1)}, u32[]{:S(2)}, u32[]{:S(2)}) collective-permute-start(f16[64,16,128]{2,1,0:T(8,128)(2,1)S(1)} %collective-permute-done.23), channel_id=1, source_target_pairs={{0,4},{4,0},{8,12},{12,8},{16,20},{20,16},{24,28},{28,24},{1,5},{5... | collective-permute-start | bytes 786440 | tf_op jit(solution)/shard_map/panel_cores/ppermute | solution.py:478
  99.2 2.0 %collective-permute-start.28 = (f32[4,256,128]{2,1,0:T(8,128)S(1)}, f32[4,256,128]{2,1,0:T(8,128)S(1)}, u32[]{:S(2)}, u32[]{:S(2)}) collective-permute-start(f32[4,256,128]{2,1,0:T(8,128)S(1)} %get-tuple-element.73), channel_id=1, source_target_pairs={{0,4},{4,0},{8,12},{12,8},{16,20},{20,16},{24,28},{28,24},{1,5},{5... | collective-permute-start | bytes 1572872 | tf_op jit(solution)/shard_map/cross_sum/ppermute | solution.py:478
  101.3 14.6 %collective-permute-start.29 = (f32[256,128]{1,0:T(8,128)S(1)}, f32[256,128]{1,0:T(8,128)S(1)}, u32[]{:S(2)}, u32[]{:S(2)}) collective-permute-start(f32[256,128]{1,0:T(8,128)S(1)} %get-tuple-element.79), channel_id=1, source_target_pairs={{0,8},{4,12},{8,16},{12,20},{16,24},{20,28},{24,0},{28,4},{1,9},{5... | collective-permute-start | bytes 393224 | tf_op jit(solution)/shard_map/cross_sum/ppermute | solution.py:481
  101.4 14.6 %collective-permute-start.31 = (f32[256,128]{1,0:T(8,128)S(1)}, f32[256,128]{1,0:T(8,128)S(1)}, u32[]{:S(2)}, u32[]{:S(2)}) collective-permute-start(f32[256,128]{1,0:T(8,128)S(1)} %get-tuple-element.80), channel_id=1, source_target_pairs={{0,24},{4,28},{8,0},{12,4},{16,8},{20,12},{24,16},{28,20},{1,25},{... | collective-permute-start | bytes 393224 | tf_op jit(solution)/shard_map/cross_sum/ppermute | solution.py:481
  105.2 12.1 %collective-permute-start.30 = (f32[256,128]{1,0:T(8,128)S(1)}, f32[256,128]{1,0:T(8,128)S(1)}, u32[]{:S(2)}, u32[]{:S(2)}) collective-permute-start(f32[256,128]{1,0:T(8,128)S(1)} %get-tuple-element.81), channel_id=1, source_target_pairs={{0,16},{4,20},{8,24},{12,28},{16,0},{20,4},{24,8},{28,12},{1,17},{... | collective-permute-start | bytes 393224 | tf_op jit(solution)/shard_map/cross_sum/ppermute | solution.py:481
